TPU v7x, 32 devices: a whole 2x2x4 slice. The times are simulated.
32 devices in a mesh: dp: 4 (over y, x), mp: 8 (over z, core).
Axes of the slice: x: 2, y: 2, z: 4, core: 2. Of those that a mesh axis runs over, the one named last changes fastest.
Arguments:
- hidden_policy: bfloat16 [64, 16, 2048], P('dp', None, 'mp'), may hold values from -6 to 6
- hidden_reference: bfloat16 [64, 16, 2048], P('dp', None, 'mp'), may hold values from -6 to 6
- ffn_gain_policy: float32 [2048], replicated, may hold values from 0.1 to 1.9
- ffn_gain_reference: float32 [2048], replicated, may hold values from 0.1 to 1.9
- up_policy: bfloat16 [2048, 4096], P(None, 'mp'), may hold values from -0.125 to 0.125
- up_reference: bfloat16 [2048, 4096], P(None, 'mp'), may hold values from -0.125 to 0.125
- down_policy: bfloat16 [4096, 2048], P('mp'), may hold values from -0.125 to 0.125
- down_reference: bfloat16 [4096, 2048], P('mp'), may hold values from -0.125 to 0.125
- final_gain_policy: float32 [2048], replicated, may hold values from 0.1 to 1.9
- final_gain_reference: float32 [2048], replicated, may hold values from 0.1 to 1.9
- out_policy: bfloat16 [2048, 7168], P('dp', 'mp'), may hold values from -4 to 4
- out_reference: bfloat16 [2048, 7168], P('dp', 'mp'), may hold values from -4 to 4
- move_plan: int32 [64], replicated, may hold values from 0 to 63, as said below
- lengths: int32 [64], P('dp'), may hold values from 1 to 16, 512 in all
- targets: int32 [64, 16], P('dp'), may hold values from 0 to 7167
Outputs:
- token_diff: float32 [64, 16], P('dp')
- seq_diff: float32 [64], P('dp')
Inputs may be any that keep to these rules, and one draw needn't show every extreme that they name: `move_plan`: A permutation of the slots; slot // 16 is the owning index of dp, each owning exactly 16 requests; from one index of dp to one owner go either no requests or exactly 4.
All inputs are finite; a program needn't handle non-finite values. No bound on the sum of `lengths` on one device may be relied on, other than what follows from the above.
Results may differ from a plain program's by a relative error of at most 0.0081.
Values may be sent and summed in bfloat16 or wider, within the bound.
No kernel may reach another device: no remote copies, remote signals or barrier semaphores. Data moves between devices by JAX's collectives and lax.ppermute only.
A program may use at most 64 MiB of HBM per device.

v0:
```python
import functools

import jax
import jax.numpy as jnp
from jax import lax
from jax.experimental import pallas as pl
from jax.experimental.pallas import tpu as pltpu
from jax.sharding import PartitionSpec as P

epsilon = 1e-05
params = pltpu.CompilerParams(vmem_limit_bytes=24 * 1024 * 1024)
vmem = pl.BlockSpec(memory_space=pltpu.VMEM)
smem = pl.BlockSpec(memory_space=pltpu.SMEM)


def call(kernel, out_shape, ops, scratch=()):
    specs = [smem] + [vmem] * (len(ops) - 1)
    return pl.pallas_call(
        kernel,
        out_shape=out_shape,
        in_specs=specs,
        out_specs=jax.tree.map(lambda _: vmem, out_shape),
        scratch_shapes=list(scratch),
        compiler_params=params,
    )(*ops)


def exchange(values, axis, flip):
    count = lax.axis_size(axis)
    return lax.ppermute(values, axis, [(i, i ^ flip) for i in range(count)])


def select_kernel(ids, code, *refs):
    parts, out = refs[:-1], refs[-1]
    rows = out.shape[1]
    dp = len(parts) // 2
    me = ids[0]
    wanted = me * rows + lax.broadcasted_iota(jnp.int32, (rows, code.shape[2]), 0)
    hots = [
        (code[me ^ k] == wanted).astype(jnp.float32).astype(jnp.bfloat16) for k in range(dp)
    ]
    for m in range(2):
        total = None
        for k in range(dp):
            values = parts[m * dp + k][...]
            values = values.reshape(-1, values.shape[-1])
            found = jnp.dot(hots[k], values, preferred_element_type=jnp.float32)
            total = found if total is None else total + found
        out[m] = total.astype(out.dtype)


def normalise(values, gain, chip, core, store):
    half = len(values) // 2
    width = values[0].shape[1] * len(values)
    values = [v.astype(jnp.float32) for v in values]
    center = sum(jnp.sum(v, axis=1, keepdims=True) for v in values) / width
    values = [v - center for v in values]
    spread = sum(jnp.sum(v * v, axis=1, keepdims=True) for v in values) / width
    scale = lax.rsqrt(spread + epsilon)
    for k, v in enumerate(values):
        place = 2 * (chip ^ (k % half)) + (core if k < half else 1 - core)
        store[place] = (v * scale * gain[place]).astype(jnp.bfloat16)
    return values[0]


def ffn_kernel(half, ids, *refs):
    gains, ups, downs = refs[:2], refs[2:4], refs[4:6]
    parts = refs[6 : 6 + 2 * half]
    keep, send, normed, terms = refs[6 + 2 * half :]
    chip, core = ids[1], ids[2]
    for m in range(2):
        up, down = ups[m], downs[m]
        base = normalise([part[m] for part in parts], gains[m], chip, core, normed.at[m])
        part = base.shape[1]
        pre = None
        for b in range(2 * half):
            piece = jnp.dot(
                normed[m, b], up[b * part : (b + 1) * part, :], preferred_element_type=jnp.float32
            )
            pre = piece if pre is None else pre + piece
        units = jax.nn.gelu(pre).astype(jnp.bfloat16)
        full = jnp.dot(units, down[...], preferred_element_type=jnp.float32)
        for b in range(2 * half):
            terms[m, b] = full[:, b * part : (b + 1) * part]
        for k in range(half):
            place = 2 * (chip ^ k)
            kept = terms[m, place + core]
            keep[k, m] = kept + base if k == 0 else kept
            send[k, m] = terms[m, place + 1 - core].astype(jnp.bfloat16)


def pair_kernel(ids, keep, came, own, *outs):
    own[...] = keep[0] + came[0].astype(jnp.float32)
    for k, out in enumerate(outs):
        out[...] = (keep[k + 1] + came[k + 1].astype(jnp.float32)).astype(jnp.bfloat16)


def score_kernel(half, ids, wanted, *refs):
    gains, refs = refs[:2], refs[2:]
    parts, refs = refs[: 2 * half], refs[2 * half :]
    outs, (stats, normed) = refs[:-2], refs[-2:]
    dp = len(outs) // 2
    me, chip, core = ids[0], ids[1], ids[2]
    lane = lax.broadcasted_iota(jnp.int32, (parts[0].shape[1], 128), 1)
    table = jnp.zeros(lane.shape, jnp.float32)
    ratio = 2 * half // dp
    for m in range(2):
        normalise([part[m] for part in parts], gains[m], chip, core, normed.at[m])
        part = parts[0].shape[2]
        logits = None
        for k in range(dp):
            for b in range(ratio):
                piece = jnp.dot(
                    normed[m, (me ^ k) * ratio + b],
                    outs[m * dp + k][b * part : (b + 1) * part, :],
                    preferred_element_type=jnp.float32,
                )
                logits = piece if logits is None else logits + piece
        entries = lax.broadcasted_iota(jnp.int32, logits.shape, 1) + ids[3] * logits.shape[1]
        picked = jnp.sum(jnp.where(entries == wanted[...], logits, 0.0), axis=1, keepdims=True)
        top = jnp.max(logits, axis=1, keepdims=True)
        total = jnp.sum(jnp.exp(logits - top), axis=1, keepdims=True)
        table = jnp.where(lane == m, top, table)
        table = jnp.where(lane == 2 + m, total, table)
        table = jnp.where(lane == 4 + m, picked, table)
    stats[...] = jnp.transpose(table)[:8]


def merge(ids, mine, came):
    top = jnp.maximum(mine[0:2], came[0:2])
    total = mine[2:4] * jnp.exp(mine[0:2] - top) + came[2:4] * jnp.exp(came[0:2] - top)
    return top, total, mine[4:6] + came[4:6]


def merge_kernel(ids, mine, came, out):
    out[0:2], out[2:4], out[4:6] = merge(ids, mine, came)
    out[6:8] = jnp.zeros((2, out.shape[1]), jnp.float32)


def last_kernel(ids, mine, came, out):
    top, total, picked = merge(ids, mine, came)
    logprob = picked - (top + jnp.log(total))
    out[...] = logprob[0:1] - logprob[1:2]


def local(
    hidden_policy,
    hidden_reference,
    ffn_gain_policy,
    ffn_gain_reference,
    up_policy,
    up_reference,
    down_policy,
    down_reference,
    final_gain_policy,
    final_gain_reference,
    out_policy,
    out_reference,
    move_plan,
    lengths,
    targets,
):
    dp = lax.axis_size("dp")
    mp = lax.axis_size("mp")
    half = mp // 2
    dp_index = lax.axis_index("dp")
    mp_index = lax.axis_index("mp")
    ids = jnp.stack([dp_index, mp_index // 2, mp_index % 2, mp_index]).astype(jnp.int32)
    reqs, slots, part = hidden_policy.shape
    here = reqs * slots
    rows = here // 2
    ffn_gains = (ffn_gain_policy.reshape(mp, 1, part), ffn_gain_reference.reshape(mp, 1, part))
    final_gains = (
        final_gain_policy.reshape(mp, 1, part),
        final_gain_reference.reshape(mp, 1, part),
    )
    bits = [1 << b for b in range(dp.bit_length() - 1)]

    hidden_parts = []
    for hidden in (hidden_policy, hidden_reference):
        hidden_parts += [hidden] + [exchange(hidden, "dp", k) for k in range(1, dp)]
    facts = jnp.concatenate([lengths, targets.reshape(here)])
    relative = jnp.stack([facts] + [exchange(facts, "dp", k) for k in range(1, dp)])
    order = jnp.arange(dp, dtype=jnp.int32)
    place = (order[:, None] ^ dp_index) == order[None, :]
    facts = jnp.sum(jnp.where(place[:, :, None], relative[None], 0), axis=1)
    all_lengths = facts[:, :reqs].reshape(-1)
    all_targets = facts[:, reqs:].reshape(-1)
    slot_ids = jnp.arange(dp * reqs, dtype=jnp.int32)
    positions = jnp.arange(slots, dtype=jnp.int32)

    def codes(slot):
        start = jnp.sum(jnp.where(slot_ids[None] < slot[:, None], all_lengths[None], 0), axis=1)
        live = jnp.sum(jnp.where(slot_ids[None] == slot[:, None], all_lengths[None], 0), axis=1)
        return jnp.where(
            positions[None] < live[:, None], start[:, None] + positions[None], jnp.int32(-1)
        )

    bit_orders = []
    for m in range(2):
        bit_orders.append([bits[(b ^ m) if (b ^ m) < len(bits) else b] for b in range(len(bits))])
    outs = [{0: out_policy}, {0: out_reference}]
    newest = [{0: -1}, {0: -1}]

    def forward(after):
        flat = [outs[m][k] for m in range(2) for k in newest[m]]
        after, *flat = lax.optimization_barrier((after, *flat))
        sent = []
        for m in range(2):
            for k, step in newest[m].items():
                outs[m][k] = flat.pop(0)
                sent += [(m, k, later) for later in range(step + 1, len(bits))]
            newest[m] = {}
        for m, k, step in sorted(sent, key=lambda item: item[2]):
            place = k ^ bit_orders[m][step]
            outs[m][place] = exchange(outs[m][k], "dp", bit_orders[m][step])
            newest[m][place] = step
        return after

    source_code = forward(codes(move_plan).reshape(dp, 1, here))
    moved = call(
        select_kernel,
        jax.ShapeDtypeStruct((2, rows, part), jnp.bfloat16),
        (ids, source_code, *hidden_parts),
    )

    far = sorted(range(1, half), key=lambda k: (k.bit_length() <= 1, k))

    def gather_pair(own):
        same = {0: own}
        for k in far:
            same[k] = exchange(own, "mp", 2 * k)
        same = [same[k] for k in range(half)]
        return same + [exchange(v, "mp", 1) for v in same]

    normed_scratch = pltpu.VMEM((2, mp, rows, part), jnp.bfloat16)
    block = jax.ShapeDtypeStruct((2, rows, part), jnp.bfloat16)
    keep, send = call(
        functools.partial(ffn_kernel, half),
        (
            jax.ShapeDtypeStruct((half, 2, rows, part), jnp.float32),
            jax.ShapeDtypeStruct((half, 2, rows, part), jnp.bfloat16),
        ),
        (
            ids,
            *ffn_gains,
            up_policy,
            up_reference,
            down_policy,
            down_reference,
            *gather_pair(moved),
        ),
        [normed_scratch, pltpu.VMEM((2, mp, rows, part), jnp.float32)],
    )
    came = exchange(send, "mp", 1)
    own, *pieces = call(
        pair_kernel,
        (jax.ShapeDtypeStruct((2, rows, part), jnp.float32),) + (block,) * (half - 1),
        (ids, keep, came),
    )
    arrived = {k: exchange(pieces[k - 1], "mp", 2 * k) for k in far}
    for k in range(1, half):
        own = own + arrived[k].astype(jnp.float32)
    stream = own.astype(jnp.bfloat16)
    for step in range(1, len(bits)):
        stream = forward(stream)

    owner_code = codes(slot_ids).reshape(-1)
    my_ranks = dp_index * rows + jnp.arange(rows, dtype=jnp.int32)
    wanted = jnp.sum(
        jnp.where(owner_code[None] == my_ranks[:, None], all_targets[None], 0),
        axis=1,
        keepdims=True,
    )
    stats = call(
        functools.partial(score_kernel, half),
        jax.ShapeDtypeStruct((8, rows), jnp.float32),
        (
            ids,
            wanted,
            *final_gains,
            *gather_pair(stream),
            *[outs[m][k] for m in range(2) for k in range(dp)],
        ),
        [normed_scratch],
    )
    flips = [1 << b for b in range(mp.bit_length() - 1)]
    for flip in flips[:-1]:
        stats = call(
            merge_kernel,
            jax.ShapeDtypeStruct((8, rows), jnp.float32),
            (ids, stats, exchange(stats, "mp", flip)),
        )
    diff = call(
        last_kernel,
        jax.ShapeDtypeStruct((1, rows), jnp.float32),
        (ids, stats, exchange(stats, "mp", flips[-1])),
    )
    for bit in bits:
        diff = jnp.concatenate([diff, exchange(diff, "dp", bit)])
    ranks = (order ^ dp_index)[:, None] * rows + jnp.arange(rows, dtype=jnp.int32)[None]
    my_code = codes(dp_index * reqs + jnp.arange(reqs, dtype=jnp.int32))
    hit = my_code[:, :, None] == ranks.reshape(1, 1, -1)
    token_diff = jnp.sum(jnp.where(hit, diff.reshape(1, 1, -1), 0.0), axis=2)
    return (token_diff, jnp.sum(token_diff, axis=1))


def solution(mesh):
    return jax.shard_map(
        local,
        mesh=mesh,
        in_specs=(
            P("dp", None, "mp"),
            P("dp", None, "mp"),
            P(),
            P(),
            P(None, "mp"),
            P(None, "mp"),
            P("mp", None),
            P("mp", None),
            P(),
            P(),
            P("dp", "mp"),
            P("dp", "mp"),
            P(),
            P("dp"),
            P("dp", None),
        ),
        out_specs=(P("dp", None), P("dp")),
        check_vma=False,
    )
```

profile of v0, /device:TPU:0, one launch (start us, length us, event | category | flops | bytes accessed | tf_op | source)
XLA Modules:
  0.0 141.7 jit_solution(14855369445360833860)
XLA Ops:
  2.1 2.9 %collective-permute-start = (s32[272]{0:T(512)S(1)}, s32[272]{0:T(512)S(1)}, u32[]{:S(2)}, u32[]{:S(2)}) collective-permute-start(s32[272]{0:T(512)S(1)} %pad_add_fusion.1), channel_id=1, source_target_pairs={{0,8},{8,0},{16,24},{24,16},{1,9},{9,1},{17,25},{25,17},{2,10},{10... | collective-permute-start | bytes 3272 | tf_op jit(solution)/shard_map/ppermute | solution.py:30
  6.6 2.0 %collective-permute-start.3 = (bf16[16,16,256]{2,1,0:T(8,128)(2,1)}, bf16[16,16,256]{2,1,0:T(8,128)(2,1)S(1)}, u32[]{:S(2)}, u32[]{:S(2)}) collective-permute-start(bf16[16,16,256]{2,1,0:T(8,128)(2,1)} %refs_0_.1), channel_id=1, source_target_pairs={{0,8},{8,0},{16,24},{24,16},{1,9},{9,1},{17,25},{25,17},{2,10},{10... | collective-permute-start | bytes 393224 | tf_op jit(solution)/shard_map/ppermute | solution.py:30
  10.4 1.9 %collective-permute-start.6 = (bf16[16,16,256]{2,1,0:T(8,128)(2,1)}, bf16[16,16,256]{2,1,0:T(8,128)(2,1)S(1)}, u32[]{:S(2)}, u32[]{:S(2)}) collective-permute-start(bf16[16,16,256]{2,1,0:T(8,128)(2,1)} %refs_4_.2), channel_id=1, source_target_pairs={{0,8},{8,0},{16,24},{24,16},{1,9},{9,1},{17,25},{25,17},{2,10},{10... | collective-permute-start | bytes 393224 | tf_op jit(solution)/shard_map/ppermute | solution.py:30
  16.1 2.1 %collective-permute-done.4.refs_2_ = bf16[16,16,256]{2,1,0:T(8,128)(2,1)S(1)} collective-permute-done((bf16[16,16,256]{2,1,0:T(8,128)(2,1)}, bf16[16,16,256]{2,1,0:T(8,128)(2,1)S(1)}, u32[]{:S(2)}, u32[]{:S(2)}) %collective-permute-start.4) | collective-permute-done | bytes 131104 | tf_op jit(solution)/shard_map/ppermute | solution.py:30
  18.8 3.3 %collective-permute-done.7.refs_6_ = bf16[16,16,256]{2,1,0:T(8,128)(2,1)S(1)} collective-permute-done((bf16[16,16,256]{2,1,0:T(8,128)(2,1)}, bf16[16,16,256]{2,1,0:T(8,128)(2,1)S(1)}, u32[]{:S(2)}, u32[]{:S(2)}) %collective-permute-start.7) | collective-permute-done | bytes 131104 | tf_op jit(solution)/shard_map/ppermute | solution.py:30
  26.5 2.6 %collective-permute-start.10 = (bf16[2,128,256]{2,1,0:T(8,128)(2,1)S(1)}, bf16[2,128,256]{2,1,0:T(8,128)(2,1)S(1)}, u32[]{:S(2)}, u32[]{:S(2)}) collective-permute-start(bf16[2,128,256]{2,1,0:T(8,128)(2,1)S(1)} %shard_map.158.refs_6_), channel_id=1, source_target_pairs={{0,4},{1,5},{2,6},{3,7},{4,0},{5,1},{6,2},{7,3},{8,12},{9,13},{10,... | collective-permute-start | bytes 393224 | tf_op jit(solution)/shard_map/ppermute | solution.py:30
  30.4 6.8 %collective-permute-done.10.refs_8_ = bf16[2,128,256]{2,1,0:T(8,128)(2,1)S(1)} collective-permute-done((bf16[2,128,256]{2,1,0:T(8,128)(2,1)S(1)}, bf16[2,128,256]{2,1,0:T(8,128)(2,1)S(1)}, u32[]{:S(2)}, u32[]{:S(2)}) %collective-permute-start.10) | collective-permute-done | bytes 131104 | tf_op jit(solution)/shard_map/ppermute | solution.py:30
  46.5 3.0 %shard_map.159 = (f32[4,2,128,256]{3,2,1,0:T(8,128)S(1)}, bf16[4,2,128,256]{3,2,1,0:T(8,128)(2,1)S(1)}) custom-call(s32[4]{0:T(128)S(1)} %pad_add_fusion.2.ids, f32[8,1,256]{2,1,0:T(1,128)S(1)} %bitcast.16, f32[8,1,256]{2,1,0:T(1,128)S(1)} %bitcast.17, bf16[2048,512]{1,0:T(8,128)(2,1)S(1)} %copy-done, bf16[2048,512]{1,0:T(8,128)(2,1)S(1)} %copy-done.1, ...), custom_call_target="tpu_custom_call" | custom-call | tf_op jit(solution)/shard_map/pallas_call | solution.py:18
  54.7 1.7 %collective-permute-start.17 = (bf16[2,128,256]{2,1,0:T(8,128)(2,1)S(1)}, bf16[2,128,256]{2,1,0:T(8,128)(2,1)S(1)}, u32[]{:S(2)}, u32[]{:S(2)}) collective-permute-start(bf16[2,128,256]{2,1,0:T(8,128)(2,1)S(1)} %get-tuple-element.20), channel_id=1, source_target_pairs={{0,2},{1,3},{2,0},{3,1},{4,6},{5,7},{6,4},{7,5},{8,10},{9,11},{10,... | collective-permute-start | bytes 393224 | tf_op jit(solution)/shard_map/ppermute | solution.py:30
  56.3 3.4 %collective-permute-done.17 = bf16[2,128,256]{2,1,0:T(8,128)(2,1)S(1)} collective-permute-done((bf16[2,128,256]{2,1,0:T(8,128)(2,1)S(1)}, bf16[2,128,256]{2,1,0:T(8,128)(2,1)S(1)}, u32[]{:S(2)}, u32[]{:S(2)}) %collective-permute-start.17) | collective-permute-done | bytes 131104 | tf_op jit(solution)/shard_map/ppermute | solution.py:30
  59.7 2.7 %collective-permute-start.18 = (bf16[2,128,256]{2,1,0:T(8,128)(2,1)S(1)}, bf16[2,128,256]{2,1,0:T(8,128)(2,1)S(1)}, u32[]{:S(2)}, u32[]{:S(2)}) collective-permute-start(bf16[2,128,256]{2,1,0:T(8,128)(2,1)S(1)} %get-tuple-element.21), channel_id=1, source_target_pairs={{0,4},{1,5},{2,6},{3,7},{4,0},{5,1},{6,2},{7,3},{8,12},{9,13},{10,... | collective-permute-start | bytes 393224 | tf_op jit(solution)/shard_map/ppermute | solution.py:30
  62.4 5.3 %collective-permute-done.18 = bf16[2,128,256]{2,1,0:T(8,128)(2,1)S(1)} collective-permute-done((bf16[2,128,256]{2,1,0:T(8,128)(2,1)S(1)}, bf16[2,128,256]{2,1,0:T(8,128)(2,1)S(1)}, u32[]{:S(2)}, u32[]{:S(2)}) %collective-permute-start.18) | collective-permute-done | bytes 131104 | tf_op jit(solution)/shard_map/ppermute | solution.py:30
  67.6 2.2 %collective-permute-start.19 = (bf16[2,128,256]{2,1,0:T(8,128)(2,1)S(1)}, bf16[2,128,256]{2,1,0:T(8,128)(2,1)S(1)}, u32[]{:S(2)}, u32[]{:S(2)}) collective-permute-start(bf16[2,128,256]{2,1,0:T(8,128)(2,1)S(1)} %get-tuple-element.22), channel_id=1, source_target_pairs={{0,6},{1,7},{2,4},{3,5},{4,2},{5,3},{6,0},{7,1},{8,14},{9,15},{10,... | collective-permute-start | bytes 393224 | tf_op jit(solution)/shard_map/ppermute | solution.py:30
  69.8 4.6 %collective-permute-done.19 = bf16[2,128,256]{2,1,0:T(8,128)(2,1)S(1)} collective-permute-done((bf16[2,128,256]{2,1,0:T(8,128)(2,1)S(1)}, bf16[2,128,256]{2,1,0:T(8,128)(2,1)S(1)}, u32[]{:S(2)}, u32[]{:S(2)}) %collective-permute-start.19) | collective-permute-done | bytes 131104 | tf_op jit(solution)/shard_map/ppermute | solution.py:30
  75.4 17.7 %collective-permute-done.22.refs_16_ = bf16[512,896]{1,0:T(8,128)(2,1)} collective-permute-done((bf16[512,896]{1,0:T(8,128)(2,1)S(1)}, bf16[512,896]{1,0:T(8,128)(2,1)}, u32[]{:S(2)}, u32[]{:S(2)}) %collective-permute-start.22) | collective-permute-done | bytes 917536 | tf_op jit(solution)/shard_map/ppermute | solution.py:30
  95.9 1.8 %collective-permute-start.24 = (bf16[2,128,256]{2,1,0:T(8,128)(2,1)S(1)}, bf16[2,128,256]{2,1,0:T(8,128)(2,1)S(1)}, u32[]{:S(2)}, u32[]{:S(2)}) collective-permute-start(bf16[2,128,256]{2,1,0:T(8,128)(2,1)S(1)} %add_convert_fusion.refs_2_), channel_id=1, source_target_pairs={{0,2},{1,3},{2,0},{3,1},{4,6},{5,7},{6,4},{7,5},{8,10},{9,11},{10,... | collective-permute-start | bytes 393224 | tf_op jit(solution)/shard_map/ppermute | solution.py:30
  100.3 2.0 %collective-permute-done.24.refs_3_ = bf16[2,128,256]{2,1,0:T(8,128)(2,1)S(1)} collective-permute-done((bf16[2,128,256]{2,1,0:T(8,128)(2,1)S(1)}, bf16[2,128,256]{2,1,0:T(8,128)(2,1)S(1)}, u32[]{:S(2)}, u32[]{:S(2)}) %collective-permute-start.24) | collective-permute-done | bytes 131104 | tf_op jit(solution)/shard_map/ppermute | solution.py:30
  102.4 7.1 %collective-permute-done.25.refs_4_ = bf16[2,128,256]{2,1,0:T(8,128)(2,1)S(1)} collective-permute-done((bf16[2,128,256]{2,1,0:T(8,128)(2,1)S(1)}, bf16[2,128,256]{2,1,0:T(8,128)(2,1)S(1)}, u32[]{:S(2)}, u32[]{:S(2)}) %collective-permute-start.25) | collective-permute-done | bytes 131104 | tf_op jit(solution)/shard_map/ppermute | solution.py:30
  111.4 4.0 %collective-permute-done.31.refs_13_ = bf16[512,896]{1,0:T(8,128)(2,1)} collective-permute-done((bf16[512,896]{1,0:T(8,128)(2,1)S(1)}, bf16[512,896]{1,0:T(8,128)(2,1)}, u32[]{:S(2)}, u32[]{:S(2)}) %collective-permute-start.31) | collective-permute-done | bytes 917536 | tf_op jit(solution)/shard_map/ppermute | solution.py:30
  118.2 4.1 %shard_map.161.mine = f32[8,128]{1,0:T(8,128)S(1)} custom-call(s32[4]{0:T(128)S(1)} %pad_add_fusion.2.ids, s32[128,1]{1,0:T(8,128)S(1)} %copy.19.wanted, f32[8,1,256]{2,1,0:T(1,128)S(1)} %bitcast.18, f32[8,1,256]{2,1,0:T(1,128)S(1)} %bitcast.19, bf16[2,128,256]{2,1,0:T(8,128)(2,1)S(1)} %add_convert_fusion.refs_2_, ...), custom_call_target="tpu_custom_call" | custom-call | tf_op jit(solution)/shard_map/pallas_call | solution.py:18
  124.1 2.0 %collective-permute-start.34 = (f32[8,128]{1,0:T(8,128)S(1)}, f32[8,128]{1,0:T(8,128)S(1)}, u32[]{:S(2)}, u32[]{:S(2)}) collective-permute-start(f32[8,128]{1,0:T(8,128)S(1)} %shard_map.162.mine), channel_id=1, source_target_pairs={{0,2},{1,3},{2,0},{3,1},{4,6},{5,7},{6,4},{7,5},{8,10},{9,11},{10,... | collective-permute-start | bytes 12296 | tf_op jit(solution)/shard_map/ppermute | solution.py:30
  128.4 3.1 %collective-permute-start.35 = (f32[8,128]{1,0:T(8,128)S(1)}, f32[8,128]{1,0:T(8,128)S(1)}, u32[]{:S(2)}, u32[]{:S(2)}) collective-permute-start(f32[8,128]{1,0:T(8,128)S(1)} %shard_map.163.mine), channel_id=1, source_target_pairs={{0,4},{1,5},{2,6},{3,7},{4,0},{5,1},{6,2},{7,3},{8,12},{9,13},{10,... | collective-permute-start | bytes 12296 | tf_op jit(solution)/shard_map/ppermute | solution.py:30
  135.2 2.0 %collective-permute-done.36 = f32[1,128]{1,0:T(1,128)S(1)} collective-permute-done((f32[1,128]{1,0:T(1,128)S(1)}, f32[1,128]{1,0:T(1,128)S(1)}, u32[]{:S(2)}, u32[]{:S(2)}) %collective-permute-start.36) | collective-permute-done | bytes 544 | tf_op jit(solution)/shard_map/ppermute | solution.py:30
  138.8 2.0 %collective-permute-done.37 = f32[2,128]{1,0:T(2,128)S(1)} collective-permute-done((f32[2,128]{1,0:T(2,128)S(1)}, f32[2,128]{1,0:T(2,128)S(1)}, u32[]{:S(2)}, u32[]{:S(2)}) %collective-permute-start.37) | collective-permute-done | bytes 1056 | tf_op jit(solution)/shard_map/ppermute | solution.py:30
  (130 shorter events, 50.7 us)
Async XLA Ops:
  2.1 8.2 %collective-permute-start = (s32[272]{0:T(512)S(1)}, s32[272]{0:T(512)S(1)}, u32[]{:S(2)}, u32[]{:S(2)}) collective-permute-start(s32[272]{0:T(512)S(1)} %pad_add_fusion.1), channel_id=1, source_target_pairs={{0,8},{8,0},{16,24},{24,16},{1,9},{9,1},{17,25},{25,17},{2,10},{10... | collective-permute-start | bytes 3272 | tf_op jit(solution)/shard_map/ppermute | solution.py:30
  6.6 5.8 %collective-permute-start.2 = (s32[272]{0:T(512)S(1)}, s32[272]{0:T(512)S(1)}, u32[]{:S(2)}, u32[]{:S(2)}) collective-permute-start(s32[272]{0:T(512)S(1)} %pad_add_fusion.1), channel_id=1, source_target_pairs={{0,24},{8,16},{16,8},{24,0},{1,25},{9,17},{17,9},{25,1},{2,26},{10... | collective-permute-start | bytes 3272 | tf_op jit(solution)/shard_map/ppermute | solution.py:30
  6.6 8.9 %collective-permute-start.3 = (bf16[16,16,256]{2,1,0:T(8,128)(2,1)}, bf16[16,16,256]{2,1,0:T(8,128)(2,1)S(1)}, u32[]{:S(2)}, u32[]{:S(2)}) collective-permute-start(bf16[16,16,256]{2,1,0:T(8,128)(2,1)} %refs_0_.1), channel_id=1, source_target_pairs={{0,8},{8,0},{16,24},{24,16},{1,9},{9,1},{17,25},{25,17},{2,10},{10... | collective-permute-start | bytes 393224 | tf_op jit(solution)/shard_map/ppermute | solution.py:30
  8.6 9.6 %collective-permute-start.4 = (bf16[16,16,256]{2,1,0:T(8,128)(2,1)}, bf16[16,16,256]{2,1,0:T(8,128)(2,1)S(1)}, u32[]{:S(2)}, u32[]{:S(2)}) collective-permute-start(bf16[16,16,256]{2,1,0:T(8,128)(2,1)} %refs_0_.1), channel_id=1, source_target_pairs={{0,16},{8,24},{16,0},{24,8},{1,17},{9,25},{17,1},{25,9},{2,18},{10... | collective-permute-start | bytes 393224 | tf_op jit(solution)/shard_map/ppermute | solution.py:30
  10.3 7.8 %collective-permute-start.5 = (bf16[16,16,256]{2,1,0:T(8,128)(2,1)}, bf16[16,16,256]{2,1,0:T(8,128)(2,1)S(1)}, u32[]{:S(2)}, u32[]{:S(2)}) collective-permute-start(bf16[16,16,256]{2,1,0:T(8,128)(2,1)} %refs_0_.1), channel_id=1, source_target_pairs={{0,24},{8,16},{16,8},{24,0},{1,25},{9,17},{17,9},{25,1},{2,26},{10... | collective-permute-start | bytes 393224 | tf_op jit(solution)/shard_map/ppermute | solution.py:30
  10.4 8.4 %collective-permute-start.6 = (bf16[16,16,256]{2,1,0:T(8,128)(2,1)}, bf16[16,16,256]{2,1,0:T(8,128)(2,1)S(1)}, u32[]{:S(2)}, u32[]{:S(2)}) collective-permute-start(bf16[16,16,256]{2,1,0:T(8,128)(2,1)} %refs_4_.2), channel_id=1, source_target_pairs={{0,8},{8,0},{16,24},{24,16},{1,9},{9,1},{17,25},{25,17},{2,10},{10... | collective-permute-start | bytes 393224 | tf_op jit(solution)/shard_map/ppermute | solution.py:30
  12.4 9.8 %collective-permute-start.7 = (bf16[16,16,256]{2,1,0:T(8,128)(2,1)}, bf16[16,16,256]{2,1,0:T(8,128)(2,1)S(1)}, u32[]{:S(2)}, u32[]{:S(2)}) collective-permute-start(bf16[16,16,256]{2,1,0:T(8,128)(2,1)} %refs_4_.2), channel_id=1, source_target_pairs={{0,16},{8,24},{16,0},{24,8},{1,17},{9,25},{17,1},{25,9},{2,18},{10... | collective-permute-start | bytes 393224 | tf_op jit(solution)/shard_map/ppermute | solution.py:30
  15.5 6.7 %collective-permute-start.8 = (bf16[16,16,256]{2,1,0:T(8,128)(2,1)}, bf16[16,16,256]{2,1,0:T(8,128)(2,1)S(1)}, u32[]{:S(2)}, u32[]{:S(2)}) collective-permute-start(bf16[16,16,256]{2,1,0:T(8,128)(2,1)} %refs_4_.2), channel_id=1, source_target_pairs={{0,24},{8,16},{16,8},{24,0},{1,25},{9,17},{17,9},{25,1},{2,26},{10... | collective-permute-start | bytes 393224 | tf_op jit(solution)/shard_map/ppermute | solution.py:30
  26.5 10.7 %collective-permute-start.10 = (bf16[2,128,256]{2,1,0:T(8,128)(2,1)S(1)}, bf16[2,128,256]{2,1,0:T(8,128)(2,1)S(1)}, u32[]{:S(2)}, u32[]{:S(2)}) collective-permute-start(bf16[2,128,256]{2,1,0:T(8,128)(2,1)S(1)} %shard_map.158.refs_6_), channel_id=1, source_target_pairs={{0,4},{1,5},{2,6},{3,7},{4,0},{5,1},{6,2},{7,3},{8,12},{9,13},{10,... | collective-permute-start | bytes 393224 | tf_op jit(solution)/shard_map/ppermute | solution.py:30
  29.1 8.2 %collective-permute-start.11 = (bf16[2,128,256]{2,1,0:T(8,128)(2,1)S(1)}, bf16[2,128,256]{2,1,0:T(8,128)(2,1)S(1)}, u32[]{:S(2)}, u32[]{:S(2)}) collective-permute-start(bf16[2,128,256]{2,1,0:T(8,128)(2,1)S(1)} %shard_map.158.refs_6_), channel_id=1, source_target_pairs={{0,6},{1,7},{2,4},{3,5},{4,2},{5,3},{6,0},{7,1},{8,14},{9,15},{10,... | collective-permute-start | bytes 393224 | tf_op jit(solution)/shard_map/ppermute | solution.py:30
  29.3 8.4 %collective-permute-start.12 = (bf16[2,128,256]{2,1,0:T(8,128)(2,1)S(1)}, bf16[2,128,256]{2,1,0:T(8,128)(2,1)S(1)}, u32[]{:S(2)}, u32[]{:S(2)}) collective-permute-start(bf16[2,128,256]{2,1,0:T(8,128)(2,1)S(1)} %shard_map.158.refs_6_), channel_id=1, source_target_pairs={{0,1},{1,0},{2,3},{3,2},{4,5},{5,4},{6,7},{7,6},{8,9},{9,8},{10,11... | collective-permute-start | bytes 393224 | tf_op jit(solution)/shard_map/ppermute | solution.py:30
  30.4 7.3 %collective-permute-start.13 = (bf16[2,128,256]{2,1,0:T(8,128)(2,1)S(1)}, bf16[2,128,256]{2,1,0:T(8,128)(2,1)S(1)}, u32[]{:S(2)}, u32[]{:S(2)}) collective-permute-start(bf16[2,128,256]{2,1,0:T(8,128)(2,1)S(1)} %collective-permute-done.9.refs_7_), channel_id=1, source_target_pairs={{0,1},{1,0},{2,3},{3,2},{4,5},{5,4},{6,7},{7,6},{8,9},{9,8},{10,11... | collective-permute-start | bytes 393224 | tf_op jit(solution)/shard_map/ppermute | solution.py:30
  50.0 24.5 %collective-permute-start.20 = (bf16[512,896]{1,0:T(8,128)(2,1)S(1)}, bf16[512,896]{1,0:T(8,128)(2,1)S(1)}, u32[]{:S(2)}, u32[]{:S(2)}) collective-permute-start(bf16[512,896]{1,0:T(8,128)(2,1)S(1)} %copy-done.4), channel_id=1, source_target_pairs={{0,8},{8,0},{16,24},{24,16},{1,9},{9,1},{17,25},{25,17},{2,10},{10... | collective-permute-start | bytes 2752520 | tf_op jit(solution)/shard_map/ppermute | solution.py:30
  51.2 23.3 %collective-permute-start.21 = (bf16[512,896]{1,0:T(8,128)(2,1)S(1)}, bf16[512,896]{1,0:T(8,128)(2,1)S(1)}, u32[]{:S(2)}, u32[]{:S(2)}) collective-permute-start(bf16[512,896]{1,0:T(8,128)(2,1)S(1)} %copy-done.4), channel_id=1, source_target_pairs={{0,16},{8,24},{16,0},{24,8},{1,17},{9,25},{17,1},{25,9},{2,18},{10... | collective-permute-start | bytes 2752520 | tf_op jit(solution)/shard_map/ppermute | solution.py:30
  51.7 41.4 %collective-permute-start.22 = (bf16[512,896]{1,0:T(8,128)(2,1)S(1)}, bf16[512,896]{1,0:T(8,128)(2,1)}, u32[]{:S(2)}, u32[]{:S(2)}) collective-permute-start(bf16[512,896]{1,0:T(8,128)(2,1)S(1)} %copy-done.5), channel_id=1, source_target_pairs={{0,16},{8,24},{16,0},{24,8},{1,17},{9,25},{17,1},{25,9},{2,18},{10... | collective-permute-start | bytes 2752520 | tf_op jit(solution)/shard_map/ppermute | solution.py:30
  53.2 39.9 %collective-permute-start.23 = (bf16[512,896]{1,0:T(8,128)(2,1)S(1)}, bf16[512,896]{1,0:T(8,128)(2,1)S(1)}, u32[]{:S(2)}, u32[]{:S(2)}) collective-permute-start(bf16[512,896]{1,0:T(8,128)(2,1)S(1)} %copy-done.5), channel_id=1, source_target_pairs={{0,8},{8,0},{16,24},{24,16},{1,9},{9,1},{17,25},{25,17},{2,10},{10... | collective-permute-start | bytes 2752520 | tf_op jit(solution)/shard_map/ppermute | solution.py:30
  59.7 7.9 %collective-permute-start.18 = (bf16[2,128,256]{2,1,0:T(8,128)(2,1)S(1)}, bf16[2,128,256]{2,1,0:T(8,128)(2,1)S(1)}, u32[]{:S(2)}, u32[]{:S(2)}) collective-permute-start(bf16[2,128,256]{2,1,0:T(8,128)(2,1)S(1)} %get-tuple-element.21), channel_id=1, source_target_pairs={{0,4},{1,5},{2,6},{3,7},{4,0},{5,1},{6,2},{7,3},{8,12},{9,13},{10,... | collective-permute-start | bytes 393224 | tf_op jit(solution)/shard_map/ppermute | solution.py:30
  67.6 6.8 %collective-permute-start.19 = (bf16[2,128,256]{2,1,0:T(8,128)(2,1)S(1)}, bf16[2,128,256]{2,1,0:T(8,128)(2,1)S(1)}, u32[]{:S(2)}, u32[]{:S(2)}) collective-permute-start(bf16[2,128,256]{2,1,0:T(8,128)(2,1)S(1)} %get-tuple-element.22), channel_id=1, source_target_pairs={{0,6},{1,7},{2,4},{3,5},{4,2},{5,3},{6,0},{7,1},{8,14},{9,15},{10,... | collective-permute-start | bytes 393224 | tf_op jit(solution)/shard_map/ppermute | solution.py:30
  94.0 21.4 %collective-permute-start.31 = (bf16[512,896]{1,0:T(8,128)(2,1)S(1)}, bf16[512,896]{1,0:T(8,128)(2,1)}, u32[]{:S(2)}, u32[]{:S(2)}) collective-permute-start(bf16[512,896]{1,0:T(8,128)(2,1)S(1)} %collective-permute-done.20.refs_11_), channel_id=1, source_target_pairs={{0,16},{8,24},{16,0},{24,8},{1,17},{9,25},{17,1},{25,9},{2,18},{10... | collective-permute-start | bytes 2752520 | tf_op jit(solution)/shard_map/ppermute | solution.py:30
  94.5 21.3 %collective-permute-start.32 = (bf16[512,896]{1,0:T(8,128)(2,1)}, bf16[512,896]{1,0:T(8,128)(2,1)}, u32[]{:S(2)}, u32[]{:S(2)}) collective-permute-start(bf16[512,896]{1,0:T(8,128)(2,1)} %collective-permute-done.22.refs_16_), channel_id=1, source_target_pairs={{0,8},{8,0},{16,24},{24,16},{1,9},{9,1},{17,25},{25,17},{2,10},{10... | collective-permute-start | bytes 2752520 | tf_op jit(solution)/shard_map/ppermute | solution.py:30
  95.9 6.4 %collective-permute-start.24 = (bf16[2,128,256]{2,1,0:T(8,128)(2,1)S(1)}, bf16[2,128,256]{2,1,0:T(8,128)(2,1)S(1)}, u32[]{:S(2)}, u32[]{:S(2)}) collective-permute-start(bf16[2,128,256]{2,1,0:T(8,128)(2,1)S(1)} %add_convert_fusion.refs_2_), channel_id=1, source_target_pairs={{0,2},{1,3},{2,0},{3,1},{4,6},{5,7},{6,4},{7,5},{8,10},{9,11},{10,... | collective-permute-start | bytes 393224 | tf_op jit(solution)/shard_map/ppermute | solution.py:30
  97.7 11.8 %collective-permute-start.25 = (bf16[2,128,256]{2,1,0:T(8,128)(2,1)S(1)}, bf16[2,128,256]{2,1,0:T(8,128)(2,1)S(1)}, u32[]{:S(2)}, u32[]{:S(2)}) collective-permute-start(bf16[2,128,256]{2,1,0:T(8,128)(2,1)S(1)} %add_convert_fusion.refs_2_), channel_id=1, source_target_pairs={{0,4},{1,5},{2,6},{3,7},{4,0},{5,1},{6,2},{7,3},{8,12},{9,13},{10,... | collective-permute-start | bytes 393224 | tf_op jit(solution)/shard_map/ppermute | solution.py:30
  99.0 10.4 %collective-permute-start.26 = (bf16[2,128,256]{2,1,0:T(8,128)(2,1)S(1)}, bf16[2,128,256]{2,1,0:T(8,128)(2,1)S(1)}, u32[]{:S(2)}, u32[]{:S(2)}) collective-permute-start(bf16[2,128,256]{2,1,0:T(8,128)(2,1)S(1)} %add_convert_fusion.refs_2_), channel_id=1, source_target_pairs={{0,6},{1,7},{2,4},{3,5},{4,2},{5,3},{6,0},{7,1},{8,14},{9,15},{10,... | collective-permute-start | bytes 393224 | tf_op jit(solution)/shard_map/ppermute | solution.py:30
  102.3 7.7 %collective-permute-start.27 = (bf16[2,128,256]{2,1,0:T(8,128)(2,1)S(1)}, bf16[2,128,256]{2,1,0:T(8,128)(2,1)S(1)}, u32[]{:S(2)}, u32[]{:S(2)}) collective-permute-start(bf16[2,128,256]{2,1,0:T(8,128)(2,1)S(1)} %add_convert_fusion.refs_2_), channel_id=1, source_target_pairs={{0,1},{1,0},{2,3},{3,2},{4,5},{5,4},{6,7},{7,6},{8,9},{9,8},{10,11... | collective-permute-start | bytes 393224 | tf_op jit(solution)/shard_map/ppermute | solution.py:30
  (30 other events, 199.7 us)
where the time goes:
time: 142 us
  waiting for transfers between devices  68.6 us (48%)
  starting transfers between devices  43 us (30%)
  local copies, waits for them, and re-layouts  15.5 us (11%)
  Pallas kernels  10.3 us (7%)
  other arithmetic  3.52 us (2%)
    ppermute x38, waiting for transfers between devices, exchange(): return lax.ppermute(values, axis, [(i, i ^ flip) for i in range(count)])  68.6 us
    ppermute x38, starting transfers between devices, exchange(): return lax.ppermute(values, axis, [(i, i ^ flip) for i in range(count)])  43 us
    unnamed x34, local copies, waits for them, and re-layouts  13.9 us
    pallas_call x7, Pallas kernels, call(): pl.pallas_call(kernel, out_shape=out_shape, in_specs=specs, out_specs=jax...  10.3 us
  transfers between devices with their start and end apart: 38, of which 23 were waited for; matrix products, arithmetic and copies ran while one was open for 2% of the time, Pallas kernels for 0%

commit v1 on v0

--- a/solution.py
+++ b/solution.py
@@ -11,10 +11,15 @@
 params = pltpu.CompilerParams(vmem_limit_bytes=24 * 1024 * 1024)
 vmem = pl.BlockSpec(memory_space=pltpu.VMEM)
 smem = pl.BlockSpec(memory_space=pltpu.SMEM)
-
-
-def call(kernel, out_shape, ops, scratch=()):
-    specs = [smem] + [vmem] * (len(ops) - 1)
+anywhere = pl.BlockSpec(memory_space=pltpu.HBM)
+
+
+def call(kernel, out_shape, ops, scratch=(), far=()):
+    specs = [smem] + [anywhere if i in far else vmem for i in range(1, len(ops))]
+    ops = [
+        pltpu.with_memory_space_constraint(op, pltpu.HBM) if i in far else op
+        for i, op in enumerate(ops)
+    ]
     return pl.pallas_call(
         kernel,
         out_shape=out_shape,
@@ -30,15 +35,28 @@
     return lax.ppermute(values, axis, [(i, i ^ flip) for i in range(count)])
 
 
-def select_kernel(ids, code, *refs):
-    parts, out = refs[:-1], refs[-1]
+def fetch(sources, targets, sems):
+    copies = [
+        pltpu.make_async_copy(source, target, sems.at[i])
+        for i, (source, target) in enumerate(zip(sources, targets))
+    ]
+    for copy in copies:
+        copy.start()
+    return copies
+
+
+def select_kernel(dp, ids, code, *refs):
+    parts, (out, own, sems) = list(refs[: 2 * dp]), refs[2 * dp :]
+    copies = fetch([parts[0], parts[dp]], [own.at[0], own.at[1]], sems)
     rows = out.shape[1]
-    dp = len(parts) // 2
     me = ids[0]
     wanted = me * rows + lax.broadcasted_iota(jnp.int32, (rows, code.shape[2]), 0)
     hots = [
         (code[me ^ k] == wanted).astype(jnp.float32).astype(jnp.bfloat16) for k in range(dp)
     ]
+    for m in range(2):
+        copies[m].wait()
+        parts[m * dp] = own.at[m]
     for m in range(2):
         total = None
         for k in range(dp):
@@ -49,44 +67,54 @@
         out[m] = total.astype(out.dtype)
 
 
-def normalise(values, gain, chip, core, store):
+def normalise(values, gain, chip, core, scaled, normed):
     half = len(values) // 2
-    width = values[0].shape[1] * len(values)
+    part = values[0].shape[1]
+    width = part * len(values)
     values = [v.astype(jnp.float32) for v in values]
     center = sum(jnp.sum(v, axis=1, keepdims=True) for v in values) / width
     values = [v - center for v in values]
     spread = sum(jnp.sum(v * v, axis=1, keepdims=True) for v in values) / width
     scale = lax.rsqrt(spread + epsilon)
     for k, v in enumerate(values):
-        place = 2 * (chip ^ (k % half)) + (core if k < half else 1 - core)
-        store[place] = (v * scale * gain[place]).astype(jnp.bfloat16)
+        scaled[2 * (chip ^ (k % half)) + (core if k < half else 1 - core)] = v * scale
+    for b in range(2 * half):
+        normed[b] = (scaled[b] * gain[:, b * part : (b + 1) * part]).astype(jnp.bfloat16)
     return values[0]
 
 
 def ffn_kernel(half, ids, *refs):
-    gains, ups, downs = refs[:2], refs[2:4], refs[4:6]
     parts = refs[6 : 6 + 2 * half]
-    keep, send, normed, terms = refs[6 + 2 * half :]
+    keep, send, gains, scaled, normed, up_store, down_store, sems = refs[6 + 2 * half :]
+    copies = fetch(
+        [refs[0], refs[2], refs[4], refs[1], refs[3], refs[5]],
+        [store.at[m] for m in range(2) for store in (gains, up_store, down_store)],
+        sems,
+    )
     chip, core = ids[1], ids[2]
     for m in range(2):
-        up, down = ups[m], downs[m]
-        base = normalise([part[m] for part in parts], gains[m], chip, core, normed.at[m])
+        copies[3 * m].wait()
+        base = normalise([part[m] for part in parts], gains[m], chip, core, scaled, normed)
         part = base.shape[1]
+        copies[3 * m + 1].wait()
         pre = None
         for b in range(2 * half):
             piece = jnp.dot(
-                normed[m, b], up[b * part : (b + 1) * part, :], preferred_element_type=jnp.float32
+                normed[b],
+                up_store[m, b * part : (b + 1) * part, :],
+                preferred_element_type=jnp.float32,
             )
             pre = piece if pre is None else pre + piece
         units = jax.nn.gelu(pre).astype(jnp.bfloat16)
-        full = jnp.dot(units, down[...], preferred_element_type=jnp.float32)
+        copies[3 * m + 2].wait()
+        full = jnp.dot(units, down_store[m], preferred_element_type=jnp.float32)
         for b in range(2 * half):
-            terms[m, b] = full[:, b * part : (b + 1) * part]
+            scaled[b] = full[:, b * part : (b + 1) * part]
         for k in range(half):
             place = 2 * (chip ^ k)
-            kept = terms[m, place + core]
+            kept = scaled[place + core]
             keep[k, m] = kept + base if k == 0 else kept
-            send[k, m] = terms[m, place + 1 - core].astype(jnp.bfloat16)
+            send[k, m] = scaled[place + 1 - core].astype(jnp.bfloat16)
 
 
 def pair_kernel(ids, keep, came, own, *outs):
@@ -96,22 +124,29 @@
 
 
 def score_kernel(half, ids, wanted, *refs):
-    gains, refs = refs[:2], refs[2:]
-    parts, refs = refs[: 2 * half], refs[2 * half :]
-    outs, (stats, normed) = refs[:-2], refs[-2:]
+    parts = refs[2 : 2 + 2 * half]
+    *outs, stats, gains, scaled, normed, out_store, sems = refs[2 + 2 * half :]
     dp = len(outs) // 2
+    copies = fetch(
+        [refs[0], outs[0], refs[1], outs[dp]],
+        [store.at[m] for m in range(2) for store in (gains, out_store)],
+        sems,
+    )
     me, chip, core = ids[0], ids[1], ids[2]
     lane = lax.broadcasted_iota(jnp.int32, (parts[0].shape[1], 128), 1)
     table = jnp.zeros(lane.shape, jnp.float32)
     ratio = 2 * half // dp
     for m in range(2):
-        normalise([part[m] for part in parts], gains[m], chip, core, normed.at[m])
+        copies[2 * m].wait()
+        normalise([part[m] for part in parts], gains[m], chip, core, scaled, normed)
         part = parts[0].shape[2]
+        copies[2 * m + 1].wait()
+        outs[m * dp] = out_store.at[m]
         logits = None
         for k in range(dp):
             for b in range(ratio):
                 piece = jnp.dot(
-                    normed[m, (me ^ k) * ratio + b],
+                    normed[(me ^ k) * ratio + b],
                     outs[m * dp + k][b * part : (b + 1) * part, :],
                     preferred_element_type=jnp.float32,
                 )
@@ -169,23 +204,31 @@
     reqs, slots, part = hidden_policy.shape
     here = reqs * slots
     rows = here // 2
-    ffn_gains = (ffn_gain_policy.reshape(mp, 1, part), ffn_gain_reference.reshape(mp, 1, part))
-    final_gains = (
-        final_gain_policy.reshape(mp, 1, part),
-        final_gain_reference.reshape(mp, 1, part),
-    )
+    ffn_gains = (ffn_gain_policy.reshape(1, -1), ffn_gain_reference.reshape(1, -1))
+    final_gains = (final_gain_policy.reshape(1, -1), final_gain_reference.reshape(1, -1))
     bits = [1 << b for b in range(dp.bit_length() - 1)]
 
-    hidden_parts = []
-    for hidden in (hidden_policy, hidden_reference):
-        hidden_parts += [hidden] + [exchange(hidden, "dp", k) for k in range(1, dp)]
-    facts = jnp.concatenate([lengths, targets.reshape(here)])
-    relative = jnp.stack([facts] + [exchange(facts, "dp", k) for k in range(1, dp)])
+    bit_orders = []
+    for m in range(2):
+        bit_orders.append([bits[(b ^ m) if (b ^ m) < len(bits) else b] for b in range(len(bits))])
+
+    def spread_step(blocks, step, places):
+        for m in range(2):
+            bit = bit_orders[m][step]
+            for k in [k for k in blocks[m] if places(m, k)]:
+                blocks[m][k ^ bit] = exchange(blocks[m][k], "dp", bit)
+
+    hiddens = [{0: hidden_policy}, {0: hidden_reference}]
+    for step in range(len(bits)):
+        spread_step(hiddens, step, lambda m, k: True)
+    hidden_parts = [hiddens[m][k] for m in range(2) for k in range(dp)]
+
     order = jnp.arange(dp, dtype=jnp.int32)
-    place = (order[:, None] ^ dp_index) == order[None, :]
-    facts = jnp.sum(jnp.where(place[:, :, None], relative[None], 0), axis=1)
-    all_lengths = facts[:, :reqs].reshape(-1)
-    all_targets = facts[:, reqs:].reshape(-1)
+    facts = lax.all_gather(
+        jnp.concatenate([lengths[:, None], targets], axis=1), "dp", axis=0, tiled=True
+    )
+    all_lengths = facts[:, 0]
+    all_targets = facts[:, 1:].reshape(-1)
     slot_ids = jnp.arange(dp * reqs, dtype=jnp.int32)
     positions = jnp.arange(slots, dtype=jnp.int32)
 
@@ -196,33 +239,26 @@
             positions[None] < live[:, None], start[:, None] + positions[None], jnp.int32(-1)
         )
 
-    bit_orders = []
-    for m in range(2):
-        bit_orders.append([bits[(b ^ m) if (b ^ m) < len(bits) else b] for b in range(len(bits))])
-    outs = [{0: out_policy}, {0: out_reference}]
-    newest = [{0: -1}, {0: -1}]
-
-    def forward(after):
-        flat = [outs[m][k] for m in range(2) for k in newest[m]]
-        after, *flat = lax.optimization_barrier((after, *flat))
-        sent = []
-        for m in range(2):
-            for k, step in newest[m].items():
-                outs[m][k] = flat.pop(0)
-                sent += [(m, k, later) for later in range(step + 1, len(bits))]
-            newest[m] = {}
-        for m, k, step in sorted(sent, key=lambda item: item[2]):
-            place = k ^ bit_orders[m][step]
-            outs[m][place] = exchange(outs[m][k], "dp", bit_orders[m][step])
-            newest[m][place] = step
-        return after
-
-    source_code = forward(codes(move_plan).reshape(dp, 1, here))
+    source_code = codes(move_plan).reshape(dp, 1, here)
     moved = call(
-        select_kernel,
+        functools.partial(select_kernel, dp),
         jax.ShapeDtypeStruct((2, rows, part), jnp.bfloat16),
         (ids, source_code, *hidden_parts),
-    )
+        [pltpu.VMEM((2,) + hidden_policy.shape, jnp.bfloat16), pltpu.SemaphoreType.DMA((2,))],
+        far=(2, 2 + dp),
+    )
+
+    outs = [{0: out_policy}, {0: out_reference}]
+
+    def after(first, step, places):
+        flat = [(m, k) for m in range(2) for k in outs[m]]
+        first, *values = lax.optimization_barrier((first, *[outs[m][k] for m, k in flat]))
+        for (m, k), value in zip(flat, values):
+            outs[m][k] = value
+        spread_step(outs, step, places)
+        return first
+
+    moved = after(moved, 0, lambda m, k: True)
 
     far = sorted(range(1, half), key=lambda k: (k.bit_length() <= 1, k))
 
@@ -233,7 +269,12 @@
         same = [same[k] for k in range(half)]
         return same + [exchange(v, "mp", 1) for v in same]
 
-    normed_scratch = pltpu.VMEM((2, mp, rows, part), jnp.bfloat16)
+    gain_scratch = pltpu.VMEM((2, 1, part * mp), jnp.float32)
+    scaled_scratch = pltpu.VMEM((mp, rows, part), jnp.float32)
+    normed_scratch = pltpu.VMEM((mp, rows, part), jnp.bfloat16)
+    parts = gather_pair(moved)
+    if len(bits) > 1:
+        parts[-1] = after(parts[-1], 1, lambda m, k: k == 0)
     block = jax.ShapeDtypeStruct((2, rows, part), jnp.bfloat16)
     keep, send = call(
         functools.partial(ffn_kernel, half),
@@ -248,9 +289,17 @@
             up_reference,
             down_policy,
             down_reference,
-            *gather_pair(moved),
+            *parts,
         ),
-        [normed_scratch, pltpu.VMEM((2, mp, rows, part), jnp.float32)],
+        [
+            gain_scratch,
+            scaled_scratch,
+            normed_scratch,
+            pltpu.VMEM((2,) + up_policy.shape, jnp.bfloat16),
+            pltpu.VMEM((2,) + down_policy.shape, jnp.bfloat16),
+            pltpu.SemaphoreType.DMA((6,)),
+        ],
+        far=range(1, 7),
     )
     came = exchange(send, "mp", 1)
     own, *pieces = call(
@@ -262,8 +311,10 @@
     for k in range(1, half):
         own = own + arrived[k].astype(jnp.float32)
     stream = own.astype(jnp.bfloat16)
-    for step in range(1, len(bits)):
-        stream = forward(stream)
+    if len(bits) > 1:
+        stream = after(stream, 1, lambda m, k: k == bit_orders[m][0])
+    for step in range(2, len(bits)):
+        stream = after(stream, step, lambda m, k: True)
 
     owner_code = codes(slot_ids).reshape(-1)
     my_ranks = dp_index * rows + jnp.arange(rows, dtype=jnp.int32)
@@ -282,7 +333,14 @@
             *gather_pair(stream),
             *[outs[m][k] for m in range(2) for k in range(dp)],
         ),
-        [normed_scratch],
+        [
+            gain_scratch,
+            scaled_scratch,
+            normed_scratch,
+            pltpu.VMEM((2,) + out_policy.shape, jnp.bfloat16),
+            pltpu.SemaphoreType.DMA((4,)),
+        ],
+        far=(2, 3, 4 + mp, 4 + mp + dp),
     )
     flips = [1 << b for b in range(mp.bit_length() - 1)]
     for flip in flips[:-1]:

time: 142 us -> 121 us (0.85)
  waiting for transfers between devices: 68.6 us -> 54 us
  local copies, waits for them, and re-layouts: 15.5 us -> 3.9 us
  blocking collectives: 0 us -> 8.61 us
  starting transfers between devices: 43 us -> 35.9 us
  Pallas kernels: 10.3 us -> 14.5 us
    ppermute x38 -> x35, waiting for transfers between devices: 68.6 us -> 54 us  [exchange(): return lax.ppermute(values, axis, [(i, i ^ flip) for i in range(count)])]
    unnamed x34 -> x4, local copies, waits for them, and re-layouts: 13.9 us -> 2.15 us
    all_gather x0 -> x1, blocking collectives: none -> 8.61 us  [local(): lax.all_gather(jnp.concatenate([lengths[:, None], targets], axis=1), 'dp'...]
    ppermute x38 -> x35, starting transfers between devices: 43 us -> 35.9 us  [exchange(): return lax.ppermute(values, axis, [(i, i ^ flip) for i in range(count)])]
    pallas_call x7, Pallas kernels: 10.3 us -> 14.5 us  [call(): pl.pallas_call(kernel, out_shape=out_shape, in_specs=specs, out_specs=jax...]
  transfers between devices with their start and end apart: 38 -> 35, of which waited for: 23 -> 21; matrix products, arithmetic and copies ran while one was open for 2% -> 3% of each run, Pallas kernels for 0% -> 5%
where the time goes in v1:
time: 121 us
  waiting for transfers between devices  54 us (45%)
  starting transfers between devices  35.9 us (30%)
  Pallas kernels  14.5 us (12%)
  blocking collectives  8.61 us (7%)
  local copies, waits for them, and re-layouts  3.9 us (3%)
  other arithmetic  3.37 us (3%)
    ppermute x35, waiting for transfers between devices, exchange(): return lax.ppermute(values, axis, [(i, i ^ flip) for i in range(count)])  54 us
    ppermute x35, starting transfers between devices, exchange(): return lax.ppermute(values, axis, [(i, i ^ flip) for i in range(count)])  35.9 us
    pallas_call x7, Pallas kernels, call(): pl.pallas_call(kernel, out_shape=out_shape, in_specs=specs, out_specs=jax...  14.5 us
    all_gather x1, blocking collectives, local(): lax.all_gather(jnp.concatenate([lengths[:, None], targets], axis=1), 'dp'...  8.61 us
  transfers between devices with their start and end apart: 35, of which 21 were waited for; matrix products, arithmetic and copies ran while one was open for 3% of the time, Pallas kernels for 5%

profile of v1, /device:TPU:0, one launch (start us, length us, event | category | flops | bytes accessed | tf_op | source)
XLA Modules:
  0.0 121.1 jit_solution(13665466250737386217)
XLA Ops:
  0.6 3.0 %collective-permute-start = (bf16[16,16,256]{2,1,0:T(8,128)(2,1)}, bf16[16,16,256]{2,1,0:T(8,128)(2,1)S(1)}, u32[]{:S(2)}, u32[]{:S(2)}) collective-permute-start(bf16[16,16,256]{2,1,0:T(8,128)(2,1)} %refs_0_.1), channel_id=1, source_target_pairs={{0,8},{8,0},{16,24},{24,16},{1,9},{9,1},{17,25},{25,17},{2,10},{10... | collective-permute-start | bytes 393224 | tf_op jit(solution)/shard_map/ppermute | solution.py:35
  7.2 8.6 %all_gather.3 = s32[64,17]{1,0:T(8,128)S(1)} all-gather(s32[16,17]{1,0:T(8,128)S(1)} %pad_add_fusion), channel_id=1, replica_groups=mesh['dp'=4,'mp'=8] {'dp'}, dimensions={0}, use_global_device_ids=true | all-gather | bytes 5440 | tf_op jit(solution)/shard_map/all_gather | solution.py:227
  19.6 2.8 %collective-permute-done.2.refs_3_ = bf16[16,16,256]{2,1,0:T(8,128)(2,1)S(1)} collective-permute-done((bf16[16,16,256]{2,1,0:T(8,128)(2,1)S(1)}, bf16[16,16,256]{2,1,0:T(8,128)(2,1)S(1)}, u32[]{:S(2)}, u32[]{:S(2)}) %collective-permute-start.2) | collective-permute-done | bytes 131104 | tf_op jit(solution)/shard_map/ppermute | solution.py:35
  24.0 1.8 %shard_map.158.refs_6_ = bf16[2,128,256]{2,1,0:T(8,128)(2,1)S(1)} custom-call(s32[4]{0:T(128)S(1)} %pad_add_fusion.1.ids, s32[4,1,256]{2,1,0:T(1,128)S(1)} %compare_select_fusion.code, bf16[16,16,256]{2,1,0:T(8,128)(2,1)} %refs_0_.1, bf16[16,16,256]{2,1,0:T(8,128)(2,1)S(1)} %collective-permute-done.refs_1_, ...), custom_call_target="tpu_custom_call" | custom-call | tf_op jit(solution)/shard_map/pallas_call | solution.py:23
  27.9 3.6 %collective-permute-start.8 = (bf16[2,128,256]{2,1,0:T(8,128)(2,1)S(1)}, bf16[2,128,256]{2,1,0:T(8,128)(2,1)S(1)}, u32[]{:S(2)}, u32[]{:S(2)}) collective-permute-start(bf16[2,128,256]{2,1,0:T(8,128)(2,1)S(1)} %shard_map.158.refs_6_), channel_id=1, source_target_pairs={{0,6},{1,7},{2,4},{3,5},{4,2},{5,3},{6,0},{7,1},{8,14},{9,15},{10,... | collective-permute-start | bytes 393224 | tf_op jit(solution)/shard_map/ppermute | solution.py:35
  32.3 2.5 %collective-permute-done.8.refs_9_ = bf16[2,128,256]{2,1,0:T(8,128)(2,1)S(1)} collective-permute-done((bf16[2,128,256]{2,1,0:T(8,128)(2,1)S(1)}, bf16[2,128,256]{2,1,0:T(8,128)(2,1)S(1)}, u32[]{:S(2)}, u32[]{:S(2)}) %collective-permute-start.8) | collective-permute-done | bytes 131104 | tf_op jit(solution)/shard_map/ppermute | solution.py:35
  34.8 3.1 %collective-permute-done.6.refs_7_ = bf16[2,128,256]{2,1,0:T(8,128)(2,1)S(1)} collective-permute-done((bf16[2,128,256]{2,1,0:T(8,128)(2,1)S(1)}, bf16[2,128,256]{2,1,0:T(8,128)(2,1)S(1)}, u32[]{:S(2)}, u32[]{:S(2)}) %collective-permute-start.6) | collective-permute-done | bytes 131104 | tf_op jit(solution)/shard_map/ppermute | solution.py:35
  38.5 6.7 %collective-permute-done.13.refs_11_ = bf16[512,896]{1,0:T(8,128)(2,1)S(1)} collective-permute-done((bf16[512,896]{1,0:T(8,128)(2,1)}, bf16[512,896]{1,0:T(8,128)(2,1)S(1)}, u32[]{:S(2)}, u32[]{:S(2)}) %collective-permute-start.13) | collective-permute-done | bytes 917536 | tf_op jit(solution)/shard_map/ppermute | solution.py:35
  46.6 1.8 %collective-permute-start.19 = (bf16[512,896]{1,0:T(8,128)(2,1)}, bf16[512,896]{1,0:T(8,128)(2,1)S(1)}, u32[]{:S(2)}, u32[]{:S(2)}) collective-permute-start(bf16[512,896]{1,0:T(8,128)(2,1)} %refs_10_), channel_id=1, source_target_pairs={{0,16},{8,24},{16,0},{24,8},{1,17},{9,25},{17,1},{25,9},{2,18},{10... | collective-permute-start | bytes 2752520 | tf_op jit(solution)/shard_map/ppermute | solution.py:35
  48.6 5.0 %shard_map.159 = (f32[4,2,128,256]{3,2,1,0:T(8,128)S(1)}, bf16[4,2,128,256]{3,2,1,0:T(8,128)(2,1)S(1)}) custom-call(s32[4]{0:T(128)S(1)} %pad_add_fusion.1.ids, f32[1,2048]{1,0:T(1,128)} %bitcast.14, f32[1,2048]{1,0:T(1,128)} %bitcast.15, bf16[2048,512]{1,0:T(8,128)(2,1)} %refs_2_.1, bf16[2048,512]{1,0:T(8,128)(2,1)} %refs_3_.1, bf16[512,2048]{1,0:T(8,128)(2,1)} %refs_4_.3, ...), custom_call_target="tpu_custom_call" | custom-call | tf_op jit(solution)/shard_map/pallas_call | solution.py:23
  53.7 1.9 %collective-permute-done.15.came = bf16[4,2,128,256]{3,2,1,0:T(8,128)(2,1)S(1)} collective-permute-done((bf16[4,2,128,256]{3,2,1,0:T(8,128)(2,1)S(1)}, bf16[4,2,128,256]{3,2,1,0:T(8,128)(2,1)S(1)}, u32[]{:S(2)}, u32[]{:S(2)}) %collective-permute-start.15) | collective-permute-done | bytes 524320 | tf_op jit(solution)/shard_map/ppermute | solution.py:35
  56.2 2.0 %collective-permute-start.16 = (bf16[2,128,256]{2,1,0:T(8,128)(2,1)S(1)}, bf16[2,128,256]{2,1,0:T(8,128)(2,1)S(1)}, u32[]{:S(2)}, u32[]{:S(2)}) collective-permute-start(bf16[2,128,256]{2,1,0:T(8,128)(2,1)S(1)} %get-tuple-element.30), channel_id=1, source_target_pairs={{0,2},{1,3},{2,0},{3,1},{4,6},{5,7},{6,4},{7,5},{8,10},{9,11},{10,... | collective-permute-start | bytes 393224 | tf_op jit(solution)/shard_map/ppermute | solution.py:35
  58.2 2.6 %collective-permute-start.17 = (bf16[2,128,256]{2,1,0:T(8,128)(2,1)S(1)}, bf16[2,128,256]{2,1,0:T(8,128)(2,1)S(1)}, u32[]{:S(2)}, u32[]{:S(2)}) collective-permute-start(bf16[2,128,256]{2,1,0:T(8,128)(2,1)S(1)} %get-tuple-element.31), channel_id=1, source_target_pairs={{0,4},{1,5},{2,6},{3,7},{4,0},{5,1},{6,2},{7,3},{8,12},{9,13},{10,... | collective-permute-start | bytes 393224 | tf_op jit(solution)/shard_map/ppermute | solution.py:35
  60.8 3.1 %collective-permute-done.16 = bf16[2,128,256]{2,1,0:T(8,128)(2,1)S(1)} collective-permute-done((bf16[2,128,256]{2,1,0:T(8,128)(2,1)S(1)}, bf16[2,128,256]{2,1,0:T(8,128)(2,1)S(1)}, u32[]{:S(2)}, u32[]{:S(2)}) %collective-permute-start.16) | collective-permute-done | bytes 131104 | tf_op jit(solution)/shard_map/ppermute | solution.py:35
  63.9 7.2 %collective-permute-done.17 = bf16[2,128,256]{2,1,0:T(8,128)(2,1)S(1)} collective-permute-done((bf16[2,128,256]{2,1,0:T(8,128)(2,1)S(1)}, bf16[2,128,256]{2,1,0:T(8,128)(2,1)S(1)}, u32[]{:S(2)}, u32[]{:S(2)}) %collective-permute-start.17) | collective-permute-done | bytes 131104 | tf_op jit(solution)/shard_map/ppermute | solution.py:35
  74.2 2.3 %collective-permute-start.21 = (bf16[2,128,256]{2,1,0:T(8,128)(2,1)S(1)}, bf16[2,128,256]{2,1,0:T(8,128)(2,1)S(1)}, u32[]{:S(2)}, u32[]{:S(2)}) collective-permute-start(bf16[2,128,256]{2,1,0:T(8,128)(2,1)S(1)} %add_convert_fusion.refs_2_), channel_id=1, source_target_pairs={{0,2},{1,3},{2,0},{3,1},{4,6},{5,7},{6,4},{7,5},{8,10},{9,11},{10,... | collective-permute-start | bytes 393224 | tf_op jit(solution)/shard_map/ppermute | solution.py:35
  78.9 1.8 %collective-permute-done.21.refs_3_ = bf16[2,128,256]{2,1,0:T(8,128)(2,1)S(1)} collective-permute-done((bf16[2,128,256]{2,1,0:T(8,128)(2,1)S(1)}, bf16[2,128,256]{2,1,0:T(8,128)(2,1)S(1)}, u32[]{:S(2)}, u32[]{:S(2)}) %collective-permute-start.21) | collective-permute-done | bytes 131104 | tf_op jit(solution)/shard_map/ppermute | solution.py:35
  80.9 7.2 %collective-permute-done.22.refs_4_ = bf16[2,128,256]{2,1,0:T(8,128)(2,1)S(1)} collective-permute-done((bf16[2,128,256]{2,1,0:T(8,128)(2,1)S(1)}, bf16[2,128,256]{2,1,0:T(8,128)(2,1)S(1)}, u32[]{:S(2)}, u32[]{:S(2)}) %collective-permute-start.22) | collective-permute-done | bytes 131104 | tf_op jit(solution)/shard_map/ppermute | solution.py:35
  90.0 2.5 %collective-permute-done.28.refs_13_ = bf16[512,896]{1,0:T(8,128)(2,1)} collective-permute-done((bf16[512,896]{1,0:T(8,128)(2,1)S(1)}, bf16[512,896]{1,0:T(8,128)(2,1)}, u32[]{:S(2)}, u32[]{:S(2)}) %collective-permute-start.28) | collective-permute-done | bytes 917536 | tf_op jit(solution)/shard_map/ppermute | solution.py:35
  95.0 5.4 %shard_map.161.mine = f32[8,128]{1,0:T(8,128)S(1)} custom-call(s32[4]{0:T(128)S(1)} %pad_add_fusion.1.ids, s32[128,1]{1,0:T(8,128)S(1)} %copy.22.wanted, f32[1,2048]{1,0:T(1,128)} %bitcast.16, f32[1,2048]{1,0:T(1,128)} %bitcast.17, bf16[2,128,256]{2,1,0:T(8,128)(2,1)S(1)} %add_convert_fusion.refs_2_, ...), custom_call_target="tpu_custom_call" | custom-call | tf_op jit(solution)/shard_map/pallas_call | solution.py:23
  102.2 3.3 %collective-permute-start.31 = (f32[8,128]{1,0:T(8,128)S(1)}, f32[8,128]{1,0:T(8,128)S(1)}, u32[]{:S(2)}, u32[]{:S(2)}) collective-permute-start(f32[8,128]{1,0:T(8,128)S(1)} %shard_map.162.mine), channel_id=1, source_target_pairs={{0,2},{1,3},{2,0},{3,1},{4,6},{5,7},{6,4},{7,5},{8,10},{9,11},{10,... | collective-permute-start | bytes 12296 | tf_op jit(solution)/shard_map/ppermute | solution.py:35
  107.7 3.1 %collective-permute-start.32 = (f32[8,128]{1,0:T(8,128)S(1)}, f32[8,128]{1,0:T(8,128)S(1)}, u32[]{:S(2)}, u32[]{:S(2)}) collective-permute-start(f32[8,128]{1,0:T(8,128)S(1)} %shard_map.163.mine), channel_id=1, source_target_pairs={{0,4},{1,5},{2,6},{3,7},{4,0},{5,1},{6,2},{7,3},{8,12},{9,13},{10,... | collective-permute-start | bytes 12296 | tf_op jit(solution)/shard_map/ppermute | solution.py:35
  113.6 3.0 %collective-permute-done.33 = f32[1,128]{1,0:T(1,128)S(1)} collective-permute-done((f32[1,128]{1,0:T(1,128)S(1)}, f32[1,128]{1,0:T(1,128)S(1)}, u32[]{:S(2)}, u32[]{:S(2)}) %collective-permute-start.33) | collective-permute-done | bytes 544 | tf_op jit(solution)/shard_map/ppermute | solution.py:35
  117.2 3.0 %collective-permute-done.34 = f32[2,128]{1,0:T(2,128)S(1)} collective-permute-done((f32[2,128]{1,0:T(2,128)S(1)}, f32[2,128]{1,0:T(2,128)S(1)}, u32[]{:S(2)}, u32[]{:S(2)}) %collective-permute-start.34) | collective-permute-done | bytes 1056 | tf_op jit(solution)/shard_map/ppermute | solution.py:35
  (88 shorter events, 32.8 us)
Async XLA Ops:
  0.6 16.8 %collective-permute-start = (bf16[16,16,256]{2,1,0:T(8,128)(2,1)}, bf16[16,16,256]{2,1,0:T(8,128)(2,1)S(1)}, u32[]{:S(2)}, u32[]{:S(2)}) collective-permute-start(bf16[16,16,256]{2,1,0:T(8,128)(2,1)} %refs_0_.1), channel_id=1, source_target_pairs={{0,8},{8,0},{16,24},{24,16},{1,9},{9,1},{17,25},{25,17},{2,10},{10... | collective-permute-start | bytes 393224 | tf_op jit(solution)/shard_map/ppermute | solution.py:35
  3.6 16.0 %collective-permute-start.1 = (bf16[16,16,256]{2,1,0:T(8,128)(2,1)}, bf16[16,16,256]{2,1,0:T(8,128)(2,1)S(1)}, u32[]{:S(2)}, u32[]{:S(2)}) collective-permute-start(bf16[16,16,256]{2,1,0:T(8,128)(2,1)} %refs_0_.1), channel_id=1, source_target_pairs={{0,16},{8,24},{16,0},{24,8},{1,17},{9,25},{17,1},{25,9},{2,18},{10... | collective-permute-start | bytes 393224 | tf_op jit(solution)/shard_map/ppermute | solution.py:35
  5.2 13.9 %collective-permute-start.4 = (bf16[16,16,256]{2,1,0:T(8,128)(2,1)}, bf16[16,16,256]{2,1,0:T(8,128)(2,1)S(1)}, u32[]{:S(2)}, u32[]{:S(2)}) collective-permute-start(bf16[16,16,256]{2,1,0:T(8,128)(2,1)} %refs_4_.2), channel_id=1, source_target_pairs={{0,16},{8,24},{16,0},{24,8},{1,17},{9,25},{17,1},{25,9},{2,18},{10... | collective-permute-start | bytes 393224 | tf_op jit(solution)/shard_map/ppermute | solution.py:35
  5.7 14.0 %collective-permute-start.3 = (bf16[16,16,256]{2,1,0:T(8,128)(2,1)}, bf16[16,16,256]{2,1,0:T(8,128)(2,1)S(1)}, u32[]{:S(2)}, u32[]{:S(2)}) collective-permute-start(bf16[16,16,256]{2,1,0:T(8,128)(2,1)} %refs_4_.2), channel_id=1, source_target_pairs={{0,8},{8,0},{16,24},{24,16},{1,9},{9,1},{17,25},{25,17},{2,10},{10... | collective-permute-start | bytes 393224 | tf_op jit(solution)/shard_map/ppermute | solution.py:35
  17.4 5.0 %collective-permute-start.2 = (bf16[16,16,256]{2,1,0:T(8,128)(2,1)S(1)}, bf16[16,16,256]{2,1,0:T(8,128)(2,1)S(1)}, u32[]{:S(2)}, u32[]{:S(2)}) collective-permute-start(bf16[16,16,256]{2,1,0:T(8,128)(2,1)S(1)} %collective-permute-done.refs_1_), channel_id=1, source_target_pairs={{0,16},{8,24},{16,0},{24,8},{1,17},{9,25},{17,1},{25,9},{2,18},{10... | collective-permute-start | bytes 393224 | tf_op jit(solution)/shard_map/ppermute | solution.py:35
  25.8 19.4 %collective-permute-start.13 = (bf16[512,896]{1,0:T(8,128)(2,1)}, bf16[512,896]{1,0:T(8,128)(2,1)S(1)}, u32[]{:S(2)}, u32[]{:S(2)}) collective-permute-start(bf16[512,896]{1,0:T(8,128)(2,1)} %refs_10_), channel_id=1, source_target_pairs={{0,8},{8,0},{16,24},{24,16},{1,9},{9,1},{17,25},{25,17},{2,10},{10... | collective-permute-start | bytes 2752520 | tf_op jit(solution)/shard_map/ppermute | solution.py:35
  26.4 20.2 %collective-permute-start.14 = (bf16[512,896]{1,0:T(8,128)(2,1)}, bf16[512,896]{1,0:T(8,128)(2,1)S(1)}, u32[]{:S(2)}, u32[]{:S(2)}) collective-permute-start(bf16[512,896]{1,0:T(8,128)(2,1)} %refs_14_), channel_id=1, source_target_pairs={{0,16},{8,24},{16,0},{24,8},{1,17},{9,25},{17,1},{25,9},{2,18},{10... | collective-permute-start | bytes 2752520 | tf_op jit(solution)/shard_map/ppermute | solution.py:35
  27.9 6.9 %collective-permute-start.8 = (bf16[2,128,256]{2,1,0:T(8,128)(2,1)S(1)}, bf16[2,128,256]{2,1,0:T(8,128)(2,1)S(1)}, u32[]{:S(2)}, u32[]{:S(2)}) collective-permute-start(bf16[2,128,256]{2,1,0:T(8,128)(2,1)S(1)} %shard_map.158.refs_6_), channel_id=1, source_target_pairs={{0,6},{1,7},{2,4},{3,5},{4,2},{5,3},{6,0},{7,1},{8,14},{9,15},{10,... | collective-permute-start | bytes 393224 | tf_op jit(solution)/shard_map/ppermute | solution.py:35
  31.5 6.4 %collective-permute-start.6 = (bf16[2,128,256]{2,1,0:T(8,128)(2,1)S(1)}, bf16[2,128,256]{2,1,0:T(8,128)(2,1)S(1)}, u32[]{:S(2)}, u32[]{:S(2)}) collective-permute-start(bf16[2,128,256]{2,1,0:T(8,128)(2,1)S(1)} %shard_map.158.refs_6_), channel_id=1, source_target_pairs={{0,2},{1,3},{2,0},{3,1},{4,6},{5,7},{6,4},{7,5},{8,10},{9,11},{10,... | collective-permute-start | bytes 393224 | tf_op jit(solution)/shard_map/ppermute | solution.py:35
  31.5 6.4 %collective-permute-start.7 = (bf16[2,128,256]{2,1,0:T(8,128)(2,1)S(1)}, bf16[2,128,256]{2,1,0:T(8,128)(2,1)S(1)}, u32[]{:S(2)}, u32[]{:S(2)}) collective-permute-start(bf16[2,128,256]{2,1,0:T(8,128)(2,1)S(1)} %shard_map.158.refs_6_), channel_id=1, source_target_pairs={{0,4},{1,5},{2,6},{3,7},{4,0},{5,1},{6,2},{7,3},{8,12},{9,13},{10,... | collective-permute-start | bytes 393224 | tf_op jit(solution)/shard_map/ppermute | solution.py:35
  37.9 10.7 %collective-permute-start.9 = (bf16[2,128,256]{2,1,0:T(8,128)(2,1)S(1)}, bf16[2,128,256]{2,1,0:T(8,128)(2,1)S(1)}, u32[]{:S(2)}, u32[]{:S(2)}) collective-permute-start(bf16[2,128,256]{2,1,0:T(8,128)(2,1)S(1)} %shard_map.158.refs_6_), channel_id=1, source_target_pairs={{0,1},{1,0},{2,3},{3,2},{4,5},{5,4},{6,7},{7,6},{8,9},{9,8},{10,11... | collective-permute-start | bytes 393224 | tf_op jit(solution)/shard_map/ppermute | solution.py:35
  37.9 10.7 %collective-permute-start.10 = (bf16[2,128,256]{2,1,0:T(8,128)(2,1)S(1)}, bf16[2,128,256]{2,1,0:T(8,128)(2,1)S(1)}, u32[]{:S(2)}, u32[]{:S(2)}) collective-permute-start(bf16[2,128,256]{2,1,0:T(8,128)(2,1)S(1)} %collective-permute-done.6.refs_7_), channel_id=1, source_target_pairs={{0,1},{1,0},{2,3},{3,2},{4,5},{5,4},{6,7},{7,6},{8,9},{9,8},{10,11... | collective-permute-start | bytes 393224 | tf_op jit(solution)/shard_map/ppermute | solution.py:35
  38.4 10.2 %collective-permute-start.11 = (bf16[2,128,256]{2,1,0:T(8,128)(2,1)S(1)}, bf16[2,128,256]{2,1,0:T(8,128)(2,1)S(1)}, u32[]{:S(2)}, u32[]{:S(2)}) collective-permute-start(bf16[2,128,256]{2,1,0:T(8,128)(2,1)S(1)} %collective-permute-done.7.refs_8_), channel_id=1, source_target_pairs={{0,1},{1,0},{2,3},{3,2},{4,5},{5,4},{6,7},{7,6},{8,9},{9,8},{10,11... | collective-permute-start | bytes 393224 | tf_op jit(solution)/shard_map/ppermute | solution.py:35
  46.6 24.6 %collective-permute-start.19 = (bf16[512,896]{1,0:T(8,128)(2,1)}, bf16[512,896]{1,0:T(8,128)(2,1)S(1)}, u32[]{:S(2)}, u32[]{:S(2)}) collective-permute-start(bf16[512,896]{1,0:T(8,128)(2,1)} %refs_10_), channel_id=1, source_target_pairs={{0,16},{8,24},{16,0},{24,8},{1,17},{9,25},{17,1},{25,9},{2,18},{10... | collective-permute-start | bytes 2752520 | tf_op jit(solution)/shard_map/ppermute | solution.py:35
  48.4 22.7 %collective-permute-start.20 = (bf16[512,896]{1,0:T(8,128)(2,1)}, bf16[512,896]{1,0:T(8,128)(2,1)S(1)}, u32[]{:S(2)}, u32[]{:S(2)}) collective-permute-start(bf16[512,896]{1,0:T(8,128)(2,1)} %refs_14_), channel_id=1, source_target_pairs={{0,8},{8,0},{16,24},{24,16},{1,9},{9,1},{17,25},{25,17},{2,10},{10... | collective-permute-start | bytes 2752520 | tf_op jit(solution)/shard_map/ppermute | solution.py:35
  56.2 7.7 %collective-permute-start.16 = (bf16[2,128,256]{2,1,0:T(8,128)(2,1)S(1)}, bf16[2,128,256]{2,1,0:T(8,128)(2,1)S(1)}, u32[]{:S(2)}, u32[]{:S(2)}) collective-permute-start(bf16[2,128,256]{2,1,0:T(8,128)(2,1)S(1)} %get-tuple-element.30), channel_id=1, source_target_pairs={{0,2},{1,3},{2,0},{3,1},{4,6},{5,7},{6,4},{7,5},{8,10},{9,11},{10,... | collective-permute-start | bytes 393224 | tf_op jit(solution)/shard_map/ppermute | solution.py:35
  58.2 12.9 %collective-permute-start.17 = (bf16[2,128,256]{2,1,0:T(8,128)(2,1)S(1)}, bf16[2,128,256]{2,1,0:T(8,128)(2,1)S(1)}, u32[]{:S(2)}, u32[]{:S(2)}) collective-permute-start(bf16[2,128,256]{2,1,0:T(8,128)(2,1)S(1)} %get-tuple-element.31), channel_id=1, source_target_pairs={{0,4},{1,5},{2,6},{3,7},{4,0},{5,1},{6,2},{7,3},{8,12},{9,13},{10,... | collective-permute-start | bytes 393224 | tf_op jit(solution)/shard_map/ppermute | solution.py:35
  60.8 10.3 %collective-permute-start.18 = (bf16[2,128,256]{2,1,0:T(8,128)(2,1)S(1)}, bf16[2,128,256]{2,1,0:T(8,128)(2,1)S(1)}, u32[]{:S(2)}, u32[]{:S(2)}) collective-permute-start(bf16[2,128,256]{2,1,0:T(8,128)(2,1)S(1)} %get-tuple-element.32), channel_id=1, source_target_pairs={{0,6},{1,7},{2,4},{3,5},{4,2},{5,3},{6,0},{7,1},{8,14},{9,15},{10,... | collective-permute-start | bytes 393224 | tf_op jit(solution)/shard_map/ppermute | solution.py:35
  72.2 20.4 %collective-permute-start.28 = (bf16[512,896]{1,0:T(8,128)(2,1)S(1)}, bf16[512,896]{1,0:T(8,128)(2,1)}, u32[]{:S(2)}, u32[]{:S(2)}) collective-permute-start(bf16[512,896]{1,0:T(8,128)(2,1)S(1)} %collective-permute-done.13.refs_11_), channel_id=1, source_target_pairs={{0,16},{8,24},{16,0},{24,8},{1,17},{9,25},{17,1},{25,9},{2,18},{10... | collective-permute-start | bytes 2752520 | tf_op jit(solution)/shard_map/ppermute | solution.py:35
  73.7 20.1 %collective-permute-start.29 = (bf16[512,896]{1,0:T(8,128)(2,1)S(1)}, bf16[512,896]{1,0:T(8,128)(2,1)}, u32[]{:S(2)}, u32[]{:S(2)}) collective-permute-start(bf16[512,896]{1,0:T(8,128)(2,1)S(1)} %collective-permute-done.14.refs_16_), channel_id=1, source_target_pairs={{0,8},{8,0},{16,24},{24,16},{1,9},{9,1},{17,25},{25,17},{2,10},{10... | collective-permute-start | bytes 2752520 | tf_op jit(solution)/shard_map/ppermute | solution.py:35
  74.2 6.6 %collective-permute-start.21 = (bf16[2,128,256]{2,1,0:T(8,128)(2,1)S(1)}, bf16[2,128,256]{2,1,0:T(8,128)(2,1)S(1)}, u32[]{:S(2)}, u32[]{:S(2)}) collective-permute-start(bf16[2,128,256]{2,1,0:T(8,128)(2,1)S(1)} %add_convert_fusion.refs_2_), channel_id=1, source_target_pairs={{0,2},{1,3},{2,0},{3,1},{4,6},{5,7},{6,4},{7,5},{8,10},{9,11},{10,... | collective-permute-start | bytes 393224 | tf_op jit(solution)/shard_map/ppermute | solution.py:35
  76.5 11.6 %collective-permute-start.22 = (bf16[2,128,256]{2,1,0:T(8,128)(2,1)S(1)}, bf16[2,128,256]{2,1,0:T(8,128)(2,1)S(1)}, u32[]{:S(2)}, u32[]{:S(2)}) collective-permute-start(bf16[2,128,256]{2,1,0:T(8,128)(2,1)S(1)} %add_convert_fusion.refs_2_), channel_id=1, source_target_pairs={{0,4},{1,5},{2,6},{3,7},{4,0},{5,1},{6,2},{7,3},{8,12},{9,13},{10,... | collective-permute-start | bytes 393224 | tf_op jit(solution)/shard_map/ppermute | solution.py:35
  77.5 10.6 %collective-permute-start.23 = (bf16[2,128,256]{2,1,0:T(8,128)(2,1)S(1)}, bf16[2,128,256]{2,1,0:T(8,128)(2,1)S(1)}, u32[]{:S(2)}, u32[]{:S(2)}) collective-permute-start(bf16[2,128,256]{2,1,0:T(8,128)(2,1)S(1)} %add_convert_fusion.refs_2_), channel_id=1, source_target_pairs={{0,6},{1,7},{2,4},{3,5},{4,2},{5,3},{6,0},{7,1},{8,14},{9,15},{10,... | collective-permute-start | bytes 393224 | tf_op jit(solution)/shard_map/ppermute | solution.py:35
  80.8 7.8 %collective-permute-start.24 = (bf16[2,128,256]{2,1,0:T(8,128)(2,1)S(1)}, bf16[2,128,256]{2,1,0:T(8,128)(2,1)S(1)}, u32[]{:S(2)}, u32[]{:S(2)}) collective-permute-start(bf16[2,128,256]{2,1,0:T(8,128)(2,1)S(1)} %add_convert_fusion.refs_2_), channel_id=1, source_target_pairs={{0,1},{1,0},{2,3},{3,2},{4,5},{5,4},{6,7},{7,6},{8,9},{9,8},{10,11... | collective-permute-start | bytes 393224 | tf_op jit(solution)/shard_map/ppermute | solution.py:35
  (13 other events, 35.4 us)

commit v2 on v1

--- a/solution.py
+++ b/solution.py
@@ -8,13 +8,12 @@
 from jax.sharding import PartitionSpec as P
 
 epsilon = 1e-05
-params = pltpu.CompilerParams(vmem_limit_bytes=24 * 1024 * 1024)
 vmem = pl.BlockSpec(memory_space=pltpu.VMEM)
 smem = pl.BlockSpec(memory_space=pltpu.SMEM)
 anywhere = pl.BlockSpec(memory_space=pltpu.HBM)
 
 
-def call(kernel, out_shape, ops, scratch=(), far=()):
+def call(kernel, out_shape, ops, scratch=(), far=(), mib=4):
     specs = [smem] + [anywhere if i in far else vmem for i in range(1, len(ops))]
     ops = [
         pltpu.with_memory_space_constraint(op, pltpu.HBM) if i in far else op
@@ -26,7 +25,7 @@
         in_specs=specs,
         out_specs=jax.tree.map(lambda _: vmem, out_shape),
         scratch_shapes=list(scratch),
-        compiler_params=params,
+        compiler_params=pltpu.CompilerParams(vmem_limit_bytes=mib * 1024 * 1024),
     )(*ops)
 
 
@@ -45,22 +44,57 @@
     return copies
 
 
-def select_kernel(dp, ids, code, *refs):
+def pack_kernel(lengths, targets_far, hidden, out, targets, sems):
+    reqs = hidden.shape[0]
+    copies = fetch([targets_far, hidden], [targets, out.at[pl.ds(0, reqs)]], sems)
+    copies[0].wait()
+    slots, part = targets.shape[1], hidden.shape[2]
+    row = lax.broadcasted_iota(jnp.int32, (slots, part), 0)
+    lane = lax.broadcasted_iota(jnp.int32, (slots, part), 1)
+    high = lax.shift_right_logical(targets[...], 7)
+    low = targets[...] - high * 128
+    block = jnp.zeros((reqs, part), jnp.float32)
+    for first, values in ((1, high), (1 + slots, low)):
+        spot = (lane == row + first).astype(jnp.float32).astype(jnp.bfloat16)
+        values = values.astype(jnp.float32).astype(jnp.bfloat16)
+        block = block + jnp.dot(values, spot, preferred_element_type=jnp.float32)
+    row = lax.broadcasted_iota(jnp.int32, (reqs, part), 0)
+    lane = lax.broadcasted_iota(jnp.int32, (reqs, part), 1)
+    for r in range(reqs):
+        here = jnp.logical_and(row == r, lane == 0)
+        block = jnp.where(here, lengths[r].astype(jnp.float32), block)
+    out[reqs] = block.astype(jnp.bfloat16)
+    copies[1].wait()
+
+
+def select_kernel(dp, ids, plan, *refs):
     parts, (out, own, sems) = list(refs[: 2 * dp]), refs[2 * dp :]
-    copies = fetch([parts[0], parts[dp]], [own.at[0], own.at[1]], sems)
+    (copy,) = fetch([parts[0]], [own], sems)
+    parts[0] = own
     rows = out.shape[1]
+    reqs, slots, _ = own.shape
+    here = reqs * slots
     me = ids[0]
-    wanted = me * rows + lax.broadcasted_iota(jnp.int32, (rows, code.shape[2]), 0)
-    hots = [
-        (code[me ^ k] == wanted).astype(jnp.float32).astype(jnp.bfloat16) for k in range(dp)
+    lengths = [
+        parts[dp + k][reqs].astype(jnp.float32)[:, 0:1].astype(jnp.int32) for k in range(dp)
     ]
-    for m in range(2):
-        copies[m].wait()
-        parts[m * dp] = own.at[m]
+    lengths = jnp.concatenate(lengths, axis=0)
+    row = lax.broadcasted_iota(jnp.int32, (reqs, here), 0)
+    slot = jnp.concatenate([row + (me ^ k) * reqs for k in range(dp)], axis=0)
+    position = lax.rem(lax.broadcasted_iota(jnp.int32, (1, here), 1), slots)
+    wanted = me * rows + lax.broadcasted_iota(jnp.int32, (rows, here), 0)
+    hots = []
+    for k in range(dp):
+        owner = plan[me ^ k]
+        start = jnp.sum(jnp.where(slot < owner, lengths, 0), axis=0, keepdims=True)
+        live = jnp.sum(jnp.where(slot == owner, lengths, 0), axis=0, keepdims=True)
+        code = jnp.where(position < live, start + position, -1)
+        hots.append((code == wanted).astype(jnp.float32).astype(jnp.bfloat16))
+    copy.wait()
     for m in range(2):
         total = None
         for k in range(dp):
-            values = parts[m * dp + k][...]
+            values = parts[m * dp + k][0:reqs]
             values = values.reshape(-1, values.shape[-1])
             found = jnp.dot(hots[k], values, preferred_element_type=jnp.float32)
             total = found if total is None else total + found
@@ -218,18 +252,33 @@
             for k in [k for k in blocks[m] if places(m, k)]:
                 blocks[m][k ^ bit] = exchange(blocks[m][k], "dp", bit)
 
-    hiddens = [{0: hidden_policy}, {0: hidden_reference}]
+    packed = call(
+        pack_kernel,
+        jax.ShapeDtypeStruct((reqs + 1, slots, part), jnp.bfloat16),
+        (lengths, targets, hidden_reference),
+        [pltpu.VMEM(targets.shape, jnp.int32), pltpu.SemaphoreType.DMA((2,))],
+        far=(1, 2),
+    )
+    hiddens = [{0: hidden_policy}, {0: packed}]
+    outs = [{0: out_policy}, {0: out_reference}]
+
+    def wait_for(first, places):
+        flat = [(m, k) for m in range(2) for k in outs[m] if places(m, k)]
+        first, *values = lax.optimization_barrier((first, *[outs[m][k] for m, k in flat]))
+        for (m, k), value in zip(flat, values):
+            outs[m][k] = value
+        return first
+
     for step in range(len(bits)):
         spread_step(hiddens, step, lambda m, k: True)
     hidden_parts = [hiddens[m][k] for m in range(2) for k in range(dp)]
 
     order = jnp.arange(dp, dtype=jnp.int32)
-    facts = lax.all_gather(
-        jnp.concatenate([lengths[:, None], targets], axis=1), "dp", axis=0, tiled=True
-    )
-    all_lengths = facts[:, 0]
-    all_targets = facts[:, 1:].reshape(-1)
-    slot_ids = jnp.arange(dp * reqs, dtype=jnp.int32)
+    facts = jnp.stack([hiddens[1][k][reqs, :, : 2 * slots + 1] for k in range(dp)])
+    facts = facts.astype(jnp.float32).astype(jnp.int32)
+    all_lengths = facts[:, :, 0].reshape(-1)
+    all_targets = (facts[:, :, 1 : slots + 1] * 128 + facts[:, :, slots + 1 :]).reshape(-1)
+    slot_ids = ((order ^ dp_index)[:, None] * reqs + jnp.arange(reqs, dtype=jnp.int32)).reshape(-1)
     positions = jnp.arange(slots, dtype=jnp.int32)
 
     def codes(slot):
@@ -239,26 +288,16 @@
             positions[None] < live[:, None], start[:, None] + positions[None], jnp.int32(-1)
         )
 
-    source_code = codes(move_plan).reshape(dp, 1, here)
+    plan = jnp.repeat(move_plan, slots).reshape(dp, 1, here)
     moved = call(
         functools.partial(select_kernel, dp),
         jax.ShapeDtypeStruct((2, rows, part), jnp.bfloat16),
-        (ids, source_code, *hidden_parts),
-        [pltpu.VMEM((2,) + hidden_policy.shape, jnp.bfloat16), pltpu.SemaphoreType.DMA((2,))],
-        far=(2, 2 + dp),
-    )
-
-    outs = [{0: out_policy}, {0: out_reference}]
-
-    def after(first, step, places):
-        flat = [(m, k) for m in range(2) for k in outs[m]]
-        first, *values = lax.optimization_barrier((first, *[outs[m][k] for m, k in flat]))
-        for (m, k), value in zip(flat, values):
-            outs[m][k] = value
-        spread_step(outs, step, places)
-        return first
-
-    moved = after(moved, 0, lambda m, k: True)
+        (ids, plan, *hidden_parts),
+        [pltpu.VMEM(hidden_policy.shape, jnp.bfloat16), pltpu.SemaphoreType.DMA((1,))],
+        far=(2,),
+    )
+    moved = wait_for(moved, lambda m, k: True)
+    spread_step(outs, 0, lambda m, k: True)
 
     far = sorted(range(1, half), key=lambda k: (k.bit_length() <= 1, k))
 
@@ -274,7 +313,9 @@
     normed_scratch = pltpu.VMEM((mp, rows, part), jnp.bfloat16)
     parts = gather_pair(moved)
     if len(bits) > 1:
-        parts[-1] = after(parts[-1], 1, lambda m, k: k == 0)
+        parts[-1] = wait_for(parts[-1], lambda m, k: k == 0)
+        later = [{0: outs[m][0]} for m in range(2)]
+        spread_step(later, 1, lambda m, k: True)
     block = jax.ShapeDtypeStruct((2, rows, part), jnp.bfloat16)
     keep, send = call(
         functools.partial(ffn_kernel, half),
@@ -300,8 +341,9 @@
             pltpu.SemaphoreType.DMA((6,)),
         ],
         far=range(1, 7),
-    )
-    came = exchange(send, "mp", 1)
+        mib=16,
+    )
+    came = wait_for(exchange(send, "mp", 1), lambda m, k: k > 0)
     own, *pieces = call(
         pair_kernel,
         (jax.ShapeDtypeStruct((2, rows, part), jnp.float32),) + (block,) * (half - 1),
@@ -312,9 +354,13 @@
         own = own + arrived[k].astype(jnp.float32)
     stream = own.astype(jnp.bfloat16)
     if len(bits) > 1:
-        stream = after(stream, 1, lambda m, k: k == bit_orders[m][0])
+        spread_step(outs, 1, lambda m, k: k == bit_orders[m][0])
+        for m in range(2):
+            outs[m].update(later[m])
+        stream = wait_for(stream, lambda m, k: k != bits[0] + bits[1])
     for step in range(2, len(bits)):
-        stream = after(stream, step, lambda m, k: True)
+        stream = wait_for(stream, lambda m, k: True)
+        spread_step(outs, step, lambda m, k: True)
 
     owner_code = codes(slot_ids).reshape(-1)
     my_ranks = dp_index * rows + jnp.arange(rows, dtype=jnp.int32)
@@ -341,6 +387,7 @@
             pltpu.SemaphoreType.DMA((4,)),
         ],
         far=(2, 3, 4 + mp, 4 + mp + dp),
+        mib=16,
     )
     flips = [1 << b for b in range(mp.bit_length() - 1)]
     for flip in flips[:-1]:
@@ -354,11 +401,10 @@
         jax.ShapeDtypeStruct((1, rows), jnp.float32),
         (ids, stats, exchange(stats, "mp", flips[-1])),
     )
-    for bit in bits:
-        diff = jnp.concatenate([diff, exchange(diff, "dp", bit)])
-    ranks = (order ^ dp_index)[:, None] * rows + jnp.arange(rows, dtype=jnp.int32)[None]
+    diff = jnp.concatenate([diff] + [exchange(diff, "dp", k) for k in range(1, dp)])
+    ranks = ((order ^ dp_index)[:, None] * rows + jnp.arange(rows, dtype=jnp.int32)).reshape(-1)
     my_code = codes(dp_index * reqs + jnp.arange(reqs, dtype=jnp.int32))
-    hit = my_code[:, :, None] == ranks.reshape(1, 1, -1)
+    hit = my_code[:, :, None] == ranks[None, None]
     token_diff = jnp.sum(jnp.where(hit, diff.reshape(1, 1, -1), 0.0), axis=2)
     return (token_diff, jnp.sum(token_diff, axis=1))
 

time: 121 us -> 109 us (0.901)
  blocking collectives: 8.61 us -> 0 us
  waiting for transfers between devices: 54 us -> 46.6 us
  Pallas kernels: 14.5 us -> 17.8 us
    all_gather x1 -> x0, blocking collectives: 8.61 us -> none  [local(): lax.all_gather(jnp.concatenate([lengths[:, None], targets], axis=1), 'dp'...]
    ppermute x35 -> x36, waiting for transfers between devices: 54 us -> 46.6 us  [exchange(): return lax.ppermute(values, axis, [(i, i ^ flip) for i in range(count)])]
    pallas_call x7 -> x8, Pallas kernels: 14.5 us -> 17.8 us  [call(): pl.pallas_call(kernel, out_shape=out_shape, in_specs=specs, out_specs=jax...]
    slice x2 -> x5, local copies, waits for them, and re-layouts: 0.18 us -> 2.16 us  [the longest x4 2.02 us: local(): hiddens[1][k][reqs, :, :2 * slots + 1]]
    ppermute x35 -> x36, starting transfers between devices: 35.9 us -> 34.7 us  [exchange(): return lax.ppermute(values, axis, [(i, i ^ flip) for i in range(count)])]
  transfers between devices with their start and end apart: 35 -> 36, of which waited for: 21 -> 27; matrix products, arithmetic and copies ran while one was open for 3% -> 6% of each run, Pallas kernels for 5% -> 7%
where the time goes in v2:
time: 109 us; the launch traced here: 108 us
  waiting for transfers between devices  46.6 us (43%)
  starting transfers between devices  34.7 us (32%)
  Pallas kernels  17.8 us (16%)
  local copies, waits for them, and re-layouts  4.86 us (4%)
  other arithmetic  3.52 us (3%)
    ppermute x36, waiting for transfers between devices, exchange(): return lax.ppermute(values, axis, [(i, i ^ flip) for i in range(count)])  46.6 us
    ppermute x36, starting transfers between devices, exchange(): return lax.ppermute(values, axis, [(i, i ^ flip) for i in range(count)])  34.7 us
    pallas_call x8, Pallas kernels, call(): pl.pallas_call(kernel, out_shape=out_shape, in_specs=specs, out_specs=jax...  17.8 us
  transfers between devices with their start and end apart: 36, of which 27 were waited for; matrix products, arithmetic and copies ran while one was open for 6% of the time, Pallas kernels for 7%

profile of v2, /device:TPU:0, one launch (start us, length us, event | category | flops | bytes accessed | tf_op | source)
XLA Modules:
  0.0 108.3 jit_solution(12250562257663868663)
XLA Ops:
  1.3 1.5 %shard_map.158.refs_4_ = bf16[17,16,256]{2,1,0:T(8,128)(2,1)S(1)} custom-call(s32[16]{0:T(128)S(1)} %copy-done.4, s32[16,16]{1,0:T(8,128)} %targets_far.1, bf16[16,16,256]{2,1,0:T(8,128)(2,1)} %hidden.1), custom_call_target="tpu_custom_call" | custom-call | tf_op jit(solution)/shard_map/pallas_call | solution.py:22
  2.8 3.0 %collective-permute-start.1 = (bf16[17,16,256]{2,1,0:T(8,128)(2,1)S(1)}, bf16[17,16,256]{2,1,0:T(8,128)(2,1)S(1)}, u32[]{:S(2)}, u32[]{:S(2)}) collective-permute-start(bf16[17,16,256]{2,1,0:T(8,128)(2,1)S(1)} %shard_map.158.refs_4_), channel_id=1, source_target_pairs={{0,16},{8,24},{16,0},{24,8},{1,17},{9,25},{17,1},{25,9},{2,18},{10... | collective-permute-start | bytes 417800 | tf_op jit(solution)/shard_map/ppermute | solution.py:34
  5.8 1.5 %collective-permute-start.3 = (bf16[16,16,256]{2,1,0:T(8,128)(2,1)}, bf16[16,16,256]{2,1,0:T(8,128)(2,1)S(1)}, u32[]{:S(2)}, u32[]{:S(2)}) collective-permute-start(bf16[16,16,256]{2,1,0:T(8,128)(2,1)} %refs_0_.1), channel_id=1, source_target_pairs={{0,8},{8,0},{16,24},{24,16},{1,9},{9,1},{17,25},{25,17},{2,10},{10... | collective-permute-start | bytes 393224 | tf_op jit(solution)/shard_map/ppermute | solution.py:34
  7.8 1.6 %collective-permute-done.1.refs_6_ = bf16[17,16,256]{2,1,0:T(8,128)(2,1)S(1)} collective-permute-done((bf16[17,16,256]{2,1,0:T(8,128)(2,1)S(1)}, bf16[17,16,256]{2,1,0:T(8,128)(2,1)S(1)}, u32[]{:S(2)}, u32[]{:S(2)}) %collective-permute-start.1) | collective-permute-done | bytes 139296 | tf_op jit(solution)/shard_map/ppermute | solution.py:34
  9.5 1.7 %collective-permute-start.2 = (bf16[17,16,256]{2,1,0:T(8,128)(2,1)S(1)}, bf16[17,16,256]{2,1,0:T(8,128)(2,1)S(1)}, u32[]{:S(2)}, u32[]{:S(2)}) collective-permute-start(bf16[17,16,256]{2,1,0:T(8,128)(2,1)S(1)} %collective-permute-done.1.refs_6_), channel_id=1, source_target_pairs={{0,8},{8,0},{16,24},{24,16},{1,9},{9,1},{17,25},{25,17},{2,10},{10... | collective-permute-start | bytes 417800 | tf_op jit(solution)/shard_map/ppermute | solution.py:34
  11.2 1.5 %collective-permute-start.4 = (bf16[16,16,256]{2,1,0:T(8,128)(2,1)}, bf16[16,16,256]{2,1,0:T(8,128)(2,1)S(1)}, u32[]{:S(2)}, u32[]{:S(2)}) collective-permute-start(bf16[16,16,256]{2,1,0:T(8,128)(2,1)} %refs_0_.1), channel_id=1, source_target_pairs={{0,16},{8,24},{16,0},{24,8},{1,17},{9,25},{17,1},{25,9},{2,18},{10... | collective-permute-start | bytes 393224 | tf_op jit(solution)/shard_map/ppermute | solution.py:34
  14.2 2.7 %collective-permute-done.4.refs_2_ = bf16[16,16,256]{2,1,0:T(8,128)(2,1)S(1)} collective-permute-done((bf16[16,16,256]{2,1,0:T(8,128)(2,1)}, bf16[16,16,256]{2,1,0:T(8,128)(2,1)S(1)}, u32[]{:S(2)}, u32[]{:S(2)}) %collective-permute-start.4) | collective-permute-done | bytes 131104 | tf_op jit(solution)/shard_map/ppermute | solution.py:34
  18.3 1.8 %shard_map.159.refs_6_ = bf16[2,128,256]{2,1,0:T(8,128)(2,1)S(1)} custom-call(s32[4]{0:T(128)S(1)} %pad_add_fusion.ids, s32[4,1,256]{2,1,0:T(1,128)S(1)} %broadcast_in_dim.109.plan, bf16[16,16,256]{2,1,0:T(8,128)(2,1)} %refs_0_.1, bf16[16,16,256]{2,1,0:T(8,128)(2,1)S(1)} %collective-permute-done.3.refs_1_, ...), custom_call_target="tpu_custom_call" | custom-call | tf_op jit(solution)/shard_map/pallas_call | solution.py:22
  20.1 3.7 %collective-permute-start.8 = (bf16[2,128,256]{2,1,0:T(8,128)(2,1)S(1)}, bf16[2,128,256]{2,1,0:T(8,128)(2,1)S(1)}, u32[]{:S(2)}, u32[]{:S(2)}) collective-permute-start(bf16[2,128,256]{2,1,0:T(8,128)(2,1)S(1)} %shard_map.159.refs_6_), channel_id=1, source_target_pairs={{0,6},{1,7},{2,4},{3,5},{4,2},{5,3},{6,0},{7,1},{8,14},{9,15},{10,... | collective-permute-start | bytes 393224 | tf_op jit(solution)/shard_map/ppermute | solution.py:34
  24.4 1.5 %collective-permute-start.15 = (bf16[512,896]{1,0:T(8,128)(2,1)}, bf16[512,896]{1,0:T(8,128)(2,1)S(1)}, u32[]{:S(2)}, u32[]{:S(2)}) collective-permute-start(bf16[512,896]{1,0:T(8,128)(2,1)} %refs_14_), channel_id=1, source_target_pairs={{0,16},{8,24},{16,0},{24,8},{1,17},{9,25},{17,1},{25,9},{2,18},{10... | collective-permute-start | bytes 2752520 | tf_op jit(solution)/shard_map/ppermute | solution.py:34
  27.4 5.7 %collective-permute-done.6.refs_7_ = bf16[2,128,256]{2,1,0:T(8,128)(2,1)S(1)} collective-permute-done((bf16[2,128,256]{2,1,0:T(8,128)(2,1)S(1)}, bf16[2,128,256]{2,1,0:T(8,128)(2,1)S(1)}, u32[]{:S(2)}, u32[]{:S(2)}) %collective-permute-start.6) | collective-permute-done | bytes 131104 | tf_op jit(solution)/shard_map/ppermute | solution.py:34
  35.0 5.8 %shard_map.160 = (f32[4,2,128,256]{3,2,1,0:T(8,128)S(1)}, bf16[4,2,128,256]{3,2,1,0:T(8,128)(2,1)}) custom-call(s32[4]{0:T(128)S(1)} %pad_add_fusion.ids, f32[1,2048]{1,0:T(1,128)} %bitcast.13, f32[1,2048]{1,0:T(1,128)} %bitcast.14, bf16[2048,512]{1,0:T(8,128)(2,1)} %refs_2_.1, bf16[2048,512]{1,0:T(8,128)(2,1)} %refs_3_.1, bf16[512,2048]{1,0:T(8,128)(2,1)} %refs_4_.1, ...), custom_call_target="tpu_custom_call" | custom-call | tf_op jit(solution)/shard_map/pallas_call | solution.py:22
  46.8 1.5 %collective-permute-start.18 = (bf16[2,128,256]{2,1,0:T(8,128)(2,1)}, bf16[2,128,256]{2,1,0:T(8,128)(2,1)S(1)}, u32[]{:S(2)}, u32[]{:S(2)}) collective-permute-start(bf16[2,128,256]{2,1,0:T(8,128)(2,1)} %get-tuple-element.34), channel_id=1, source_target_pairs={{0,6},{1,7},{2,4},{3,5},{4,2},{5,3},{6,0},{7,1},{8,14},{9,15},{10,... | collective-permute-start | bytes 393224 | tf_op jit(solution)/shard_map/ppermute | solution.py:34
  48.3 2.9 %collective-permute-start.16 = (bf16[2,128,256]{2,1,0:T(8,128)(2,1)}, bf16[2,128,256]{2,1,0:T(8,128)(2,1)S(1)}, u32[]{:S(2)}, u32[]{:S(2)}) collective-permute-start(bf16[2,128,256]{2,1,0:T(8,128)(2,1)} %get-tuple-element.32), channel_id=1, source_target_pairs={{0,2},{1,3},{2,0},{3,1},{4,6},{5,7},{6,4},{7,5},{8,10},{9,11},{10,... | collective-permute-start | bytes 393224 | tf_op jit(solution)/shard_map/ppermute | solution.py:34
  53.3 1.9 %collective-permute-done.18 = bf16[2,128,256]{2,1,0:T(8,128)(2,1)S(1)} collective-permute-done((bf16[2,128,256]{2,1,0:T(8,128)(2,1)}, bf16[2,128,256]{2,1,0:T(8,128)(2,1)S(1)}, u32[]{:S(2)}, u32[]{:S(2)}) %collective-permute-start.18) | collective-permute-done | bytes 131104 | tf_op jit(solution)/shard_map/ppermute | solution.py:34
  56.1 3.3 %collective-permute-done.17 = bf16[2,128,256]{2,1,0:T(8,128)(2,1)S(1)} collective-permute-done((bf16[2,128,256]{2,1,0:T(8,128)(2,1)}, bf16[2,128,256]{2,1,0:T(8,128)(2,1)S(1)}, u32[]{:S(2)}, u32[]{:S(2)}) %collective-permute-start.17) | collective-permute-done | bytes 131104 | tf_op jit(solution)/shard_map/ppermute | solution.py:34
  61.7 2.9 %collective-permute-done.19.refs_12_ = bf16[512,896]{1,0:T(8,128)(2,1)} collective-permute-done((bf16[512,896]{1,0:T(8,128)(2,1)}, bf16[512,896]{1,0:T(8,128)(2,1)}, u32[]{:S(2)}, u32[]{:S(2)}) %collective-permute-start.19) | collective-permute-done | bytes 917536 | tf_op jit(solution)/shard_map/ppermute | solution.py:34
  66.1 3.2 %collective-permute-start.22 = (bf16[2,128,256]{2,1,0:T(8,128)(2,1)S(1)}, bf16[2,128,256]{2,1,0:T(8,128)(2,1)S(1)}, u32[]{:S(2)}, u32[]{:S(2)}) collective-permute-start(bf16[2,128,256]{2,1,0:T(8,128)(2,1)S(1)} %add_convert_fusion.refs_2_), channel_id=1, source_target_pairs={{0,4},{1,5},{2,6},{3,7},{4,0},{5,1},{6,2},{7,3},{8,12},{9,13},{10,... | collective-permute-start | bytes 393224 | tf_op jit(solution)/shard_map/ppermute | solution.py:34
  70.5 1.7 %collective-permute-done.21.refs_3_ = bf16[2,128,256]{2,1,0:T(8,128)(2,1)S(1)} collective-permute-done((bf16[2,128,256]{2,1,0:T(8,128)(2,1)S(1)}, bf16[2,128,256]{2,1,0:T(8,128)(2,1)S(1)}, u32[]{:S(2)}, u32[]{:S(2)}) %collective-permute-start.21) | collective-permute-done | bytes 131104 | tf_op jit(solution)/shard_map/ppermute | solution.py:34
  72.6 5.1 %collective-permute-done.22.refs_4_ = bf16[2,128,256]{2,1,0:T(8,128)(2,1)S(1)} collective-permute-done((bf16[2,128,256]{2,1,0:T(8,128)(2,1)S(1)}, bf16[2,128,256]{2,1,0:T(8,128)(2,1)S(1)}, u32[]{:S(2)}, u32[]{:S(2)}) %collective-permute-start.22) | collective-permute-done | bytes 131104 | tf_op jit(solution)/shard_map/ppermute | solution.py:34
  79.7 4.1 %collective-permute-done.28.refs_13_ = bf16[512,896]{1,0:T(8,128)(2,1)S(1)} collective-permute-done((bf16[512,896]{1,0:T(8,128)(2,1)S(1)}, bf16[512,896]{1,0:T(8,128)(2,1)S(1)}, u32[]{:S(2)}, u32[]{:S(2)}) %collective-permute-start.28) | collective-permute-done | bytes 917536 | tf_op jit(solution)/shard_map/ppermute | solution.py:34
  84.6 5.7 %shard_map.162.mine = f32[8,128]{1,0:T(8,128)S(1)} custom-call(s32[4]{0:T(128)S(1)} %pad_add_fusion.ids, s32[128,1]{1,0:T(8,128)S(1)} %copy.19.wanted, f32[1,2048]{1,0:T(1,128)} %bitcast.15, f32[1,2048]{1,0:T(1,128)} %bitcast.16, bf16[2,128,256]{2,1,0:T(8,128)(2,1)S(1)} %add_convert_fusion.refs_2_, bf16[2,128,256]{2,1,0:T(8,128)(2,1)S(1)} %collective-permute-done.21.refs_3_, ...), custom_call_target="tpu_custom_call" | custom-call | tf_op jit(solution)/shard_map/pallas_call | solution.py:22
  92.2 3.6 %collective-permute-done.31.came = f32[8,128]{1,0:T(8,128)S(1)} collective-permute-done((f32[8,128]{1,0:T(8,128)S(1)}, f32[8,128]{1,0:T(8,128)S(1)}, u32[]{:S(2)}, u32[]{:S(2)}) %collective-permute-start.31) | collective-permute-done | bytes 4128 | tf_op jit(solution)/shard_map/ppermute | solution.py:34
  97.7 3.1 %collective-permute-done.32.came = f32[8,128]{1,0:T(8,128)S(1)} collective-permute-done((f32[8,128]{1,0:T(8,128)S(1)}, f32[8,128]{1,0:T(8,128)S(1)}, u32[]{:S(2)}, u32[]{:S(2)}) %collective-permute-start.32) | collective-permute-done | bytes 4128 | tf_op jit(solution)/shard_map/ppermute | solution.py:34
  (98 shorter events, 36.4 us)
Async XLA Ops:
  2.8 6.7 %collective-permute-start.1 = (bf16[17,16,256]{2,1,0:T(8,128)(2,1)S(1)}, bf16[17,16,256]{2,1,0:T(8,128)(2,1)S(1)}, u32[]{:S(2)}, u32[]{:S(2)}) collective-permute-start(bf16[17,16,256]{2,1,0:T(8,128)(2,1)S(1)} %shard_map.158.refs_4_), channel_id=1, source_target_pairs={{0,16},{8,24},{16,0},{24,8},{1,17},{9,25},{17,1},{25,9},{2,18},{10... | collective-permute-start | bytes 417800 | tf_op jit(solution)/shard_map/ppermute | solution.py:34
  5.8 6.9 %collective-permute-start.3 = (bf16[16,16,256]{2,1,0:T(8,128)(2,1)}, bf16[16,16,256]{2,1,0:T(8,128)(2,1)S(1)}, u32[]{:S(2)}, u32[]{:S(2)}) collective-permute-start(bf16[16,16,256]{2,1,0:T(8,128)(2,1)} %refs_0_.1), channel_id=1, source_target_pairs={{0,8},{8,0},{16,24},{24,16},{1,9},{9,1},{17,25},{25,17},{2,10},{10... | collective-permute-start | bytes 393224 | tf_op jit(solution)/shard_map/ppermute | solution.py:34
  7.3 9.6 %collective-permute-start = (bf16[17,16,256]{2,1,0:T(8,128)(2,1)S(1)}, bf16[17,16,256]{2,1,0:T(8,128)(2,1)S(1)}, u32[]{:S(2)}, u32[]{:S(2)}) collective-permute-start(bf16[17,16,256]{2,1,0:T(8,128)(2,1)S(1)} %shard_map.158.refs_4_), channel_id=1, source_target_pairs={{0,8},{8,0},{16,24},{24,16},{1,9},{9,1},{17,25},{25,17},{2,10},{10... | collective-permute-start | bytes 417800 | tf_op jit(solution)/shard_map/ppermute | solution.py:34
  9.5 8.8 %collective-permute-start.2 = (bf16[17,16,256]{2,1,0:T(8,128)(2,1)S(1)}, bf16[17,16,256]{2,1,0:T(8,128)(2,1)S(1)}, u32[]{:S(2)}, u32[]{:S(2)}) collective-permute-start(bf16[17,16,256]{2,1,0:T(8,128)(2,1)S(1)} %collective-permute-done.1.refs_6_), channel_id=1, source_target_pairs={{0,8},{8,0},{16,24},{24,16},{1,9},{9,1},{17,25},{25,17},{2,10},{10... | collective-permute-start | bytes 417800 | tf_op jit(solution)/shard_map/ppermute | solution.py:34
  11.2 5.7 %collective-permute-start.4 = (bf16[16,16,256]{2,1,0:T(8,128)(2,1)}, bf16[16,16,256]{2,1,0:T(8,128)(2,1)S(1)}, u32[]{:S(2)}, u32[]{:S(2)}) collective-permute-start(bf16[16,16,256]{2,1,0:T(8,128)(2,1)} %refs_0_.1), channel_id=1, source_target_pairs={{0,16},{8,24},{16,0},{24,8},{1,17},{9,25},{17,1},{25,9},{2,18},{10... | collective-permute-start | bytes 393224 | tf_op jit(solution)/shard_map/ppermute | solution.py:34
  12.7 5.6 %collective-permute-start.5 = (bf16[16,16,256]{2,1,0:T(8,128)(2,1)S(1)}, bf16[16,16,256]{2,1,0:T(8,128)(2,1)S(1)}, u32[]{:S(2)}, u32[]{:S(2)}) collective-permute-start(bf16[16,16,256]{2,1,0:T(8,128)(2,1)S(1)} %collective-permute-done.3.refs_1_), channel_id=1, source_target_pairs={{0,16},{8,24},{16,0},{24,8},{1,17},{9,25},{17,1},{25,9},{2,18},{10... | collective-permute-start | bytes 393224 | tf_op jit(solution)/shard_map/ppermute | solution.py:34
  20.1 7.3 %collective-permute-start.8 = (bf16[2,128,256]{2,1,0:T(8,128)(2,1)S(1)}, bf16[2,128,256]{2,1,0:T(8,128)(2,1)S(1)}, u32[]{:S(2)}, u32[]{:S(2)}) collective-permute-start(bf16[2,128,256]{2,1,0:T(8,128)(2,1)S(1)} %shard_map.159.refs_6_), channel_id=1, source_target_pairs={{0,6},{1,7},{2,4},{3,5},{4,2},{5,3},{6,0},{7,1},{8,14},{9,15},{10,... | collective-permute-start | bytes 393224 | tf_op jit(solution)/shard_map/ppermute | solution.py:34
  23.8 20.0 %collective-permute-start.14 = (bf16[512,896]{1,0:T(8,128)(2,1)}, bf16[512,896]{1,0:T(8,128)(2,1)S(1)}, u32[]{:S(2)}, u32[]{:S(2)}) collective-permute-start(bf16[512,896]{1,0:T(8,128)(2,1)} %refs_10_), channel_id=1, source_target_pairs={{0,8},{8,0},{16,24},{24,16},{1,9},{9,1},{17,25},{25,17},{2,10},{10... | collective-permute-start | bytes 2752520 | tf_op jit(solution)/shard_map/ppermute | solution.py:34
  24.4 20.3 %collective-permute-start.15 = (bf16[512,896]{1,0:T(8,128)(2,1)}, bf16[512,896]{1,0:T(8,128)(2,1)S(1)}, u32[]{:S(2)}, u32[]{:S(2)}) collective-permute-start(bf16[512,896]{1,0:T(8,128)(2,1)} %refs_14_), channel_id=1, source_target_pairs={{0,16},{8,24},{16,0},{24,8},{1,17},{9,25},{17,1},{25,9},{2,18},{10... | collective-permute-start | bytes 2752520 | tf_op jit(solution)/shard_map/ppermute | solution.py:34
  25.8 7.3 %collective-permute-start.6 = (bf16[2,128,256]{2,1,0:T(8,128)(2,1)S(1)}, bf16[2,128,256]{2,1,0:T(8,128)(2,1)S(1)}, u32[]{:S(2)}, u32[]{:S(2)}) collective-permute-start(bf16[2,128,256]{2,1,0:T(8,128)(2,1)S(1)} %shard_map.159.refs_6_), channel_id=1, source_target_pairs={{0,2},{1,3},{2,0},{3,1},{4,6},{5,7},{6,4},{7,5},{8,10},{9,11},{10,... | collective-permute-start | bytes 393224 | tf_op jit(solution)/shard_map/ppermute | solution.py:34
  25.8 7.3 %collective-permute-start.7 = (bf16[2,128,256]{2,1,0:T(8,128)(2,1)S(1)}, bf16[2,128,256]{2,1,0:T(8,128)(2,1)S(1)}, u32[]{:S(2)}, u32[]{:S(2)}) collective-permute-start(bf16[2,128,256]{2,1,0:T(8,128)(2,1)S(1)} %shard_map.159.refs_6_), channel_id=1, source_target_pairs={{0,4},{1,5},{2,6},{3,7},{4,0},{5,1},{6,2},{7,3},{8,12},{9,13},{10,... | collective-permute-start | bytes 393224 | tf_op jit(solution)/shard_map/ppermute | solution.py:34
  27.4 6.3 %collective-permute-start.12 = (bf16[2,128,256]{2,1,0:T(8,128)(2,1)S(1)}, bf16[2,128,256]{2,1,0:T(8,128)(2,1)S(1)}, u32[]{:S(2)}, u32[]{:S(2)}) collective-permute-start(bf16[2,128,256]{2,1,0:T(8,128)(2,1)S(1)} %collective-permute-done.8.refs_9_), channel_id=1, source_target_pairs={{0,1},{1,0},{2,3},{3,2},{4,5},{5,4},{6,7},{7,6},{8,9},{9,8},{10,11... | collective-permute-start | bytes 393224 | tf_op jit(solution)/shard_map/ppermute | solution.py:34
  41.1 23.5 %collective-permute-start.19 = (bf16[512,896]{1,0:T(8,128)(2,1)}, bf16[512,896]{1,0:T(8,128)(2,1)}, u32[]{:S(2)}, u32[]{:S(2)}) collective-permute-start(bf16[512,896]{1,0:T(8,128)(2,1)} %refs_10_), channel_id=1, source_target_pairs={{0,16},{8,24},{16,0},{24,8},{1,17},{9,25},{17,1},{25,9},{2,18},{10... | collective-permute-start | bytes 2752520 | tf_op jit(solution)/shard_map/ppermute | solution.py:34
  42.4 23.5 %collective-permute-start.20 = (bf16[512,896]{1,0:T(8,128)(2,1)}, bf16[512,896]{1,0:T(8,128)(2,1)}, u32[]{:S(2)}, u32[]{:S(2)}) collective-permute-start(bf16[512,896]{1,0:T(8,128)(2,1)} %refs_14_), channel_id=1, source_target_pairs={{0,8},{8,0},{16,24},{24,16},{1,9},{9,1},{17,25},{25,17},{2,10},{10... | collective-permute-start | bytes 2752520 | tf_op jit(solution)/shard_map/ppermute | solution.py:34
  46.8 8.4 %collective-permute-start.18 = (bf16[2,128,256]{2,1,0:T(8,128)(2,1)}, bf16[2,128,256]{2,1,0:T(8,128)(2,1)S(1)}, u32[]{:S(2)}, u32[]{:S(2)}) collective-permute-start(bf16[2,128,256]{2,1,0:T(8,128)(2,1)} %get-tuple-element.34), channel_id=1, source_target_pairs={{0,6},{1,7},{2,4},{3,5},{4,2},{5,3},{6,0},{7,1},{8,14},{9,15},{10,... | collective-permute-start | bytes 393224 | tf_op jit(solution)/shard_map/ppermute | solution.py:34
  48.3 11.1 %collective-permute-start.17 = (bf16[2,128,256]{2,1,0:T(8,128)(2,1)}, bf16[2,128,256]{2,1,0:T(8,128)(2,1)S(1)}, u32[]{:S(2)}, u32[]{:S(2)}) collective-permute-start(bf16[2,128,256]{2,1,0:T(8,128)(2,1)} %get-tuple-element.33), channel_id=1, source_target_pairs={{0,4},{1,5},{2,6},{3,7},{4,0},{5,1},{6,2},{7,3},{8,12},{9,13},{10,... | collective-permute-start | bytes 393224 | tf_op jit(solution)/shard_map/ppermute | solution.py:34
  48.3 12.4 %collective-permute-start.16 = (bf16[2,128,256]{2,1,0:T(8,128)(2,1)}, bf16[2,128,256]{2,1,0:T(8,128)(2,1)S(1)}, u32[]{:S(2)}, u32[]{:S(2)}) collective-permute-start(bf16[2,128,256]{2,1,0:T(8,128)(2,1)} %get-tuple-element.32), channel_id=1, source_target_pairs={{0,2},{1,3},{2,0},{3,1},{4,6},{5,7},{6,4},{7,5},{8,10},{9,11},{10,... | collective-permute-start | bytes 393224 | tf_op jit(solution)/shard_map/ppermute | solution.py:34
  55.2 28.6 %collective-permute-start.28 = (bf16[512,896]{1,0:T(8,128)(2,1)S(1)}, bf16[512,896]{1,0:T(8,128)(2,1)S(1)}, u32[]{:S(2)}, u32[]{:S(2)}) collective-permute-start(bf16[512,896]{1,0:T(8,128)(2,1)S(1)} %collective-permute-done.14.refs_11_), channel_id=1, source_target_pairs={{0,16},{8,24},{16,0},{24,8},{1,17},{9,25},{17,1},{25,9},{2,18},{10... | collective-permute-start | bytes 2752520 | tf_op jit(solution)/shard_map/ppermute | solution.py:34
  59.3 25.2 %collective-permute-start.29 = (bf16[512,896]{1,0:T(8,128)(2,1)S(1)}, bf16[512,896]{1,0:T(8,128)(2,1)}, u32[]{:S(2)}, u32[]{:S(2)}) collective-permute-start(bf16[512,896]{1,0:T(8,128)(2,1)S(1)} %collective-permute-done.15.refs_16_), channel_id=1, source_target_pairs={{0,8},{8,0},{16,24},{24,16},{1,9},{9,1},{17,25},{25,17},{2,10},{10... | collective-permute-start | bytes 2752520 | tf_op jit(solution)/shard_map/ppermute | solution.py:34
  66.0 6.2 %collective-permute-start.21 = (bf16[2,128,256]{2,1,0:T(8,128)(2,1)S(1)}, bf16[2,128,256]{2,1,0:T(8,128)(2,1)S(1)}, u32[]{:S(2)}, u32[]{:S(2)}) collective-permute-start(bf16[2,128,256]{2,1,0:T(8,128)(2,1)S(1)} %add_convert_fusion.refs_2_), channel_id=1, source_target_pairs={{0,2},{1,3},{2,0},{3,1},{4,6},{5,7},{6,4},{7,5},{8,10},{9,11},{10,... | collective-permute-start | bytes 393224 | tf_op jit(solution)/shard_map/ppermute | solution.py:34
  66.1 11.7 %collective-permute-start.22 = (bf16[2,128,256]{2,1,0:T(8,128)(2,1)S(1)}, bf16[2,128,256]{2,1,0:T(8,128)(2,1)S(1)}, u32[]{:S(2)}, u32[]{:S(2)}) collective-permute-start(bf16[2,128,256]{2,1,0:T(8,128)(2,1)S(1)} %add_convert_fusion.refs_2_), channel_id=1, source_target_pairs={{0,4},{1,5},{2,6},{3,7},{4,0},{5,1},{6,2},{7,3},{8,12},{9,13},{10,... | collective-permute-start | bytes 393224 | tf_op jit(solution)/shard_map/ppermute | solution.py:34
  69.3 8.4 %collective-permute-start.23 = (bf16[2,128,256]{2,1,0:T(8,128)(2,1)S(1)}, bf16[2,128,256]{2,1,0:T(8,128)(2,1)S(1)}, u32[]{:S(2)}, u32[]{:S(2)}) collective-permute-start(bf16[2,128,256]{2,1,0:T(8,128)(2,1)S(1)} %add_convert_fusion.refs_2_), channel_id=1, source_target_pairs={{0,6},{1,7},{2,4},{3,5},{4,2},{5,3},{6,0},{7,1},{8,14},{9,15},{10,... | collective-permute-start | bytes 393224 | tf_op jit(solution)/shard_map/ppermute | solution.py:34
  72.2 6.1 %collective-permute-start.24 = (bf16[2,128,256]{2,1,0:T(8,128)(2,1)S(1)}, bf16[2,128,256]{2,1,0:T(8,128)(2,1)S(1)}, u32[]{:S(2)}, u32[]{:S(2)}) collective-permute-start(bf16[2,128,256]{2,1,0:T(8,128)(2,1)S(1)} %add_convert_fusion.refs_2_), channel_id=1, source_target_pairs={{0,1},{1,0},{2,3},{3,2},{4,5},{5,4},{6,7},{7,6},{8,9},{9,8},{10,11... | collective-permute-start | bytes 393224 | tf_op jit(solution)/shard_map/ppermute | solution.py:34
  96.3 4.6 %collective-permute-start.32 = (f32[8,128]{1,0:T(8,128)S(1)}, f32[8,128]{1,0:T(8,128)S(1)}, u32[]{:S(2)}, u32[]{:S(2)}) collective-permute-start(f32[8,128]{1,0:T(8,128)S(1)} %shard_map.164.mine), channel_id=1, source_target_pairs={{0,4},{1,5},{2,6},{3,7},{4,0},{5,1},{6,2},{7,3},{8,12},{9,13},{10,... | collective-permute-start | bytes 12296 | tf_op jit(solution)/shard_map/ppermute | solution.py:34
  (18 other events, 51.0 us)

commit v3 on v2

--- a/solution.py
+++ b/solution.py
@@ -68,16 +68,16 @@
 
 
 def select_kernel(dp, ids, plan, *refs):
-    parts, (out, own, sems) = list(refs[: 2 * dp]), refs[2 * dp :]
+    parts, (out, facts, own, sems) = list(refs[: 2 * dp]), refs[2 * dp :]
     (copy,) = fetch([parts[0]], [own], sems)
     parts[0] = own
     rows = out.shape[1]
     reqs, slots, _ = own.shape
     here = reqs * slots
     me = ids[0]
-    lengths = [
-        parts[dp + k][reqs].astype(jnp.float32)[:, 0:1].astype(jnp.int32) for k in range(dp)
-    ]
+    for k in range(dp):
+        facts[k] = parts[dp + k][reqs].astype(jnp.float32)
+    lengths = [facts[k][:, 0:1].astype(jnp.int32) for k in range(dp)]
     lengths = jnp.concatenate(lengths, axis=0)
     row = lax.broadcasted_iota(jnp.int32, (reqs, here), 0)
     slot = jnp.concatenate([row + (me ^ k) * reqs for k in range(dp)], axis=0)
@@ -101,7 +101,7 @@
         out[m] = total.astype(out.dtype)
 
 
-def normalise(values, gain, chip, core, scaled, normed):
+def normalise(values, gain, chip, core, scaled, store):
     half = len(values) // 2
     part = values[0].shape[1]
     width = part * len(values)
@@ -113,35 +113,33 @@
     for k, v in enumerate(values):
         scaled[2 * (chip ^ (k % half)) + (core if k < half else 1 - core)] = v * scale
     for b in range(2 * half):
-        normed[b] = (scaled[b] * gain[:, b * part : (b + 1) * part]).astype(jnp.bfloat16)
+        store(b, (scaled[b] * gain[:, b * part : (b + 1) * part]).astype(jnp.bfloat16))
     return values[0]
 
 
+def load_kernel(*refs):
+    count = (len(refs) - 2) // 2
+    for copy in fetch(refs[1 : 1 + count], refs[1 + count : -1], refs[-1]):
+        copy.wait()
+
+
 def ffn_kernel(half, ids, *refs):
+    gains_far, ups, downs = refs[:2], refs[2:4], refs[4:6]
     parts = refs[6 : 6 + 2 * half]
-    keep, send, gains, scaled, normed, up_store, down_store, sems = refs[6 + 2 * half :]
-    copies = fetch(
-        [refs[0], refs[2], refs[4], refs[1], refs[3], refs[5]],
-        [store.at[m] for m in range(2) for store in (gains, up_store, down_store)],
-        sems,
-    )
+    keep, send, gains, scaled, normed, sems = refs[6 + 2 * half :]
+    copies = fetch(gains_far, [gains.at[0], gains.at[1]], sems)
     chip, core = ids[1], ids[2]
+    part = parts[0].shape[2]
+
+    def store(b, values):
+        normed[:, b * part : (b + 1) * part] = values
+
     for m in range(2):
-        copies[3 * m].wait()
-        base = normalise([part[m] for part in parts], gains[m], chip, core, scaled, normed)
-        part = base.shape[1]
-        copies[3 * m + 1].wait()
-        pre = None
-        for b in range(2 * half):
-            piece = jnp.dot(
-                normed[b],
-                up_store[m, b * part : (b + 1) * part, :],
-                preferred_element_type=jnp.float32,
-            )
-            pre = piece if pre is None else pre + piece
+        copies[m].wait()
+        base = normalise([part[m] for part in parts], gains[m], chip, core, scaled, store)
+        pre = jnp.dot(normed[...], ups[m][...], preferred_element_type=jnp.float32)
         units = jax.nn.gelu(pre).astype(jnp.bfloat16)
-        copies[3 * m + 2].wait()
-        full = jnp.dot(units, down_store[m], preferred_element_type=jnp.float32)
+        full = jnp.dot(units, downs[m][...], preferred_element_type=jnp.float32)
         for b in range(2 * half):
             scaled[b] = full[:, b * part : (b + 1) * part]
         for k in range(half):
@@ -170,21 +168,23 @@
     lane = lax.broadcasted_iota(jnp.int32, (parts[0].shape[1], 128), 1)
     table = jnp.zeros(lane.shape, jnp.float32)
     ratio = 2 * half // dp
+    part = parts[0].shape[2]
+
+    def store(b, values):
+        normed[b // ratio, :, b % ratio * part : (b % ratio + 1) * part] = values
+
     for m in range(2):
         copies[2 * m].wait()
-        normalise([part[m] for part in parts], gains[m], chip, core, scaled, normed)
-        part = parts[0].shape[2]
-        copies[2 * m + 1].wait()
-        outs[m * dp] = out_store.at[m]
+        normalise([part[m] for part in parts], gains[m], chip, core, scaled, store)
         logits = None
-        for k in range(dp):
-            for b in range(ratio):
-                piece = jnp.dot(
-                    normed[(me ^ k) * ratio + b],
-                    outs[m * dp + k][b * part : (b + 1) * part, :],
-                    preferred_element_type=jnp.float32,
-                )
-                logits = piece if logits is None else logits + piece
+        for k in [*range(1, dp), 0]:
+            if k == 0:
+                copies[2 * m + 1].wait()
+                outs[m * dp] = out_store.at[m]
+            piece = jnp.dot(
+                normed[me ^ k], outs[m * dp + k][...], preferred_element_type=jnp.float32
+            )
+            logits = piece if logits is None else logits + piece
         entries = lax.broadcasted_iota(jnp.int32, logits.shape, 1) + ids[3] * logits.shape[1]
         picked = jnp.sum(jnp.where(entries == wanted[...], logits, 0.0), axis=1, keepdims=True)
         top = jnp.max(logits, axis=1, keepdims=True)
@@ -195,19 +195,21 @@
     stats[...] = jnp.transpose(table)[:8]
 
 
-def merge(ids, mine, came):
-    top = jnp.maximum(mine[0:2], came[0:2])
-    total = mine[2:4] * jnp.exp(mine[0:2] - top) + came[2:4] * jnp.exp(came[0:2] - top)
-    return top, total, mine[4:6] + came[4:6]
-
-
-def merge_kernel(ids, mine, came, out):
-    out[0:2], out[2:4], out[4:6] = merge(ids, mine, came)
+def merge(tables):
+    top = functools.reduce(jnp.maximum, [t[0:2] for t in tables])
+    total = sum(t[2:4] * jnp.exp(t[0:2] - top) for t in tables)
+    return top, total, sum(t[4:6] for t in tables)
+
+
+def merge_kernel(ids, *refs):
+    out = refs[-1]
+    out[0:2], out[2:4], out[4:6] = merge(refs[:-1])
     out[6:8] = jnp.zeros((2, out.shape[1]), jnp.float32)
 
 
-def last_kernel(ids, mine, came, out):
-    top, total, picked = merge(ids, mine, came)
+def last_kernel(ids, *refs):
+    out = refs[-1]
+    top, total, picked = merge(refs[:-1])
     logprob = picked - (top + jnp.log(total))
     out[...] = logprob[0:1] - logprob[1:2]
 
@@ -264,18 +266,32 @@
 
     def wait_for(first, places):
         flat = [(m, k) for m in range(2) for k in outs[m] if places(m, k)]
-        first, *values = lax.optimization_barrier((first, *[outs[m][k] for m, k in flat]))
+        first, values = lax.optimization_barrier((first, [outs[m][k] for m, k in flat]))
         for (m, k), value in zip(flat, values):
             outs[m][k] = value
         return first
 
-    for step in range(len(bits)):
-        spread_step(hiddens, step, lambda m, k: True)
+    for m in range(2):
+        for k in range(1, dp):
+            hiddens[m][k] = exchange(hiddens[m][0], "dp", k)
+    hiddens = wait_for(hiddens, lambda m, k: True)
+    spread_step(outs, 0, lambda m, k: True)
     hidden_parts = [hiddens[m][k] for m in range(2) for k in range(dp)]
 
     order = jnp.arange(dp, dtype=jnp.int32)
-    facts = jnp.stack([hiddens[1][k][reqs, :, : 2 * slots + 1] for k in range(dp)])
-    facts = facts.astype(jnp.float32).astype(jnp.int32)
+    plan = jnp.repeat(move_plan, slots).reshape(dp, 1, here)
+    moved, facts = call(
+        functools.partial(select_kernel, dp),
+        (
+            jax.ShapeDtypeStruct((2, rows, part), jnp.bfloat16),
+            jax.ShapeDtypeStruct((dp, reqs, part), jnp.float32),
+        ),
+        (ids, plan, *hidden_parts),
+        [pltpu.VMEM(hidden_policy.shape, jnp.bfloat16), pltpu.SemaphoreType.DMA((1,))],
+        far=(2,),
+    )
+
+    facts = facts[:, :, : 2 * slots + 1].astype(jnp.int32)
     all_lengths = facts[:, :, 0].reshape(-1)
     all_targets = (facts[:, :, 1 : slots + 1] * 128 + facts[:, :, slots + 1 :]).reshape(-1)
     slot_ids = ((order ^ dp_index)[:, None] * reqs + jnp.arange(reqs, dtype=jnp.int32)).reshape(-1)
@@ -288,17 +304,6 @@
             positions[None] < live[:, None], start[:, None] + positions[None], jnp.int32(-1)
         )
 
-    plan = jnp.repeat(move_plan, slots).reshape(dp, 1, here)
-    moved = call(
-        functools.partial(select_kernel, dp),
-        jax.ShapeDtypeStruct((2, rows, part), jnp.bfloat16),
-        (ids, plan, *hidden_parts),
-        [pltpu.VMEM(hidden_policy.shape, jnp.bfloat16), pltpu.SemaphoreType.DMA((1,))],
-        far=(2,),
-    )
-    moved = wait_for(moved, lambda m, k: True)
-    spread_step(outs, 0, lambda m, k: True)
-
     far = sorted(range(1, half), key=lambda k: (k.bit_length() <= 1, k))
 
     def gather_pair(own):
@@ -310,46 +315,46 @@
 
     gain_scratch = pltpu.VMEM((2, 1, part * mp), jnp.float32)
     scaled_scratch = pltpu.VMEM((mp, rows, part), jnp.float32)
-    normed_scratch = pltpu.VMEM((mp, rows, part), jnp.bfloat16)
     parts = gather_pair(moved)
     if len(bits) > 1:
-        parts[-1] = wait_for(parts[-1], lambda m, k: k == 0)
+        parts[-1] = wait_for(parts[-1], lambda m, k: True)
         later = [{0: outs[m][0]} for m in range(2)]
         spread_step(later, 1, lambda m, k: True)
     block = jax.ShapeDtypeStruct((2, rows, part), jnp.bfloat16)
+    weights = (up_policy, up_reference, down_policy, down_reference)
+    weights = call(
+        load_kernel,
+        tuple(jax.ShapeDtypeStruct(w.shape, w.dtype) for w in weights),
+        (ids, *weights),
+        [pltpu.SemaphoreType.DMA((4,))],
+        far=range(1, 5),
+        mib=12,
+    )
     keep, send = call(
         functools.partial(ffn_kernel, half),
         (
             jax.ShapeDtypeStruct((half, 2, rows, part), jnp.float32),
             jax.ShapeDtypeStruct((half, 2, rows, part), jnp.bfloat16),
         ),
-        (
-            ids,
-            *ffn_gains,
-            up_policy,
-            up_reference,
-            down_policy,
-            down_reference,
-            *parts,
-        ),
+        (ids, *ffn_gains, *weights, *parts),
         [
             gain_scratch,
             scaled_scratch,
-            normed_scratch,
-            pltpu.VMEM((2,) + up_policy.shape, jnp.bfloat16),
-            pltpu.VMEM((2,) + down_policy.shape, jnp.bfloat16),
-            pltpu.SemaphoreType.DMA((6,)),
+            pltpu.VMEM((rows, part * mp), jnp.bfloat16),
+            pltpu.SemaphoreType.DMA((2,)),
         ],
-        far=range(1, 7),
+        far=(1, 2),
         mib=16,
     )
-    came = wait_for(exchange(send, "mp", 1), lambda m, k: k > 0)
+    came = exchange(send, "mp", 1)
     own, *pieces = call(
         pair_kernel,
         (jax.ShapeDtypeStruct((2, rows, part), jnp.float32),) + (block,) * (half - 1),
         (ids, keep, came),
     )
     arrived = {k: exchange(pieces[k - 1], "mp", 2 * k) for k in far}
+    if len(bits) > 1:
+        arrived[far[0]] = wait_for(arrived[far[0]], lambda m, k: k == bit_orders[m][0])
     for k in range(1, half):
         own = own + arrived[k].astype(jnp.float32)
     stream = own.astype(jnp.bfloat16)
@@ -382,26 +387,25 @@
         [
             gain_scratch,
             scaled_scratch,
-            normed_scratch,
+            pltpu.VMEM((dp, rows, part * mp // dp), jnp.bfloat16),
             pltpu.VMEM((2,) + out_policy.shape, jnp.bfloat16),
             pltpu.SemaphoreType.DMA((4,)),
         ],
         far=(2, 3, 4 + mp, 4 + mp + dp),
         mib=16,
     )
-    flips = [1 << b for b in range(mp.bit_length() - 1)]
-    for flip in flips[:-1]:
-        stats = call(
-            merge_kernel,
-            jax.ShapeDtypeStruct((8, rows), jnp.float32),
-            (ids, stats, exchange(stats, "mp", flip)),
-        )
+    stats = call(
+        merge_kernel,
+        jax.ShapeDtypeStruct((8, rows), jnp.float32),
+        (ids, stats, exchange(stats, "mp", 1)),
+    )
     diff = call(
         last_kernel,
         jax.ShapeDtypeStruct((1, rows), jnp.float32),
-        (ids, stats, exchange(stats, "mp", flips[-1])),
-    )
-    diff = jnp.concatenate([diff] + [exchange(diff, "dp", k) for k in range(1, dp)])
+        (ids, stats, *[exchange(stats, "mp", 2 * k) for k in far]),
+    )
+    for bit in bits:
+        diff = jnp.concatenate([diff, exchange(diff, "dp", bit)])
     ranks = ((order ^ dp_index)[:, None] * rows + jnp.arange(rows, dtype=jnp.int32)).reshape(-1)
     my_code = codes(dp_index * reqs + jnp.arange(reqs, dtype=jnp.int32))
     hit = my_code[:, :, None] == ranks[None, None]

time: 109 us -> 116 us (1.064)
  waiting for transfers between devices: 46.6 us -> 55.2 us
  local copies, waits for them, and re-layouts: 4.86 us -> 2.13 us
  Pallas kernels: 17.8 us -> 20.1 us
  other arithmetic: 3.52 us -> 2.06 us
    ppermute x36, waiting for transfers between devices: 46.6 us -> 55.2 us  [exchange(): return lax.ppermute(values, axis, [(i, i ^ flip) for i in range(count)])]
    pallas_call x8, Pallas kernels: 17.8 us -> 20.1 us  [call(): pl.pallas_call(kernel, out_shape=out_shape, in_specs=specs, out_specs=jax...]
    slice x4 -> x0, local copies, waits for them, and re-layouts: 2.02 us -> none  [local(): hiddens[1][k][reqs, :, :2 * slots + 1]]
  transfers between devices with their start and end apart: 36 -> 36, of which waited for: 27 -> 19; matrix products, arithmetic and copies ran while one was open for 6% -> 2% of each run, Pallas kernels for 7% -> 7%
where the time goes in v3:
time: 116 us
  waiting for transfers between devices  55.2 us (48%)
  starting transfers between devices  35.5 us (31%)
  Pallas kernels  20.1 us (17%)
  local copies, waits for them, and re-layouts  2.13 us (2%)
  other arithmetic  2.06 us (2%)
    ppermute x36, waiting for transfers between devices, exchange(): return lax.ppermute(values, axis, [(i, i ^ flip) for i in range(count)])  55.2 us
    ppermute x36, starting transfers between devices, exchange(): return lax.ppermute(values, axis, [(i, i ^ flip) for i in range(count)])  35.5 us
    pallas_call x8, Pallas kernels, call(): pl.pallas_call(kernel, out_shape=out_shape, in_specs=specs, out_specs=jax...  20.1 us
  transfers between devices with their start and end apart: 36, of which 19 were waited for; matrix products, arithmetic and copies ran while one was open for 2% of the time, Pallas kernels for 7%

profile of v3, /device:TPU:0, one launch (start us, length us, event | category | flops | bytes accessed | tf_op | source)
XLA Modules:
  0.0 115.9 jit_solution(17172482244452352931)
XLA Ops:
  0.6 3.0 %collective-permute-start = (bf16[16,16,256]{2,1,0:T(8,128)(2,1)}, bf16[16,16,256]{2,1,0:T(8,128)(2,1)S(1)}, u32[]{:S(2)}, u32[]{:S(2)}) collective-permute-start(bf16[16,16,256]{2,1,0:T(8,128)(2,1)} %refs_0_), channel_id=1, source_target_pairs={{0,8},{8,0},{16,24},{24,16},{1,9},{9,1},{17,25},{25,17},{2,10},{10... | collective-permute-start | bytes 393224 | tf_op jit(solution)/shard_map/ppermute | solution.py:34
  5.9 2.0 %collective-permute-start.4 = (bf16[17,16,256]{2,1,0:T(8,128)(2,1)S(1)}, bf16[17,16,256]{2,1,0:T(8,128)(2,1)S(1)}, u32[]{:S(2)}, u32[]{:S(2)}) collective-permute-start(bf16[17,16,256]{2,1,0:T(8,128)(2,1)S(1)} %shard_map.158.refs_4_), channel_id=1, source_target_pairs={{0,16},{8,24},{16,0},{24,8},{1,17},{9,25},{17,1},{25,9},{2,18},{10... | collective-permute-start | bytes 417800 | tf_op jit(solution)/shard_map/ppermute | solution.py:34
  10.9 8.8 %collective-permute-done.1.refs_2_ = bf16[16,16,256]{2,1,0:T(8,128)(2,1)S(1)} collective-permute-done((bf16[16,16,256]{2,1,0:T(8,128)(2,1)}, bf16[16,16,256]{2,1,0:T(8,128)(2,1)S(1)}, u32[]{:S(2)}, u32[]{:S(2)}) %collective-permute-start.1) | collective-permute-done | bytes 131104 | tf_op jit(solution)/shard_map/ppermute | solution.py:34
  19.7 1.7 %collective-permute-start.13 = (bf16[512,896]{1,0:T(8,128)(2,1)}, bf16[512,896]{1,0:T(8,128)(2,1)S(1)}, u32[]{:S(2)}, u32[]{:S(2)}) collective-permute-start(bf16[512,896]{1,0:T(8,128)(2,1)} %refs_10_), channel_id=1, source_target_pairs={{0,8},{8,0},{16,24},{24,16},{1,9},{9,1},{17,25},{25,17},{2,10},{10... | collective-permute-start | bytes 2752520 | tf_op jit(solution)/shard_map/ppermute | solution.py:34
  21.4 1.6 %collective-permute-start.14 = (bf16[512,896]{1,0:T(8,128)(2,1)}, bf16[512,896]{1,0:T(8,128)(2,1)S(1)}, u32[]{:S(2)}, u32[]{:S(2)}) collective-permute-start(bf16[512,896]{1,0:T(8,128)(2,1)} %refs_14_), channel_id=1, source_target_pairs={{0,16},{8,24},{16,0},{24,8},{1,17},{9,25},{17,1},{25,9},{2,18},{10... | collective-permute-start | bytes 2752520 | tf_op jit(solution)/shard_map/ppermute | solution.py:34
  24.0 1.8 %shard_map.159 = (bf16[2,128,256]{2,1,0:T(8,128)(2,1)S(1)}, f32[4,16,256]{2,1,0:T(8,128)S(1)}) custom-call(s32[4]{0:T(128)S(1)} %pad_add_fusion.ids.refs_0_, s32[4,1,256]{2,1,0:T(1,128)S(1)} %broadcast_in_dim.98.plan, bf16[16,16,256]{2,1,0:T(8,128)(2,1)} %refs_0_, bf16[16,16,256]{2,1,0:T(8,128)(2,1)S(1)} %collective-permute-done.refs_1_, ...), custom_call_target="tpu_custom_call" | custom-call | tf_op jit(solution)/shard_map/pallas_call | solution.py:22
  25.8 3.6 %collective-permute-start.8 = (bf16[2,128,256]{2,1,0:T(8,128)(2,1)S(1)}, bf16[2,128,256]{2,1,0:T(8,128)(2,1)S(1)}, u32[]{:S(2)}, u32[]{:S(2)}) collective-permute-start(bf16[2,128,256]{2,1,0:T(8,128)(2,1)S(1)} %get-tuple-element.52.refs_6_), channel_id=1, source_target_pairs={{0,6},{1,7},{2,4},{3,5},{4,2},{5,3},{6,0},{7,1},{8,14},{9,15},{10,... | collective-permute-start | bytes 393224 | tf_op jit(solution)/shard_map/ppermute | solution.py:34
  30.2 3.3 %collective-permute-done.8.refs_9_ = bf16[2,128,256]{2,1,0:T(8,128)(2,1)S(1)} collective-permute-done((bf16[2,128,256]{2,1,0:T(8,128)(2,1)S(1)}, bf16[2,128,256]{2,1,0:T(8,128)(2,1)S(1)}, u32[]{:S(2)}, u32[]{:S(2)}) %collective-permute-start.8) | collective-permute-done | bytes 131104 | tf_op jit(solution)/shard_map/ppermute | solution.py:34
  33.5 1.7 %collective-permute-done.6.refs_7_ = bf16[2,128,256]{2,1,0:T(8,128)(2,1)S(1)} collective-permute-done((bf16[2,128,256]{2,1,0:T(8,128)(2,1)S(1)}, bf16[2,128,256]{2,1,0:T(8,128)(2,1)S(1)}, u32[]{:S(2)}, u32[]{:S(2)}) %collective-permute-start.6) | collective-permute-done | bytes 131104 | tf_op jit(solution)/shard_map/ppermute | solution.py:34
  35.2 3.6 %collective-permute-done.7.refs_8_ = bf16[2,128,256]{2,1,0:T(8,128)(2,1)S(1)} collective-permute-done((bf16[2,128,256]{2,1,0:T(8,128)(2,1)S(1)}, bf16[2,128,256]{2,1,0:T(8,128)(2,1)S(1)}, u32[]{:S(2)}, u32[]{:S(2)}) %collective-permute-start.7) | collective-permute-done | bytes 131104 | tf_op jit(solution)/shard_map/ppermute | solution.py:34
  39.3 4.0 %shard_map.160 = (bf16[2048,512]{1,0:T(8,128)(2,1)S(1)}, bf16[2048,512]{1,0:T(8,128)(2,1)S(1)}, bf16[512,2048]{1,0:T(8,128)(2,1)S(1)}, bf16[512,2048]{1,0:T(8,128)(2,1)S(1)}) custom-call(s32[4]{0:T(128)S(1)} %pad_add_fusion.ids.refs_0_, bf16[2048,512]{1,0:T(8,128)(2,1)} %refs_1_.1, bf16[2048,512]{1,0:T(8,128)(2,1)} %refs_2_.1, bf16[512,2048]{1,0:T(8,128)(2,1)} %refs_3_.1, ...), custom_call_target="tpu_custom_call" | custom-call | tf_op jit(solution)/shard_map/pallas_call | solution.py:22
  43.4 5.0 %shard_map.161 = (f32[4,2,128,256]{3,2,1,0:T(8,128)S(1)}, bf16[4,2,128,256]{3,2,1,0:T(8,128)(2,1)}) custom-call(s32[4]{0:T(128)S(1)} %pad_add_fusion.ids.refs_0_, f32[1,2048]{1,0:T(1,128)} %bitcast.13, f32[1,2048]{1,0:T(1,128)} %bitcast.14, bf16[2048,512]{1,0:T(8,128)(2,1)S(1)} %get-tuple-element.48.refs_2_, ...), custom_call_target="tpu_custom_call" | custom-call | tf_op jit(solution)/shard_map/pallas_call | solution.py:22
  51.2 2.1 %collective-permute-start.17 = (bf16[2,128,256]{2,1,0:T(8,128)(2,1)S(1)}, bf16[2,128,256]{2,1,0:T(8,128)(2,1)S(1)}, u32[]{:S(2)}, u32[]{:S(2)}) collective-permute-start(bf16[2,128,256]{2,1,0:T(8,128)(2,1)S(1)} %get-tuple-element.60), channel_id=1, source_target_pairs={{0,4},{1,5},{2,6},{3,7},{4,0},{5,1},{6,2},{7,3},{8,12},{9,13},{10,... | collective-permute-start | bytes 393224 | tf_op jit(solution)/shard_map/ppermute | solution.py:34
  55.7 8.0 %collective-permute-done.17 = bf16[2,128,256]{2,1,0:T(8,128)(2,1)S(1)} collective-permute-done((bf16[2,128,256]{2,1,0:T(8,128)(2,1)S(1)}, bf16[2,128,256]{2,1,0:T(8,128)(2,1)S(1)}, u32[]{:S(2)}, u32[]{:S(2)}) %collective-permute-start.17) | collective-permute-done | bytes 131104 | tf_op jit(solution)/shard_map/ppermute | solution.py:34
  63.7 2.1 %collective-permute-start.29 = (bf16[512,896]{1,0:T(8,128)(2,1)S(1)}, bf16[512,896]{1,0:T(8,128)(2,1)}, u32[]{:S(2)}, u32[]{:S(2)}) collective-permute-start(bf16[512,896]{1,0:T(8,128)(2,1)S(1)} %collective-permute-done.14.refs_16_), channel_id=1, source_target_pairs={{0,8},{8,0},{16,24},{24,16},{1,9},{9,1},{17,25},{25,17},{2,10},{10... | collective-permute-start | bytes 2752520 | tf_op jit(solution)/shard_map/ppermute | solution.py:34
  65.9 6.2 %collective-permute-done.19.refs_12_ = bf16[512,896]{1,0:T(8,128)(2,1)} collective-permute-done((bf16[512,896]{1,0:T(8,128)(2,1)}, bf16[512,896]{1,0:T(8,128)(2,1)}, u32[]{:S(2)}, u32[]{:S(2)}) %collective-permute-start.19) | collective-permute-done | bytes 917536 | tf_op jit(solution)/shard_map/ppermute | solution.py:34
  74.1 2.7 %collective-permute-start.22 = (bf16[2,128,256]{2,1,0:T(8,128)(2,1)S(1)}, bf16[2,128,256]{2,1,0:T(8,128)(2,1)S(1)}, u32[]{:S(2)}, u32[]{:S(2)}) collective-permute-start(bf16[2,128,256]{2,1,0:T(8,128)(2,1)S(1)} %add_convert_fusion.refs_2_), channel_id=1, source_target_pairs={{0,4},{1,5},{2,6},{3,7},{4,0},{5,1},{6,2},{7,3},{8,12},{9,13},{10,... | collective-permute-start | bytes 393224 | tf_op jit(solution)/shard_map/ppermute | solution.py:34
  79.1 6.6 %collective-permute-done.22.refs_4_ = bf16[2,128,256]{2,1,0:T(8,128)(2,1)S(1)} collective-permute-done((bf16[2,128,256]{2,1,0:T(8,128)(2,1)S(1)}, bf16[2,128,256]{2,1,0:T(8,128)(2,1)S(1)}, u32[]{:S(2)}, u32[]{:S(2)}) %collective-permute-start.22) | collective-permute-done | bytes 131104 | tf_op jit(solution)/shard_map/ppermute | solution.py:34
  87.7 3.4 %collective-permute-done.28.refs_13_ = bf16[512,896]{1,0:T(8,128)(2,1)S(1)} collective-permute-done((bf16[512,896]{1,0:T(8,128)(2,1)S(1)}, bf16[512,896]{1,0:T(8,128)(2,1)S(1)}, u32[]{:S(2)}, u32[]{:S(2)}) %collective-permute-start.28) | collective-permute-done | bytes 917536 | tf_op jit(solution)/shard_map/ppermute | solution.py:34
  91.6 6.0 %shard_map.163.refs_0_ = f32[8,128]{1,0:T(8,128)S(1)} custom-call(s32[4]{0:T(128)S(1)} %pad_add_fusion.ids.refs_0_, s32[128,1]{1,0:T(8,128)S(1)} %copy.19.wanted, f32[1,2048]{1,0:T(1,128)} %bitcast.15, f32[1,2048]{1,0:T(1,128)} %bitcast.16, bf16[2,128,256]{2,1,0:T(8,128)(2,1)S(1)} %add_convert_fusion.refs_2_, ...), custom_call_target="tpu_custom_call" | custom-call | tf_op jit(solution)/shard_map/pallas_call | solution.py:22
  99.4 2.3 %collective-permute-start.31 = (f32[8,128]{1,0:T(8,128)S(1)}, f32[8,128]{1,0:T(8,128)S(1)}, u32[]{:S(2)}, u32[]{:S(2)}) collective-permute-start(f32[8,128]{1,0:T(8,128)S(1)} %shard_map.164.refs_0_), channel_id=1, source_target_pairs={{0,4},{1,5},{2,6},{3,7},{4,0},{5,1},{6,2},{7,3},{8,12},{9,13},{10,... | collective-permute-start | bytes 12296 | tf_op jit(solution)/shard_map/ppermute | solution.py:34
  104.0 3.2 %collective-permute-done.32.refs_2_ = f32[8,128]{1,0:T(8,128)S(1)} collective-permute-done((f32[8,128]{1,0:T(8,128)S(1)}, f32[8,128]{1,0:T(8,128)S(1)}, u32[]{:S(2)}, u32[]{:S(2)}) %collective-permute-start.32) | collective-permute-done | bytes 4128 | tf_op jit(solution)/shard_map/ppermute | solution.py:34
  108.9 2.4 %collective-permute-done.34 = f32[1,128]{1,0:T(1,128)S(1)} collective-permute-done((f32[1,128]{1,0:T(1,128)S(1)}, f32[1,128]{1,0:T(1,128)S(1)}, u32[]{:S(2)}, u32[]{:S(2)}) %collective-permute-start.34) | collective-permute-done | bytes 544 | tf_op jit(solution)/shard_map/ppermute | solution.py:34
  112.0 2.9 %collective-permute-done.35 = f32[2,128]{1,0:T(2,128)S(1)} collective-permute-done((f32[2,128]{1,0:T(2,128)S(1)}, f32[2,128]{1,0:T(2,128)S(1)}, u32[]{:S(2)}, u32[]{:S(2)}) %collective-permute-start.35) | collective-permute-done | bytes 1056 | tf_op jit(solution)/shard_map/ppermute | solution.py:34
  (85 shorter events, 27.1 us)
Async XLA Ops:
  0.6 10.2 %collective-permute-start = (bf16[16,16,256]{2,1,0:T(8,128)(2,1)}, bf16[16,16,256]{2,1,0:T(8,128)(2,1)S(1)}, u32[]{:S(2)}, u32[]{:S(2)}) collective-permute-start(bf16[16,16,256]{2,1,0:T(8,128)(2,1)} %refs_0_), channel_id=1, source_target_pairs={{0,8},{8,0},{16,24},{24,16},{1,9},{9,1},{17,25},{25,17},{2,10},{10... | collective-permute-start | bytes 393224 | tf_op jit(solution)/shard_map/ppermute | solution.py:34
  5.8 13.9 %collective-permute-start.3 = (bf16[17,16,256]{2,1,0:T(8,128)(2,1)S(1)}, bf16[17,16,256]{2,1,0:T(8,128)(2,1)S(1)}, u32[]{:S(2)}, u32[]{:S(2)}) collective-permute-start(bf16[17,16,256]{2,1,0:T(8,128)(2,1)S(1)} %shard_map.158.refs_4_), channel_id=1, source_target_pairs={{0,8},{8,0},{16,24},{24,16},{1,9},{9,1},{17,25},{25,17},{2,10},{10... | collective-permute-start | bytes 417800 | tf_op jit(solution)/shard_map/ppermute | solution.py:34
  5.9 13.8 %collective-permute-start.4 = (bf16[17,16,256]{2,1,0:T(8,128)(2,1)S(1)}, bf16[17,16,256]{2,1,0:T(8,128)(2,1)S(1)}, u32[]{:S(2)}, u32[]{:S(2)}) collective-permute-start(bf16[17,16,256]{2,1,0:T(8,128)(2,1)S(1)} %shard_map.158.refs_4_), channel_id=1, source_target_pairs={{0,16},{8,24},{16,0},{24,8},{1,17},{9,25},{17,1},{25,9},{2,18},{10... | collective-permute-start | bytes 417800 | tf_op jit(solution)/shard_map/ppermute | solution.py:34
  7.9 11.8 %collective-permute-start.5 = (bf16[17,16,256]{2,1,0:T(8,128)(2,1)S(1)}, bf16[17,16,256]{2,1,0:T(8,128)(2,1)S(1)}, u32[]{:S(2)}, u32[]{:S(2)}) collective-permute-start(bf16[17,16,256]{2,1,0:T(8,128)(2,1)S(1)} %shard_map.158.refs_4_), channel_id=1, source_target_pairs={{0,24},{8,16},{16,8},{24,0},{1,25},{9,17},{17,9},{25,1},{2,26},{10... | collective-permute-start | bytes 417800 | tf_op jit(solution)/shard_map/ppermute | solution.py:34
  9.3 10.3 %collective-permute-start.1 = (bf16[16,16,256]{2,1,0:T(8,128)(2,1)}, bf16[16,16,256]{2,1,0:T(8,128)(2,1)S(1)}, u32[]{:S(2)}, u32[]{:S(2)}) collective-permute-start(bf16[16,16,256]{2,1,0:T(8,128)(2,1)} %refs_0_), channel_id=1, source_target_pairs={{0,16},{8,24},{16,0},{24,8},{1,17},{9,25},{17,1},{25,9},{2,18},{10... | collective-permute-start | bytes 393224 | tf_op jit(solution)/shard_map/ppermute | solution.py:34
  10.9 8.8 %collective-permute-start.2 = (bf16[16,16,256]{2,1,0:T(8,128)(2,1)}, bf16[16,16,256]{2,1,0:T(8,128)(2,1)S(1)}, u32[]{:S(2)}, u32[]{:S(2)}) collective-permute-start(bf16[16,16,256]{2,1,0:T(8,128)(2,1)} %refs_0_), channel_id=1, source_target_pairs={{0,24},{8,16},{16,8},{24,0},{1,25},{9,17},{17,9},{25,1},{2,26},{10... | collective-permute-start | bytes 393224 | tf_op jit(solution)/shard_map/ppermute | solution.py:34
  19.7 23.7 %collective-permute-start.13 = (bf16[512,896]{1,0:T(8,128)(2,1)}, bf16[512,896]{1,0:T(8,128)(2,1)S(1)}, u32[]{:S(2)}, u32[]{:S(2)}) collective-permute-start(bf16[512,896]{1,0:T(8,128)(2,1)} %refs_10_), channel_id=1, source_target_pairs={{0,8},{8,0},{16,24},{24,16},{1,9},{9,1},{17,25},{25,17},{2,10},{10... | collective-permute-start | bytes 2752520 | tf_op jit(solution)/shard_map/ppermute | solution.py:34
  21.4 21.9 %collective-permute-start.14 = (bf16[512,896]{1,0:T(8,128)(2,1)}, bf16[512,896]{1,0:T(8,128)(2,1)S(1)}, u32[]{:S(2)}, u32[]{:S(2)}) collective-permute-start(bf16[512,896]{1,0:T(8,128)(2,1)} %refs_14_), channel_id=1, source_target_pairs={{0,16},{8,24},{16,0},{24,8},{1,17},{9,25},{17,1},{25,9},{2,18},{10... | collective-permute-start | bytes 2752520 | tf_op jit(solution)/shard_map/ppermute | solution.py:34
  25.8 7.8 %collective-permute-start.8 = (bf16[2,128,256]{2,1,0:T(8,128)(2,1)S(1)}, bf16[2,128,256]{2,1,0:T(8,128)(2,1)S(1)}, u32[]{:S(2)}, u32[]{:S(2)}) collective-permute-start(bf16[2,128,256]{2,1,0:T(8,128)(2,1)S(1)} %get-tuple-element.52.refs_6_), channel_id=1, source_target_pairs={{0,6},{1,7},{2,4},{3,5},{4,2},{5,3},{6,0},{7,1},{8,14},{9,15},{10,... | collective-permute-start | bytes 393224 | tf_op jit(solution)/shard_map/ppermute | solution.py:34
  29.4 5.8 %collective-permute-start.6 = (bf16[2,128,256]{2,1,0:T(8,128)(2,1)S(1)}, bf16[2,128,256]{2,1,0:T(8,128)(2,1)S(1)}, u32[]{:S(2)}, u32[]{:S(2)}) collective-permute-start(bf16[2,128,256]{2,1,0:T(8,128)(2,1)S(1)} %get-tuple-element.52.refs_6_), channel_id=1, source_target_pairs={{0,2},{1,3},{2,0},{3,1},{4,6},{5,7},{6,4},{7,5},{8,10},{9,11},{10,... | collective-permute-start | bytes 393224 | tf_op jit(solution)/shard_map/ppermute | solution.py:34
  29.4 9.4 %collective-permute-start.7 = (bf16[2,128,256]{2,1,0:T(8,128)(2,1)S(1)}, bf16[2,128,256]{2,1,0:T(8,128)(2,1)S(1)}, u32[]{:S(2)}, u32[]{:S(2)}) collective-permute-start(bf16[2,128,256]{2,1,0:T(8,128)(2,1)S(1)} %get-tuple-element.52.refs_6_), channel_id=1, source_target_pairs={{0,4},{1,5},{2,6},{3,7},{4,0},{5,1},{6,2},{7,3},{8,12},{9,13},{10,... | collective-permute-start | bytes 393224 | tf_op jit(solution)/shard_map/ppermute | solution.py:34
  35.2 8.2 %collective-permute-start.9 = (bf16[2,128,256]{2,1,0:T(8,128)(2,1)S(1)}, bf16[2,128,256]{2,1,0:T(8,128)(2,1)S(1)}, u32[]{:S(2)}, u32[]{:S(2)}) collective-permute-start(bf16[2,128,256]{2,1,0:T(8,128)(2,1)S(1)} %get-tuple-element.52.refs_6_), channel_id=1, source_target_pairs={{0,1},{1,0},{2,3},{3,2},{4,5},{5,4},{6,7},{7,6},{8,9},{9,8},{10,11... | collective-permute-start | bytes 393224 | tf_op jit(solution)/shard_map/ppermute | solution.py:34
  48.5 23.5 %collective-permute-start.19 = (bf16[512,896]{1,0:T(8,128)(2,1)}, bf16[512,896]{1,0:T(8,128)(2,1)}, u32[]{:S(2)}, u32[]{:S(2)}) collective-permute-start(bf16[512,896]{1,0:T(8,128)(2,1)} %refs_10_), channel_id=1, source_target_pairs={{0,16},{8,24},{16,0},{24,8},{1,17},{9,25},{17,1},{25,9},{2,18},{10... | collective-permute-start | bytes 2752520 | tf_op jit(solution)/shard_map/ppermute | solution.py:34
  49.2 23.5 %collective-permute-start.20 = (bf16[512,896]{1,0:T(8,128)(2,1)}, bf16[512,896]{1,0:T(8,128)(2,1)}, u32[]{:S(2)}, u32[]{:S(2)}) collective-permute-start(bf16[512,896]{1,0:T(8,128)(2,1)} %refs_14_), channel_id=1, source_target_pairs={{0,8},{8,0},{16,24},{24,16},{1,9},{9,1},{17,25},{25,17},{2,10},{10... | collective-permute-start | bytes 2752520 | tf_op jit(solution)/shard_map/ppermute | solution.py:34
  51.2 12.5 %collective-permute-start.17 = (bf16[2,128,256]{2,1,0:T(8,128)(2,1)S(1)}, bf16[2,128,256]{2,1,0:T(8,128)(2,1)S(1)}, u32[]{:S(2)}, u32[]{:S(2)}) collective-permute-start(bf16[2,128,256]{2,1,0:T(8,128)(2,1)S(1)} %get-tuple-element.60), channel_id=1, source_target_pairs={{0,4},{1,5},{2,6},{3,7},{4,0},{5,1},{6,2},{7,3},{8,12},{9,13},{10,... | collective-permute-start | bytes 393224 | tf_op jit(solution)/shard_map/ppermute | solution.py:34
  53.3 10.4 %collective-permute-start.16 = (bf16[2,128,256]{2,1,0:T(8,128)(2,1)S(1)}, bf16[2,128,256]{2,1,0:T(8,128)(2,1)S(1)}, u32[]{:S(2)}, u32[]{:S(2)}) collective-permute-start(bf16[2,128,256]{2,1,0:T(8,128)(2,1)S(1)} %get-tuple-element.59), channel_id=1, source_target_pairs={{0,2},{1,3},{2,0},{3,1},{4,6},{5,7},{6,4},{7,5},{8,10},{9,11},{10,... | collective-permute-start | bytes 393224 | tf_op jit(solution)/shard_map/ppermute | solution.py:34
  54.9 10.9 %collective-permute-start.18 = (bf16[2,128,256]{2,1,0:T(8,128)(2,1)S(1)}, bf16[2,128,256]{2,1,0:T(8,128)(2,1)S(1)}, u32[]{:S(2)}, u32[]{:S(2)}) collective-permute-start(bf16[2,128,256]{2,1,0:T(8,128)(2,1)S(1)} %get-tuple-element.64), channel_id=1, source_target_pairs={{0,6},{1,7},{2,4},{3,5},{4,2},{5,3},{6,0},{7,1},{8,14},{9,15},{10,... | collective-permute-start | bytes 393224 | tf_op jit(solution)/shard_map/ppermute | solution.py:34
  63.7 27.4 %collective-permute-start.28 = (bf16[512,896]{1,0:T(8,128)(2,1)S(1)}, bf16[512,896]{1,0:T(8,128)(2,1)S(1)}, u32[]{:S(2)}, u32[]{:S(2)}) collective-permute-start(bf16[512,896]{1,0:T(8,128)(2,1)S(1)} %collective-permute-done.13.refs_11_), channel_id=1, source_target_pairs={{0,16},{8,24},{16,0},{24,8},{1,17},{9,25},{17,1},{25,9},{2,18},{10... | collective-permute-start | bytes 2752520 | tf_op jit(solution)/shard_map/ppermute | solution.py:34
  63.7 27.9 %collective-permute-start.29 = (bf16[512,896]{1,0:T(8,128)(2,1)S(1)}, bf16[512,896]{1,0:T(8,128)(2,1)}, u32[]{:S(2)}, u32[]{:S(2)}) collective-permute-start(bf16[512,896]{1,0:T(8,128)(2,1)S(1)} %collective-permute-done.14.refs_16_), channel_id=1, source_target_pairs={{0,8},{8,0},{16,24},{24,16},{1,9},{9,1},{17,25},{25,17},{2,10},{10... | collective-permute-start | bytes 2752520 | tf_op jit(solution)/shard_map/ppermute | solution.py:34
  72.7 6.0 %collective-permute-start.21 = (bf16[2,128,256]{2,1,0:T(8,128)(2,1)S(1)}, bf16[2,128,256]{2,1,0:T(8,128)(2,1)S(1)}, u32[]{:S(2)}, u32[]{:S(2)}) collective-permute-start(bf16[2,128,256]{2,1,0:T(8,128)(2,1)S(1)} %add_convert_fusion.refs_2_), channel_id=1, source_target_pairs={{0,2},{1,3},{2,0},{3,1},{4,6},{5,7},{6,4},{7,5},{8,10},{9,11},{10,... | collective-permute-start | bytes 393224 | tf_op jit(solution)/shard_map/ppermute | solution.py:34
  74.1 11.7 %collective-permute-start.22 = (bf16[2,128,256]{2,1,0:T(8,128)(2,1)S(1)}, bf16[2,128,256]{2,1,0:T(8,128)(2,1)S(1)}, u32[]{:S(2)}, u32[]{:S(2)}) collective-permute-start(bf16[2,128,256]{2,1,0:T(8,128)(2,1)S(1)} %add_convert_fusion.refs_2_), channel_id=1, source_target_pairs={{0,4},{1,5},{2,6},{3,7},{4,0},{5,1},{6,2},{7,3},{8,12},{9,13},{10,... | collective-permute-start | bytes 393224 | tf_op jit(solution)/shard_map/ppermute | solution.py:34
  76.7 9.0 %collective-permute-start.23 = (bf16[2,128,256]{2,1,0:T(8,128)(2,1)S(1)}, bf16[2,128,256]{2,1,0:T(8,128)(2,1)S(1)}, u32[]{:S(2)}, u32[]{:S(2)}) collective-permute-start(bf16[2,128,256]{2,1,0:T(8,128)(2,1)S(1)} %add_convert_fusion.refs_2_), channel_id=1, source_target_pairs={{0,6},{1,7},{2,4},{3,5},{4,2},{5,3},{6,0},{7,1},{8,14},{9,15},{10,... | collective-permute-start | bytes 393224 | tf_op jit(solution)/shard_map/ppermute | solution.py:34
  78.7 7.5 %collective-permute-start.24 = (bf16[2,128,256]{2,1,0:T(8,128)(2,1)S(1)}, bf16[2,128,256]{2,1,0:T(8,128)(2,1)S(1)}, u32[]{:S(2)}, u32[]{:S(2)}) collective-permute-start(bf16[2,128,256]{2,1,0:T(8,128)(2,1)S(1)} %add_convert_fusion.refs_2_), channel_id=1, source_target_pairs={{0,1},{1,0},{2,3},{3,2},{4,5},{5,4},{6,7},{7,6},{8,9},{9,8},{10,11... | collective-permute-start | bytes 393224 | tf_op jit(solution)/shard_map/ppermute | solution.py:34
  101.8 5.4 %collective-permute-start.32 = (f32[8,128]{1,0:T(8,128)S(1)}, f32[8,128]{1,0:T(8,128)S(1)}, u32[]{:S(2)}, u32[]{:S(2)}) collective-permute-start(f32[8,128]{1,0:T(8,128)S(1)} %shard_map.164.refs_0_), channel_id=1, source_target_pairs={{0,6},{1,7},{2,4},{3,5},{4,2},{5,3},{6,0},{7,1},{8,14},{9,15},{10,... | collective-permute-start | bytes 12296 | tf_op jit(solution)/shard_map/ppermute | solution.py:34
  (13 other events, 39.0 us)

commit v4 on v3

--- a/solution.py
+++ b/solution.py
@@ -101,7 +101,7 @@
         out[m] = total.astype(out.dtype)
 
 
-def normalise(values, gain, chip, core, scaled, store):
+def normalise(values, gain, chip, core, store):
     half = len(values) // 2
     part = values[0].shape[1]
     width = part * len(values)
@@ -111,9 +111,8 @@
     spread = sum(jnp.sum(v * v, axis=1, keepdims=True) for v in values) / width
     scale = lax.rsqrt(spread + epsilon)
     for k, v in enumerate(values):
-        scaled[2 * (chip ^ (k % half)) + (core if k < half else 1 - core)] = v * scale
-    for b in range(2 * half):
-        store(b, (scaled[b] * gain[:, b * part : (b + 1) * part]).astype(jnp.bfloat16))
+        place = 2 * (chip ^ (k % half)) + (core if k < half else 1 - core)
+        store[place] = (v * scale * gain[place]).astype(jnp.bfloat16)
     return values[0]
 
 
@@ -123,30 +122,37 @@
         copy.wait()
 
 
+def blocks_dot(normed, weight, order):
+    part = normed.shape[2]
+    total = None
+    for b, place in enumerate(order):
+        rows = weight[b * part : (b + 1) * part, :]
+        piece = jnp.dot(normed[place], rows, preferred_element_type=jnp.float32)
+        total = piece if total is None else total + piece
+    return total
+
+
 def ffn_kernel(half, ids, *refs):
-    gains_far, ups, downs = refs[:2], refs[2:4], refs[4:6]
+    gains, ups, downs = refs[:2], refs[2:4], refs[4:6]
     parts = refs[6 : 6 + 2 * half]
-    keep, send, gains, scaled, normed, sems = refs[6 + 2 * half :]
-    copies = fetch(gains_far, [gains.at[0], gains.at[1]], sems)
+    keep, send, normed, terms = refs[6 + 2 * half :]
     chip, core = ids[1], ids[2]
     part = parts[0].shape[2]
-
-    def store(b, values):
-        normed[:, b * part : (b + 1) * part] = values
-
+    bases = [
+        normalise([part[m] for part in parts], gains[m], chip, core, normed.at[m])
+        for m in range(2)
+    ]
     for m in range(2):
-        copies[m].wait()
-        base = normalise([part[m] for part in parts], gains[m], chip, core, scaled, store)
-        pre = jnp.dot(normed[...], ups[m][...], preferred_element_type=jnp.float32)
+        pre = blocks_dot(normed.at[m], ups[m], range(2 * half))
         units = jax.nn.gelu(pre).astype(jnp.bfloat16)
         full = jnp.dot(units, downs[m][...], preferred_element_type=jnp.float32)
         for b in range(2 * half):
-            scaled[b] = full[:, b * part : (b + 1) * part]
+            terms[m, b] = full[:, b * part : (b + 1) * part]
         for k in range(half):
             place = 2 * (chip ^ k)
-            kept = scaled[place + core]
-            keep[k, m] = kept + base if k == 0 else kept
-            send[k, m] = scaled[place + 1 - core].astype(jnp.bfloat16)
+            kept = terms[m, place + core]
+            keep[k, m] = kept + bases[m] if k == 0 else kept
+            send[k, m] = terms[m, place + 1 - core].astype(jnp.bfloat16)
 
 
 def pair_kernel(ids, keep, came, own, *outs):
@@ -156,34 +162,24 @@
 
 
 def score_kernel(half, ids, wanted, *refs):
-    parts = refs[2 : 2 + 2 * half]
-    *outs, stats, gains, scaled, normed, out_store, sems = refs[2 + 2 * half :]
+    gains, parts = refs[:2], refs[2 : 2 + 2 * half]
+    *outs, stats, normed, out_store, sems = refs[2 + 2 * half :]
     dp = len(outs) // 2
-    copies = fetch(
-        [refs[0], outs[0], refs[1], outs[dp]],
-        [store.at[m] for m in range(2) for store in (gains, out_store)],
-        sems,
-    )
+    copies = fetch([outs[0], outs[dp]], [out_store.at[0], out_store.at[1]], sems)
     me, chip, core = ids[0], ids[1], ids[2]
     lane = lax.broadcasted_iota(jnp.int32, (parts[0].shape[1], 128), 1)
     table = jnp.zeros(lane.shape, jnp.float32)
     ratio = 2 * half // dp
-    part = parts[0].shape[2]
-
-    def store(b, values):
-        normed[b // ratio, :, b % ratio * part : (b % ratio + 1) * part] = values
-
     for m in range(2):
-        copies[2 * m].wait()
-        normalise([part[m] for part in parts], gains[m], chip, core, scaled, store)
+        normalise([part[m] for part in parts], gains[m], chip, core, normed.at[m])
+    for m in range(2):
         logits = None
         for k in [*range(1, dp), 0]:
             if k == 0:
-                copies[2 * m + 1].wait()
+                copies[m].wait()
                 outs[m * dp] = out_store.at[m]
-            piece = jnp.dot(
-                normed[me ^ k], outs[m * dp + k][...], preferred_element_type=jnp.float32
-            )
+            order = [(me ^ k) * ratio + b for b in range(ratio)]
+            piece = blocks_dot(normed.at[m], outs[m * dp + k], order)
             logits = piece if logits is None else logits + piece
         entries = lax.broadcasted_iota(jnp.int32, logits.shape, 1) + ids[3] * logits.shape[1]
         picked = jnp.sum(jnp.where(entries == wanted[...], logits, 0.0), axis=1, keepdims=True)
@@ -240,8 +236,9 @@
     reqs, slots, part = hidden_policy.shape
     here = reqs * slots
     rows = here // 2
-    ffn_gains = (ffn_gain_policy.reshape(1, -1), ffn_gain_reference.reshape(1, -1))
-    final_gains = (final_gain_policy.reshape(1, -1), final_gain_reference.reshape(1, -1))
+    ffn_gains = (ffn_gain_policy, ffn_gain_reference)
+    final_gains = (final_gain_policy, final_gain_reference)
+    gains = [gain.reshape(mp, 1, part) for gain in (*ffn_gains, *final_gains)]
     bits = [1 << b for b in range(dp.bit_length() - 1)]
 
     bit_orders = []
@@ -271,9 +268,8 @@
             outs[m][k] = value
         return first
 
-    for m in range(2):
-        for k in range(1, dp):
-            hiddens[m][k] = exchange(hiddens[m][0], "dp", k)
+    for step in range(len(bits)):
+        spread_step(hiddens, step, lambda m, k: True)
     hiddens = wait_for(hiddens, lambda m, k: True)
     spread_step(outs, 0, lambda m, k: True)
     hidden_parts = [hiddens[m][k] for m in range(2) for k in range(dp)]
@@ -306,46 +302,43 @@
 
     far = sorted(range(1, half), key=lambda k: (k.bit_length() <= 1, k))
 
-    def gather_pair(own):
+    def gather_pair(own, loaded=()):
         same = {0: own}
         for k in far:
             same[k] = exchange(own, "mp", 2 * k)
+        same[far[0]], loaded = lax.optimization_barrier((same[far[0]], loaded))
         same = [same[k] for k in range(half)]
-        return same + [exchange(v, "mp", 1) for v in same]
-
-    gain_scratch = pltpu.VMEM((2, 1, part * mp), jnp.float32)
-    scaled_scratch = pltpu.VMEM((mp, rows, part), jnp.float32)
-    parts = gather_pair(moved)
-    if len(bits) > 1:
-        parts[-1] = wait_for(parts[-1], lambda m, k: True)
-        later = [{0: outs[m][0]} for m in range(2)]
-        spread_step(later, 1, lambda m, k: True)
-    block = jax.ShapeDtypeStruct((2, rows, part), jnp.bfloat16)
-    weights = (up_policy, up_reference, down_policy, down_reference)
-    weights = call(
+        return same + [exchange(v, "mp", 1) for v in same], loaded
+
+    weights = (up_policy, up_reference, down_policy, down_reference, *gains)
+    moved, weights = lax.optimization_barrier((moved, weights))
+    loaded = call(
         load_kernel,
         tuple(jax.ShapeDtypeStruct(w.shape, w.dtype) for w in weights),
         (ids, *weights),
-        [pltpu.SemaphoreType.DMA((4,))],
-        far=range(1, 5),
+        [pltpu.SemaphoreType.DMA((len(weights),))],
+        far=range(1, 1 + len(weights)),
         mib=12,
     )
+    parts, loaded = gather_pair(moved, loaded)
+    block = jax.ShapeDtypeStruct((2, rows, part), jnp.bfloat16)
     keep, send = call(
         functools.partial(ffn_kernel, half),
         (
             jax.ShapeDtypeStruct((half, 2, rows, part), jnp.float32),
             jax.ShapeDtypeStruct((half, 2, rows, part), jnp.bfloat16),
         ),
-        (ids, *ffn_gains, *weights, *parts),
+        (ids, *loaded[4:6], *loaded[:4], *parts),
         [
-            gain_scratch,
-            scaled_scratch,
-            pltpu.VMEM((rows, part * mp), jnp.bfloat16),
-            pltpu.SemaphoreType.DMA((2,)),
+            pltpu.VMEM((2, mp, rows, part), jnp.bfloat16),
+            pltpu.VMEM((2, mp, rows, part), jnp.float32),
         ],
-        far=(1, 2),
-        mib=16,
-    )
+        mib=14,
+    )
+    send = wait_for(send, lambda m, k: True)
+    if len(bits) > 1:
+        later = [{0: outs[m][0]} for m in range(2)]
+        spread_step(later, 1, lambda m, k: True)
     came = exchange(send, "mp", 1)
     own, *pieces = call(
         pair_kernel,
@@ -380,19 +373,17 @@
         (
             ids,
             wanted,
-            *final_gains,
-            *gather_pair(stream),
+            *loaded[6:],
+            *gather_pair(stream)[0],
             *[outs[m][k] for m in range(2) for k in range(dp)],
         ),
         [
-            gain_scratch,
-            scaled_scratch,
-            pltpu.VMEM((dp, rows, part * mp // dp), jnp.bfloat16),
+            pltpu.VMEM((2, mp, rows, part), jnp.bfloat16),
             pltpu.VMEM((2,) + out_policy.shape, jnp.bfloat16),
-            pltpu.SemaphoreType.DMA((4,)),
+            pltpu.SemaphoreType.DMA((2,)),
         ],
-        far=(2, 3, 4 + mp, 4 + mp + dp),
-        mib=16,
+        far=(4 + mp, 4 + mp + dp),
+        mib=14,
     )
     stats = call(
         merge_kernel,
@@ -404,8 +395,7 @@
         jax.ShapeDtypeStruct((1, rows), jnp.float32),
         (ids, stats, *[exchange(stats, "mp", 2 * k) for k in far]),
     )
-    for bit in bits:
-        diff = jnp.concatenate([diff, exchange(diff, "dp", bit)])
+    diff = jnp.concatenate([diff] + [exchange(diff, "dp", k) for k in range(1, dp)])
     ranks = ((order ^ dp_index)[:, None] * rows + jnp.arange(rows, dtype=jnp.int32)).reshape(-1)
     my_code = codes(dp_index * reqs + jnp.arange(reqs, dtype=jnp.int32))
     hit = my_code[:, :, None] == ranks[None, None]

time: 116 us -> 113 us (0.974)
  waiting for transfers between devices: 55.2 us -> 43.4 us
  starting transfers between devices: 35.5 us -> 41.8 us
  local copies, waits for them, and re-layouts: 2.13 us -> 6.38 us
  Pallas kernels: 20.1 us -> 18.1 us
    ppermute x36 -> x37, waiting for transfers between devices: 55.2 us -> 43.4 us  [exchange(): return lax.ppermute(values, axis, [(i, i ^ flip) for i in range(count)])]
    ppermute x36 -> x37, starting transfers between devices: 35.5 us -> 41.8 us  [exchange(): return lax.ppermute(values, axis, [(i, i ^ flip) for i in range(count)])]
    unnamed x2 -> x10, local copies, waits for them, and re-layouts: 0.65 us -> 4.91 us
    pallas_call x8, Pallas kernels: 20.1 us -> 18.1 us  [call(): pl.pallas_call(kernel, out_shape=out_shape, in_specs=specs, out_specs=jax...]
  transfers between devices with their start and end apart: 36 -> 37, of which waited for: 19 -> 21; matrix products, arithmetic and copies ran while one was open for 2% -> 2% of each run, Pallas kernels for 7% -> 9%
where the time goes in v4:
time: 113 us
  waiting for transfers between devices  43.4 us (38%)
  starting transfers between devices  41.8 us (37%)
  Pallas kernels  18.1 us (16%)
  local copies, waits for them, and re-layouts  6.38 us (6%)
  other arithmetic  2.05 us (2%)
    ppermute x37, waiting for transfers between devices, exchange(): return lax.ppermute(values, axis, [(i, i ^ flip) for i in range(count)])  43.4 us
    ppermute x37, starting transfers between devices, exchange(): return lax.ppermute(values, axis, [(i, i ^ flip) for i in range(count)])  41.8 us
    pallas_call x8, Pallas kernels, call(): pl.pallas_call(kernel, out_shape=out_shape, in_specs=specs, out_specs=jax...  18.1 us
    unnamed x10, local copies, waits for them, and re-layouts  4.91 us
  transfers between devices with their start and end apart: 37, of which 21 were waited for; matrix products, arithmetic and copies ran while one was open for 2% of the time, Pallas kernels for 9%

profile of v4, /device:TPU:0, one launch (start us, length us, event | category | flops | bytes accessed | tf_op | source)
XLA Modules:
  0.0 112.5 jit_solution(3904243628226556453)
XLA Ops:
  2.8 3.0 %collective-permute-start.4 = (bf16[17,16,256]{2,1,0:T(8,128)(2,1)S(1)}, bf16[17,16,256]{2,1,0:T(8,128)(2,1)S(1)}, u32[]{:S(2)}, u32[]{:S(2)}) collective-permute-start(bf16[17,16,256]{2,1,0:T(8,128)(2,1)S(1)} %shard_map.158.refs_4_), channel_id=1, source_target_pairs={{0,16},{8,24},{16,0},{24,8},{1,17},{9,25},{17,1},{25,9},{2,18},{10... | collective-permute-start | bytes 417800 | tf_op jit(solution)/shard_map/ppermute | solution.py:34
  5.8 1.5 %collective-permute-start = (bf16[16,16,256]{2,1,0:T(8,128)(2,1)}, bf16[16,16,256]{2,1,0:T(8,128)(2,1)S(1)}, u32[]{:S(2)}, u32[]{:S(2)}) collective-permute-start(bf16[16,16,256]{2,1,0:T(8,128)(2,1)} %refs_0_), channel_id=1, source_target_pairs={{0,8},{8,0},{16,24},{24,16},{1,9},{9,1},{17,25},{25,17},{2,10},{10... | collective-permute-start | bytes 393224 | tf_op jit(solution)/shard_map/ppermute | solution.py:34
  7.8 1.6 %collective-permute-done.4.refs_6_ = bf16[17,16,256]{2,1,0:T(8,128)(2,1)S(1)} collective-permute-done((bf16[17,16,256]{2,1,0:T(8,128)(2,1)S(1)}, bf16[17,16,256]{2,1,0:T(8,128)(2,1)S(1)}, u32[]{:S(2)}, u32[]{:S(2)}) %collective-permute-start.4) | collective-permute-done | bytes 139296 | tf_op jit(solution)/shard_map/ppermute | solution.py:34
  9.5 1.7 %collective-permute-start.5 = (bf16[17,16,256]{2,1,0:T(8,128)(2,1)S(1)}, bf16[17,16,256]{2,1,0:T(8,128)(2,1)S(1)}, u32[]{:S(2)}, u32[]{:S(2)}) collective-permute-start(bf16[17,16,256]{2,1,0:T(8,128)(2,1)S(1)} %collective-permute-done.4.refs_6_), channel_id=1, source_target_pairs={{0,8},{8,0},{16,24},{24,16},{1,9},{9,1},{17,25},{25,17},{2,10},{10... | collective-permute-start | bytes 417800 | tf_op jit(solution)/shard_map/ppermute | solution.py:34
  11.2 1.5 %collective-permute-start.1 = (bf16[16,16,256]{2,1,0:T(8,128)(2,1)}, bf16[16,16,256]{2,1,0:T(8,128)(2,1)S(1)}, u32[]{:S(2)}, u32[]{:S(2)}) collective-permute-start(bf16[16,16,256]{2,1,0:T(8,128)(2,1)} %refs_0_), channel_id=1, source_target_pairs={{0,16},{8,24},{16,0},{24,8},{1,17},{9,25},{17,1},{25,9},{2,18},{10... | collective-permute-start | bytes 393224 | tf_op jit(solution)/shard_map/ppermute | solution.py:34
  13.2 3.7 %collective-permute-done.1.refs_2_ = bf16[16,16,256]{2,1,0:T(8,128)(2,1)S(1)} collective-permute-done((bf16[16,16,256]{2,1,0:T(8,128)(2,1)}, bf16[16,16,256]{2,1,0:T(8,128)(2,1)S(1)}, u32[]{:S(2)}, u32[]{:S(2)}) %collective-permute-start.1) | collective-permute-done | bytes 131104 | tf_op jit(solution)/shard_map/ppermute | solution.py:34
  21.3 1.8 %shard_map.159 = (bf16[2,128,256]{2,1,0:T(8,128)(2,1)S(1)}, f32[4,16,256]{2,1,0:T(8,128)S(1)}) custom-call(s32[4]{0:T(128)S(1)} %pad_add_fusion.ids.refs_0_, s32[4,1,256]{2,1,0:T(1,128)S(1)} %broadcast_in_dim.98.plan, bf16[16,16,256]{2,1,0:T(8,128)(2,1)} %refs_0_, bf16[16,16,256]{2,1,0:T(8,128)(2,1)S(1)} %collective-permute-done.refs_1_, ...), custom_call_target="tpu_custom_call" | custom-call | tf_op jit(solution)/shard_map/pallas_call | solution.py:22
  23.1 2.7 %collective-permute-start.6 = (bf16[2,128,256]{2,1,0:T(8,128)(2,1)S(1)}, bf16[2,128,256]{2,1,0:T(8,128)(2,1)S(1)}, u32[]{:S(2)}, u32[]{:S(2)}) collective-permute-start(bf16[2,128,256]{2,1,0:T(8,128)(2,1)S(1)} %get-tuple-element.71.refs_6_), channel_id=1, source_target_pairs={{0,4},{1,5},{2,6},{3,7},{4,0},{5,1},{6,2},{7,3},{8,12},{9,13},{10,... | collective-permute-start | bytes 393224 | tf_op jit(solution)/shard_map/ppermute | solution.py:34
  25.8 1.6 %collective-permute-start.7 = (bf16[2,128,256]{2,1,0:T(8,128)(2,1)S(1)}, bf16[2,128,256]{2,1,0:T(8,128)(2,1)S(1)}, u32[]{:S(2)}, u32[]{:S(2)}) collective-permute-start(bf16[2,128,256]{2,1,0:T(8,128)(2,1)S(1)} %get-tuple-element.71.refs_6_), channel_id=1, source_target_pairs={{0,2},{1,3},{2,0},{3,1},{4,6},{5,7},{6,4},{7,5},{8,10},{9,11},{10,... | collective-permute-start | bytes 393224 | tf_op jit(solution)/shard_map/ppermute | solution.py:34
  27.6 4.8 %collective-permute-done.6.refs_8_ = bf16[2,128,256]{2,1,0:T(8,128)(2,1)S(1)} collective-permute-done((bf16[2,128,256]{2,1,0:T(8,128)(2,1)S(1)}, bf16[2,128,256]{2,1,0:T(8,128)(2,1)S(1)}, u32[]{:S(2)}, u32[]{:S(2)}) %collective-permute-start.6) | collective-permute-done | bytes 131104 | tf_op jit(solution)/shard_map/ppermute | solution.py:34
  32.4 4.1 %shard_map.160 = (bf16[2048,512]{1,0:T(8,128)(2,1)S(1)}, bf16[2048,512]{1,0:T(8,128)(2,1)S(1)}, bf16[512,2048]{1,0:T(8,128)(2,1)S(1)}, bf16[512,2048]{1,0:T(8,12...) custom-call(s32[4]{0:T(128)S(1)} %pad_add_fusion.ids.refs_0_, ...), custom_call_target="tpu_custom_call" | custom-call | tf_op jit(solution)/shard_map/pallas_call | solution.py:22
  38.6 3.9 %shard_map.161 = (f32[4,2,128,256]{3,2,1,0:T(8,128)S(1)}, bf16[4,2,128,256]{3,2,1,0:T(8,128)(2,1)}) custom-call(s32[4]{0:T(128)S(1)} %pad_add_fusion.ids.refs_0_, f32[8,1,256]{2,1,0:T(1,128)S(1)} %get-tuple-element.90.refs_0_, f32[8,1,256]{2,1,0:T(1,128)S(1)} %get-tuple-element.91.refs_1_, bf16[2048,512]{1,0:T(8,128)(2,1)S(1)} %get-tuple-element.92.refs_2_, ...), custom_call_target="tpu_custom_call" | custom-call | tf_op jit(solution)/shard_map/pallas_call | solution.py:22
  46.4 4.7 %collective-permute-start.16 = (bf16[2,128,256]{2,1,0:T(8,128)(2,1)S(1)}, bf16[2,128,256]{2,1,0:T(8,128)(2,1)S(1)}, u32[]{:S(2)}, u32[]{:S(2)}) collective-permute-start(bf16[2,128,256]{2,1,0:T(8,128)(2,1)S(1)} %get-tuple-element.103), channel_id=1, source_target_pairs={{0,2},{1,3},{2,0},{3,1},{4,6},{5,7},{6,4},{7,5},{8,10},{9,11},{10,... | collective-permute-start | bytes 393224 | tf_op jit(solution)/shard_map/ppermute | solution.py:34
  51.1 4.1 %collective-permute-done.17 = bf16[2,128,256]{2,1,0:T(8,128)(2,1)S(1)} collective-permute-done((bf16[2,128,256]{2,1,0:T(8,128)(2,1)S(1)}, bf16[2,128,256]{2,1,0:T(8,128)(2,1)S(1)}, u32[]{:S(2)}, u32[]{:S(2)}) %collective-permute-start.17) | collective-permute-done | bytes 131104 | tf_op jit(solution)/shard_map/ppermute | solution.py:34
  57.2 2.6 %collective-permute-done.18 = bf16[2,128,256]{2,1,0:T(8,128)(2,1)S(1)} collective-permute-done((bf16[2,128,256]{2,1,0:T(8,128)(2,1)S(1)}, bf16[2,128,256]{2,1,0:T(8,128)(2,1)S(1)}, u32[]{:S(2)}, u32[]{:S(2)}) %collective-permute-start.18) | collective-permute-done | bytes 131104 | tf_op jit(solution)/shard_map/ppermute | solution.py:34
  59.9 6.5 %collective-permute-done.19.refs_12_ = bf16[512,896]{1,0:T(8,128)(2,1)S(1)} collective-permute-done((bf16[512,896]{1,0:T(8,128)(2,1)}, bf16[512,896]{1,0:T(8,128)(2,1)S(1)}, u32[]{:S(2)}, u32[]{:S(2)}) %collective-permute-start.19) | collective-permute-done | bytes 917536 | tf_op jit(solution)/shard_map/ppermute | solution.py:34
  69.1 4.8 %collective-permute-start.21 = (bf16[2,128,256]{2,1,0:T(8,128)(2,1)S(1)}, bf16[2,128,256]{2,1,0:T(8,128)(2,1)S(1)}, u32[]{:S(2)}, u32[]{:S(2)}) collective-permute-start(bf16[2,128,256]{2,1,0:T(8,128)(2,1)S(1)} %add_convert_fusion.refs_2_), channel_id=1, source_target_pairs={{0,2},{1,3},{2,0},{3,1},{4,6},{5,7},{6,4},{7,5},{8,10},{9,11},{10,... | collective-permute-start | bytes 393224 | tf_op jit(solution)/shard_map/ppermute | solution.py:34
  73.9 5.4 %collective-permute-done.22.refs_4_ = bf16[2,128,256]{2,1,0:T(8,128)(2,1)S(1)} collective-permute-done((bf16[2,128,256]{2,1,0:T(8,128)(2,1)S(1)}, bf16[2,128,256]{2,1,0:T(8,128)(2,1)S(1)}, u32[]{:S(2)}, u32[]{:S(2)}) %collective-permute-start.22) | collective-permute-done | bytes 131104 | tf_op jit(solution)/shard_map/ppermute | solution.py:34
  82.8 2.5 %collective-permute-done.28.refs_13_ = bf16[512,896]{1,0:T(8,128)(2,1)S(1)} collective-permute-done((bf16[512,896]{1,0:T(8,128)(2,1)S(1)}, bf16[512,896]{1,0:T(8,128)(2,1)S(1)}, u32[]{:S(2)}, u32[]{:S(2)}) %collective-permute-start.28) | collective-permute-done | bytes 917536 | tf_op jit(solution)/shard_map/ppermute | solution.py:34
  88.4 5.2 %shard_map.163.refs_0_ = f32[8,128]{1,0:T(8,128)S(1)} custom-call(s32[4]{0:T(128)S(1)} %pad_add_fusion.ids.refs_0_, s32[128,1]{1,0:T(8,128)S(1)} %copy.19.wanted, f32[8,1,256]{2,1,0:T(1,128)S(1)} %get-tuple-element.88.refs_0_, f32[8,1,256]{2,1,0:T(1,128)S(1)} %get-tuple-element.89.refs_1_, bf16[2,128,256]{2,1,0:T(8,128)(2,1)S(1)} %add_convert_fusion.refs_2_, ...), custom_call_target="tpu_custom_call" | custom-call | tf_op jit(solution)/shard_map/pallas_call | solution.py:22
  96.1 4.3 %collective-permute-start.32 = (f32[8,128]{1,0:T(8,128)S(1)}, f32[8,128]{1,0:T(8,128)S(1)}, u32[]{:S(2)}, u32[]{:S(2)}) collective-permute-start(f32[8,128]{1,0:T(8,128)S(1)} %shard_map.164.refs_0_), channel_id=1, source_target_pairs={{0,6},{1,7},{2,4},{3,5},{4,2},{5,3},{6,0},{7,1},{8,14},{9,15},{10,... | collective-permute-start | bytes 12296 | tf_op jit(solution)/shard_map/ppermute | solution.py:34
  102.0 2.0 %collective-permute-done.33.refs_3_ = f32[8,128]{1,0:T(8,128)S(1)} collective-permute-done((f32[8,128]{1,0:T(8,128)S(1)}, f32[8,128]{1,0:T(8,128)S(1)}, u32[]{:S(2)}, u32[]{:S(2)}) %collective-permute-start.33) | collective-permute-done | bytes 4128 | tf_op jit(solution)/shard_map/ppermute | solution.py:34
  105.6 1.5 %collective-permute-start.35 = (f32[1,128]{1,0:T(1,128)S(1)}, f32[1,128]{1,0:T(1,128)S(1)}, u32[]{:S(2)}, u32[]{:S(2)}) collective-permute-start(f32[1,128]{1,0:T(1,128)S(1)} %shard_map.165), channel_id=1, source_target_pairs={{0,16},{8,24},{16,0},{24,8},{1,17},{9,25},{17,1},{25,9},{2,18},{10... | collective-permute-start | bytes 1544 | tf_op jit(solution)/shard_map/ppermute | solution.py:34
  109.1 2.4 %collective-permute-done.36 = f32[1,128]{1,0:T(1,128)S(1)} collective-permute-done((f32[1,128]{1,0:T(1,128)S(1)}, f32[1,128]{1,0:T(1,128)S(1)}, u32[]{:S(2)}, u32[]{:S(2)}) %collective-permute-start.36) | collective-permute-done | bytes 544 | tf_op jit(solution)/shard_map/ppermute | solution.py:34
  (94 shorter events, 33.8 us)
Async XLA Ops:
  2.8 6.7 %collective-permute-start.4 = (bf16[17,16,256]{2,1,0:T(8,128)(2,1)S(1)}, bf16[17,16,256]{2,1,0:T(8,128)(2,1)S(1)}, u32[]{:S(2)}, u32[]{:S(2)}) collective-permute-start(bf16[17,16,256]{2,1,0:T(8,128)(2,1)S(1)} %shard_map.158.refs_4_), channel_id=1, source_target_pairs={{0,16},{8,24},{16,0},{24,8},{1,17},{9,25},{17,1},{25,9},{2,18},{10... | collective-permute-start | bytes 417800 | tf_op jit(solution)/shard_map/ppermute | solution.py:34
  5.8 6.9 %collective-permute-start = (bf16[16,16,256]{2,1,0:T(8,128)(2,1)}, bf16[16,16,256]{2,1,0:T(8,128)(2,1)S(1)}, u32[]{:S(2)}, u32[]{:S(2)}) collective-permute-start(bf16[16,16,256]{2,1,0:T(8,128)(2,1)} %refs_0_), channel_id=1, source_target_pairs={{0,8},{8,0},{16,24},{24,16},{1,9},{9,1},{17,25},{25,17},{2,10},{10... | collective-permute-start | bytes 393224 | tf_op jit(solution)/shard_map/ppermute | solution.py:34
  7.3 9.6 %collective-permute-start.3 = (bf16[17,16,256]{2,1,0:T(8,128)(2,1)S(1)}, bf16[17,16,256]{2,1,0:T(8,128)(2,1)S(1)}, u32[]{:S(2)}, u32[]{:S(2)}) collective-permute-start(bf16[17,16,256]{2,1,0:T(8,128)(2,1)S(1)} %shard_map.158.refs_4_), channel_id=1, source_target_pairs={{0,8},{8,0},{16,24},{24,16},{1,9},{9,1},{17,25},{25,17},{2,10},{10... | collective-permute-start | bytes 417800 | tf_op jit(solution)/shard_map/ppermute | solution.py:34
  9.5 8.8 %collective-permute-start.5 = (bf16[17,16,256]{2,1,0:T(8,128)(2,1)S(1)}, bf16[17,16,256]{2,1,0:T(8,128)(2,1)S(1)}, u32[]{:S(2)}, u32[]{:S(2)}) collective-permute-start(bf16[17,16,256]{2,1,0:T(8,128)(2,1)S(1)} %collective-permute-done.4.refs_6_), channel_id=1, source_target_pairs={{0,8},{8,0},{16,24},{24,16},{1,9},{9,1},{17,25},{25,17},{2,10},{10... | collective-permute-start | bytes 417800 | tf_op jit(solution)/shard_map/ppermute | solution.py:34
  11.2 5.7 %collective-permute-start.1 = (bf16[16,16,256]{2,1,0:T(8,128)(2,1)}, bf16[16,16,256]{2,1,0:T(8,128)(2,1)S(1)}, u32[]{:S(2)}, u32[]{:S(2)}) collective-permute-start(bf16[16,16,256]{2,1,0:T(8,128)(2,1)} %refs_0_), channel_id=1, source_target_pairs={{0,16},{8,24},{16,0},{24,8},{1,17},{9,25},{17,1},{25,9},{2,18},{10... | collective-permute-start | bytes 393224 | tf_op jit(solution)/shard_map/ppermute | solution.py:34
  12.7 5.6 %collective-permute-start.2 = (bf16[16,16,256]{2,1,0:T(8,128)(2,1)S(1)}, bf16[16,16,256]{2,1,0:T(8,128)(2,1)S(1)}, u32[]{:S(2)}, u32[]{:S(2)}) collective-permute-start(bf16[16,16,256]{2,1,0:T(8,128)(2,1)S(1)} %collective-permute-done.refs_1_), channel_id=1, source_target_pairs={{0,16},{8,24},{16,0},{24,8},{1,17},{9,25},{17,1},{25,9},{2,18},{10... | collective-permute-start | bytes 393224 | tf_op jit(solution)/shard_map/ppermute | solution.py:34
  18.3 24.2 %collective-permute-start.13 = (bf16[512,896]{1,0:T(8,128)(2,1)}, bf16[512,896]{1,0:T(8,128)(2,1)S(1)}, u32[]{:S(2)}, u32[]{:S(2)}) collective-permute-start(bf16[512,896]{1,0:T(8,128)(2,1)} %refs_10_), channel_id=1, source_target_pairs={{0,8},{8,0},{16,24},{24,16},{1,9},{9,1},{17,25},{25,17},{2,10},{10... | collective-permute-start | bytes 2752520 | tf_op jit(solution)/shard_map/ppermute | solution.py:34
  18.9 23.6 %collective-permute-start.14 = (bf16[512,896]{1,0:T(8,128)(2,1)}, bf16[512,896]{1,0:T(8,128)(2,1)S(1)}, u32[]{:S(2)}, u32[]{:S(2)}) collective-permute-start(bf16[512,896]{1,0:T(8,128)(2,1)} %refs_14_), channel_id=1, source_target_pairs={{0,16},{8,24},{16,0},{24,8},{1,17},{9,25},{17,1},{25,9},{2,18},{10... | collective-permute-start | bytes 2752520 | tf_op jit(solution)/shard_map/ppermute | solution.py:34
  23.1 9.3 %collective-permute-start.6 = (bf16[2,128,256]{2,1,0:T(8,128)(2,1)S(1)}, bf16[2,128,256]{2,1,0:T(8,128)(2,1)S(1)}, u32[]{:S(2)}, u32[]{:S(2)}) collective-permute-start(bf16[2,128,256]{2,1,0:T(8,128)(2,1)S(1)} %get-tuple-element.71.refs_6_), channel_id=1, source_target_pairs={{0,4},{1,5},{2,6},{3,7},{4,0},{5,1},{6,2},{7,3},{8,12},{9,13},{10,... | collective-permute-start | bytes 393224 | tf_op jit(solution)/shard_map/ppermute | solution.py:34
  25.8 10.7 %collective-permute-start.7 = (bf16[2,128,256]{2,1,0:T(8,128)(2,1)S(1)}, bf16[2,128,256]{2,1,0:T(8,128)(2,1)S(1)}, u32[]{:S(2)}, u32[]{:S(2)}) collective-permute-start(bf16[2,128,256]{2,1,0:T(8,128)(2,1)S(1)} %get-tuple-element.71.refs_6_), channel_id=1, source_target_pairs={{0,2},{1,3},{2,0},{3,1},{4,6},{5,7},{6,4},{7,5},{8,10},{9,11},{10,... | collective-permute-start | bytes 393224 | tf_op jit(solution)/shard_map/ppermute | solution.py:34
  27.3 9.7 %collective-permute-start.8 = (bf16[2,128,256]{2,1,0:T(8,128)(2,1)S(1)}, bf16[2,128,256]{2,1,0:T(8,128)(2,1)S(1)}, u32[]{:S(2)}, u32[]{:S(2)}) collective-permute-start(bf16[2,128,256]{2,1,0:T(8,128)(2,1)S(1)} %get-tuple-element.71.refs_6_), channel_id=1, source_target_pairs={{0,6},{1,7},{2,4},{3,5},{4,2},{5,3},{6,0},{7,1},{8,14},{9,15},{10,... | collective-permute-start | bytes 393224 | tf_op jit(solution)/shard_map/ppermute | solution.py:34
  32.4 4.8 %collective-permute-start.9 = (bf16[2,128,256]{2,1,0:T(8,128)(2,1)S(1)}, bf16[2,128,256]{2,1,0:T(8,128)(2,1)S(1)}, u32[]{:S(2)}, u32[]{:S(2)}) collective-permute-start(bf16[2,128,256]{2,1,0:T(8,128)(2,1)S(1)} %get-tuple-element.71.refs_6_), channel_id=1, source_target_pairs={{0,1},{1,0},{2,3},{3,2},{4,5},{5,4},{6,7},{7,6},{8,9},{9,8},{10,11... | collective-permute-start | bytes 393224 | tf_op jit(solution)/shard_map/ppermute | solution.py:34
  43.0 23.4 %collective-permute-start.19 = (bf16[512,896]{1,0:T(8,128)(2,1)}, bf16[512,896]{1,0:T(8,128)(2,1)S(1)}, u32[]{:S(2)}, u32[]{:S(2)}) collective-permute-start(bf16[512,896]{1,0:T(8,128)(2,1)} %refs_10_), channel_id=1, source_target_pairs={{0,16},{8,24},{16,0},{24,8},{1,17},{9,25},{17,1},{25,9},{2,18},{10... | collective-permute-start | bytes 2752520 | tf_op jit(solution)/shard_map/ppermute | solution.py:34
  43.9 23.4 %collective-permute-start.20 = (bf16[512,896]{1,0:T(8,128)(2,1)}, bf16[512,896]{1,0:T(8,128)(2,1)S(1)}, u32[]{:S(2)}, u32[]{:S(2)}) collective-permute-start(bf16[512,896]{1,0:T(8,128)(2,1)} %refs_14_), channel_id=1, source_target_pairs={{0,8},{8,0},{16,24},{24,16},{1,9},{9,1},{17,25},{25,17},{2,10},{10... | collective-permute-start | bytes 2752520 | tf_op jit(solution)/shard_map/ppermute | solution.py:34
  45.7 9.6 %collective-permute-start.17 = (bf16[2,128,256]{2,1,0:T(8,128)(2,1)S(1)}, bf16[2,128,256]{2,1,0:T(8,128)(2,1)S(1)}, u32[]{:S(2)}, u32[]{:S(2)}) collective-permute-start(bf16[2,128,256]{2,1,0:T(8,128)(2,1)S(1)} %get-tuple-element.104), channel_id=1, source_target_pairs={{0,4},{1,5},{2,6},{3,7},{4,0},{5,1},{6,2},{7,3},{8,12},{9,13},{10,... | collective-permute-start | bytes 393224 | tf_op jit(solution)/shard_map/ppermute | solution.py:34
  46.4 10.1 %collective-permute-start.16 = (bf16[2,128,256]{2,1,0:T(8,128)(2,1)S(1)}, bf16[2,128,256]{2,1,0:T(8,128)(2,1)S(1)}, u32[]{:S(2)}, u32[]{:S(2)}) collective-permute-start(bf16[2,128,256]{2,1,0:T(8,128)(2,1)S(1)} %get-tuple-element.103), channel_id=1, source_target_pairs={{0,2},{1,3},{2,0},{3,1},{4,6},{5,7},{6,4},{7,5},{8,10},{9,11},{10,... | collective-permute-start | bytes 393224 | tf_op jit(solution)/shard_map/ppermute | solution.py:34
  51.1 8.7 %collective-permute-start.18 = (bf16[2,128,256]{2,1,0:T(8,128)(2,1)S(1)}, bf16[2,128,256]{2,1,0:T(8,128)(2,1)S(1)}, u32[]{:S(2)}, u32[]{:S(2)}) collective-permute-start(bf16[2,128,256]{2,1,0:T(8,128)(2,1)S(1)} %get-tuple-element.108), channel_id=1, source_target_pairs={{0,6},{1,7},{2,4},{3,5},{4,2},{5,3},{6,0},{7,1},{8,14},{9,15},{10,... | collective-permute-start | bytes 393224 | tf_op jit(solution)/shard_map/ppermute | solution.py:34
  55.2 30.0 %collective-permute-start.28 = (bf16[512,896]{1,0:T(8,128)(2,1)S(1)}, bf16[512,896]{1,0:T(8,128)(2,1)S(1)}, u32[]{:S(2)}, u32[]{:S(2)}) collective-permute-start(bf16[512,896]{1,0:T(8,128)(2,1)S(1)} %collective-permute-done.13.refs_11_), channel_id=1, source_target_pairs={{0,16},{8,24},{16,0},{24,8},{1,17},{9,25},{17,1},{25,9},{2,18},{10... | collective-permute-start | bytes 2752520 | tf_op jit(solution)/shard_map/ppermute | solution.py:34
  56.5 29.6 %collective-permute-start.29 = (bf16[512,896]{1,0:T(8,128)(2,1)S(1)}, bf16[512,896]{1,0:T(8,128)(2,1)}, u32[]{:S(2)}, u32[]{:S(2)}) collective-permute-start(bf16[512,896]{1,0:T(8,128)(2,1)S(1)} %collective-permute-done.14.refs_16_), channel_id=1, source_target_pairs={{0,8},{8,0},{16,24},{24,16},{1,9},{9,1},{17,25},{25,17},{2,10},{10... | collective-permute-start | bytes 2752520 | tf_op jit(solution)/shard_map/ppermute | solution.py:34
  68.3 11.0 %collective-permute-start.22 = (bf16[2,128,256]{2,1,0:T(8,128)(2,1)S(1)}, bf16[2,128,256]{2,1,0:T(8,128)(2,1)S(1)}, u32[]{:S(2)}, u32[]{:S(2)}) collective-permute-start(bf16[2,128,256]{2,1,0:T(8,128)(2,1)S(1)} %add_convert_fusion.refs_2_), channel_id=1, source_target_pairs={{0,4},{1,5},{2,6},{3,7},{4,0},{5,1},{6,2},{7,3},{8,12},{9,13},{10,... | collective-permute-start | bytes 393224 | tf_op jit(solution)/shard_map/ppermute | solution.py:34
  69.1 10.6 %collective-permute-start.21 = (bf16[2,128,256]{2,1,0:T(8,128)(2,1)S(1)}, bf16[2,128,256]{2,1,0:T(8,128)(2,1)S(1)}, u32[]{:S(2)}, u32[]{:S(2)}) collective-permute-start(bf16[2,128,256]{2,1,0:T(8,128)(2,1)S(1)} %add_convert_fusion.refs_2_), channel_id=1, source_target_pairs={{0,2},{1,3},{2,0},{3,1},{4,6},{5,7},{6,4},{7,5},{8,10},{9,11},{10,... | collective-permute-start | bytes 393224 | tf_op jit(solution)/shard_map/ppermute | solution.py:34
  73.9 7.3 %collective-permute-start.23 = (bf16[2,128,256]{2,1,0:T(8,128)(2,1)S(1)}, bf16[2,128,256]{2,1,0:T(8,128)(2,1)S(1)}, u32[]{:S(2)}, u32[]{:S(2)}) collective-permute-start(bf16[2,128,256]{2,1,0:T(8,128)(2,1)S(1)} %add_convert_fusion.refs_2_), channel_id=1, source_target_pairs={{0,6},{1,7},{2,4},{3,5},{4,2},{5,3},{6,0},{7,1},{8,14},{9,15},{10,... | collective-permute-start | bytes 393224 | tf_op jit(solution)/shard_map/ppermute | solution.py:34
  95.4 5.7 %collective-permute-start.31 = (f32[8,128]{1,0:T(8,128)S(1)}, f32[8,128]{1,0:T(8,128)S(1)}, u32[]{:S(2)}, u32[]{:S(2)}) collective-permute-start(f32[8,128]{1,0:T(8,128)S(1)} %shard_map.164.refs_0_), channel_id=1, source_target_pairs={{0,4},{1,5},{2,6},{3,7},{4,0},{5,1},{6,2},{7,3},{8,12},{9,13},{10,... | collective-permute-start | bytes 12296 | tf_op jit(solution)/shard_map/ppermute | solution.py:34
  96.1 5.9 %collective-permute-start.32 = (f32[8,128]{1,0:T(8,128)S(1)}, f32[8,128]{1,0:T(8,128)S(1)}, u32[]{:S(2)}, u32[]{:S(2)}) collective-permute-start(f32[8,128]{1,0:T(8,128)S(1)} %shard_map.164.refs_0_), channel_id=1, source_target_pairs={{0,6},{1,7},{2,4},{3,5},{4,2},{5,3},{6,0},{7,1},{8,14},{9,15},{10,... | collective-permute-start | bytes 12296 | tf_op jit(solution)/shard_map/ppermute | solution.py:34
  (18 other events, 36.2 us)

commit v5 on v4

--- a/solution.py
+++ b/solution.py
@@ -101,7 +101,7 @@
         out[m] = total.astype(out.dtype)
 
 
-def normalise(values, gain, chip, core, store):
+def normalise(values, gain, chip, core, store, copy):
     half = len(values) // 2
     part = values[0].shape[1]
     width = part * len(values)
@@ -110,16 +110,11 @@
     values = [v - center for v in values]
     spread = sum(jnp.sum(v * v, axis=1, keepdims=True) for v in values) / width
     scale = lax.rsqrt(spread + epsilon)
+    copy.wait()
     for k, v in enumerate(values):
         place = 2 * (chip ^ (k % half)) + (core if k < half else 1 - core)
         store[place] = (v * scale * gain[place]).astype(jnp.bfloat16)
     return values[0]
-
-
-def load_kernel(*refs):
-    count = (len(refs) - 2) // 2
-    for copy in fetch(refs[1 : 1 + count], refs[1 + count : -1], refs[-1]):
-        copy.wait()
 
 
 def blocks_dot(normed, weight, order):
@@ -133,19 +128,23 @@
 
 
 def ffn_kernel(half, ids, *refs):
-    gains, ups, downs = refs[:2], refs[2:4], refs[4:6]
     parts = refs[6 : 6 + 2 * half]
-    keep, send, normed, terms = refs[6 + 2 * half :]
+    keep, send, gains, ups, downs, normed, terms, sems = refs[6 + 2 * half :]
+    copies = fetch(
+        refs[:6], [store.at[m] for store in (gains, ups, downs) for m in range(2)], sems
+    )
     chip, core = ids[1], ids[2]
     part = parts[0].shape[2]
     bases = [
-        normalise([part[m] for part in parts], gains[m], chip, core, normed.at[m])
+        normalise([part[m] for part in parts], gains.at[m], chip, core, normed.at[m], copies[m])
         for m in range(2)
     ]
     for m in range(2):
-        pre = blocks_dot(normed.at[m], ups[m], range(2 * half))
+        copies[2 + m].wait()
+        pre = blocks_dot(normed.at[m], ups.at[m], range(2 * half))
         units = jax.nn.gelu(pre).astype(jnp.bfloat16)
-        full = jnp.dot(units, downs[m][...], preferred_element_type=jnp.float32)
+        copies[4 + m].wait()
+        full = jnp.dot(units, downs[m], preferred_element_type=jnp.float32)
         for b in range(2 * half):
             terms[m, b] = full[:, b * part : (b + 1) * part]
         for k in range(half):
@@ -162,21 +161,26 @@
 
 
 def score_kernel(half, ids, wanted, *refs):
-    gains, parts = refs[:2], refs[2 : 2 + 2 * half]
-    *outs, stats, normed, out_store, sems = refs[2 + 2 * half :]
+    parts = refs[2 : 2 + 2 * half]
+    *outs, stats, gains, normed, out_store, sems = refs[2 + 2 * half :]
     dp = len(outs) // 2
-    copies = fetch([outs[0], outs[dp]], [out_store.at[0], out_store.at[1]], sems)
+    copies = fetch(
+        [refs[0], refs[1], outs[0], outs[dp]],
+        [store.at[m] for store in (gains, out_store) for m in range(2)],
+        sems,
+    )
     me, chip, core = ids[0], ids[1], ids[2]
     lane = lax.broadcasted_iota(jnp.int32, (parts[0].shape[1], 128), 1)
     table = jnp.zeros(lane.shape, jnp.float32)
     ratio = 2 * half // dp
     for m in range(2):
-        normalise([part[m] for part in parts], gains[m], chip, core, normed.at[m])
+        values = [part[m] for part in parts]
+        normalise(values, gains.at[m], chip, core, normed.at[m], copies[m])
     for m in range(2):
         logits = None
         for k in [*range(1, dp), 0]:
             if k == 0:
-                copies[m].wait()
+                copies[2 + m].wait()
                 outs[m * dp] = out_store.at[m]
             order = [(me ^ k) * ratio + b for b in range(ratio)]
             piece = blocks_dot(normed.at[m], outs[m * dp + k], order)
@@ -302,25 +306,19 @@
 
     far = sorted(range(1, half), key=lambda k: (k.bit_length() <= 1, k))
 
-    def gather_pair(own, loaded=()):
+    def gather_pair(own):
         same = {0: own}
         for k in far:
             same[k] = exchange(own, "mp", 2 * k)
-        same[far[0]], loaded = lax.optimization_barrier((same[far[0]], loaded))
         same = [same[k] for k in range(half)]
-        return same + [exchange(v, "mp", 1) for v in same], loaded
-
-    weights = (up_policy, up_reference, down_policy, down_reference, *gains)
-    moved, weights = lax.optimization_barrier((moved, weights))
-    loaded = call(
-        load_kernel,
-        tuple(jax.ShapeDtypeStruct(w.shape, w.dtype) for w in weights),
-        (ids, *weights),
-        [pltpu.SemaphoreType.DMA((len(weights),))],
-        far=range(1, 1 + len(weights)),
-        mib=12,
-    )
-    parts, loaded = gather_pair(moved, loaded)
+        return same + [exchange(v, "mp", 1) for v in same]
+
+    parts = gather_pair(moved)
+    if len(bits) > 1:
+        parts[-1] = wait_for(parts[-1], lambda m, k: k == 0)
+        later = [{0: outs[m][0]} for m in range(2)]
+        spread_step(later, 1, lambda m, k: True)
+    gain_scratch = pltpu.VMEM((2, mp, 1, part), jnp.float32)
     block = jax.ShapeDtypeStruct((2, rows, part), jnp.bfloat16)
     keep, send = call(
         functools.partial(ffn_kernel, half),
@@ -328,17 +326,19 @@
             jax.ShapeDtypeStruct((half, 2, rows, part), jnp.float32),
             jax.ShapeDtypeStruct((half, 2, rows, part), jnp.bfloat16),
         ),
-        (ids, *loaded[4:6], *loaded[:4], *parts),
+        (ids, *gains[:2], up_policy, up_reference, down_policy, down_reference, *parts),
         [
+            gain_scratch,
+            pltpu.VMEM((2,) + up_policy.shape, jnp.bfloat16),
+            pltpu.VMEM((2,) + down_policy.shape, jnp.bfloat16),
             pltpu.VMEM((2, mp, rows, part), jnp.bfloat16),
             pltpu.VMEM((2, mp, rows, part), jnp.float32),
+            pltpu.SemaphoreType.DMA((6,)),
         ],
-        mib=14,
-    )
-    send = wait_for(send, lambda m, k: True)
-    if len(bits) > 1:
-        later = [{0: outs[m][0]} for m in range(2)]
-        spread_step(later, 1, lambda m, k: True)
+        far=range(1, 7),
+        mib=22,
+    )
+    send = wait_for(send, lambda m, k: k > 0)
     came = exchange(send, "mp", 1)
     own, *pieces = call(
         pair_kernel,
@@ -347,15 +347,13 @@
     )
     arrived = {k: exchange(pieces[k - 1], "mp", 2 * k) for k in far}
     if len(bits) > 1:
-        arrived[far[0]] = wait_for(arrived[far[0]], lambda m, k: k == bit_orders[m][0])
+        for m in range(2):
+            outs[m].update(later[m])
+        arrived[far[0]] = wait_for(arrived[far[0]], lambda m, k: True)
+        spread_step(outs, 1, lambda m, k: k == bit_orders[m][0])
     for k in range(1, half):
         own = own + arrived[k].astype(jnp.float32)
     stream = own.astype(jnp.bfloat16)
-    if len(bits) > 1:
-        spread_step(outs, 1, lambda m, k: k == bit_orders[m][0])
-        for m in range(2):
-            outs[m].update(later[m])
-        stream = wait_for(stream, lambda m, k: k != bits[0] + bits[1])
     for step in range(2, len(bits)):
         stream = wait_for(stream, lambda m, k: True)
         spread_step(outs, step, lambda m, k: True)
@@ -373,16 +371,17 @@
         (
             ids,
             wanted,
-            *loaded[6:],
-            *gather_pair(stream)[0],
+            *gains[2:],
+            *gather_pair(stream),
             *[outs[m][k] for m in range(2) for k in range(dp)],
         ),
         [
+            gain_scratch,
             pltpu.VMEM((2, mp, rows, part), jnp.bfloat16),
             pltpu.VMEM((2,) + out_policy.shape, jnp.bfloat16),
-            pltpu.SemaphoreType.DMA((2,)),
+            pltpu.SemaphoreType.DMA((4,)),
         ],
-        far=(4 + mp, 4 + mp + dp),
+        far=(2, 3, 4 + mp, 4 + mp + dp),
         mib=14,
     )
     stats = call(

time: 113 us -> 104 us (0.920)
  starting transfers between devices: 41.8 us -> 37 us
  local copies, waits for them, and re-layouts: 6.38 us -> 2.12 us
  waiting for transfers between devices: 43.4 us -> 46.2 us
  Pallas kernels: 18.1 us -> 15.9 us
    ppermute x37, starting transfers between devices: 41.8 us -> 37 us  [exchange(): return lax.ppermute(values, axis, [(i, i ^ flip) for i in range(count)])]
    unnamed x10 -> x2, local copies, waits for them, and re-layouts: 4.91 us -> 0.65 us
    ppermute x37, waiting for transfers between devices: 43.4 us -> 46.2 us  [exchange(): return lax.ppermute(values, axis, [(i, i ^ flip) for i in range(count)])]
    pallas_call x8 -> x7, Pallas kernels: 18.1 us -> 15.9 us  [call(): pl.pallas_call(kernel, out_shape=out_shape, in_specs=specs, out_specs=jax...]
  transfers between devices with their start and end apart: 37 -> 37, of which waited for: 21 -> 24; matrix products, arithmetic and copies ran while one was open for 2% -> 2% of each run, Pallas kernels for 9% -> 8%
where the time goes in v5:
time: 104 us
  waiting for transfers between devices  46.2 us (44%)
  starting transfers between devices  37 us (36%)
  Pallas kernels  15.9 us (15%)
  local copies, waits for them, and re-layouts  2.12 us (2%)
  other arithmetic  2.06 us (2%)
    ppermute x37, waiting for transfers between devices, exchange(): return lax.ppermute(values, axis, [(i, i ^ flip) for i in range(count)])  46.2 us
    ppermute x37, starting transfers between devices, exchange(): return lax.ppermute(values, axis, [(i, i ^ flip) for i in range(count)])  37 us
    pallas_call x7, Pallas kernels, call(): pl.pallas_call(kernel, out_shape=out_shape, in_specs=specs, out_specs=jax...  15.9 us
  transfers between devices with their start and end apart: 37, of which 24 were waited for; matrix products, arithmetic and copies ran while one was open for 2% of the time, Pallas kernels for 8%

profile of v5, /device:TPU:0, one launch (start us, length us, event | category | flops | bytes accessed | tf_op | source)
XLA Modules:
  0.0 104.0 jit_solution(12116999688048748534)
XLA Ops:
  1.3 1.5 %shard_map.158.refs_4_ = bf16[17,16,256]{2,1,0:T(8,128)(2,1)S(1)} custom-call(s32[16]{0:T(128)S(1)} %copy-done, s32[16,16]{1,0:T(8,128)} %targets_far.1, bf16[16,16,256]{2,1,0:T(8,128)(2,1)} %hidden.1), custom_call_target="tpu_custom_call" | custom-call | tf_op jit(solution)/shard_map/pallas_call | solution.py:22
  2.8 3.0 %collective-permute-start.4 = (bf16[17,16,256]{2,1,0:T(8,128)(2,1)S(1)}, bf16[17,16,256]{2,1,0:T(8,128)(2,1)S(1)}, u32[]{:S(2)}, u32[]{:S(2)}) collective-permute-start(bf16[17,16,256]{2,1,0:T(8,128)(2,1)S(1)} %shard_map.158.refs_4_), channel_id=1, source_target_pairs={{0,16},{8,24},{16,0},{24,8},{1,17},{9,25},{17,1},{25,9},{2,18},{10... | collective-permute-start | bytes 417800 | tf_op jit(solution)/shard_map/ppermute | solution.py:34
  5.8 1.5 %collective-permute-start = (bf16[16,16,256]{2,1,0:T(8,128)(2,1)}, bf16[16,16,256]{2,1,0:T(8,128)(2,1)S(1)}, u32[]{:S(2)}, u32[]{:S(2)}) collective-permute-start(bf16[16,16,256]{2,1,0:T(8,128)(2,1)} %refs_0_), channel_id=1, source_target_pairs={{0,8},{8,0},{16,24},{24,16},{1,9},{9,1},{17,25},{25,17},{2,10},{10... | collective-permute-start | bytes 393224 | tf_op jit(solution)/shard_map/ppermute | solution.py:34
  7.8 1.6 %collective-permute-done.4.refs_6_ = bf16[17,16,256]{2,1,0:T(8,128)(2,1)S(1)} collective-permute-done((bf16[17,16,256]{2,1,0:T(8,128)(2,1)S(1)}, bf16[17,16,256]{2,1,0:T(8,128)(2,1)S(1)}, u32[]{:S(2)}, u32[]{:S(2)}) %collective-permute-start.4) | collective-permute-done | bytes 139296 | tf_op jit(solution)/shard_map/ppermute | solution.py:34
  9.5 1.7 %collective-permute-start.5 = (bf16[17,16,256]{2,1,0:T(8,128)(2,1)S(1)}, bf16[17,16,256]{2,1,0:T(8,128)(2,1)S(1)}, u32[]{:S(2)}, u32[]{:S(2)}) collective-permute-start(bf16[17,16,256]{2,1,0:T(8,128)(2,1)S(1)} %collective-permute-done.4.refs_6_), channel_id=1, source_target_pairs={{0,8},{8,0},{16,24},{24,16},{1,9},{9,1},{17,25},{25,17},{2,10},{10... | collective-permute-start | bytes 417800 | tf_op jit(solution)/shard_map/ppermute | solution.py:34
  11.2 1.5 %collective-permute-start.1 = (bf16[16,16,256]{2,1,0:T(8,128)(2,1)}, bf16[16,16,256]{2,1,0:T(8,128)(2,1)S(1)}, u32[]{:S(2)}, u32[]{:S(2)}) collective-permute-start(bf16[16,16,256]{2,1,0:T(8,128)(2,1)} %refs_0_), channel_id=1, source_target_pairs={{0,16},{8,24},{16,0},{24,8},{1,17},{9,25},{17,1},{25,9},{2,18},{10... | collective-permute-start | bytes 393224 | tf_op jit(solution)/shard_map/ppermute | solution.py:34
  13.2 3.7 %collective-permute-done.1.refs_2_ = bf16[16,16,256]{2,1,0:T(8,128)(2,1)S(1)} collective-permute-done((bf16[16,16,256]{2,1,0:T(8,128)(2,1)}, bf16[16,16,256]{2,1,0:T(8,128)(2,1)S(1)}, u32[]{:S(2)}, u32[]{:S(2)}) %collective-permute-start.1) | collective-permute-done | bytes 131104 | tf_op jit(solution)/shard_map/ppermute | solution.py:34
  21.3 1.8 %shard_map.159 = (bf16[2,128,256]{2,1,0:T(8,128)(2,1)S(1)}, f32[4,16,256]{2,1,0:T(8,128)S(1)}) custom-call(s32[4]{0:T(128)S(1)} %pad_add_fusion.ids, s32[4,1,256]{2,1,0:T(1,128)S(1)} %broadcast_in_dim.98.plan, bf16[16,16,256]{2,1,0:T(8,128)(2,1)} %refs_0_, bf16[16,16,256]{2,1,0:T(8,128)(2,1)S(1)} %collective-permute-done.refs_1_, ...), custom_call_target="tpu_custom_call" | custom-call | tf_op jit(solution)/shard_map/pallas_call | solution.py:22
  23.1 3.7 %collective-permute-start.8 = (bf16[2,128,256]{2,1,0:T(8,128)(2,1)S(1)}, bf16[2,128,256]{2,1,0:T(8,128)(2,1)S(1)}, u32[]{:S(2)}, u32[]{:S(2)}) collective-permute-start(bf16[2,128,256]{2,1,0:T(8,128)(2,1)S(1)} %get-tuple-element.42.refs_6_), channel_id=1, source_target_pairs={{0,6},{1,7},{2,4},{3,5},{4,2},{5,3},{6,0},{7,1},{8,14},{9,15},{10,... | collective-permute-start | bytes 393224 | tf_op jit(solution)/shard_map/ppermute | solution.py:34
  27.6 3.7 %collective-permute-done.8.refs_9_ = bf16[2,128,256]{2,1,0:T(8,128)(2,1)S(1)} collective-permute-done((bf16[2,128,256]{2,1,0:T(8,128)(2,1)S(1)}, bf16[2,128,256]{2,1,0:T(8,128)(2,1)S(1)}, u32[]{:S(2)}, u32[]{:S(2)}) %collective-permute-start.8) | collective-permute-done | bytes 131104 | tf_op jit(solution)/shard_map/ppermute | solution.py:34
  31.3 1.5 %collective-permute-done.6.refs_7_ = bf16[2,128,256]{2,1,0:T(8,128)(2,1)S(1)} collective-permute-done((bf16[2,128,256]{2,1,0:T(8,128)(2,1)S(1)}, bf16[2,128,256]{2,1,0:T(8,128)(2,1)S(1)}, u32[]{:S(2)}, u32[]{:S(2)}) %collective-permute-start.6) | collective-permute-done | bytes 131104 | tf_op jit(solution)/shard_map/ppermute | solution.py:34
  32.8 2.8 %collective-permute-done.7.refs_8_ = bf16[2,128,256]{2,1,0:T(8,128)(2,1)S(1)} collective-permute-done((bf16[2,128,256]{2,1,0:T(8,128)(2,1)S(1)}, bf16[2,128,256]{2,1,0:T(8,128)(2,1)S(1)}, u32[]{:S(2)}, u32[]{:S(2)}) %collective-permute-start.7) | collective-permute-done | bytes 131104 | tf_op jit(solution)/shard_map/ppermute | solution.py:34
  38.5 5.8 %shard_map.160 = (f32[4,2,128,256]{3,2,1,0:T(8,128)S(1)}, bf16[4,2,128,256]{3,2,1,0:T(8,128)(2,1)}) custom-call(s32[4]{0:T(128)S(1)} %pad_add_fusion.ids, f32[8,1,256]{2,1,0:T(1,128)} %bitcast.13, f32[8,1,256]{2,1,0:T(1,128)} %bitcast.14, bf16[2048,512]{1,0:T(8,128)(2,1)} %refs_2_.1, bf16[2048,512]{1,0:T(8,128)(2,1)} %refs_3_.1, bf16[512,2048]{1,0:T(8,128)(2,1)} %refs_4_.1, ...), custom_call_target="tpu_custom_call" | custom-call | tf_op jit(solution)/shard_map/pallas_call | solution.py:22
  44.6 1.9 %collective-permute-done.15.came = bf16[4,2,128,256]{3,2,1,0:T(8,128)(2,1)S(1)} collective-permute-done((bf16[4,2,128,256]{3,2,1,0:T(8,128)(2,1)}, bf16[4,2,128,256]{3,2,1,0:T(8,128)(2,1)S(1)}, u32[]{:S(2)}, u32[]{:S(2)}) %collective-permute-start.15) | collective-permute-done | bytes 524320 | tf_op jit(solution)/shard_map/ppermute | solution.py:34
  47.1 2.6 %collective-permute-start.20 = (bf16[2,128,256]{2,1,0:T(8,128)(2,1)S(1)}, bf16[2,128,256]{2,1,0:T(8,128)(2,1)S(1)}, u32[]{:S(2)}, u32[]{:S(2)}) collective-permute-start(bf16[2,128,256]{2,1,0:T(8,128)(2,1)S(1)} %get-tuple-element.57), channel_id=1, source_target_pairs={{0,6},{1,7},{2,4},{3,5},{4,2},{5,3},{6,0},{7,1},{8,14},{9,15},{10,... | collective-permute-start | bytes 393224 | tf_op jit(solution)/shard_map/ppermute | solution.py:34
  49.8 1.8 %collective-permute-start.16 = (bf16[2,128,256]{2,1,0:T(8,128)(2,1)S(1)}, bf16[2,128,256]{2,1,0:T(8,128)(2,1)S(1)}, u32[]{:S(2)}, u32[]{:S(2)}) collective-permute-start(bf16[2,128,256]{2,1,0:T(8,128)(2,1)S(1)} %get-tuple-element.50), channel_id=1, source_target_pairs={{0,2},{1,3},{2,0},{3,1},{4,6},{5,7},{6,4},{7,5},{8,10},{9,11},{10,... | collective-permute-start | bytes 393224 | tf_op jit(solution)/shard_map/ppermute | solution.py:34
  51.6 7.5 %collective-permute-done.18.refs_12_ = bf16[512,896]{1,0:T(8,128)(2,1)} collective-permute-done((bf16[512,896]{1,0:T(8,128)(2,1)}, bf16[512,896]{1,0:T(8,128)(2,1)}, u32[]{:S(2)}, u32[]{:S(2)}) %collective-permute-start.18) | collective-permute-done | bytes 917536 | tf_op jit(solution)/shard_map/ppermute | solution.py:34
  60.4 1.5 %collective-permute-start.28 = (bf16[512,896]{1,0:T(8,128)(2,1)S(1)}, bf16[512,896]{1,0:T(8,128)(2,1)S(1)}, u32[]{:S(2)}, u32[]{:S(2)}) collective-permute-start(bf16[512,896]{1,0:T(8,128)(2,1)S(1)} %collective-permute-done.13.refs_11_), channel_id=1, source_target_pairs={{0,16},{8,24},{16,0},{24,8},{1,17},{9,25},{17,1},{25,9},{2,18},{10... | collective-permute-start | bytes 2752520 | tf_op jit(solution)/shard_map/ppermute | solution.py:34
  63.4 2.7 %collective-permute-start.22 = (bf16[2,128,256]{2,1,0:T(8,128)(2,1)S(1)}, bf16[2,128,256]{2,1,0:T(8,128)(2,1)S(1)}, u32[]{:S(2)}, u32[]{:S(2)}) collective-permute-start(bf16[2,128,256]{2,1,0:T(8,128)(2,1)S(1)} %add_convert_fusion.refs_2_), channel_id=1, source_target_pairs={{0,4},{1,5},{2,6},{3,7},{4,0},{5,1},{6,2},{7,3},{8,12},{9,13},{10,... | collective-permute-start | bytes 393224 | tf_op jit(solution)/shard_map/ppermute | solution.py:34
  67.2 1.5 %collective-permute-done.21.refs_3_ = bf16[2,128,256]{2,1,0:T(8,128)(2,1)S(1)} collective-permute-done((bf16[2,128,256]{2,1,0:T(8,128)(2,1)S(1)}, bf16[2,128,256]{2,1,0:T(8,128)(2,1)S(1)}, u32[]{:S(2)}, u32[]{:S(2)}) %collective-permute-start.21) | collective-permute-done | bytes 131104 | tf_op jit(solution)/shard_map/ppermute | solution.py:34
  69.1 6.2 %collective-permute-done.22.refs_4_ = bf16[2,128,256]{2,1,0:T(8,128)(2,1)S(1)} collective-permute-done((bf16[2,128,256]{2,1,0:T(8,128)(2,1)S(1)}, bf16[2,128,256]{2,1,0:T(8,128)(2,1)S(1)}, u32[]{:S(2)}, u32[]{:S(2)}) %collective-permute-start.22) | collective-permute-done | bytes 131104 | tf_op jit(solution)/shard_map/ppermute | solution.py:34
  77.4 5.3 %collective-permute-done.28.refs_13_ = bf16[512,896]{1,0:T(8,128)(2,1)S(1)} collective-permute-done((bf16[512,896]{1,0:T(8,128)(2,1)S(1)}, bf16[512,896]{1,0:T(8,128)(2,1)S(1)}, u32[]{:S(2)}, u32[]{:S(2)}) %collective-permute-start.28) | collective-permute-done | bytes 917536 | tf_op jit(solution)/shard_map/ppermute | solution.py:34
  83.7 5.1 %shard_map.162.refs_0_ = f32[8,128]{1,0:T(8,128)S(1)} custom-call(s32[4]{0:T(128)S(1)} %pad_add_fusion.ids, s32[128,1]{1,0:T(8,128)S(1)} %copy.19.wanted, f32[8,1,256]{2,1,0:T(1,128)} %bitcast.15, f32[8,1,256]{2,1,0:T(1,128)} %bitcast.16, bf16[2,128,256]{2,1,0:T(8,128)(2,1)S(1)} %add_convert_fusion.refs_2_, ...), custom_call_target="tpu_custom_call" | custom-call | tf_op jit(solution)/shard_map/pallas_call | solution.py:22
  90.7 2.4 %collective-permute-start.32 = (f32[8,128]{1,0:T(8,128)S(1)}, f32[8,128]{1,0:T(8,128)S(1)}, u32[]{:S(2)}, u32[]{:S(2)}) collective-permute-start(f32[8,128]{1,0:T(8,128)S(1)} %shard_map.163.refs_0_), channel_id=1, source_target_pairs={{0,6},{1,7},{2,4},{3,5},{4,2},{5,3},{6,0},{7,1},{8,14},{9,15},{10,... | collective-permute-start | bytes 12296 | tf_op jit(solution)/shard_map/ppermute | solution.py:34
  (85 shorter events, 30.8 us)
Async XLA Ops:
  2.8 6.7 %collective-permute-start.4 = (bf16[17,16,256]{2,1,0:T(8,128)(2,1)S(1)}, bf16[17,16,256]{2,1,0:T(8,128)(2,1)S(1)}, u32[]{:S(2)}, u32[]{:S(2)}) collective-permute-start(bf16[17,16,256]{2,1,0:T(8,128)(2,1)S(1)} %shard_map.158.refs_4_), channel_id=1, source_target_pairs={{0,16},{8,24},{16,0},{24,8},{1,17},{9,25},{17,1},{25,9},{2,18},{10... | collective-permute-start | bytes 417800 | tf_op jit(solution)/shard_map/ppermute | solution.py:34
  5.8 6.9 %collective-permute-start = (bf16[16,16,256]{2,1,0:T(8,128)(2,1)}, bf16[16,16,256]{2,1,0:T(8,128)(2,1)S(1)}, u32[]{:S(2)}, u32[]{:S(2)}) collective-permute-start(bf16[16,16,256]{2,1,0:T(8,128)(2,1)} %refs_0_), channel_id=1, source_target_pairs={{0,8},{8,0},{16,24},{24,16},{1,9},{9,1},{17,25},{25,17},{2,10},{10... | collective-permute-start | bytes 393224 | tf_op jit(solution)/shard_map/ppermute | solution.py:34
  7.3 9.6 %collective-permute-start.3 = (bf16[17,16,256]{2,1,0:T(8,128)(2,1)S(1)}, bf16[17,16,256]{2,1,0:T(8,128)(2,1)S(1)}, u32[]{:S(2)}, u32[]{:S(2)}) collective-permute-start(bf16[17,16,256]{2,1,0:T(8,128)(2,1)S(1)} %shard_map.158.refs_4_), channel_id=1, source_target_pairs={{0,8},{8,0},{16,24},{24,16},{1,9},{9,1},{17,25},{25,17},{2,10},{10... | collective-permute-start | bytes 417800 | tf_op jit(solution)/shard_map/ppermute | solution.py:34
  9.5 8.8 %collective-permute-start.5 = (bf16[17,16,256]{2,1,0:T(8,128)(2,1)S(1)}, bf16[17,16,256]{2,1,0:T(8,128)(2,1)S(1)}, u32[]{:S(2)}, u32[]{:S(2)}) collective-permute-start(bf16[17,16,256]{2,1,0:T(8,128)(2,1)S(1)} %collective-permute-done.4.refs_6_), channel_id=1, source_target_pairs={{0,8},{8,0},{16,24},{24,16},{1,9},{9,1},{17,25},{25,17},{2,10},{10... | collective-permute-start | bytes 417800 | tf_op jit(solution)/shard_map/ppermute | solution.py:34
  11.2 5.7 %collective-permute-start.1 = (bf16[16,16,256]{2,1,0:T(8,128)(2,1)}, bf16[16,16,256]{2,1,0:T(8,128)(2,1)S(1)}, u32[]{:S(2)}, u32[]{:S(2)}) collective-permute-start(bf16[16,16,256]{2,1,0:T(8,128)(2,1)} %refs_0_), channel_id=1, source_target_pairs={{0,16},{8,24},{16,0},{24,8},{1,17},{9,25},{17,1},{25,9},{2,18},{10... | collective-permute-start | bytes 393224 | tf_op jit(solution)/shard_map/ppermute | solution.py:34
  12.7 5.6 %collective-permute-start.2 = (bf16[16,16,256]{2,1,0:T(8,128)(2,1)S(1)}, bf16[16,16,256]{2,1,0:T(8,128)(2,1)S(1)}, u32[]{:S(2)}, u32[]{:S(2)}) collective-permute-start(bf16[16,16,256]{2,1,0:T(8,128)(2,1)S(1)} %collective-permute-done.refs_1_), channel_id=1, source_target_pairs={{0,16},{8,24},{16,0},{24,8},{1,17},{9,25},{17,1},{25,9},{2,18},{10... | collective-permute-start | bytes 393224 | tf_op jit(solution)/shard_map/ppermute | solution.py:34
  18.3 26.0 %collective-permute-start.13 = (bf16[512,896]{1,0:T(8,128)(2,1)}, bf16[512,896]{1,0:T(8,128)(2,1)S(1)}, u32[]{:S(2)}, u32[]{:S(2)}) collective-permute-start(bf16[512,896]{1,0:T(8,128)(2,1)} %refs_10_), channel_id=1, source_target_pairs={{0,8},{8,0},{16,24},{24,16},{1,9},{9,1},{17,25},{25,17},{2,10},{10... | collective-permute-start | bytes 2752520 | tf_op jit(solution)/shard_map/ppermute | solution.py:34
  18.9 25.4 %collective-permute-start.14 = (bf16[512,896]{1,0:T(8,128)(2,1)}, bf16[512,896]{1,0:T(8,128)(2,1)S(1)}, u32[]{:S(2)}, u32[]{:S(2)}) collective-permute-start(bf16[512,896]{1,0:T(8,128)(2,1)} %refs_14_), channel_id=1, source_target_pairs={{0,16},{8,24},{16,0},{24,8},{1,17},{9,25},{17,1},{25,9},{2,18},{10... | collective-permute-start | bytes 2752520 | tf_op jit(solution)/shard_map/ppermute | solution.py:34
  23.1 8.2 %collective-permute-start.8 = (bf16[2,128,256]{2,1,0:T(8,128)(2,1)S(1)}, bf16[2,128,256]{2,1,0:T(8,128)(2,1)S(1)}, u32[]{:S(2)}, u32[]{:S(2)}) collective-permute-start(bf16[2,128,256]{2,1,0:T(8,128)(2,1)S(1)} %get-tuple-element.42.refs_6_), channel_id=1, source_target_pairs={{0,6},{1,7},{2,4},{3,5},{4,2},{5,3},{6,0},{7,1},{8,14},{9,15},{10,... | collective-permute-start | bytes 393224 | tf_op jit(solution)/shard_map/ppermute | solution.py:34
  26.8 6.0 %collective-permute-start.6 = (bf16[2,128,256]{2,1,0:T(8,128)(2,1)S(1)}, bf16[2,128,256]{2,1,0:T(8,128)(2,1)S(1)}, u32[]{:S(2)}, u32[]{:S(2)}) collective-permute-start(bf16[2,128,256]{2,1,0:T(8,128)(2,1)S(1)} %get-tuple-element.42.refs_6_), channel_id=1, source_target_pairs={{0,2},{1,3},{2,0},{3,1},{4,6},{5,7},{6,4},{7,5},{8,10},{9,11},{10,... | collective-permute-start | bytes 393224 | tf_op jit(solution)/shard_map/ppermute | solution.py:34
  26.8 8.8 %collective-permute-start.7 = (bf16[2,128,256]{2,1,0:T(8,128)(2,1)S(1)}, bf16[2,128,256]{2,1,0:T(8,128)(2,1)S(1)}, u32[]{:S(2)}, u32[]{:S(2)}) collective-permute-start(bf16[2,128,256]{2,1,0:T(8,128)(2,1)S(1)} %get-tuple-element.42.refs_6_), channel_id=1, source_target_pairs={{0,4},{1,5},{2,6},{3,7},{4,0},{5,1},{6,2},{7,3},{8,12},{9,13},{10,... | collective-permute-start | bytes 393224 | tf_op jit(solution)/shard_map/ppermute | solution.py:34
  36.1 22.9 %collective-permute-start.18 = (bf16[512,896]{1,0:T(8,128)(2,1)}, bf16[512,896]{1,0:T(8,128)(2,1)}, u32[]{:S(2)}, u32[]{:S(2)}) collective-permute-start(bf16[512,896]{1,0:T(8,128)(2,1)} %refs_10_), channel_id=1, source_target_pairs={{0,16},{8,24},{16,0},{24,8},{1,17},{9,25},{17,1},{25,9},{2,18},{10... | collective-permute-start | bytes 2752520 | tf_op jit(solution)/shard_map/ppermute | solution.py:34
  37.1 22.6 %collective-permute-start.19 = (bf16[512,896]{1,0:T(8,128)(2,1)}, bf16[512,896]{1,0:T(8,128)(2,1)}, u32[]{:S(2)}, u32[]{:S(2)}) collective-permute-start(bf16[512,896]{1,0:T(8,128)(2,1)} %refs_14_), channel_id=1, source_target_pairs={{0,8},{8,0},{16,24},{24,16},{1,9},{9,1},{17,25},{25,17},{2,10},{10... | collective-permute-start | bytes 2752520 | tf_op jit(solution)/shard_map/ppermute | solution.py:34
  47.1 15.4 %collective-permute-start.20 = (bf16[2,128,256]{2,1,0:T(8,128)(2,1)S(1)}, bf16[2,128,256]{2,1,0:T(8,128)(2,1)S(1)}, u32[]{:S(2)}, u32[]{:S(2)}) collective-permute-start(bf16[2,128,256]{2,1,0:T(8,128)(2,1)S(1)} %get-tuple-element.57), channel_id=1, source_target_pairs={{0,6},{1,7},{2,4},{3,5},{4,2},{5,3},{6,0},{7,1},{8,14},{9,15},{10,... | collective-permute-start | bytes 393224 | tf_op jit(solution)/shard_map/ppermute | solution.py:34
  49.8 10.7 %collective-permute-start.17 = (bf16[2,128,256]{2,1,0:T(8,128)(2,1)S(1)}, bf16[2,128,256]{2,1,0:T(8,128)(2,1)S(1)}, u32[]{:S(2)}, u32[]{:S(2)}) collective-permute-start(bf16[2,128,256]{2,1,0:T(8,128)(2,1)S(1)} %get-tuple-element.51), channel_id=1, source_target_pairs={{0,4},{1,5},{2,6},{3,7},{4,0},{5,1},{6,2},{7,3},{8,12},{9,13},{10,... | collective-permute-start | bytes 393224 | tf_op jit(solution)/shard_map/ppermute | solution.py:34
  49.8 12.7 %collective-permute-start.16 = (bf16[2,128,256]{2,1,0:T(8,128)(2,1)S(1)}, bf16[2,128,256]{2,1,0:T(8,128)(2,1)S(1)}, u32[]{:S(2)}, u32[]{:S(2)}) collective-permute-start(bf16[2,128,256]{2,1,0:T(8,128)(2,1)S(1)} %get-tuple-element.50), channel_id=1, source_target_pairs={{0,2},{1,3},{2,0},{3,1},{4,6},{5,7},{6,4},{7,5},{8,10},{9,11},{10,... | collective-permute-start | bytes 393224 | tf_op jit(solution)/shard_map/ppermute | solution.py:34
  60.4 22.2 %collective-permute-start.28 = (bf16[512,896]{1,0:T(8,128)(2,1)S(1)}, bf16[512,896]{1,0:T(8,128)(2,1)S(1)}, u32[]{:S(2)}, u32[]{:S(2)}) collective-permute-start(bf16[512,896]{1,0:T(8,128)(2,1)S(1)} %collective-permute-done.13.refs_11_), channel_id=1, source_target_pairs={{0,16},{8,24},{16,0},{24,8},{1,17},{9,25},{17,1},{25,9},{2,18},{10... | collective-permute-start | bytes 2752520 | tf_op jit(solution)/shard_map/ppermute | solution.py:34
  62.0 21.7 %collective-permute-start.29 = (bf16[512,896]{1,0:T(8,128)(2,1)S(1)}, bf16[512,896]{1,0:T(8,128)(2,1)}, u32[]{:S(2)}, u32[]{:S(2)}) collective-permute-start(bf16[512,896]{1,0:T(8,128)(2,1)S(1)} %collective-permute-done.14.refs_16_), channel_id=1, source_target_pairs={{0,8},{8,0},{16,24},{24,16},{1,9},{9,1},{17,25},{25,17},{2,10},{10... | collective-permute-start | bytes 2752520 | tf_op jit(solution)/shard_map/ppermute | solution.py:34
  62.6 6.2 %collective-permute-start.21 = (bf16[2,128,256]{2,1,0:T(8,128)(2,1)S(1)}, bf16[2,128,256]{2,1,0:T(8,128)(2,1)S(1)}, u32[]{:S(2)}, u32[]{:S(2)}) collective-permute-start(bf16[2,128,256]{2,1,0:T(8,128)(2,1)S(1)} %add_convert_fusion.refs_2_), channel_id=1, source_target_pairs={{0,2},{1,3},{2,0},{3,1},{4,6},{5,7},{6,4},{7,5},{8,10},{9,11},{10,... | collective-permute-start | bytes 393224 | tf_op jit(solution)/shard_map/ppermute | solution.py:34
  63.4 12.0 %collective-permute-start.22 = (bf16[2,128,256]{2,1,0:T(8,128)(2,1)S(1)}, bf16[2,128,256]{2,1,0:T(8,128)(2,1)S(1)}, u32[]{:S(2)}, u32[]{:S(2)}) collective-permute-start(bf16[2,128,256]{2,1,0:T(8,128)(2,1)S(1)} %add_convert_fusion.refs_2_), channel_id=1, source_target_pairs={{0,4},{1,5},{2,6},{3,7},{4,0},{5,1},{6,2},{7,3},{8,12},{9,13},{10,... | collective-permute-start | bytes 393224 | tf_op jit(solution)/shard_map/ppermute | solution.py:34
  66.0 9.3 %collective-permute-start.23 = (bf16[2,128,256]{2,1,0:T(8,128)(2,1)S(1)}, bf16[2,128,256]{2,1,0:T(8,128)(2,1)S(1)}, u32[]{:S(2)}, u32[]{:S(2)}) collective-permute-start(bf16[2,128,256]{2,1,0:T(8,128)(2,1)S(1)} %add_convert_fusion.refs_2_), channel_id=1, source_target_pairs={{0,6},{1,7},{2,4},{3,5},{4,2},{5,3},{6,0},{7,1},{8,14},{9,15},{10,... | collective-permute-start | bytes 393224 | tf_op jit(solution)/shard_map/ppermute | solution.py:34
  68.7 7.2 %collective-permute-start.24 = (bf16[2,128,256]{2,1,0:T(8,128)(2,1)S(1)}, bf16[2,128,256]{2,1,0:T(8,128)(2,1)S(1)}, u32[]{:S(2)}, u32[]{:S(2)}) collective-permute-start(bf16[2,128,256]{2,1,0:T(8,128)(2,1)S(1)} %add_convert_fusion.refs_2_), channel_id=1, source_target_pairs={{0,1},{1,0},{2,3},{3,2},{4,5},{5,4},{6,7},{7,6},{8,9},{9,8},{10,11... | collective-permute-start | bytes 393224 | tf_op jit(solution)/shard_map/ppermute | solution.py:34
  90.6 4.6 %collective-permute-start.31 = (f32[8,128]{1,0:T(8,128)S(1)}, f32[8,128]{1,0:T(8,128)S(1)}, u32[]{:S(2)}, u32[]{:S(2)}) collective-permute-start(f32[8,128]{1,0:T(8,128)S(1)} %shard_map.163.refs_0_), channel_id=1, source_target_pairs={{0,4},{1,5},{2,6},{3,7},{4,0},{5,1},{6,2},{7,3},{8,12},{9,13},{10,... | collective-permute-start | bytes 12296 | tf_op jit(solution)/shard_map/ppermute | solution.py:34
  90.7 5.5 %collective-permute-start.32 = (f32[8,128]{1,0:T(8,128)S(1)}, f32[8,128]{1,0:T(8,128)S(1)}, u32[]{:S(2)}, u32[]{:S(2)}) collective-permute-start(f32[8,128]{1,0:T(8,128)S(1)} %shard_map.163.refs_0_), channel_id=1, source_target_pairs={{0,6},{1,7},{2,4},{3,5},{4,2},{5,3},{6,0},{7,1},{8,14},{9,15},{10,... | collective-permute-start | bytes 12296 | tf_op jit(solution)/shard_map/ppermute | solution.py:34
  (14 other events, 35.9 us)

commit v6 on v5

--- a/solution.py
+++ b/solution.py
@@ -14,7 +14,7 @@
 
 
 def call(kernel, out_shape, ops, scratch=(), far=(), mib=4):
-    specs = [smem] + [anywhere if i in far else vmem for i in range(1, len(ops))]
+    specs = [anywhere if i in far else vmem if i else smem for i in range(len(ops))]
     ops = [
         pltpu.with_memory_space_constraint(op, pltpu.HBM) if i in far else op
         for i, op in enumerate(ops)
@@ -44,10 +44,12 @@
     return copies
 
 
-def pack_kernel(lengths, targets_far, hidden, out, targets, sems):
+def pack_kernel(lengths_far, targets_far, hidden, out, lengths, targets, sems):
     reqs = hidden.shape[0]
-    copies = fetch([targets_far, hidden], [targets, out.at[pl.ds(0, reqs)]], sems)
-    copies[0].wait()
+    copies = fetch(
+        [lengths_far, targets_far, hidden], [lengths, targets, out.at[pl.ds(0, reqs)]], sems
+    )
+    copies[1].wait()
     slots, part = targets.shape[1], hidden.shape[2]
     row = lax.broadcasted_iota(jnp.int32, (slots, part), 0)
     lane = lax.broadcasted_iota(jnp.int32, (slots, part), 1)
@@ -60,16 +62,17 @@
         block = block + jnp.dot(values, spot, preferred_element_type=jnp.float32)
     row = lax.broadcasted_iota(jnp.int32, (reqs, part), 0)
     lane = lax.broadcasted_iota(jnp.int32, (reqs, part), 1)
+    copies[0].wait()
     for r in range(reqs):
         here = jnp.logical_and(row == r, lane == 0)
         block = jnp.where(here, lengths[r].astype(jnp.float32), block)
     out[reqs] = block.astype(jnp.bfloat16)
-    copies[1].wait()
-
-
-def select_kernel(dp, ids, plan, *refs):
-    parts, (out, facts, own, sems) = list(refs[: 2 * dp]), refs[2 * dp :]
-    (copy,) = fetch([parts[0]], [own], sems)
+    copies[2].wait()
+
+
+def select_kernel(dp, ids, plan_far, *refs):
+    parts, (out, facts, own, plan, sems) = list(refs[: 2 * dp]), refs[2 * dp :]
+    plan_copy, copy = fetch([plan_far, parts[0]], [plan, own], sems)
     parts[0] = own
     rows = out.shape[1]
     reqs, slots, _ = own.shape
@@ -83,9 +86,13 @@
     slot = jnp.concatenate([row + (me ^ k) * reqs for k in range(dp)], axis=0)
     position = lax.rem(lax.broadcasted_iota(jnp.int32, (1, here), 1), slots)
     wanted = me * rows + lax.broadcasted_iota(jnp.int32, (rows, here), 0)
+    request = lax.div(lax.broadcasted_iota(jnp.int32, (1, here), 1), slots)
     hots = []
+    plan_copy.wait()
     for k in range(dp):
-        owner = plan[me ^ k]
+        owner = jnp.zeros((1, here), jnp.int32)
+        for r in range(reqs):
+            owner = jnp.where(request == r, plan[(me ^ k) * reqs + r], owner)
         start = jnp.sum(jnp.where(slot < owner, lengths, 0), axis=0, keepdims=True)
         live = jnp.sum(jnp.where(slot == owner, lengths, 0), axis=0, keepdims=True)
         code = jnp.where(position < live, start + position, -1)
@@ -160,31 +167,40 @@
         out[...] = (keep[k + 1] + came[k + 1].astype(jnp.float32)).astype(jnp.bfloat16)
 
 
-def score_kernel(half, ids, wanted, *refs):
+def score_kernel(half, dp, ids, *refs):
     parts = refs[2 : 2 + 2 * half]
-    *outs, stats, gains, normed, out_store, sems = refs[2 + 2 * half :]
-    dp = len(outs) // 2
+    *outs, partial, tail, gains, normed, out_store, sems = refs[2 + 2 * half :]
+    here = dp - 1
     copies = fetch(
-        [refs[0], refs[1], outs[0], outs[dp]],
+        [refs[0], refs[1], outs[0], outs[here]],
         [store.at[m] for store in (gains, out_store) for m in range(2)],
         sems,
     )
     me, chip, core = ids[0], ids[1], ids[2]
-    lane = lax.broadcasted_iota(jnp.int32, (parts[0].shape[1], 128), 1)
-    table = jnp.zeros(lane.shape, jnp.float32)
     ratio = 2 * half // dp
+    part = parts[0].shape[2]
     for m in range(2):
         values = [part[m] for part in parts]
         normalise(values, gains.at[m], chip, core, normed.at[m], copies[m])
+        for b in range(ratio):
+            tail[m, :, b * part : (b + 1) * part] = normed[m, (me ^ here) * ratio + b]
     for m in range(2):
         logits = None
-        for k in [*range(1, dp), 0]:
+        for k in [*range(1, here), 0]:
             if k == 0:
                 copies[2 + m].wait()
-                outs[m * dp] = out_store.at[m]
+                outs[m * here] = out_store.at[m]
             order = [(me ^ k) * ratio + b for b in range(ratio)]
-            piece = blocks_dot(normed.at[m], outs[m * dp + k], order)
+            piece = blocks_dot(normed.at[m], outs[m * here + k], order)
             logits = piece if logits is None else logits + piece
+        partial[m] = logits
+
+
+def finish_kernel(ids, wanted, partial, tail, last_policy, last_reference, stats):
+    lane = lax.broadcasted_iota(jnp.int32, (tail.shape[1], 128), 1)
+    table = jnp.zeros(lane.shape, jnp.float32)
+    for m, last in enumerate((last_policy, last_reference)):
+        logits = partial[m] + jnp.dot(tail[m], last[...], preferred_element_type=jnp.float32)
         entries = lax.broadcasted_iota(jnp.int32, logits.shape, 1) + ids[3] * logits.shape[1]
         picked = jnp.sum(jnp.where(entries == wanted[...], logits, 0.0), axis=1, keepdims=True)
         top = jnp.max(logits, axis=1, keepdims=True)
@@ -259,8 +275,12 @@
         pack_kernel,
         jax.ShapeDtypeStruct((reqs + 1, slots, part), jnp.bfloat16),
         (lengths, targets, hidden_reference),
-        [pltpu.VMEM(targets.shape, jnp.int32), pltpu.SemaphoreType.DMA((2,))],
-        far=(1, 2),
+        [
+            pltpu.SMEM(lengths.shape, jnp.int32),
+            pltpu.VMEM(targets.shape, jnp.int32),
+            pltpu.SemaphoreType.DMA((3,)),
+        ],
+        far=(0, 1, 2),
     )
     hiddens = [{0: hidden_policy}, {0: packed}]
     outs = [{0: out_policy}, {0: out_reference}]
@@ -279,16 +299,19 @@
     hidden_parts = [hiddens[m][k] for m in range(2) for k in range(dp)]
 
     order = jnp.arange(dp, dtype=jnp.int32)
-    plan = jnp.repeat(move_plan, slots).reshape(dp, 1, here)
     moved, facts = call(
         functools.partial(select_kernel, dp),
         (
             jax.ShapeDtypeStruct((2, rows, part), jnp.bfloat16),
             jax.ShapeDtypeStruct((dp, reqs, part), jnp.float32),
         ),
-        (ids, plan, *hidden_parts),
-        [pltpu.VMEM(hidden_policy.shape, jnp.bfloat16), pltpu.SemaphoreType.DMA((1,))],
-        far=(2,),
+        (ids, move_plan, *hidden_parts),
+        [
+            pltpu.VMEM(hidden_policy.shape, jnp.bfloat16),
+            pltpu.SMEM(move_plan.shape, jnp.int32),
+            pltpu.SemaphoreType.DMA((2,)),
+        ],
+        far=(1, 2),
     )
 
     facts = facts[:, :, : 2 * slots + 1].astype(jnp.int32)
@@ -365,15 +388,17 @@
         axis=1,
         keepdims=True,
     )
-    stats = call(
-        functools.partial(score_kernel, half),
-        jax.ShapeDtypeStruct((8, rows), jnp.float32),
+    partial, tail = call(
+        functools.partial(score_kernel, half, dp),
+        (
+            jax.ShapeDtypeStruct((2, rows, out_policy.shape[1]), jnp.float32),
+            jax.ShapeDtypeStruct((2, rows, out_policy.shape[0]), jnp.bfloat16),
+        ),
         (
             ids,
-            wanted,
             *gains[2:],
             *gather_pair(stream),
-            *[outs[m][k] for m in range(2) for k in range(dp)],
+            *[outs[m][k] for m in range(2) for k in range(dp - 1)],
         ),
         [
             gain_scratch,
@@ -381,8 +406,14 @@
             pltpu.VMEM((2,) + out_policy.shape, jnp.bfloat16),
             pltpu.SemaphoreType.DMA((4,)),
         ],
-        far=(2, 3, 4 + mp, 4 + mp + dp),
+        far=(1, 2, 3 + mp, 2 + mp + dp),
         mib=14,
+    )
+    stats = call(
+        finish_kernel,
+        jax.ShapeDtypeStruct((8, rows), jnp.float32),
+        (ids, wanted, partial, tail, outs[0][dp - 1], outs[1][dp - 1]),
+        mib=8,
     )
     stats = call(
         merge_kernel,

time: 104 us -> 99.3 us (0.955)
  waiting for transfers between devices: 46.2 us -> 42.3 us
  local copies, waits for them, and re-layouts: 2.12 us -> 0.58 us
    ppermute x37, waiting for transfers between devices: 46.2 us -> 42.3 us  [exchange(): return lax.ppermute(values, axis, [(i, i ^ flip) for i in range(count)])]
    pallas_call x7 -> x8, Pallas kernels: 15.9 us -> 15.3 us  [call(): pl.pallas_call(kernel, out_shape=out_shape, in_specs=specs, out_specs=jax...]
  transfers between devices with their start and end apart: 37 -> 37, of which waited for: 24 -> 20; matrix products, arithmetic and copies ran while one was open for 2% -> 2% of each run, Pallas kernels for 8% -> 12%
where the time goes in v6:
time: 99.3 us; the launch traced here: 99 us
  waiting for transfers between devices  42.3 us (43%)
  starting transfers between devices  38 us (38%)
  Pallas kernels  15.3 us (15%)
  other arithmetic  2.04 us (2%)
    ppermute x37, waiting for transfers between devices, exchange(): return lax.ppermute(values, axis, [(i, i ^ flip) for i in range(count)])  42.3 us
    ppermute x37, starting transfers between devices, exchange(): return lax.ppermute(values, axis, [(i, i ^ flip) for i in range(count)])  38 us
    pallas_call x8, Pallas kernels, call(): pl.pallas_call(kernel, out_shape=out_shape, in_specs=specs, out_specs=jax...  15.3 us
  transfers between devices with their start and end apart: 37, of which 20 were waited for; matrix products, arithmetic and copies ran while one was open for 2% of the time, Pallas kernels for 12%

profile of v6, /device:TPU:0, one launch (start us, length us, event | category | flops | bytes accessed | tf_op | source)
XLA Modules:
  0.0 99.0 jit_solution(5769467434471726630)
XLA Ops:
  1.6 3.0 %collective-permute-start.4 = (bf16[17,16,256]{2,1,0:T(8,128)(2,1)S(1)}, bf16[17,16,256]{2,1,0:T(8,128)(2,1)S(1)}, u32[]{:S(2)}, u32[]{:S(2)}) collective-permute-start(bf16[17,16,256]{2,1,0:T(8,128)(2,1)S(1)} %shard_map.158.refs_4_), channel_id=1, source_target_pairs={{0,16},{8,24},{16,0},{24,8},{1,17},{9,25},{17,1},{25,9},{2,18},{10... | collective-permute-start | bytes 417800 | tf_op jit(solution)/shard_map/ppermute | solution.py:34
  6.6 1.6 %collective-permute-done.4.refs_6_ = bf16[17,16,256]{2,1,0:T(8,128)(2,1)S(1)} collective-permute-done((bf16[17,16,256]{2,1,0:T(8,128)(2,1)S(1)}, bf16[17,16,256]{2,1,0:T(8,128)(2,1)S(1)}, u32[]{:S(2)}, u32[]{:S(2)}) %collective-permute-start.4) | collective-permute-done | bytes 139296 | tf_op jit(solution)/shard_map/ppermute | solution.py:34
  8.3 1.7 %collective-permute-start.5 = (bf16[17,16,256]{2,1,0:T(8,128)(2,1)S(1)}, bf16[17,16,256]{2,1,0:T(8,128)(2,1)S(1)}, u32[]{:S(2)}, u32[]{:S(2)}) collective-permute-start(bf16[17,16,256]{2,1,0:T(8,128)(2,1)S(1)} %collective-permute-done.4.refs_6_), channel_id=1, source_target_pairs={{0,8},{8,0},{16,24},{24,16},{1,9},{9,1},{17,25},{25,17},{2,10},{10... | collective-permute-start | bytes 417800 | tf_op jit(solution)/shard_map/ppermute | solution.py:34
  10.0 1.5 %collective-permute-start.1 = (bf16[16,16,256]{2,1,0:T(8,128)(2,1)}, bf16[16,16,256]{2,1,0:T(8,128)(2,1)S(1)}, u32[]{:S(2)}, u32[]{:S(2)}) collective-permute-start(bf16[16,16,256]{2,1,0:T(8,128)(2,1)} %refs_0_), channel_id=1, source_target_pairs={{0,16},{8,24},{16,0},{24,8},{1,17},{9,25},{17,1},{25,9},{2,18},{10... | collective-permute-start | bytes 393224 | tf_op jit(solution)/shard_map/ppermute | solution.py:34
  12.0 3.7 %collective-permute-done.1.refs_2_ = bf16[16,16,256]{2,1,0:T(8,128)(2,1)S(1)} collective-permute-done((bf16[16,16,256]{2,1,0:T(8,128)(2,1)}, bf16[16,16,256]{2,1,0:T(8,128)(2,1)S(1)}, u32[]{:S(2)}, u32[]{:S(2)}) %collective-permute-start.1) | collective-permute-done | bytes 131104 | tf_op jit(solution)/shard_map/ppermute | solution.py:34
  19.2 1.8 %shard_map.159 = (bf16[2,128,256]{2,1,0:T(8,128)(2,1)S(1)}, f32[4,16,256]{2,1,0:T(8,128)S(1)}) custom-call(s32[4]{0:T(128)S(1)} %pad_add_fusion.ids, s32[64]{0:T(128)} %plan_far.1, bf16[16,16,256]{2,1,0:T(8,128)(2,1)} %refs_0_, bf16[16,16,256]{2,1,0:T(8,128)(2,1)S(1)} %collective-permute-done.refs_1_, ...), custom_call_target="tpu_custom_call" | custom-call | tf_op jit(solution)/shard_map/pallas_call | solution.py:22
  21.0 3.7 %collective-permute-start.8 = (bf16[2,128,256]{2,1,0:T(8,128)(2,1)S(1)}, bf16[2,128,256]{2,1,0:T(8,128)(2,1)S(1)}, u32[]{:S(2)}, u32[]{:S(2)}) collective-permute-start(bf16[2,128,256]{2,1,0:T(8,128)(2,1)S(1)} %get-tuple-element.44.refs_6_), channel_id=1, source_target_pairs={{0,6},{1,7},{2,4},{3,5},{4,2},{5,3},{6,0},{7,1},{8,14},{9,15},{10,... | collective-permute-start | bytes 393224 | tf_op jit(solution)/shard_map/ppermute | solution.py:34
  25.5 3.7 %collective-permute-done.8.refs_9_ = bf16[2,128,256]{2,1,0:T(8,128)(2,1)S(1)} collective-permute-done((bf16[2,128,256]{2,1,0:T(8,128)(2,1)S(1)}, bf16[2,128,256]{2,1,0:T(8,128)(2,1)S(1)}, u32[]{:S(2)}, u32[]{:S(2)}) %collective-permute-start.8) | collective-permute-done | bytes 131104 | tf_op jit(solution)/shard_map/ppermute | solution.py:34
  29.2 1.5 %collective-permute-done.6.refs_7_ = bf16[2,128,256]{2,1,0:T(8,128)(2,1)S(1)} collective-permute-done((bf16[2,128,256]{2,1,0:T(8,128)(2,1)S(1)}, bf16[2,128,256]{2,1,0:T(8,128)(2,1)S(1)}, u32[]{:S(2)}, u32[]{:S(2)}) %collective-permute-start.6) | collective-permute-done | bytes 131104 | tf_op jit(solution)/shard_map/ppermute | solution.py:34
  30.7 2.8 %collective-permute-done.7.refs_8_ = bf16[2,128,256]{2,1,0:T(8,128)(2,1)S(1)} collective-permute-done((bf16[2,128,256]{2,1,0:T(8,128)(2,1)S(1)}, bf16[2,128,256]{2,1,0:T(8,128)(2,1)S(1)}, u32[]{:S(2)}, u32[]{:S(2)}) %collective-permute-start.7) | collective-permute-done | bytes 131104 | tf_op jit(solution)/shard_map/ppermute | solution.py:34
  36.4 5.0 %shard_map.160 = (f32[4,2,128,256]{3,2,1,0:T(8,128)S(1)}, bf16[4,2,128,256]{3,2,1,0:T(8,128)(2,1)S(1)}) custom-call(s32[4]{0:T(128)S(1)} %pad_add_fusion.ids, f32[8,1,256]{2,1,0:T(1,128)} %bitcast.13, f32[8,1,256]{2,1,0:T(1,128)} %bitcast.14, bf16[2048,512]{1,0:T(8,128)(2,1)} %refs_2_.1, bf16[2048,512]{1,0:T(8,128)(2,1)} %refs_3_.1, ...), custom_call_target="tpu_custom_call" | custom-call | tf_op jit(solution)/shard_map/pallas_call | solution.py:22
  41.7 1.7 %collective-permute-done.15.came = bf16[4,2,128,256]{3,2,1,0:T(8,128)(2,1)S(1)} collective-permute-done((bf16[4,2,128,256]{3,2,1,0:T(8,128)(2,1)S(1)}, bf16[4,2,128,256]{3,2,1,0:T(8,128)(2,1)S(1)}, u32[]{:S(2)}, u32[]{:S(2)}) %collective-permute-start.15) | collective-permute-done | bytes 524320 | tf_op jit(solution)/shard_map/ppermute | solution.py:34
  44.0 2.5 %collective-permute-start.17 = (bf16[2,128,256]{2,1,0:T(8,128)(2,1)S(1)}, bf16[2,128,256]{2,1,0:T(8,128)(2,1)S(1)}, u32[]{:S(2)}, u32[]{:S(2)}) collective-permute-start(bf16[2,128,256]{2,1,0:T(8,128)(2,1)S(1)} %get-tuple-element.53), channel_id=1, source_target_pairs={{0,4},{1,5},{2,6},{3,7},{4,0},{5,1},{6,2},{7,3},{8,12},{9,13},{10,... | collective-permute-start | bytes 393224 | tf_op jit(solution)/shard_map/ppermute | solution.py:34
  48.5 9.3 %collective-permute-done.18.refs_12_ = bf16[512,896]{1,0:T(8,128)(2,1)} collective-permute-done((bf16[512,896]{1,0:T(8,128)(2,1)}, bf16[512,896]{1,0:T(8,128)(2,1)}, u32[]{:S(2)}, u32[]{:S(2)}) %collective-permute-start.18) | collective-permute-done | bytes 917536 | tf_op jit(solution)/shard_map/ppermute | solution.py:34
  58.9 1.5 %collective-permute-start.29 = (bf16[512,896]{1,0:T(8,128)(2,1)}, bf16[512,896]{1,0:T(8,128)(2,1)S(1)}, u32[]{:S(2)}, u32[]{:S(2)}) collective-permute-start(bf16[512,896]{1,0:T(8,128)(2,1)} %collective-permute-done.14.refs_15_), channel_id=1, source_target_pairs={{0,8},{8,0},{16,24},{24,16},{1,9},{9,1},{17,25},{25,17},{2,10},{10... | collective-permute-start | bytes 2752520 | tf_op jit(solution)/shard_map/ppermute | solution.py:34
  60.5 1.6 %collective-permute-start.21 = (bf16[2,128,256]{2,1,0:T(8,128)(2,1)S(1)}, bf16[2,128,256]{2,1,0:T(8,128)(2,1)S(1)}, u32[]{:S(2)}, u32[]{:S(2)}) collective-permute-start(bf16[2,128,256]{2,1,0:T(8,128)(2,1)S(1)} %add_convert_fusion.refs_2_), channel_id=1, source_target_pairs={{0,2},{1,3},{2,0},{3,1},{4,6},{5,7},{6,4},{7,5},{8,10},{9,11},{10,... | collective-permute-start | bytes 393224 | tf_op jit(solution)/shard_map/ppermute | solution.py:34
  62.2 2.7 %collective-permute-start.22 = (bf16[2,128,256]{2,1,0:T(8,128)(2,1)S(1)}, bf16[2,128,256]{2,1,0:T(8,128)(2,1)S(1)}, u32[]{:S(2)}, u32[]{:S(2)}) collective-permute-start(bf16[2,128,256]{2,1,0:T(8,128)(2,1)S(1)} %add_convert_fusion.refs_2_), channel_id=1, source_target_pairs={{0,4},{1,5},{2,6},{3,7},{4,0},{5,1},{6,2},{7,3},{8,12},{9,13},{10,... | collective-permute-start | bytes 393224 | tf_op jit(solution)/shard_map/ppermute | solution.py:34
  65.1 1.5 %collective-permute-done.21.refs_3_ = bf16[2,128,256]{2,1,0:T(8,128)(2,1)S(1)} collective-permute-done((bf16[2,128,256]{2,1,0:T(8,128)(2,1)S(1)}, bf16[2,128,256]{2,1,0:T(8,128)(2,1)S(1)}, u32[]{:S(2)}, u32[]{:S(2)}) %collective-permute-start.21) | collective-permute-done | bytes 131104 | tf_op jit(solution)/shard_map/ppermute | solution.py:34
  67.0 6.1 %collective-permute-done.22.refs_4_ = bf16[2,128,256]{2,1,0:T(8,128)(2,1)S(1)} collective-permute-done((bf16[2,128,256]{2,1,0:T(8,128)(2,1)S(1)}, bf16[2,128,256]{2,1,0:T(8,128)(2,1)S(1)}, u32[]{:S(2)}, u32[]{:S(2)}) %collective-permute-start.22) | collective-permute-done | bytes 131104 | tf_op jit(solution)/shard_map/ppermute | solution.py:34
  75.1 4.6 %shard_map.162 = (f32[2,128,896]{2,1,0:T(8,128)S(1)}, bf16[2,128,512]{2,1,0:T(8,128)(2,1)S(1)}) custom-call(s32[4]{0:T(128)S(1)} %pad_add_fusion.ids, f32[8,1,256]{2,1,0:T(1,128)} %bitcast.15, f32[8,1,256]{2,1,0:T(1,128)} %bitcast.16, bf16[2,128,256]{2,1,0:T(8,128)(2,1)S(1)} %add_convert_fusion.refs_2_, ...), custom_call_target="tpu_custom_call" | custom-call | tf_op jit(solution)/shard_map/pallas_call | solution.py:22
  83.1 1.8 %collective-permute-start.31 = (f32[8,128]{1,0:T(8,128)S(1)}, f32[8,128]{1,0:T(8,128)S(1)}, u32[]{:S(2)}, u32[]{:S(2)}) collective-permute-start(f32[8,128]{1,0:T(8,128)S(1)} %shard_map.164.refs_0_), channel_id=1, source_target_pairs={{0,4},{1,5},{2,6},{3,7},{4,0},{5,1},{6,2},{7,3},{8,12},{9,13},{10,... | collective-permute-start | bytes 12296 | tf_op jit(solution)/shard_map/ppermute | solution.py:34
  84.9 1.9 %collective-permute-start.32 = (f32[8,128]{1,0:T(8,128)S(1)}, f32[8,128]{1,0:T(8,128)S(1)}, u32[]{:S(2)}, u32[]{:S(2)}) collective-permute-start(f32[8,128]{1,0:T(8,128)S(1)} %shard_map.164.refs_0_), channel_id=1, source_target_pairs={{0,6},{1,7},{2,4},{3,5},{4,2},{5,3},{6,0},{7,1},{8,14},{9,15},{10,... | collective-permute-start | bytes 12296 | tf_op jit(solution)/shard_map/ppermute | solution.py:34
  87.7 2.6 %collective-permute-done.32.refs_2_ = f32[8,128]{1,0:T(8,128)S(1)} collective-permute-done((f32[8,128]{1,0:T(8,128)S(1)}, f32[8,128]{1,0:T(8,128)S(1)}, u32[]{:S(2)}, u32[]{:S(2)}) %collective-permute-start.32) | collective-permute-done | bytes 4128 | tf_op jit(solution)/shard_map/ppermute | solution.py:34
  95.9 2.1 %collective-permute-done.36 = f32[1,128]{1,0:T(1,128)S(1)} collective-permute-done((f32[1,128]{1,0:T(1,128)S(1)}, f32[1,128]{1,0:T(1,128)S(1)}, u32[]{:S(2)}, u32[]{:S(2)}) %collective-permute-start.36) | collective-permute-done | bytes 544 | tf_op jit(solution)/shard_map/ppermute | solution.py:34
  (81 shorter events, 28.3 us)
Async XLA Ops:
  1.6 6.7 %collective-permute-start.4 = (bf16[17,16,256]{2,1,0:T(8,128)(2,1)S(1)}, bf16[17,16,256]{2,1,0:T(8,128)(2,1)S(1)}, u32[]{:S(2)}, u32[]{:S(2)}) collective-permute-start(bf16[17,16,256]{2,1,0:T(8,128)(2,1)S(1)} %shard_map.158.refs_4_), channel_id=1, source_target_pairs={{0,16},{8,24},{16,0},{24,8},{1,17},{9,25},{17,1},{25,9},{2,18},{10... | collective-permute-start | bytes 417800 | tf_op jit(solution)/shard_map/ppermute | solution.py:34
  4.6 6.9 %collective-permute-start = (bf16[16,16,256]{2,1,0:T(8,128)(2,1)}, bf16[16,16,256]{2,1,0:T(8,128)(2,1)S(1)}, u32[]{:S(2)}, u32[]{:S(2)}) collective-permute-start(bf16[16,16,256]{2,1,0:T(8,128)(2,1)} %refs_0_), channel_id=1, source_target_pairs={{0,8},{8,0},{16,24},{24,16},{1,9},{9,1},{17,25},{25,17},{2,10},{10... | collective-permute-start | bytes 393224 | tf_op jit(solution)/shard_map/ppermute | solution.py:34
  6.1 9.6 %collective-permute-start.3 = (bf16[17,16,256]{2,1,0:T(8,128)(2,1)S(1)}, bf16[17,16,256]{2,1,0:T(8,128)(2,1)S(1)}, u32[]{:S(2)}, u32[]{:S(2)}) collective-permute-start(bf16[17,16,256]{2,1,0:T(8,128)(2,1)S(1)} %shard_map.158.refs_4_), channel_id=1, source_target_pairs={{0,8},{8,0},{16,24},{24,16},{1,9},{9,1},{17,25},{25,17},{2,10},{10... | collective-permute-start | bytes 417800 | tf_op jit(solution)/shard_map/ppermute | solution.py:34
  8.3 8.8 %collective-permute-start.5 = (bf16[17,16,256]{2,1,0:T(8,128)(2,1)S(1)}, bf16[17,16,256]{2,1,0:T(8,128)(2,1)S(1)}, u32[]{:S(2)}, u32[]{:S(2)}) collective-permute-start(bf16[17,16,256]{2,1,0:T(8,128)(2,1)S(1)} %collective-permute-done.4.refs_6_), channel_id=1, source_target_pairs={{0,8},{8,0},{16,24},{24,16},{1,9},{9,1},{17,25},{25,17},{2,10},{10... | collective-permute-start | bytes 417800 | tf_op jit(solution)/shard_map/ppermute | solution.py:34
  10.0 5.7 %collective-permute-start.1 = (bf16[16,16,256]{2,1,0:T(8,128)(2,1)}, bf16[16,16,256]{2,1,0:T(8,128)(2,1)S(1)}, u32[]{:S(2)}, u32[]{:S(2)}) collective-permute-start(bf16[16,16,256]{2,1,0:T(8,128)(2,1)} %refs_0_), channel_id=1, source_target_pairs={{0,16},{8,24},{16,0},{24,8},{1,17},{9,25},{17,1},{25,9},{2,18},{10... | collective-permute-start | bytes 393224 | tf_op jit(solution)/shard_map/ppermute | solution.py:34
  11.5 5.6 %collective-permute-start.2 = (bf16[16,16,256]{2,1,0:T(8,128)(2,1)S(1)}, bf16[16,16,256]{2,1,0:T(8,128)(2,1)S(1)}, u32[]{:S(2)}, u32[]{:S(2)}) collective-permute-start(bf16[16,16,256]{2,1,0:T(8,128)(2,1)S(1)} %collective-permute-done.refs_1_), channel_id=1, source_target_pairs={{0,16},{8,24},{16,0},{24,8},{1,17},{9,25},{17,1},{25,9},{2,18},{10... | collective-permute-start | bytes 393224 | tf_op jit(solution)/shard_map/ppermute | solution.py:34
  17.1 24.3 %collective-permute-start.13 = (bf16[512,896]{1,0:T(8,128)(2,1)}, bf16[512,896]{1,0:T(8,128)(2,1)S(1)}, u32[]{:S(2)}, u32[]{:S(2)}) collective-permute-start(bf16[512,896]{1,0:T(8,128)(2,1)} %refs_10_), channel_id=1, source_target_pairs={{0,8},{8,0},{16,24},{24,16},{1,9},{9,1},{17,25},{25,17},{2,10},{10... | collective-permute-start | bytes 2752520 | tf_op jit(solution)/shard_map/ppermute | solution.py:34
  17.7 23.7 %collective-permute-start.14 = (bf16[512,896]{1,0:T(8,128)(2,1)}, bf16[512,896]{1,0:T(8,128)(2,1)}, u32[]{:S(2)}, u32[]{:S(2)}) collective-permute-start(bf16[512,896]{1,0:T(8,128)(2,1)} %refs_13_), channel_id=1, source_target_pairs={{0,16},{8,24},{16,0},{24,8},{1,17},{9,25},{17,1},{25,9},{2,18},{10... | collective-permute-start | bytes 2752520 | tf_op jit(solution)/shard_map/ppermute | solution.py:34
  21.0 8.2 %collective-permute-start.8 = (bf16[2,128,256]{2,1,0:T(8,128)(2,1)S(1)}, bf16[2,128,256]{2,1,0:T(8,128)(2,1)S(1)}, u32[]{:S(2)}, u32[]{:S(2)}) collective-permute-start(bf16[2,128,256]{2,1,0:T(8,128)(2,1)S(1)} %get-tuple-element.44.refs_6_), channel_id=1, source_target_pairs={{0,6},{1,7},{2,4},{3,5},{4,2},{5,3},{6,0},{7,1},{8,14},{9,15},{10,... | collective-permute-start | bytes 393224 | tf_op jit(solution)/shard_map/ppermute | solution.py:34
  24.7 6.0 %collective-permute-start.6 = (bf16[2,128,256]{2,1,0:T(8,128)(2,1)S(1)}, bf16[2,128,256]{2,1,0:T(8,128)(2,1)S(1)}, u32[]{:S(2)}, u32[]{:S(2)}) collective-permute-start(bf16[2,128,256]{2,1,0:T(8,128)(2,1)S(1)} %get-tuple-element.44.refs_6_), channel_id=1, source_target_pairs={{0,2},{1,3},{2,0},{3,1},{4,6},{5,7},{6,4},{7,5},{8,10},{9,11},{10,... | collective-permute-start | bytes 393224 | tf_op jit(solution)/shard_map/ppermute | solution.py:34
  24.7 8.8 %collective-permute-start.7 = (bf16[2,128,256]{2,1,0:T(8,128)(2,1)S(1)}, bf16[2,128,256]{2,1,0:T(8,128)(2,1)S(1)}, u32[]{:S(2)}, u32[]{:S(2)}) collective-permute-start(bf16[2,128,256]{2,1,0:T(8,128)(2,1)S(1)} %get-tuple-element.44.refs_6_), channel_id=1, source_target_pairs={{0,4},{1,5},{2,6},{3,7},{4,0},{5,1},{6,2},{7,3},{8,12},{9,13},{10,... | collective-permute-start | bytes 393224 | tf_op jit(solution)/shard_map/ppermute | solution.py:34
  34.1 23.8 %collective-permute-start.18 = (bf16[512,896]{1,0:T(8,128)(2,1)}, bf16[512,896]{1,0:T(8,128)(2,1)}, u32[]{:S(2)}, u32[]{:S(2)}) collective-permute-start(bf16[512,896]{1,0:T(8,128)(2,1)} %refs_10_), channel_id=1, source_target_pairs={{0,16},{8,24},{16,0},{24,8},{1,17},{9,25},{17,1},{25,9},{2,18},{10... | collective-permute-start | bytes 2752520 | tf_op jit(solution)/shard_map/ppermute | solution.py:34
  35.1 22.8 %collective-permute-start.19 = (bf16[512,896]{1,0:T(8,128)(2,1)}, bf16[512,896]{1,0:T(8,128)(2,1)}, u32[]{:S(2)}, u32[]{:S(2)}) collective-permute-start(bf16[512,896]{1,0:T(8,128)(2,1)} %refs_13_), channel_id=1, source_target_pairs={{0,8},{8,0},{16,24},{24,16},{1,9},{9,1},{17,25},{25,17},{2,10},{10... | collective-permute-start | bytes 2752520 | tf_op jit(solution)/shard_map/ppermute | solution.py:34
  44.0 13.8 %collective-permute-start.17 = (bf16[2,128,256]{2,1,0:T(8,128)(2,1)S(1)}, bf16[2,128,256]{2,1,0:T(8,128)(2,1)S(1)}, u32[]{:S(2)}, u32[]{:S(2)}) collective-permute-start(bf16[2,128,256]{2,1,0:T(8,128)(2,1)S(1)} %get-tuple-element.53), channel_id=1, source_target_pairs={{0,4},{1,5},{2,6},{3,7},{4,0},{5,1},{6,2},{7,3},{8,12},{9,13},{10,... | collective-permute-start | bytes 393224 | tf_op jit(solution)/shard_map/ppermute | solution.py:34
  46.5 13.9 %collective-permute-start.16 = (bf16[2,128,256]{2,1,0:T(8,128)(2,1)S(1)}, bf16[2,128,256]{2,1,0:T(8,128)(2,1)S(1)}, u32[]{:S(2)}, u32[]{:S(2)}) collective-permute-start(bf16[2,128,256]{2,1,0:T(8,128)(2,1)S(1)} %get-tuple-element.52), channel_id=1, source_target_pairs={{0,2},{1,3},{2,0},{3,1},{4,6},{5,7},{6,4},{7,5},{8,10},{9,11},{10,... | collective-permute-start | bytes 393224 | tf_op jit(solution)/shard_map/ppermute | solution.py:34
  47.2 13.1 %collective-permute-start.20 = (bf16[2,128,256]{2,1,0:T(8,128)(2,1)S(1)}, bf16[2,128,256]{2,1,0:T(8,128)(2,1)S(1)}, u32[]{:S(2)}, u32[]{:S(2)}) collective-permute-start(bf16[2,128,256]{2,1,0:T(8,128)(2,1)S(1)} %get-tuple-element.59), channel_id=1, source_target_pairs={{0,6},{1,7},{2,4},{3,5},{4,2},{5,3},{6,0},{7,1},{8,14},{9,15},{10,... | collective-permute-start | bytes 393224 | tf_op jit(solution)/shard_map/ppermute | solution.py:34
  57.9 21.8 %collective-permute-start.28 = (bf16[512,896]{1,0:T(8,128)(2,1)S(1)}, bf16[512,896]{1,0:T(8,128)(2,1)S(1)}, u32[]{:S(2)}, u32[]{:S(2)}) collective-permute-start(bf16[512,896]{1,0:T(8,128)(2,1)S(1)} %collective-permute-done.13.refs_11_), channel_id=1, source_target_pairs={{0,16},{8,24},{16,0},{24,8},{1,17},{9,25},{17,1},{25,9},{2,18},{10... | collective-permute-start | bytes 2752520 | tf_op jit(solution)/shard_map/ppermute | solution.py:34
  58.9 21.2 %collective-permute-start.29 = (bf16[512,896]{1,0:T(8,128)(2,1)}, bf16[512,896]{1,0:T(8,128)(2,1)S(1)}, u32[]{:S(2)}, u32[]{:S(2)}) collective-permute-start(bf16[512,896]{1,0:T(8,128)(2,1)} %collective-permute-done.14.refs_15_), channel_id=1, source_target_pairs={{0,8},{8,0},{16,24},{24,16},{1,9},{9,1},{17,25},{25,17},{2,10},{10... | collective-permute-start | bytes 2752520 | tf_op jit(solution)/shard_map/ppermute | solution.py:34
  60.5 6.1 %collective-permute-start.21 = (bf16[2,128,256]{2,1,0:T(8,128)(2,1)S(1)}, bf16[2,128,256]{2,1,0:T(8,128)(2,1)S(1)}, u32[]{:S(2)}, u32[]{:S(2)}) collective-permute-start(bf16[2,128,256]{2,1,0:T(8,128)(2,1)S(1)} %add_convert_fusion.refs_2_), channel_id=1, source_target_pairs={{0,2},{1,3},{2,0},{3,1},{4,6},{5,7},{6,4},{7,5},{8,10},{9,11},{10,... | collective-permute-start | bytes 393224 | tf_op jit(solution)/shard_map/ppermute | solution.py:34
  62.2 10.9 %collective-permute-start.22 = (bf16[2,128,256]{2,1,0:T(8,128)(2,1)S(1)}, bf16[2,128,256]{2,1,0:T(8,128)(2,1)S(1)}, u32[]{:S(2)}, u32[]{:S(2)}) collective-permute-start(bf16[2,128,256]{2,1,0:T(8,128)(2,1)S(1)} %add_convert_fusion.refs_2_), channel_id=1, source_target_pairs={{0,4},{1,5},{2,6},{3,7},{4,0},{5,1},{6,2},{7,3},{8,12},{9,13},{10,... | collective-permute-start | bytes 393224 | tf_op jit(solution)/shard_map/ppermute | solution.py:34
  64.8 8.2 %collective-permute-start.23 = (bf16[2,128,256]{2,1,0:T(8,128)(2,1)S(1)}, bf16[2,128,256]{2,1,0:T(8,128)(2,1)S(1)}, u32[]{:S(2)}, u32[]{:S(2)}) collective-permute-start(bf16[2,128,256]{2,1,0:T(8,128)(2,1)S(1)} %add_convert_fusion.refs_2_), channel_id=1, source_target_pairs={{0,6},{1,7},{2,4},{3,5},{4,2},{5,3},{6,0},{7,1},{8,14},{9,15},{10,... | collective-permute-start | bytes 393224 | tf_op jit(solution)/shard_map/ppermute | solution.py:34
  66.6 7.0 %collective-permute-start.24 = (bf16[2,128,256]{2,1,0:T(8,128)(2,1)S(1)}, bf16[2,128,256]{2,1,0:T(8,128)(2,1)S(1)}, u32[]{:S(2)}, u32[]{:S(2)}) collective-permute-start(bf16[2,128,256]{2,1,0:T(8,128)(2,1)S(1)} %add_convert_fusion.refs_2_), channel_id=1, source_target_pairs={{0,1},{1,0},{2,3},{3,2},{4,5},{5,4},{6,7},{7,6},{8,9},{9,8},{10,11... | collective-permute-start | bytes 393224 | tf_op jit(solution)/shard_map/ppermute | solution.py:34
  83.1 4.6 %collective-permute-start.31 = (f32[8,128]{1,0:T(8,128)S(1)}, f32[8,128]{1,0:T(8,128)S(1)}, u32[]{:S(2)}, u32[]{:S(2)}) collective-permute-start(f32[8,128]{1,0:T(8,128)S(1)} %shard_map.164.refs_0_), channel_id=1, source_target_pairs={{0,4},{1,5},{2,6},{3,7},{4,0},{5,1},{6,2},{7,3},{8,12},{9,13},{10,... | collective-permute-start | bytes 12296 | tf_op jit(solution)/shard_map/ppermute | solution.py:34
  84.9 5.4 %collective-permute-start.32 = (f32[8,128]{1,0:T(8,128)S(1)}, f32[8,128]{1,0:T(8,128)S(1)}, u32[]{:S(2)}, u32[]{:S(2)}) collective-permute-start(f32[8,128]{1,0:T(8,128)S(1)} %shard_map.164.refs_0_), channel_id=1, source_target_pairs={{0,6},{1,7},{2,4},{3,5},{4,2},{5,3},{6,0},{7,1},{8,14},{9,15},{10,... | collective-permute-start | bytes 12296 | tf_op jit(solution)/shard_map/ppermute | solution.py:34
  (13 other events, 35.0 us)

commit v7 on v6

--- a/solution.py
+++ b/solution.py
@@ -293,7 +293,14 @@
         return first
 
     for step in range(len(bits)):
-        spread_step(hiddens, step, lambda m, k: True)
+        spread_step(hiddens, step, lambda m, k: k == 0)
+        if step:
+            blocks, place = hiddens[0], bit_orders[0][step]
+            passed = [k for k in blocks if 0 < k and not k & place]
+            values = [blocks[k] for k in passed]
+            blocks[place], values = lax.optimization_barrier((blocks[place], values))
+            blocks.update(zip(passed, values))
+        spread_step(hiddens, step, lambda m, k: 0 < k and not k & bit_orders[m][step])
     hiddens = wait_for(hiddens, lambda m, k: True)
     spread_step(outs, 0, lambda m, k: True)
     hidden_parts = [hiddens[m][k] for m in range(2) for k in range(dp)]

time: 99.3 us -> 98.9 us (level)
  transfers between devices with their start and end apart: 37 -> 37, of which waited for: 20 -> 23; matrix products, arithmetic and copies ran while one was open for 2% -> 2% of each run, Pallas kernels for 12% -> 12%
where the time goes in v7:
time: 98.9 us; the launch traced here: 98.6 us
  waiting for transfers between devices  42.6 us (43%)
  starting transfers between devices  37.3 us (38%)
  Pallas kernels  15.3 us (15%)
  other arithmetic  2.04 us (2%)
    ppermute x37, waiting for transfers between devices, exchange(): return lax.ppermute(values, axis, [(i, i ^ flip) for i in range(count)])  42.6 us
    ppermute x37, starting transfers between devices, exchange(): return lax.ppermute(values, axis, [(i, i ^ flip) for i in range(count)])  37.3 us
    pallas_call x8, Pallas kernels, call(): pl.pallas_call(kernel, out_shape=out_shape, in_specs=specs, out_specs=jax...  15.3 us
  transfers between devices with their start and end apart: 37, of which 23 were waited for; matrix products, arithmetic and copies ran while one was open for 2% of the time, Pallas kernels for 12%

profile of v7, /device:TPU:0, one launch (start us, length us, event | category | flops | bytes accessed | tf_op | source)
XLA Modules:
  0.0 98.6 jit_solution(13117933306354536012)
XLA Ops:
  1.6 3.0 %collective-permute-start.4 = (bf16[17,16,256]{2,1,0:T(8,128)(2,1)S(1)}, bf16[17,16,256]{2,1,0:T(8,128)(2,1)S(1)}, u32[]{:S(2)}, u32[]{:S(2)}) collective-permute-start(bf16[17,16,256]{2,1,0:T(8,128)(2,1)S(1)} %shard_map.158.refs_4_), channel_id=1, source_target_pairs={{0,16},{8,24},{16,0},{24,8},{1,17},{9,25},{17,1},{25,9},{2,18},{10... | collective-permute-start | bytes 417800 | tf_op jit(solution)/shard_map/ppermute | solution.py:34
  4.7 1.9 %collective-permute-start.1 = (bf16[16,16,256]{2,1,0:T(8,128)(2,1)}, bf16[16,16,256]{2,1,0:T(8,128)(2,1)S(1)}, u32[]{:S(2)}, u32[]{:S(2)}) collective-permute-start(bf16[16,16,256]{2,1,0:T(8,128)(2,1)} %refs_0_), channel_id=1, source_target_pairs={{0,8},{8,0},{16,24},{24,16},{1,9},{9,1},{17,25},{25,17},{2,10},{10... | collective-permute-start | bytes 393224 | tf_op jit(solution)/shard_map/ppermute | solution.py:34
  6.7 2.4 %collective-permute-done.4.refs_6_ = bf16[17,16,256]{2,1,0:T(8,128)(2,1)S(1)} collective-permute-done((bf16[17,16,256]{2,1,0:T(8,128)(2,1)S(1)}, bf16[17,16,256]{2,1,0:T(8,128)(2,1)S(1)}, u32[]{:S(2)}, u32[]{:S(2)}) %collective-permute-start.4) | collective-permute-done | bytes 139296 | tf_op jit(solution)/shard_map/ppermute | solution.py:34
  9.1 2.0 %collective-permute-start.5 = (bf16[17,16,256]{2,1,0:T(8,128)(2,1)S(1)}, bf16[17,16,256]{2,1,0:T(8,128)(2,1)S(1)}, u32[]{:S(2)}, u32[]{:S(2)}) collective-permute-start(bf16[17,16,256]{2,1,0:T(8,128)(2,1)S(1)} %collective-permute-done.4.refs_6_), channel_id=1, source_target_pairs={{0,8},{8,0},{16,24},{24,16},{1,9},{9,1},{17,25},{25,17},{2,10},{10... | collective-permute-start | bytes 417800 | tf_op jit(solution)/shard_map/ppermute | solution.py:34
  11.3 2.0 %collective-permute-start.2 = (bf16[16,16,256]{2,1,0:T(8,128)(2,1)S(1)}, bf16[16,16,256]{2,1,0:T(8,128)(2,1)S(1)}, u32[]{:S(2)}, u32[]{:S(2)}) collective-permute-start(bf16[16,16,256]{2,1,0:T(8,128)(2,1)S(1)} %collective-permute-done.1.refs_1_), channel_id=1, source_target_pairs={{0,16},{8,24},{16,0},{24,8},{1,17},{9,25},{17,1},{25,9},{2,18},{10... | collective-permute-start | bytes 393224 | tf_op jit(solution)/shard_map/ppermute | solution.py:34
  14.3 2.0 %collective-permute-done.2.refs_3_ = bf16[16,16,256]{2,1,0:T(8,128)(2,1)S(1)} collective-permute-done((bf16[16,16,256]{2,1,0:T(8,128)(2,1)S(1)}, bf16[16,16,256]{2,1,0:T(8,128)(2,1)S(1)}, u32[]{:S(2)}, u32[]{:S(2)}) %collective-permute-start.2) | collective-permute-done | bytes 131104 | tf_op jit(solution)/shard_map/ppermute | solution.py:34
  16.3 1.9 %collective-permute-start.13 = (bf16[512,896]{1,0:T(8,128)(2,1)}, bf16[512,896]{1,0:T(8,128)(2,1)S(1)}, u32[]{:S(2)}, u32[]{:S(2)}) collective-permute-start(bf16[512,896]{1,0:T(8,128)(2,1)} %refs_10_), channel_id=1, source_target_pairs={{0,8},{8,0},{16,24},{24,16},{1,9},{9,1},{17,25},{25,17},{2,10},{10... | collective-permute-start | bytes 2752520 | tf_op jit(solution)/shard_map/ppermute | solution.py:34
  19.8 1.8 %shard_map.159 = (bf16[2,128,256]{2,1,0:T(8,128)(2,1)S(1)}, f32[4,16,256]{2,1,0:T(8,128)S(1)}) custom-call(s32[4]{0:T(128)S(1)} %pad_add_fusion.ids, s32[64]{0:T(128)} %plan_far.1, bf16[16,16,256]{2,1,0:T(8,128)(2,1)} %refs_0_, bf16[16,16,256]{2,1,0:T(8,128)(2,1)S(1)} %collective-permute-done.1.refs_1_, ...), custom_call_target="tpu_custom_call" | custom-call | tf_op jit(solution)/shard_map/pallas_call | solution.py:22
  21.6 3.7 %collective-permute-start.8 = (bf16[2,128,256]{2,1,0:T(8,128)(2,1)S(1)}, bf16[2,128,256]{2,1,0:T(8,128)(2,1)S(1)}, u32[]{:S(2)}, u32[]{:S(2)}) collective-permute-start(bf16[2,128,256]{2,1,0:T(8,128)(2,1)S(1)} %get-tuple-element.48.refs_6_), channel_id=1, source_target_pairs={{0,6},{1,7},{2,4},{3,5},{4,2},{5,3},{6,0},{7,1},{8,14},{9,15},{10,... | collective-permute-start | bytes 393224 | tf_op jit(solution)/shard_map/ppermute | solution.py:34
  26.1 3.6 %collective-permute-done.8.refs_9_ = bf16[2,128,256]{2,1,0:T(8,128)(2,1)S(1)} collective-permute-done((bf16[2,128,256]{2,1,0:T(8,128)(2,1)S(1)}, bf16[2,128,256]{2,1,0:T(8,128)(2,1)S(1)}, u32[]{:S(2)}, u32[]{:S(2)}) %collective-permute-start.8) | collective-permute-done | bytes 131104 | tf_op jit(solution)/shard_map/ppermute | solution.py:34
  29.7 1.6 %collective-permute-done.6.refs_7_ = bf16[2,128,256]{2,1,0:T(8,128)(2,1)S(1)} collective-permute-done((bf16[2,128,256]{2,1,0:T(8,128)(2,1)S(1)}, bf16[2,128,256]{2,1,0:T(8,128)(2,1)S(1)}, u32[]{:S(2)}, u32[]{:S(2)}) %collective-permute-start.6) | collective-permute-done | bytes 131104 | tf_op jit(solution)/shard_map/ppermute | solution.py:34
  31.3 2.7 %collective-permute-done.7.refs_8_ = bf16[2,128,256]{2,1,0:T(8,128)(2,1)S(1)} collective-permute-done((bf16[2,128,256]{2,1,0:T(8,128)(2,1)S(1)}, bf16[2,128,256]{2,1,0:T(8,128)(2,1)S(1)}, u32[]{:S(2)}, u32[]{:S(2)}) %collective-permute-start.7) | collective-permute-done | bytes 131104 | tf_op jit(solution)/shard_map/ppermute | solution.py:34
  35.9 5.0 %shard_map.160 = (f32[4,2,128,256]{3,2,1,0:T(8,128)S(1)}, bf16[4,2,128,256]{3,2,1,0:T(8,128)(2,1)S(1)}) custom-call(s32[4]{0:T(128)S(1)} %pad_add_fusion.ids, f32[8,1,256]{2,1,0:T(1,128)} %bitcast.13, f32[8,1,256]{2,1,0:T(1,128)} %bitcast.14, bf16[2048,512]{1,0:T(8,128)(2,1)} %refs_2_.1, bf16[2048,512]{1,0:T(8,128)(2,1)} %refs_3_.1, ...), custom_call_target="tpu_custom_call" | custom-call | tf_op jit(solution)/shard_map/pallas_call | solution.py:22
  41.3 1.7 %collective-permute-done.15.came = bf16[4,2,128,256]{3,2,1,0:T(8,128)(2,1)S(1)} collective-permute-done((bf16[4,2,128,256]{3,2,1,0:T(8,128)(2,1)S(1)}, bf16[4,2,128,256]{3,2,1,0:T(8,128)(2,1)S(1)}, u32[]{:S(2)}, u32[]{:S(2)}) %collective-permute-start.15) | collective-permute-done | bytes 524320 | tf_op jit(solution)/shard_map/ppermute | solution.py:34
  43.6 2.6 %collective-permute-start.17 = (bf16[2,128,256]{2,1,0:T(8,128)(2,1)S(1)}, bf16[2,128,256]{2,1,0:T(8,128)(2,1)S(1)}, u32[]{:S(2)}, u32[]{:S(2)}) collective-permute-start(bf16[2,128,256]{2,1,0:T(8,128)(2,1)S(1)} %get-tuple-element.57), channel_id=1, source_target_pairs={{0,4},{1,5},{2,6},{3,7},{4,0},{5,1},{6,2},{7,3},{8,12},{9,13},{10,... | collective-permute-start | bytes 393224 | tf_op jit(solution)/shard_map/ppermute | solution.py:34
  48.0 9.8 %collective-permute-done.18.refs_12_ = bf16[512,896]{1,0:T(8,128)(2,1)} collective-permute-done((bf16[512,896]{1,0:T(8,128)(2,1)}, bf16[512,896]{1,0:T(8,128)(2,1)}, u32[]{:S(2)}, u32[]{:S(2)}) %collective-permute-start.18) | collective-permute-done | bytes 917536 | tf_op jit(solution)/shard_map/ppermute | solution.py:34
  60.0 1.6 %collective-permute-start.21 = (bf16[2,128,256]{2,1,0:T(8,128)(2,1)S(1)}, bf16[2,128,256]{2,1,0:T(8,128)(2,1)S(1)}, u32[]{:S(2)}, u32[]{:S(2)}) collective-permute-start(bf16[2,128,256]{2,1,0:T(8,128)(2,1)S(1)} %add_convert_fusion.refs_2_), channel_id=1, source_target_pairs={{0,2},{1,3},{2,0},{3,1},{4,6},{5,7},{6,4},{7,5},{8,10},{9,11},{10,... | collective-permute-start | bytes 393224 | tf_op jit(solution)/shard_map/ppermute | solution.py:34
  61.7 2.7 %collective-permute-start.22 = (bf16[2,128,256]{2,1,0:T(8,128)(2,1)S(1)}, bf16[2,128,256]{2,1,0:T(8,128)(2,1)S(1)}, u32[]{:S(2)}, u32[]{:S(2)}) collective-permute-start(bf16[2,128,256]{2,1,0:T(8,128)(2,1)S(1)} %add_convert_fusion.refs_2_), channel_id=1, source_target_pairs={{0,4},{1,5},{2,6},{3,7},{4,0},{5,1},{6,2},{7,3},{8,12},{9,13},{10,... | collective-permute-start | bytes 393224 | tf_op jit(solution)/shard_map/ppermute | solution.py:34
  66.0 6.9 %collective-permute-done.22.refs_4_ = bf16[2,128,256]{2,1,0:T(8,128)(2,1)S(1)} collective-permute-done((bf16[2,128,256]{2,1,0:T(8,128)(2,1)S(1)}, bf16[2,128,256]{2,1,0:T(8,128)(2,1)S(1)}, u32[]{:S(2)}, u32[]{:S(2)}) %collective-permute-start.22) | collective-permute-done | bytes 131104 | tf_op jit(solution)/shard_map/ppermute | solution.py:34
  74.9 4.6 %shard_map.162 = (f32[2,128,896]{2,1,0:T(8,128)S(1)}, bf16[2,128,512]{2,1,0:T(8,128)(2,1)S(1)}) custom-call(s32[4]{0:T(128)S(1)} %pad_add_fusion.ids, f32[8,1,256]{2,1,0:T(1,128)} %bitcast.15, f32[8,1,256]{2,1,0:T(1,128)} %bitcast.16, bf16[2,128,256]{2,1,0:T(8,128)(2,1)S(1)} %add_convert_fusion.refs_2_, ...), custom_call_target="tpu_custom_call" | custom-call | tf_op jit(solution)/shard_map/pallas_call | solution.py:22
  83.1 2.1 %collective-permute-start.31 = (f32[8,128]{1,0:T(8,128)S(1)}, f32[8,128]{1,0:T(8,128)S(1)}, u32[]{:S(2)}, u32[]{:S(2)}) collective-permute-start(f32[8,128]{1,0:T(8,128)S(1)} %shard_map.164.refs_0_), channel_id=1, source_target_pairs={{0,4},{1,5},{2,6},{3,7},{4,0},{5,1},{6,2},{7,3},{8,12},{9,13},{10,... | collective-permute-start | bytes 12296 | tf_op jit(solution)/shard_map/ppermute | solution.py:34
  87.7 3.0 %collective-permute-done.32.refs_2_ = f32[8,128]{1,0:T(8,128)S(1)} collective-permute-done((f32[8,128]{1,0:T(8,128)S(1)}, f32[8,128]{1,0:T(8,128)S(1)}, u32[]{:S(2)}, u32[]{:S(2)}) %collective-permute-start.32) | collective-permute-done | bytes 4128 | tf_op jit(solution)/shard_map/ppermute | solution.py:34
  93.2 1.5 %collective-permute-start.36 = (f32[1,128]{1,0:T(1,128)S(1)}, f32[1,128]{1,0:T(1,128)S(1)}, u32[]{:S(2)}, u32[]{:S(2)}) collective-permute-start(f32[1,128]{1,0:T(1,128)S(1)} %shard_map.165), channel_id=1, source_target_pairs={{0,24},{8,16},{16,8},{24,0},{1,25},{9,17},{17,9},{25,1},{2,26},{10... | collective-permute-start | bytes 1544 | tf_op jit(solution)/shard_map/ppermute | solution.py:34
  95.8 1.8 %collective-permute-done.36 = f32[1,128]{1,0:T(1,128)S(1)} collective-permute-done((f32[1,128]{1,0:T(1,128)S(1)}, f32[1,128]{1,0:T(1,128)S(1)}, u32[]{:S(2)}, u32[]{:S(2)}) %collective-permute-start.36) | collective-permute-done | bytes 544 | tf_op jit(solution)/shard_map/ppermute | solution.py:34
  (81 shorter events, 25.8 us)
Async XLA Ops:
  1.6 7.5 %collective-permute-start.4 = (bf16[17,16,256]{2,1,0:T(8,128)(2,1)S(1)}, bf16[17,16,256]{2,1,0:T(8,128)(2,1)S(1)}, u32[]{:S(2)}, u32[]{:S(2)}) collective-permute-start(bf16[17,16,256]{2,1,0:T(8,128)(2,1)S(1)} %shard_map.158.refs_4_), channel_id=1, source_target_pairs={{0,16},{8,24},{16,0},{24,8},{1,17},{9,25},{17,1},{25,9},{2,18},{10... | collective-permute-start | bytes 417800 | tf_op jit(solution)/shard_map/ppermute | solution.py:34
  4.6 6.5 %collective-permute-start = (bf16[16,16,256]{2,1,0:T(8,128)(2,1)}, bf16[16,16,256]{2,1,0:T(8,128)(2,1)S(1)}, u32[]{:S(2)}, u32[]{:S(2)}) collective-permute-start(bf16[16,16,256]{2,1,0:T(8,128)(2,1)} %refs_0_), channel_id=1, source_target_pairs={{0,16},{8,24},{16,0},{24,8},{1,17},{9,25},{17,1},{25,9},{2,18},{10... | collective-permute-start | bytes 393224 | tf_op jit(solution)/shard_map/ppermute | solution.py:34
  4.7 6.6 %collective-permute-start.1 = (bf16[16,16,256]{2,1,0:T(8,128)(2,1)}, bf16[16,16,256]{2,1,0:T(8,128)(2,1)S(1)}, u32[]{:S(2)}, u32[]{:S(2)}) collective-permute-start(bf16[16,16,256]{2,1,0:T(8,128)(2,1)} %refs_0_), channel_id=1, source_target_pairs={{0,8},{8,0},{16,24},{24,16},{1,9},{9,1},{17,25},{25,17},{2,10},{10... | collective-permute-start | bytes 393224 | tf_op jit(solution)/shard_map/ppermute | solution.py:34
  6.6 7.7 %collective-permute-start.3 = (bf16[17,16,256]{2,1,0:T(8,128)(2,1)S(1)}, bf16[17,16,256]{2,1,0:T(8,128)(2,1)S(1)}, u32[]{:S(2)}, u32[]{:S(2)}) collective-permute-start(bf16[17,16,256]{2,1,0:T(8,128)(2,1)S(1)} %shard_map.158.refs_4_), channel_id=1, source_target_pairs={{0,8},{8,0},{16,24},{24,16},{1,9},{9,1},{17,25},{25,17},{2,10},{10... | collective-permute-start | bytes 417800 | tf_op jit(solution)/shard_map/ppermute | solution.py:34
  9.1 7.2 %collective-permute-start.5 = (bf16[17,16,256]{2,1,0:T(8,128)(2,1)S(1)}, bf16[17,16,256]{2,1,0:T(8,128)(2,1)S(1)}, u32[]{:S(2)}, u32[]{:S(2)}) collective-permute-start(bf16[17,16,256]{2,1,0:T(8,128)(2,1)S(1)} %collective-permute-done.4.refs_6_), channel_id=1, source_target_pairs={{0,8},{8,0},{16,24},{24,16},{1,9},{9,1},{17,25},{25,17},{2,10},{10... | collective-permute-start | bytes 417800 | tf_op jit(solution)/shard_map/ppermute | solution.py:34
  11.3 5.0 %collective-permute-start.2 = (bf16[16,16,256]{2,1,0:T(8,128)(2,1)S(1)}, bf16[16,16,256]{2,1,0:T(8,128)(2,1)S(1)}, u32[]{:S(2)}, u32[]{:S(2)}) collective-permute-start(bf16[16,16,256]{2,1,0:T(8,128)(2,1)S(1)} %collective-permute-done.1.refs_1_), channel_id=1, source_target_pairs={{0,16},{8,24},{16,0},{24,8},{1,17},{9,25},{17,1},{25,9},{2,18},{10... | collective-permute-start | bytes 393224 | tf_op jit(solution)/shard_map/ppermute | solution.py:34
  16.3 24.6 %collective-permute-start.13 = (bf16[512,896]{1,0:T(8,128)(2,1)}, bf16[512,896]{1,0:T(8,128)(2,1)S(1)}, u32[]{:S(2)}, u32[]{:S(2)}) collective-permute-start(bf16[512,896]{1,0:T(8,128)(2,1)} %refs_10_), channel_id=1, source_target_pairs={{0,8},{8,0},{16,24},{24,16},{1,9},{9,1},{17,25},{25,17},{2,10},{10... | collective-permute-start | bytes 2752520 | tf_op jit(solution)/shard_map/ppermute | solution.py:34
  18.2 22.7 %collective-permute-start.14 = (bf16[512,896]{1,0:T(8,128)(2,1)}, bf16[512,896]{1,0:T(8,128)(2,1)}, u32[]{:S(2)}, u32[]{:S(2)}) collective-permute-start(bf16[512,896]{1,0:T(8,128)(2,1)} %refs_13_), channel_id=1, source_target_pairs={{0,16},{8,24},{16,0},{24,8},{1,17},{9,25},{17,1},{25,9},{2,18},{10... | collective-permute-start | bytes 2752520 | tf_op jit(solution)/shard_map/ppermute | solution.py:34
  21.6 8.1 %collective-permute-start.8 = (bf16[2,128,256]{2,1,0:T(8,128)(2,1)S(1)}, bf16[2,128,256]{2,1,0:T(8,128)(2,1)S(1)}, u32[]{:S(2)}, u32[]{:S(2)}) collective-permute-start(bf16[2,128,256]{2,1,0:T(8,128)(2,1)S(1)} %get-tuple-element.48.refs_6_), channel_id=1, source_target_pairs={{0,6},{1,7},{2,4},{3,5},{4,2},{5,3},{6,0},{7,1},{8,14},{9,15},{10,... | collective-permute-start | bytes 393224 | tf_op jit(solution)/shard_map/ppermute | solution.py:34
  25.3 6.0 %collective-permute-start.6 = (bf16[2,128,256]{2,1,0:T(8,128)(2,1)S(1)}, bf16[2,128,256]{2,1,0:T(8,128)(2,1)S(1)}, u32[]{:S(2)}, u32[]{:S(2)}) collective-permute-start(bf16[2,128,256]{2,1,0:T(8,128)(2,1)S(1)} %get-tuple-element.48.refs_6_), channel_id=1, source_target_pairs={{0,2},{1,3},{2,0},{3,1},{4,6},{5,7},{6,4},{7,5},{8,10},{9,11},{10,... | collective-permute-start | bytes 393224 | tf_op jit(solution)/shard_map/ppermute | solution.py:34
  25.3 8.7 %collective-permute-start.7 = (bf16[2,128,256]{2,1,0:T(8,128)(2,1)S(1)}, bf16[2,128,256]{2,1,0:T(8,128)(2,1)S(1)}, u32[]{:S(2)}, u32[]{:S(2)}) collective-permute-start(bf16[2,128,256]{2,1,0:T(8,128)(2,1)S(1)} %get-tuple-element.48.refs_6_), channel_id=1, source_target_pairs={{0,4},{1,5},{2,6},{3,7},{4,0},{5,1},{6,2},{7,3},{8,12},{9,13},{10,... | collective-permute-start | bytes 393224 | tf_op jit(solution)/shard_map/ppermute | solution.py:34
  34.5 23.3 %collective-permute-start.18 = (bf16[512,896]{1,0:T(8,128)(2,1)}, bf16[512,896]{1,0:T(8,128)(2,1)}, u32[]{:S(2)}, u32[]{:S(2)}) collective-permute-start(bf16[512,896]{1,0:T(8,128)(2,1)} %refs_10_), channel_id=1, source_target_pairs={{0,16},{8,24},{16,0},{24,8},{1,17},{9,25},{17,1},{25,9},{2,18},{10... | collective-permute-start | bytes 2752520 | tf_op jit(solution)/shard_map/ppermute | solution.py:34
  35.4 22.7 %collective-permute-start.19 = (bf16[512,896]{1,0:T(8,128)(2,1)}, bf16[512,896]{1,0:T(8,128)(2,1)}, u32[]{:S(2)}, u32[]{:S(2)}) collective-permute-start(bf16[512,896]{1,0:T(8,128)(2,1)} %refs_13_), channel_id=1, source_target_pairs={{0,8},{8,0},{16,24},{24,16},{1,9},{9,1},{17,25},{25,17},{2,10},{10... | collective-permute-start | bytes 2752520 | tf_op jit(solution)/shard_map/ppermute | solution.py:34
  43.6 14.5 %collective-permute-start.17 = (bf16[2,128,256]{2,1,0:T(8,128)(2,1)S(1)}, bf16[2,128,256]{2,1,0:T(8,128)(2,1)S(1)}, u32[]{:S(2)}, u32[]{:S(2)}) collective-permute-start(bf16[2,128,256]{2,1,0:T(8,128)(2,1)S(1)} %get-tuple-element.57), channel_id=1, source_target_pairs={{0,4},{1,5},{2,6},{3,7},{4,0},{5,1},{6,2},{7,3},{8,12},{9,13},{10,... | collective-permute-start | bytes 393224 | tf_op jit(solution)/shard_map/ppermute | solution.py:34
  46.2 13.8 %collective-permute-start.16 = (bf16[2,128,256]{2,1,0:T(8,128)(2,1)S(1)}, bf16[2,128,256]{2,1,0:T(8,128)(2,1)S(1)}, u32[]{:S(2)}, u32[]{:S(2)}) collective-permute-start(bf16[2,128,256]{2,1,0:T(8,128)(2,1)S(1)} %get-tuple-element.56), channel_id=1, source_target_pairs={{0,2},{1,3},{2,0},{3,1},{4,6},{5,7},{6,4},{7,5},{8,10},{9,11},{10,... | collective-permute-start | bytes 393224 | tf_op jit(solution)/shard_map/ppermute | solution.py:34
  46.8 13.2 %collective-permute-start.20 = (bf16[2,128,256]{2,1,0:T(8,128)(2,1)S(1)}, bf16[2,128,256]{2,1,0:T(8,128)(2,1)S(1)}, u32[]{:S(2)}, u32[]{:S(2)}) collective-permute-start(bf16[2,128,256]{2,1,0:T(8,128)(2,1)S(1)} %get-tuple-element.63), channel_id=1, source_target_pairs={{0,6},{1,7},{2,4},{3,5},{4,2},{5,3},{6,0},{7,1},{8,14},{9,15},{10,... | collective-permute-start | bytes 393224 | tf_op jit(solution)/shard_map/ppermute | solution.py:34
  58.1 21.6 %collective-permute-start.28 = (bf16[512,896]{1,0:T(8,128)(2,1)S(1)}, bf16[512,896]{1,0:T(8,128)(2,1)S(1)}, u32[]{:S(2)}, u32[]{:S(2)}) collective-permute-start(bf16[512,896]{1,0:T(8,128)(2,1)S(1)} %collective-permute-done.13.refs_11_), channel_id=1, source_target_pairs={{0,16},{8,24},{16,0},{24,8},{1,17},{9,25},{17,1},{25,9},{2,18},{10... | collective-permute-start | bytes 2752520 | tf_op jit(solution)/shard_map/ppermute | solution.py:34
  59.4 20.7 %collective-permute-start.29 = (bf16[512,896]{1,0:T(8,128)(2,1)}, bf16[512,896]{1,0:T(8,128)(2,1)S(1)}, u32[]{:S(2)}, u32[]{:S(2)}) collective-permute-start(bf16[512,896]{1,0:T(8,128)(2,1)} %collective-permute-done.14.refs_15_), channel_id=1, source_target_pairs={{0,8},{8,0},{16,24},{24,16},{1,9},{9,1},{17,25},{25,17},{2,10},{10... | collective-permute-start | bytes 2752520 | tf_op jit(solution)/shard_map/ppermute | solution.py:34
  60.0 5.6 %collective-permute-start.21 = (bf16[2,128,256]{2,1,0:T(8,128)(2,1)S(1)}, bf16[2,128,256]{2,1,0:T(8,128)(2,1)S(1)}, u32[]{:S(2)}, u32[]{:S(2)}) collective-permute-start(bf16[2,128,256]{2,1,0:T(8,128)(2,1)S(1)} %add_convert_fusion.refs_2_), channel_id=1, source_target_pairs={{0,2},{1,3},{2,0},{3,1},{4,6},{5,7},{6,4},{7,5},{8,10},{9,11},{10,... | collective-permute-start | bytes 393224 | tf_op jit(solution)/shard_map/ppermute | solution.py:34
  61.7 11.2 %collective-permute-start.22 = (bf16[2,128,256]{2,1,0:T(8,128)(2,1)S(1)}, bf16[2,128,256]{2,1,0:T(8,128)(2,1)S(1)}, u32[]{:S(2)}, u32[]{:S(2)}) collective-permute-start(bf16[2,128,256]{2,1,0:T(8,128)(2,1)S(1)} %add_convert_fusion.refs_2_), channel_id=1, source_target_pairs={{0,4},{1,5},{2,6},{3,7},{4,0},{5,1},{6,2},{7,3},{8,12},{9,13},{10,... | collective-permute-start | bytes 393224 | tf_op jit(solution)/shard_map/ppermute | solution.py:34
  64.4 8.6 %collective-permute-start.23 = (bf16[2,128,256]{2,1,0:T(8,128)(2,1)S(1)}, bf16[2,128,256]{2,1,0:T(8,128)(2,1)S(1)}, u32[]{:S(2)}, u32[]{:S(2)}) collective-permute-start(bf16[2,128,256]{2,1,0:T(8,128)(2,1)S(1)} %add_convert_fusion.refs_2_), channel_id=1, source_target_pairs={{0,6},{1,7},{2,4},{3,5},{4,2},{5,3},{6,0},{7,1},{8,14},{9,15},{10,... | collective-permute-start | bytes 393224 | tf_op jit(solution)/shard_map/ppermute | solution.py:34
  65.6 7.9 %collective-permute-start.24 = (bf16[2,128,256]{2,1,0:T(8,128)(2,1)S(1)}, bf16[2,128,256]{2,1,0:T(8,128)(2,1)S(1)}, u32[]{:S(2)}, u32[]{:S(2)}) collective-permute-start(bf16[2,128,256]{2,1,0:T(8,128)(2,1)S(1)} %add_convert_fusion.refs_2_), channel_id=1, source_target_pairs={{0,1},{1,0},{2,3},{3,2},{4,5},{5,4},{6,7},{7,6},{8,9},{9,8},{10,11... | collective-permute-start | bytes 393224 | tf_op jit(solution)/shard_map/ppermute | solution.py:34
  83.1 4.6 %collective-permute-start.31 = (f32[8,128]{1,0:T(8,128)S(1)}, f32[8,128]{1,0:T(8,128)S(1)}, u32[]{:S(2)}, u32[]{:S(2)}) collective-permute-start(f32[8,128]{1,0:T(8,128)S(1)} %shard_map.164.refs_0_), channel_id=1, source_target_pairs={{0,4},{1,5},{2,6},{3,7},{4,0},{5,1},{6,2},{7,3},{8,12},{9,13},{10,... | collective-permute-start | bytes 12296 | tf_op jit(solution)/shard_map/ppermute | solution.py:34
  85.2 5.4 %collective-permute-start.32 = (f32[8,128]{1,0:T(8,128)S(1)}, f32[8,128]{1,0:T(8,128)S(1)}, u32[]{:S(2)}, u32[]{:S(2)}) collective-permute-start(f32[8,128]{1,0:T(8,128)S(1)} %shard_map.164.refs_0_), channel_id=1, source_target_pairs={{0,6},{1,7},{2,4},{3,5},{4,2},{5,3},{6,0},{7,1},{8,14},{9,15},{10,... | collective-permute-start | bytes 12296 | tf_op jit(solution)/shard_map/ppermute | solution.py:34
  (13 other events, 34.2 us)

commit v8 on v7

--- a/solution.py
+++ b/solution.py
@@ -13,7 +13,7 @@
 anywhere = pl.BlockSpec(memory_space=pltpu.HBM)
 
 
-def call(kernel, out_shape, ops, scratch=(), far=(), mib=4):
+def call(kernel, out_shape, ops, scratch=(), far=(), mib=4, cost=None):
     specs = [anywhere if i in far else vmem if i else smem for i in range(len(ops))]
     ops = [
         pltpu.with_memory_space_constraint(op, pltpu.HBM) if i in far else op
@@ -25,6 +25,7 @@
         in_specs=specs,
         out_specs=jax.tree.map(lambda _: vmem, out_shape),
         scratch_shapes=list(scratch),
+        cost_estimate=cost and pl.CostEstimate(flops=cost, bytes_accessed=0, transcendentals=0),
         compiler_params=pltpu.CompilerParams(vmem_limit_bytes=mib * 1024 * 1024),
     )(*ops)
 
@@ -301,7 +302,10 @@
             blocks[place], values = lax.optimization_barrier((blocks[place], values))
             blocks.update(zip(passed, values))
         spread_step(hiddens, step, lambda m, k: 0 < k and not k & bit_orders[m][step])
-    hiddens = wait_for(hiddens, lambda m, k: True)
+    early = [(m, b) for m in range(2) for b in bits]
+    values = wait_for([hiddens[m][b] for m, b in early], lambda m, k: True)
+    for (m, b), value in zip(early, values):
+        hiddens[m][b] = value
     spread_step(outs, 0, lambda m, k: True)
     hidden_parts = [hiddens[m][k] for m in range(2) for k in range(dp)]
 
@@ -319,6 +323,7 @@
             pltpu.SemaphoreType.DMA((2,)),
         ],
         far=(1, 2),
+        cost=10000000000,
     )
 
     facts = facts[:, :, : 2 * slots + 1].astype(jnp.int32)

time: 98.9 us -> 97.5 us (0.986)
  waiting for transfers between devices: 42.6 us -> 37.8 us
  starting transfers between devices: 37.3 us -> 40.6 us
    ppermute x37, waiting for transfers between devices: 42.6 us -> 37.8 us  [exchange(): return lax.ppermute(values, axis, [(i, i ^ flip) for i in range(count)])]
    ppermute x37, starting transfers between devices: 37.3 us -> 40.6 us  [exchange(): return lax.ppermute(values, axis, [(i, i ^ flip) for i in range(count)])]
  transfers between devices with their start and end apart: 37 -> 37, of which waited for: 23 -> 20; matrix products, arithmetic and copies ran while one was open for 2% -> 2% of each run, Pallas kernels for 12% -> 12%
where the time goes in v8:
time: 97.5 us; the launch traced here: 97.2 us
  starting transfers between devices  40.6 us (42%)
  waiting for transfers between devices  37.8 us (39%)
  Pallas kernels  15.3 us (16%)
  other arithmetic  2.05 us (2%)
    ppermute x37, starting transfers between devices, exchange(): return lax.ppermute(values, axis, [(i, i ^ flip) for i in range(count)])  40.6 us
    ppermute x37, waiting for transfers between devices, exchange(): return lax.ppermute(values, axis, [(i, i ^ flip) for i in range(count)])  37.8 us
    pallas_call x8, Pallas kernels, call(): pl.pallas_call(kernel, out_shape=out_shape, in_specs=specs, out_specs=jax...  15.3 us
  transfers between devices with their start and end apart: 37, of which 20 were waited for; matrix products, arithmetic and copies ran while one was open for 2% of the time, Pallas kernels for 12%

profile of v8, /device:TPU:0, one launch (start us, length us, event | category | flops | bytes accessed | tf_op | source)
XLA Modules:
  0.0 97.2 jit_solution(2388824607380373805)
XLA Ops:
  1.6 3.0 %collective-permute-start.3 = (bf16[17,16,256]{2,1,0:T(8,128)(2,1)S(1)}, bf16[17,16,256]{2,1,0:T(8,128)(2,1)S(1)}, u32[]{:S(2)}, u32[]{:S(2)}) collective-permute-start(bf16[17,16,256]{2,1,0:T(8,128)(2,1)S(1)} %shard_map.158.refs_4_), channel_id=1, source_target_pairs={{0,16},{8,24},{16,0},{24,8},{1,17},{9,25},{17,1},{25,9},{2,18},{10... | collective-permute-start | bytes 417800 | tf_op jit(solution)/shard_map/ppermute | solution.py:35
  4.7 1.9 %collective-permute-start.1 = (bf16[16,16,256]{2,1,0:T(8,128)(2,1)}, bf16[16,16,256]{2,1,0:T(8,128)(2,1)S(1)}, u32[]{:S(2)}, u32[]{:S(2)}) collective-permute-start(bf16[16,16,256]{2,1,0:T(8,128)(2,1)} %refs_0_.1), channel_id=1, source_target_pairs={{0,8},{8,0},{16,24},{24,16},{1,9},{9,1},{17,25},{25,17},{2,10},{10... | collective-permute-start | bytes 393224 | tf_op jit(solution)/shard_map/ppermute | solution.py:35
  6.7 2.4 %collective-permute-done.3.refs_6_ = bf16[17,16,256]{2,1,0:T(8,128)(2,1)S(1)} collective-permute-done((bf16[17,16,256]{2,1,0:T(8,128)(2,1)S(1)}, bf16[17,16,256]{2,1,0:T(8,128)(2,1)S(1)}, u32[]{:S(2)}, u32[]{:S(2)}) %collective-permute-start.3) | collective-permute-done | bytes 139296 | tf_op jit(solution)/shard_map/ppermute | solution.py:35
  9.1 2.0 %collective-permute-start.5 = (bf16[17,16,256]{2,1,0:T(8,128)(2,1)S(1)}, bf16[17,16,256]{2,1,0:T(8,128)(2,1)S(1)}, u32[]{:S(2)}, u32[]{:S(2)}) collective-permute-start(bf16[17,16,256]{2,1,0:T(8,128)(2,1)S(1)} %collective-permute-done.3.refs_6_), channel_id=1, source_target_pairs={{0,8},{8,0},{16,24},{24,16},{1,9},{9,1},{17,25},{25,17},{2,10},{10... | collective-permute-start | bytes 417800 | tf_op jit(solution)/shard_map/ppermute | solution.py:35
  11.3 2.0 %collective-permute-start.4 = (bf16[16,16,256]{2,1,0:T(8,128)(2,1)S(1)}, bf16[16,16,256]{2,1,0:T(8,128)(2,1)S(1)}, u32[]{:S(2)}, u32[]{:S(2)}) collective-permute-start(bf16[16,16,256]{2,1,0:T(8,128)(2,1)S(1)} %collective-permute-done.1.refs_1_), channel_id=1, source_target_pairs={{0,16},{8,24},{16,0},{24,8},{1,17},{9,25},{17,1},{25,9},{2,18},{10... | collective-permute-start | bytes 393224 | tf_op jit(solution)/shard_map/ppermute | solution.py:35
  14.3 1.7 %collective-permute-start.13 = (bf16[512,896]{1,0:T(8,128)(2,1)}, bf16[512,896]{1,0:T(8,128)(2,1)S(1)}, u32[]{:S(2)}, u32[]{:S(2)}) collective-permute-start(bf16[512,896]{1,0:T(8,128)(2,1)} %refs_10_), channel_id=1, source_target_pairs={{0,8},{8,0},{16,24},{24,16},{1,9},{9,1},{17,25},{25,17},{2,10},{10... | collective-permute-start | bytes 2752520 | tf_op jit(solution)/shard_map/ppermute | solution.py:35
  16.0 1.8 %collective-permute-start.14 = (bf16[512,896]{1,0:T(8,128)(2,1)}, bf16[512,896]{1,0:T(8,128)(2,1)}, u32[]{:S(2)}, u32[]{:S(2)}) collective-permute-start(bf16[512,896]{1,0:T(8,128)(2,1)} %refs_13_), channel_id=1, source_target_pairs={{0,16},{8,24},{16,0},{24,8},{1,17},{9,25},{17,1},{25,9},{2,18},{10... | collective-permute-start | bytes 2752520 | tf_op jit(solution)/shard_map/ppermute | solution.py:35
  17.8 1.8 %shard_map.159 = (bf16[2,128,256]{2,1,0:T(8,128)(2,1)S(1)}, f32[4,16,256]{2,1,0:T(8,128)S(1)}) custom-call(s32[4]{0:T(128)S(1)} %pad_add_fusion.ids, s32[64]{0:T(128)} %plan_far.1, bf16[16,16,256]{2,1,0:T(8,128)(2,1)} %refs_0_.1, bf16[16,16,256]{2,1,0:T(8,128)(2,1)S(1)} %collective-permute-done.1.refs_1_, ...), custom_call_target="tpu_custom_call" | custom-call | flops 10000000000 | tf_op jit(solution)/shard_map/pallas_call | solution.py:22
  19.6 3.7 %collective-permute-start.8 = (bf16[2,128,256]{2,1,0:T(8,128)(2,1)S(1)}, bf16[2,128,256]{2,1,0:T(8,128)(2,1)S(1)}, u32[]{:S(2)}, u32[]{:S(2)}) collective-permute-start(bf16[2,128,256]{2,1,0:T(8,128)(2,1)S(1)} %get-tuple-element.40.refs_6_), channel_id=1, source_target_pairs={{0,6},{1,7},{2,4},{3,5},{4,2},{5,3},{6,0},{7,1},{8,14},{9,15},{10,... | collective-permute-start | bytes 393224 | tf_op jit(solution)/shard_map/ppermute | solution.py:35
  24.0 3.2 %collective-permute-done.8.refs_9_ = bf16[2,128,256]{2,1,0:T(8,128)(2,1)S(1)} collective-permute-done((bf16[2,128,256]{2,1,0:T(8,128)(2,1)S(1)}, bf16[2,128,256]{2,1,0:T(8,128)(2,1)S(1)}, u32[]{:S(2)}, u32[]{:S(2)}) %collective-permute-start.8) | collective-permute-done | bytes 131104 | tf_op jit(solution)/shard_map/ppermute | solution.py:35
  28.8 2.8 %collective-permute-done.7.refs_8_ = bf16[2,128,256]{2,1,0:T(8,128)(2,1)S(1)} collective-permute-done((bf16[2,128,256]{2,1,0:T(8,128)(2,1)S(1)}, bf16[2,128,256]{2,1,0:T(8,128)(2,1)S(1)}, u32[]{:S(2)}, u32[]{:S(2)}) %collective-permute-start.7) | collective-permute-done | bytes 131104 | tf_op jit(solution)/shard_map/ppermute | solution.py:35
  35.1 5.0 %shard_map.160 = (f32[4,2,128,256]{3,2,1,0:T(8,128)S(1)}, bf16[4,2,128,256]{3,2,1,0:T(8,128)(2,1)S(1)}) custom-call(s32[4]{0:T(128)S(1)} %pad_add_fusion.ids, f32[8,1,256]{2,1,0:T(1,128)} %bitcast.13, f32[8,1,256]{2,1,0:T(1,128)} %bitcast.14, bf16[2048,512]{1,0:T(8,128)(2,1)} %refs_2_.1, bf16[2048,512]{1,0:T(8,128)(2,1)} %refs_3_.1, ...), custom_call_target="tpu_custom_call" | custom-call | tf_op jit(solution)/shard_map/pallas_call | solution.py:22
  40.4 1.7 %collective-permute-done.15.came = bf16[4,2,128,256]{3,2,1,0:T(8,128)(2,1)S(1)} collective-permute-done((bf16[4,2,128,256]{3,2,1,0:T(8,128)(2,1)S(1)}, bf16[4,2,128,256]{3,2,1,0:T(8,128)(2,1)S(1)}, u32[]{:S(2)}, u32[]{:S(2)}) %collective-permute-start.15) | collective-permute-done | bytes 524320 | tf_op jit(solution)/shard_map/ppermute | solution.py:35
  42.7 2.1 %collective-permute-start.17 = (bf16[2,128,256]{2,1,0:T(8,128)(2,1)S(1)}, bf16[2,128,256]{2,1,0:T(8,128)(2,1)S(1)}, u32[]{:S(2)}, u32[]{:S(2)}) collective-permute-start(bf16[2,128,256]{2,1,0:T(8,128)(2,1)S(1)} %get-tuple-element.49), channel_id=1, source_target_pairs={{0,4},{1,5},{2,6},{3,7},{4,0},{5,1},{6,2},{7,3},{8,12},{9,13},{10,... | collective-permute-start | bytes 393224 | tf_op jit(solution)/shard_map/ppermute | solution.py:35
  47.2 8.5 %collective-permute-done.18.refs_12_ = bf16[512,896]{1,0:T(8,128)(2,1)} collective-permute-done((bf16[512,896]{1,0:T(8,128)(2,1)}, bf16[512,896]{1,0:T(8,128)(2,1)}, u32[]{:S(2)}, u32[]{:S(2)}) %collective-permute-start.18) | collective-permute-done | bytes 917536 | tf_op jit(solution)/shard_map/ppermute | solution.py:35
  56.0 1.7 %collective-permute-start.28 = (bf16[512,896]{1,0:T(8,128)(2,1)S(1)}, bf16[512,896]{1,0:T(8,128)(2,1)S(1)}, u32[]{:S(2)}, u32[]{:S(2)}) collective-permute-start(bf16[512,896]{1,0:T(8,128)(2,1)S(1)} %collective-permute-done.13.refs_11_), channel_id=1, source_target_pairs={{0,16},{8,24},{16,0},{24,8},{1,17},{9,25},{17,1},{25,9},{2,18},{10... | collective-permute-start | bytes 2752520 | tf_op jit(solution)/shard_map/ppermute | solution.py:35
  60.2 2.7 %collective-permute-start.22 = (bf16[2,128,256]{2,1,0:T(8,128)(2,1)S(1)}, bf16[2,128,256]{2,1,0:T(8,128)(2,1)S(1)}, u32[]{:S(2)}, u32[]{:S(2)}) collective-permute-start(bf16[2,128,256]{2,1,0:T(8,128)(2,1)S(1)} %add_convert_fusion.refs_2_), channel_id=1, source_target_pairs={{0,4},{1,5},{2,6},{3,7},{4,0},{5,1},{6,2},{7,3},{8,12},{9,13},{10,... | collective-permute-start | bytes 393224 | tf_op jit(solution)/shard_map/ppermute | solution.py:35
  63.3 1.7 %collective-permute-done.21.refs_3_ = bf16[2,128,256]{2,1,0:T(8,128)(2,1)S(1)} collective-permute-done((bf16[2,128,256]{2,1,0:T(8,128)(2,1)S(1)}, bf16[2,128,256]{2,1,0:T(8,128)(2,1)S(1)}, u32[]{:S(2)}, u32[]{:S(2)}) %collective-permute-start.21) | collective-permute-done | bytes 131104 | tf_op jit(solution)/shard_map/ppermute | solution.py:35
  65.4 6.5 %collective-permute-done.22.refs_4_ = bf16[2,128,256]{2,1,0:T(8,128)(2,1)S(1)} collective-permute-done((bf16[2,128,256]{2,1,0:T(8,128)(2,1)S(1)}, bf16[2,128,256]{2,1,0:T(8,128)(2,1)S(1)}, u32[]{:S(2)}, u32[]{:S(2)}) %collective-permute-start.22) | collective-permute-done | bytes 131104 | tf_op jit(solution)/shard_map/ppermute | solution.py:35
  74.0 4.6 %shard_map.162 = (f32[2,128,896]{2,1,0:T(8,128)S(1)}, bf16[2,128,512]{2,1,0:T(8,128)(2,1)S(1)}) custom-call(s32[4]{0:T(128)S(1)} %pad_add_fusion.ids, f32[8,1,256]{2,1,0:T(1,128)} %bitcast.15, f32[8,1,256]{2,1,0:T(1,128)} %bitcast.16, bf16[2,128,256]{2,1,0:T(8,128)(2,1)S(1)} %add_convert_fusion.refs_2_, ...), custom_call_target="tpu_custom_call" | custom-call | tf_op jit(solution)/shard_map/pallas_call | solution.py:22
  81.7 2.7 %collective-permute-start.31 = (f32[8,128]{1,0:T(8,128)S(1)}, f32[8,128]{1,0:T(8,128)S(1)}, u32[]{:S(2)}, u32[]{:S(2)}) collective-permute-start(f32[8,128]{1,0:T(8,128)S(1)} %shard_map.164.refs_0_), channel_id=1, source_target_pairs={{0,4},{1,5},{2,6},{3,7},{4,0},{5,1},{6,2},{7,3},{8,12},{9,13},{10,... | collective-permute-start | bytes 12296 | tf_op jit(solution)/shard_map/ppermute | solution.py:35
  86.2 3.5 %collective-permute-done.32.refs_2_ = f32[8,128]{1,0:T(8,128)S(1)} collective-permute-done((f32[8,128]{1,0:T(8,128)S(1)}, f32[8,128]{1,0:T(8,128)S(1)}, u32[]{:S(2)}, u32[]{:S(2)}) %collective-permute-start.32) | collective-permute-done | bytes 4128 | tf_op jit(solution)/shard_map/ppermute | solution.py:35
  91.8 2.1 %collective-permute-start.36 = (f32[1,128]{1,0:T(1,128)S(1)}, f32[1,128]{1,0:T(1,128)S(1)}, u32[]{:S(2)}, u32[]{:S(2)}) collective-permute-start(f32[1,128]{1,0:T(1,128)S(1)} %shard_map.165), channel_id=1, source_target_pairs={{0,24},{8,16},{16,8},{24,0},{1,25},{9,17},{17,9},{25,1},{2,26},{10... | collective-permute-start | bytes 1544 | tf_op jit(solution)/shard_map/ppermute | solution.py:35
  94.5 1.7 %collective-permute-done.36 = f32[1,128]{1,0:T(1,128)S(1)} collective-permute-done((f32[1,128]{1,0:T(1,128)S(1)}, f32[1,128]{1,0:T(1,128)S(1)}, u32[]{:S(2)}, u32[]{:S(2)}) %collective-permute-start.36) | collective-permute-done | bytes 544 | tf_op jit(solution)/shard_map/ppermute | solution.py:35
  (81 shorter events, 25.7 us)
Async XLA Ops:
  1.6 7.5 %collective-permute-start.3 = (bf16[17,16,256]{2,1,0:T(8,128)(2,1)S(1)}, bf16[17,16,256]{2,1,0:T(8,128)(2,1)S(1)}, u32[]{:S(2)}, u32[]{:S(2)}) collective-permute-start(bf16[17,16,256]{2,1,0:T(8,128)(2,1)S(1)} %shard_map.158.refs_4_), channel_id=1, source_target_pairs={{0,16},{8,24},{16,0},{24,8},{1,17},{9,25},{17,1},{25,9},{2,18},{10... | collective-permute-start | bytes 417800 | tf_op jit(solution)/shard_map/ppermute | solution.py:35
  4.6 6.5 %collective-permute-start = (bf16[16,16,256]{2,1,0:T(8,128)(2,1)}, bf16[16,16,256]{2,1,0:T(8,128)(2,1)S(1)}, u32[]{:S(2)}, u32[]{:S(2)}) collective-permute-start(bf16[16,16,256]{2,1,0:T(8,128)(2,1)} %refs_0_.1), channel_id=1, source_target_pairs={{0,16},{8,24},{16,0},{24,8},{1,17},{9,25},{17,1},{25,9},{2,18},{10... | collective-permute-start | bytes 393224 | tf_op jit(solution)/shard_map/ppermute | solution.py:35
  4.7 6.6 %collective-permute-start.1 = (bf16[16,16,256]{2,1,0:T(8,128)(2,1)}, bf16[16,16,256]{2,1,0:T(8,128)(2,1)S(1)}, u32[]{:S(2)}, u32[]{:S(2)}) collective-permute-start(bf16[16,16,256]{2,1,0:T(8,128)(2,1)} %refs_0_.1), channel_id=1, source_target_pairs={{0,8},{8,0},{16,24},{24,16},{1,9},{9,1},{17,25},{25,17},{2,10},{10... | collective-permute-start | bytes 393224 | tf_op jit(solution)/shard_map/ppermute | solution.py:35
  6.6 7.7 %collective-permute-start.2 = (bf16[17,16,256]{2,1,0:T(8,128)(2,1)S(1)}, bf16[17,16,256]{2,1,0:T(8,128)(2,1)S(1)}, u32[]{:S(2)}, u32[]{:S(2)}) collective-permute-start(bf16[17,16,256]{2,1,0:T(8,128)(2,1)S(1)} %shard_map.158.refs_4_), channel_id=1, source_target_pairs={{0,8},{8,0},{16,24},{24,16},{1,9},{9,1},{17,25},{25,17},{2,10},{10... | collective-permute-start | bytes 417800 | tf_op jit(solution)/shard_map/ppermute | solution.py:35
  9.1 8.7 %collective-permute-start.5 = (bf16[17,16,256]{2,1,0:T(8,128)(2,1)S(1)}, bf16[17,16,256]{2,1,0:T(8,128)(2,1)S(1)}, u32[]{:S(2)}, u32[]{:S(2)}) collective-permute-start(bf16[17,16,256]{2,1,0:T(8,128)(2,1)S(1)} %collective-permute-done.3.refs_6_), channel_id=1, source_target_pairs={{0,8},{8,0},{16,24},{24,16},{1,9},{9,1},{17,25},{25,17},{2,10},{10... | collective-permute-start | bytes 417800 | tf_op jit(solution)/shard_map/ppermute | solution.py:35
  11.3 6.4 %collective-permute-start.4 = (bf16[16,16,256]{2,1,0:T(8,128)(2,1)S(1)}, bf16[16,16,256]{2,1,0:T(8,128)(2,1)S(1)}, u32[]{:S(2)}, u32[]{:S(2)}) collective-permute-start(bf16[16,16,256]{2,1,0:T(8,128)(2,1)S(1)} %collective-permute-done.1.refs_1_), channel_id=1, source_target_pairs={{0,16},{8,24},{16,0},{24,8},{1,17},{9,25},{17,1},{25,9},{2,18},{10... | collective-permute-start | bytes 393224 | tf_op jit(solution)/shard_map/ppermute | solution.py:35
  14.3 25.8 %collective-permute-start.13 = (bf16[512,896]{1,0:T(8,128)(2,1)}, bf16[512,896]{1,0:T(8,128)(2,1)S(1)}, u32[]{:S(2)}, u32[]{:S(2)}) collective-permute-start(bf16[512,896]{1,0:T(8,128)(2,1)} %refs_10_), channel_id=1, source_target_pairs={{0,8},{8,0},{16,24},{24,16},{1,9},{9,1},{17,25},{25,17},{2,10},{10... | collective-permute-start | bytes 2752520 | tf_op jit(solution)/shard_map/ppermute | solution.py:35
  16.0 24.1 %collective-permute-start.14 = (bf16[512,896]{1,0:T(8,128)(2,1)}, bf16[512,896]{1,0:T(8,128)(2,1)}, u32[]{:S(2)}, u32[]{:S(2)}) collective-permute-start(bf16[512,896]{1,0:T(8,128)(2,1)} %refs_13_), channel_id=1, source_target_pairs={{0,16},{8,24},{16,0},{24,8},{1,17},{9,25},{17,1},{25,9},{2,18},{10... | collective-permute-start | bytes 2752520 | tf_op jit(solution)/shard_map/ppermute | solution.py:35
  19.6 7.6 %collective-permute-start.8 = (bf16[2,128,256]{2,1,0:T(8,128)(2,1)S(1)}, bf16[2,128,256]{2,1,0:T(8,128)(2,1)S(1)}, u32[]{:S(2)}, u32[]{:S(2)}) collective-permute-start(bf16[2,128,256]{2,1,0:T(8,128)(2,1)S(1)} %get-tuple-element.40.refs_6_), channel_id=1, source_target_pairs={{0,6},{1,7},{2,4},{3,5},{4,2},{5,3},{6,0},{7,1},{8,14},{9,15},{10,... | collective-permute-start | bytes 393224 | tf_op jit(solution)/shard_map/ppermute | solution.py:35
  23.3 5.5 %collective-permute-start.6 = (bf16[2,128,256]{2,1,0:T(8,128)(2,1)S(1)}, bf16[2,128,256]{2,1,0:T(8,128)(2,1)S(1)}, u32[]{:S(2)}, u32[]{:S(2)}) collective-permute-start(bf16[2,128,256]{2,1,0:T(8,128)(2,1)S(1)} %get-tuple-element.40.refs_6_), channel_id=1, source_target_pairs={{0,2},{1,3},{2,0},{3,1},{4,6},{5,7},{6,4},{7,5},{8,10},{9,11},{10,... | collective-permute-start | bytes 393224 | tf_op jit(solution)/shard_map/ppermute | solution.py:35
  23.3 8.2 %collective-permute-start.7 = (bf16[2,128,256]{2,1,0:T(8,128)(2,1)S(1)}, bf16[2,128,256]{2,1,0:T(8,128)(2,1)S(1)}, u32[]{:S(2)}, u32[]{:S(2)}) collective-permute-start(bf16[2,128,256]{2,1,0:T(8,128)(2,1)S(1)} %get-tuple-element.40.refs_6_), channel_id=1, source_target_pairs={{0,4},{1,5},{2,6},{3,7},{4,0},{5,1},{6,2},{7,3},{8,12},{9,13},{10,... | collective-permute-start | bytes 393224 | tf_op jit(solution)/shard_map/ppermute | solution.py:35
  32.1 23.7 %collective-permute-start.18 = (bf16[512,896]{1,0:T(8,128)(2,1)}, bf16[512,896]{1,0:T(8,128)(2,1)}, u32[]{:S(2)}, u32[]{:S(2)}) collective-permute-start(bf16[512,896]{1,0:T(8,128)(2,1)} %refs_10_), channel_id=1, source_target_pairs={{0,16},{8,24},{16,0},{24,8},{1,17},{9,25},{17,1},{25,9},{2,18},{10... | collective-permute-start | bytes 2752520 | tf_op jit(solution)/shard_map/ppermute | solution.py:35
  33.6 22.4 %collective-permute-start.19 = (bf16[512,896]{1,0:T(8,128)(2,1)}, bf16[512,896]{1,0:T(8,128)(2,1)}, u32[]{:S(2)}, u32[]{:S(2)}) collective-permute-start(bf16[512,896]{1,0:T(8,128)(2,1)} %refs_13_), channel_id=1, source_target_pairs={{0,8},{8,0},{16,24},{24,16},{1,9},{9,1},{17,25},{25,17},{2,10},{10... | collective-permute-start | bytes 2752520 | tf_op jit(solution)/shard_map/ppermute | solution.py:35
  42.7 13.2 %collective-permute-start.17 = (bf16[2,128,256]{2,1,0:T(8,128)(2,1)S(1)}, bf16[2,128,256]{2,1,0:T(8,128)(2,1)S(1)}, u32[]{:S(2)}, u32[]{:S(2)}) collective-permute-start(bf16[2,128,256]{2,1,0:T(8,128)(2,1)S(1)} %get-tuple-element.49), channel_id=1, source_target_pairs={{0,4},{1,5},{2,6},{3,7},{4,0},{5,1},{6,2},{7,3},{8,12},{9,13},{10,... | collective-permute-start | bytes 393224 | tf_op jit(solution)/shard_map/ppermute | solution.py:35
  44.8 13.8 %collective-permute-start.16 = (bf16[2,128,256]{2,1,0:T(8,128)(2,1)S(1)}, bf16[2,128,256]{2,1,0:T(8,128)(2,1)S(1)}, u32[]{:S(2)}, u32[]{:S(2)}) collective-permute-start(bf16[2,128,256]{2,1,0:T(8,128)(2,1)S(1)} %get-tuple-element.48), channel_id=1, source_target_pairs={{0,2},{1,3},{2,0},{3,1},{4,6},{5,7},{6,4},{7,5},{8,10},{9,11},{10,... | collective-permute-start | bytes 393224 | tf_op jit(solution)/shard_map/ppermute | solution.py:35
  45.9 12.7 %collective-permute-start.20 = (bf16[2,128,256]{2,1,0:T(8,128)(2,1)S(1)}, bf16[2,128,256]{2,1,0:T(8,128)(2,1)S(1)}, u32[]{:S(2)}, u32[]{:S(2)}) collective-permute-start(bf16[2,128,256]{2,1,0:T(8,128)(2,1)S(1)} %get-tuple-element.55), channel_id=1, source_target_pairs={{0,6},{1,7},{2,4},{3,5},{4,2},{5,3},{6,0},{7,1},{8,14},{9,15},{10,... | collective-permute-start | bytes 393224 | tf_op jit(solution)/shard_map/ppermute | solution.py:35
  56.0 22.6 %collective-permute-start.28 = (bf16[512,896]{1,0:T(8,128)(2,1)S(1)}, bf16[512,896]{1,0:T(8,128)(2,1)S(1)}, u32[]{:S(2)}, u32[]{:S(2)}) collective-permute-start(bf16[512,896]{1,0:T(8,128)(2,1)S(1)} %collective-permute-done.13.refs_11_), channel_id=1, source_target_pairs={{0,16},{8,24},{16,0},{24,8},{1,17},{9,25},{17,1},{25,9},{2,18},{10... | collective-permute-start | bytes 2752520 | tf_op jit(solution)/shard_map/ppermute | solution.py:35
  57.7 20.9 %collective-permute-start.29 = (bf16[512,896]{1,0:T(8,128)(2,1)}, bf16[512,896]{1,0:T(8,128)(2,1)S(1)}, u32[]{:S(2)}, u32[]{:S(2)}) collective-permute-start(bf16[512,896]{1,0:T(8,128)(2,1)} %collective-permute-done.14.refs_15_), channel_id=1, source_target_pairs={{0,8},{8,0},{16,24},{24,16},{1,9},{9,1},{17,25},{25,17},{2,10},{10... | collective-permute-start | bytes 2752520 | tf_op jit(solution)/shard_map/ppermute | solution.py:35
  58.7 6.3 %collective-permute-start.21 = (bf16[2,128,256]{2,1,0:T(8,128)(2,1)S(1)}, bf16[2,128,256]{2,1,0:T(8,128)(2,1)S(1)}, u32[]{:S(2)}, u32[]{:S(2)}) collective-permute-start(bf16[2,128,256]{2,1,0:T(8,128)(2,1)S(1)} %add_convert_fusion.refs_2_), channel_id=1, source_target_pairs={{0,2},{1,3},{2,0},{3,1},{4,6},{5,7},{6,4},{7,5},{8,10},{9,11},{10,... | collective-permute-start | bytes 393224 | tf_op jit(solution)/shard_map/ppermute | solution.py:35
  60.2 11.7 %collective-permute-start.22 = (bf16[2,128,256]{2,1,0:T(8,128)(2,1)S(1)}, bf16[2,128,256]{2,1,0:T(8,128)(2,1)S(1)}, u32[]{:S(2)}, u32[]{:S(2)}) collective-permute-start(bf16[2,128,256]{2,1,0:T(8,128)(2,1)S(1)} %add_convert_fusion.refs_2_), channel_id=1, source_target_pairs={{0,4},{1,5},{2,6},{3,7},{4,0},{5,1},{6,2},{7,3},{8,12},{9,13},{10,... | collective-permute-start | bytes 393224 | tf_op jit(solution)/shard_map/ppermute | solution.py:35
  62.9 9.1 %collective-permute-start.23 = (bf16[2,128,256]{2,1,0:T(8,128)(2,1)S(1)}, bf16[2,128,256]{2,1,0:T(8,128)(2,1)S(1)}, u32[]{:S(2)}, u32[]{:S(2)}) collective-permute-start(bf16[2,128,256]{2,1,0:T(8,128)(2,1)S(1)} %add_convert_fusion.refs_2_), channel_id=1, source_target_pairs={{0,6},{1,7},{2,4},{3,5},{4,2},{5,3},{6,0},{7,1},{8,14},{9,15},{10,... | collective-permute-start | bytes 393224 | tf_op jit(solution)/shard_map/ppermute | solution.py:35
  65.0 7.5 %collective-permute-start.24 = (bf16[2,128,256]{2,1,0:T(8,128)(2,1)S(1)}, bf16[2,128,256]{2,1,0:T(8,128)(2,1)S(1)}, u32[]{:S(2)}, u32[]{:S(2)}) collective-permute-start(bf16[2,128,256]{2,1,0:T(8,128)(2,1)S(1)} %add_convert_fusion.refs_2_), channel_id=1, source_target_pairs={{0,1},{1,0},{2,3},{3,2},{4,5},{5,4},{6,7},{7,6},{8,9},{9,8},{10,11... | collective-permute-start | bytes 393224 | tf_op jit(solution)/shard_map/ppermute | solution.py:35
  81.7 4.6 %collective-permute-start.31 = (f32[8,128]{1,0:T(8,128)S(1)}, f32[8,128]{1,0:T(8,128)S(1)}, u32[]{:S(2)}, u32[]{:S(2)}) collective-permute-start(f32[8,128]{1,0:T(8,128)S(1)} %shard_map.164.refs_0_), channel_id=1, source_target_pairs={{0,4},{1,5},{2,6},{3,7},{4,0},{5,1},{6,2},{7,3},{8,12},{9,13},{10,... | collective-permute-start | bytes 12296 | tf_op jit(solution)/shard_map/ppermute | solution.py:35
  84.3 5.4 %collective-permute-start.32 = (f32[8,128]{1,0:T(8,128)S(1)}, f32[8,128]{1,0:T(8,128)S(1)}, u32[]{:S(2)}, u32[]{:S(2)}) collective-permute-start(f32[8,128]{1,0:T(8,128)S(1)} %shard_map.164.refs_0_), channel_id=1, source_target_pairs={{0,6},{1,7},{2,4},{3,5},{4,2},{5,3},{6,0},{7,1},{8,14},{9,15},{10,... | collective-permute-start | bytes 12296 | tf_op jit(solution)/shard_map/ppermute | solution.py:35
  (13 other events, 36.6 us)

commit v9 on v8

--- a/solution.py
+++ b/solution.py
@@ -209,26 +209,18 @@
         table = jnp.where(lane == m, top, table)
         table = jnp.where(lane == 2 + m, total, table)
         table = jnp.where(lane == 4 + m, picked, table)
-    stats[...] = jnp.transpose(table)[:8]
-
-
-def merge(tables):
+    rows = jnp.transpose(table)[:8]
+    for j in range(stats.shape[0]):
+        stats[j] = rows
+
+
+def last_kernel(ids, every, out):
+    tables = [every[j] for j in range(every.shape[0])]
     top = functools.reduce(jnp.maximum, [t[0:2] for t in tables])
     total = sum(t[2:4] * jnp.exp(t[0:2] - top) for t in tables)
-    return top, total, sum(t[4:6] for t in tables)
-
-
-def merge_kernel(ids, *refs):
-    out = refs[-1]
-    out[0:2], out[2:4], out[4:6] = merge(refs[:-1])
-    out[6:8] = jnp.zeros((2, out.shape[1]), jnp.float32)
-
-
-def last_kernel(ids, *refs):
-    out = refs[-1]
-    top, total, picked = merge(refs[:-1])
-    logprob = picked - (top + jnp.log(total))
-    out[...] = logprob[0:1] - logprob[1:2]
+    logprob = sum(t[4:6] for t in tables) - (top + jnp.log(total))
+    for k in range(out.shape[0]):
+        out[k] = logprob[0:1] - logprob[1:2]
 
 
 def local(
@@ -423,22 +415,17 @@
     )
     stats = call(
         finish_kernel,
-        jax.ShapeDtypeStruct((8, rows), jnp.float32),
+        jax.ShapeDtypeStruct((mp, 8, rows), jnp.float32),
         (ids, wanted, partial, tail, outs[0][dp - 1], outs[1][dp - 1]),
         mib=8,
     )
-    stats = call(
-        merge_kernel,
-        jax.ShapeDtypeStruct((8, rows), jnp.float32),
-        (ids, stats, exchange(stats, "mp", 1)),
-    )
     diff = call(
         last_kernel,
-        jax.ShapeDtypeStruct((1, rows), jnp.float32),
-        (ids, stats, *[exchange(stats, "mp", 2 * k) for k in far]),
-    )
-    diff = jnp.concatenate([diff] + [exchange(diff, "dp", k) for k in range(1, dp)])
-    ranks = ((order ^ dp_index)[:, None] * rows + jnp.arange(rows, dtype=jnp.int32)).reshape(-1)
+        jax.ShapeDtypeStruct((dp, 1, rows), jnp.float32),
+        (ids, lax.all_to_all(stats, "mp", split_axis=0, concat_axis=0, tiled=True)),
+    )
+    diff = lax.all_to_all(diff, "dp", split_axis=0, concat_axis=0, tiled=True)
+    ranks = jnp.arange(dp * rows, dtype=jnp.int32)
     my_code = codes(dp_index * reqs + jnp.arange(reqs, dtype=jnp.int32))
     hit = my_code[:, :, None] == ranks[None, None]
     token_diff = jnp.sum(jnp.where(hit, diff.reshape(1, 1, -1), 0.0), axis=2)

time: 97.5 us -> 101 us (1.036)
  waiting for transfers between devices: 37.8 us -> 40.8 us
    all_to_all x0 -> x2, waiting for transfers between devices: none -> 10 us  [the longest x1 5.56 us: local(): lax.all_to_all(stats, 'mp', split_axis=0, concat_axis=0, tiled=True)]
    all_to_all x0 -> x2, starting transfers between devices: none -> 7.89 us  [the longest x1 4.67 us: local(): lax.all_to_all(stats, 'mp', split_axis=0, concat_axis=0, tiled=True)]
    ppermute x37 -> x30, starting transfers between devices: 40.6 us -> 32.9 us  [exchange(): return lax.ppermute(values, axis, [(i, i ^ flip) for i in range(count)])]
    ppermute x37 -> x30, waiting for transfers between devices: 37.8 us -> 30.7 us  [exchange(): return lax.ppermute(values, axis, [(i, i ^ flip) for i in range(count)])]
    pallas_call x8 -> x7, Pallas kernels: 15.3 us -> 15.9 us  [call(): pl.pallas_call(kernel, out_shape=out_shape, in_specs=specs, out_specs=jax...]
  transfers between devices with their start and end apart: 37 -> 32, of which waited for: 20 -> 17; matrix products, arithmetic and copies ran while one was open for 2% -> 2% of each run, Pallas kernels for 12% -> 12%
where the time goes in v9:
time: 101 us
  starting transfers between devices  40.8 us (40%)
  waiting for transfers between devices  40.8 us (40%)
  Pallas kernels  15.9 us (16%)
  other arithmetic  1.97 us (2%)
    ppermute x30, starting transfers between devices, exchange(): return lax.ppermute(values, axis, [(i, i ^ flip) for i in range(count)])  32.9 us
    ppermute x30, waiting for transfers between devices, exchange(): return lax.ppermute(values, axis, [(i, i ^ flip) for i in range(count)])  30.7 us
    pallas_call x7, Pallas kernels, call(): pl.pallas_call(kernel, out_shape=out_shape, in_specs=specs, out_specs=jax...  15.9 us
    all_to_all x1, waiting for transfers between devices, local(): lax.all_to_all(stats, 'mp', split_axis=0, concat_axis=0, tiled=True)  5.56 us
    all_to_all x1, starting transfers between devices, local(): lax.all_to_all(stats, 'mp', split_axis=0, concat_axis=0, tiled=True)  4.67 us
    all_to_all x1, waiting for transfers between devices, local(): diff = lax.all_to_all(diff, 'dp', split_axis=0, concat_axis=0, tiled=True)  4.46 us
    all_to_all x1, starting transfers between devices, local(): diff = lax.all_to_all(diff, 'dp', split_axis=0, concat_axis=0, tiled=True)  3.22 us
  transfers between devices with their start and end apart: 32, of which 17 were waited for; matrix products, arithmetic and copies ran while one was open for 2% of the time, Pallas kernels for 12%

profile of v9, /device:TPU:0, one launch (start us, length us, event | category | flops | bytes accessed | tf_op | source)
XLA Modules:
  0.0 100.8 jit_solution(10471421459428527562)
XLA Ops:
  1.6 3.0 %collective-permute-start.3 = (bf16[17,16,256]{2,1,0:T(8,128)(2,1)S(1)}, bf16[17,16,256]{2,1,0:T(8,128)(2,1)S(1)}, u32[]{:S(2)}, u32[]{:S(2)}) collective-permute-start(bf16[17,16,256]{2,1,0:T(8,128)(2,1)S(1)} %shard_map.158.refs_4_), channel_id=1, source_target_pairs={{0,16},{8,24},{16,0},{24,8},{1,17},{9,25},{17,1},{25,9},{2,18},{10... | collective-permute-start | bytes 417800 | tf_op jit(solution)/shard_map/ppermute | solution.py:35
  4.7 1.9 %collective-permute-start.1 = (bf16[16,16,256]{2,1,0:T(8,128)(2,1)}, bf16[16,16,256]{2,1,0:T(8,128)(2,1)S(1)}, u32[]{:S(2)}, u32[]{:S(2)}) collective-permute-start(bf16[16,16,256]{2,1,0:T(8,128)(2,1)} %refs_0_.1), channel_id=1, source_target_pairs={{0,8},{8,0},{16,24},{24,16},{1,9},{9,1},{17,25},{25,17},{2,10},{10... | collective-permute-start | bytes 393224 | tf_op jit(solution)/shard_map/ppermute | solution.py:35
  6.7 2.4 %collective-permute-done.3.refs_6_ = bf16[17,16,256]{2,1,0:T(8,128)(2,1)S(1)} collective-permute-done((bf16[17,16,256]{2,1,0:T(8,128)(2,1)S(1)}, bf16[17,16,256]{2,1,0:T(8,128)(2,1)S(1)}, u32[]{:S(2)}, u32[]{:S(2)}) %collective-permute-start.3) | collective-permute-done | bytes 139296 | tf_op jit(solution)/shard_map/ppermute | solution.py:35
  9.1 2.0 %collective-permute-start.5 = (bf16[17,16,256]{2,1,0:T(8,128)(2,1)S(1)}, bf16[17,16,256]{2,1,0:T(8,128)(2,1)S(1)}, u32[]{:S(2)}, u32[]{:S(2)}) collective-permute-start(bf16[17,16,256]{2,1,0:T(8,128)(2,1)S(1)} %collective-permute-done.3.refs_6_), channel_id=1, source_target_pairs={{0,8},{8,0},{16,24},{24,16},{1,9},{9,1},{17,25},{25,17},{2,10},{10... | collective-permute-start | bytes 417800 | tf_op jit(solution)/shard_map/ppermute | solution.py:35
  11.3 2.0 %collective-permute-start.4 = (bf16[16,16,256]{2,1,0:T(8,128)(2,1)S(1)}, bf16[16,16,256]{2,1,0:T(8,128)(2,1)S(1)}, u32[]{:S(2)}, u32[]{:S(2)}) collective-permute-start(bf16[16,16,256]{2,1,0:T(8,128)(2,1)S(1)} %collective-permute-done.1.refs_1_), channel_id=1, source_target_pairs={{0,16},{8,24},{16,0},{24,8},{1,17},{9,25},{17,1},{25,9},{2,18},{10... | collective-permute-start | bytes 393224 | tf_op jit(solution)/shard_map/ppermute | solution.py:35
  16.0 1.8 %collective-permute-start.14 = (bf16[512,896]{1,0:T(8,128)(2,1)}, bf16[512,896]{1,0:T(8,128)(2,1)}, u32[]{:S(2)}, u32[]{:S(2)}) collective-permute-start(bf16[512,896]{1,0:T(8,128)(2,1)} %refs_13_), channel_id=1, source_target_pairs={{0,16},{8,24},{16,0},{24,8},{1,17},{9,25},{17,1},{25,9},{2,18},{10... | collective-permute-start | bytes 2752520 | tf_op jit(solution)/shard_map/ppermute | solution.py:35
  17.8 1.8 %shard_map.159 = (bf16[2,128,256]{2,1,0:T(8,128)(2,1)S(1)}, f32[4,16,256]{2,1,0:T(8,128)S(1)}) custom-call(s32[4]{0:T(128)S(1)} %pad_add_fusion.ids, s32[64]{0:T(128)} %plan_far.1, bf16[16,16,256]{2,1,0:T(8,128)(2,1)} %refs_0_.1, bf16[16,16,256]{2,1,0:T(8,128)(2,1)S(1)} %collective-permute-done.1.refs_1_, ...), custom_call_target="tpu_custom_call" | custom-call | flops 10000000000 | tf_op jit(solution)/shard_map/pallas_call | solution.py:22
  19.6 3.7 %collective-permute-start.8 = (bf16[2,128,256]{2,1,0:T(8,128)(2,1)S(1)}, bf16[2,128,256]{2,1,0:T(8,128)(2,1)S(1)}, u32[]{:S(2)}, u32[]{:S(2)}) collective-permute-start(bf16[2,128,256]{2,1,0:T(8,128)(2,1)S(1)} %get-tuple-element.40.refs_6_), channel_id=1, source_target_pairs={{0,6},{1,7},{2,4},{3,5},{4,2},{5,3},{6,0},{7,1},{8,14},{9,15},{10,... | collective-permute-start | bytes 393224 | tf_op jit(solution)/shard_map/ppermute | solution.py:35
  24.0 3.2 %collective-permute-done.8.refs_9_ = bf16[2,128,256]{2,1,0:T(8,128)(2,1)S(1)} collective-permute-done((bf16[2,128,256]{2,1,0:T(8,128)(2,1)S(1)}, bf16[2,128,256]{2,1,0:T(8,128)(2,1)S(1)}, u32[]{:S(2)}, u32[]{:S(2)}) %collective-permute-start.8) | collective-permute-done | bytes 131104 | tf_op jit(solution)/shard_map/ppermute | solution.py:35
  28.8 2.8 %collective-permute-done.7.refs_8_ = bf16[2,128,256]{2,1,0:T(8,128)(2,1)S(1)} collective-permute-done((bf16[2,128,256]{2,1,0:T(8,128)(2,1)S(1)}, bf16[2,128,256]{2,1,0:T(8,128)(2,1)S(1)}, u32[]{:S(2)}, u32[]{:S(2)}) %collective-permute-start.7) | collective-permute-done | bytes 131104 | tf_op jit(solution)/shard_map/ppermute | solution.py:35
  35.1 5.0 %shard_map.160 = (f32[4,2,128,256]{3,2,1,0:T(8,128)S(1)}, bf16[4,2,128,256]{3,2,1,0:T(8,128)(2,1)S(1)}) custom-call(s32[4]{0:T(128)S(1)} %pad_add_fusion.ids, f32[8,1,256]{2,1,0:T(1,128)} %bitcast.10, f32[8,1,256]{2,1,0:T(1,128)} %bitcast.11, bf16[2048,512]{1,0:T(8,128)(2,1)} %refs_2_.1, bf16[2048,512]{1,0:T(8,128)(2,1)} %refs_3_.1, ...), custom_call_target="tpu_custom_call" | custom-call | tf_op jit(solution)/shard_map/pallas_call | solution.py:22
  40.4 1.7 %collective-permute-done.15.came = bf16[4,2,128,256]{3,2,1,0:T(8,128)(2,1)S(1)} collective-permute-done((bf16[4,2,128,256]{3,2,1,0:T(8,128)(2,1)S(1)}, bf16[4,2,128,256]{3,2,1,0:T(8,128)(2,1)S(1)}, u32[]{:S(2)}, u32[]{:S(2)}) %collective-permute-start.15) | collective-permute-done | bytes 524320 | tf_op jit(solution)/shard_map/ppermute | solution.py:35
  42.7 2.1 %collective-permute-start.17 = (bf16[2,128,256]{2,1,0:T(8,128)(2,1)S(1)}, bf16[2,128,256]{2,1,0:T(8,128)(2,1)S(1)}, u32[]{:S(2)}, u32[]{:S(2)}) collective-permute-start(bf16[2,128,256]{2,1,0:T(8,128)(2,1)S(1)} %get-tuple-element.49), channel_id=1, source_target_pairs={{0,4},{1,5},{2,6},{3,7},{4,0},{5,1},{6,2},{7,3},{8,12},{9,13},{10,... | collective-permute-start | bytes 393224 | tf_op jit(solution)/shard_map/ppermute | solution.py:35
  47.2 8.5 %collective-permute-done.18.refs_12_ = bf16[512,896]{1,0:T(8,128)(2,1)} collective-permute-done((bf16[512,896]{1,0:T(8,128)(2,1)}, bf16[512,896]{1,0:T(8,128)(2,1)}, u32[]{:S(2)}, u32[]{:S(2)}) %collective-permute-start.18) | collective-permute-done | bytes 917536 | tf_op jit(solution)/shard_map/ppermute | solution.py:35
  56.0 1.7 %collective-permute-start.28 = (bf16[512,896]{1,0:T(8,128)(2,1)S(1)}, bf16[512,896]{1,0:T(8,128)(2,1)S(1)}, u32[]{:S(2)}, u32[]{:S(2)}) collective-permute-start(bf16[512,896]{1,0:T(8,128)(2,1)S(1)} %collective-permute-done.13.refs_11_), channel_id=1, source_target_pairs={{0,16},{8,24},{16,0},{24,8},{1,17},{9,25},{17,1},{25,9},{2,18},{10... | collective-permute-start | bytes 2752520 | tf_op jit(solution)/shard_map/ppermute | solution.py:35
  60.2 2.7 %collective-permute-start.22 = (bf16[2,128,256]{2,1,0:T(8,128)(2,1)S(1)}, bf16[2,128,256]{2,1,0:T(8,128)(2,1)S(1)}, u32[]{:S(2)}, u32[]{:S(2)}) collective-permute-start(bf16[2,128,256]{2,1,0:T(8,128)(2,1)S(1)} %add_convert_fusion.refs_2_), channel_id=1, source_target_pairs={{0,4},{1,5},{2,6},{3,7},{4,0},{5,1},{6,2},{7,3},{8,12},{9,13},{10,... | collective-permute-start | bytes 393224 | tf_op jit(solution)/shard_map/ppermute | solution.py:35
  63.3 1.7 %collective-permute-done.21.refs_3_ = bf16[2,128,256]{2,1,0:T(8,128)(2,1)S(1)} collective-permute-done((bf16[2,128,256]{2,1,0:T(8,128)(2,1)S(1)}, bf16[2,128,256]{2,1,0:T(8,128)(2,1)S(1)}, u32[]{:S(2)}, u32[]{:S(2)}) %collective-permute-start.21) | collective-permute-done | bytes 131104 | tf_op jit(solution)/shard_map/ppermute | solution.py:35
  65.4 6.5 %collective-permute-done.22.refs_4_ = bf16[2,128,256]{2,1,0:T(8,128)(2,1)S(1)} collective-permute-done((bf16[2,128,256]{2,1,0:T(8,128)(2,1)S(1)}, bf16[2,128,256]{2,1,0:T(8,128)(2,1)S(1)}, u32[]{:S(2)}, u32[]{:S(2)}) %collective-permute-start.22) | collective-permute-done | bytes 131104 | tf_op jit(solution)/shard_map/ppermute | solution.py:35
  74.0 4.6 %shard_map.162 = (f32[2,128,896]{2,1,0:T(8,128)S(1)}, bf16[2,128,512]{2,1,0:T(8,128)(2,1)S(1)}) custom-call(s32[4]{0:T(128)S(1)} %pad_add_fusion.ids, f32[8,1,256]{2,1,0:T(1,128)} %bitcast.12, f32[8,1,256]{2,1,0:T(1,128)} %bitcast.13, bf16[2,128,256]{2,1,0:T(8,128)(2,1)S(1)} %add_convert_fusion.refs_2_, ...), custom_call_target="tpu_custom_call" | custom-call | tf_op jit(solution)/shard_map/pallas_call | solution.py:22
  78.6 1.9 %shard_map.163 = f32[8,8,128]{2,1,0:T(8,128)} custom-call(s32[4]{0:T(128)S(1)} %pad_add_fusion.ids, s32[128,1]{1,0:T(8,128)S(1)} %copy.19.wanted, f32[2,128,896]{2,1,0:T(8,128)S(1)} %get-tuple-element.62.partial, bf16[2,128,512]{2,1,0:T(8,128)(2,1)S(1)} %get-tuple-element.63.tail, bf16[512,896]{1,0:T(8,128)(2,1)S(1)} %collective-permute-done.28.last_policy, ...), custom_call_target="tpu_custom_call" | custom-call | tf_op jit(solution)/shard_map/pallas_call | solution.py:22
  80.5 4.7 %all-to-all-start = ((f32[8,8,128]{2,1,0:T(8,128)}), f32[8,8,128]{2,1,0:T(8,128)S(1)}, u32[]{:S(2)}, u32[]{:S(2)}) async-start(f32[8,8,128]{2,1,0:T(8,128)} %shard_map.163), calls=%async_computation | async-start | bytes 65536 | tf_op jit(solution)/shard_map/all_to_all | solution.py:425
  85.4 5.6 %all-to-all-done.every = f32[8,8,128]{2,1,0:T(8,128)S(1)} async-done(((f32[8,8,128]{2,1,0:T(8,128)}), f32[8,8,128]{2,1,0:T(8,128)S(1)}, u32[]{:S(2)}, u32[]{:S(2)}) %all-to-all-start) | async-done | bytes 32800 | tf_op jit(solution)/shard_map/all_to_all | solution.py:425
  92.1 3.2 %all-to-all-start.1 = ((f32[4,1,128]{2,1,0:T(1,128)}), f32[4,1,128]{2,1,0:T(1,128)S(1)}, u32[]{:S(2)}, u32[]{:S(2)}) async-start(f32[4,1,128]{2,1,0:T(1,128)} %shard_map.164), calls=%async_computation.1 | async-start | bytes 4096 | tf_op jit(solution)/shard_map/all_to_all | solution.py:427
  95.4 4.5 %all-to-all-done.1 = f32[4,1,128]{2,1,0:T(1,128)S(1)} async-done(((f32[4,1,128]{2,1,0:T(1,128)}), f32[4,1,128]{2,1,0:T(1,128)S(1)}, u32[]{:S(2)}, u32[]{:S(2)}) %all-to-all-start.1) | async-done | bytes 2080 | tf_op jit(solution)/shard_map/all_to_all | solution.py:427
  (67 shorter events, 21.1 us)
Async XLA Ops:
  1.6 7.5 %collective-permute-start.3 = (bf16[17,16,256]{2,1,0:T(8,128)(2,1)S(1)}, bf16[17,16,256]{2,1,0:T(8,128)(2,1)S(1)}, u32[]{:S(2)}, u32[]{:S(2)}) collective-permute-start(bf16[17,16,256]{2,1,0:T(8,128)(2,1)S(1)} %shard_map.158.refs_4_), channel_id=1, source_target_pairs={{0,16},{8,24},{16,0},{24,8},{1,17},{9,25},{17,1},{25,9},{2,18},{10... | collective-permute-start | bytes 417800 | tf_op jit(solution)/shard_map/ppermute | solution.py:35
  4.6 6.5 %collective-permute-start = (bf16[16,16,256]{2,1,0:T(8,128)(2,1)}, bf16[16,16,256]{2,1,0:T(8,128)(2,1)S(1)}, u32[]{:S(2)}, u32[]{:S(2)}) collective-permute-start(bf16[16,16,256]{2,1,0:T(8,128)(2,1)} %refs_0_.1), channel_id=1, source_target_pairs={{0,16},{8,24},{16,0},{24,8},{1,17},{9,25},{17,1},{25,9},{2,18},{10... | collective-permute-start | bytes 393224 | tf_op jit(solution)/shard_map/ppermute | solution.py:35
  4.7 6.6 %collective-permute-start.1 = (bf16[16,16,256]{2,1,0:T(8,128)(2,1)}, bf16[16,16,256]{2,1,0:T(8,128)(2,1)S(1)}, u32[]{:S(2)}, u32[]{:S(2)}) collective-permute-start(bf16[16,16,256]{2,1,0:T(8,128)(2,1)} %refs_0_.1), channel_id=1, source_target_pairs={{0,8},{8,0},{16,24},{24,16},{1,9},{9,1},{17,25},{25,17},{2,10},{10... | collective-permute-start | bytes 393224 | tf_op jit(solution)/shard_map/ppermute | solution.py:35
  6.6 7.7 %collective-permute-start.2 = (bf16[17,16,256]{2,1,0:T(8,128)(2,1)S(1)}, bf16[17,16,256]{2,1,0:T(8,128)(2,1)S(1)}, u32[]{:S(2)}, u32[]{:S(2)}) collective-permute-start(bf16[17,16,256]{2,1,0:T(8,128)(2,1)S(1)} %shard_map.158.refs_4_), channel_id=1, source_target_pairs={{0,8},{8,0},{16,24},{24,16},{1,9},{9,1},{17,25},{25,17},{2,10},{10... | collective-permute-start | bytes 417800 | tf_op jit(solution)/shard_map/ppermute | solution.py:35
  9.1 8.7 %collective-permute-start.5 = (bf16[17,16,256]{2,1,0:T(8,128)(2,1)S(1)}, bf16[17,16,256]{2,1,0:T(8,128)(2,1)S(1)}, u32[]{:S(2)}, u32[]{:S(2)}) collective-permute-start(bf16[17,16,256]{2,1,0:T(8,128)(2,1)S(1)} %collective-permute-done.3.refs_6_), channel_id=1, source_target_pairs={{0,8},{8,0},{16,24},{24,16},{1,9},{9,1},{17,25},{25,17},{2,10},{10... | collective-permute-start | bytes 417800 | tf_op jit(solution)/shard_map/ppermute | solution.py:35
  11.3 6.4 %collective-permute-start.4 = (bf16[16,16,256]{2,1,0:T(8,128)(2,1)S(1)}, bf16[16,16,256]{2,1,0:T(8,128)(2,1)S(1)}, u32[]{:S(2)}, u32[]{:S(2)}) collective-permute-start(bf16[16,16,256]{2,1,0:T(8,128)(2,1)S(1)} %collective-permute-done.1.refs_1_), channel_id=1, source_target_pairs={{0,16},{8,24},{16,0},{24,8},{1,17},{9,25},{17,1},{25,9},{2,18},{10... | collective-permute-start | bytes 393224 | tf_op jit(solution)/shard_map/ppermute | solution.py:35
  14.3 25.8 %collective-permute-start.13 = (bf16[512,896]{1,0:T(8,128)(2,1)}, bf16[512,896]{1,0:T(8,128)(2,1)S(1)}, u32[]{:S(2)}, u32[]{:S(2)}) collective-permute-start(bf16[512,896]{1,0:T(8,128)(2,1)} %refs_10_), channel_id=1, source_target_pairs={{0,8},{8,0},{16,24},{24,16},{1,9},{9,1},{17,25},{25,17},{2,10},{10... | collective-permute-start | bytes 2752520 | tf_op jit(solution)/shard_map/ppermute | solution.py:35
  16.0 24.1 %collective-permute-start.14 = (bf16[512,896]{1,0:T(8,128)(2,1)}, bf16[512,896]{1,0:T(8,128)(2,1)}, u32[]{:S(2)}, u32[]{:S(2)}) collective-permute-start(bf16[512,896]{1,0:T(8,128)(2,1)} %refs_13_), channel_id=1, source_target_pairs={{0,16},{8,24},{16,0},{24,8},{1,17},{9,25},{17,1},{25,9},{2,18},{10... | collective-permute-start | bytes 2752520 | tf_op jit(solution)/shard_map/ppermute | solution.py:35
  19.6 7.6 %collective-permute-start.8 = (bf16[2,128,256]{2,1,0:T(8,128)(2,1)S(1)}, bf16[2,128,256]{2,1,0:T(8,128)(2,1)S(1)}, u32[]{:S(2)}, u32[]{:S(2)}) collective-permute-start(bf16[2,128,256]{2,1,0:T(8,128)(2,1)S(1)} %get-tuple-element.40.refs_6_), channel_id=1, source_target_pairs={{0,6},{1,7},{2,4},{3,5},{4,2},{5,3},{6,0},{7,1},{8,14},{9,15},{10,... | collective-permute-start | bytes 393224 | tf_op jit(solution)/shard_map/ppermute | solution.py:35
  23.3 5.5 %collective-permute-start.6 = (bf16[2,128,256]{2,1,0:T(8,128)(2,1)S(1)}, bf16[2,128,256]{2,1,0:T(8,128)(2,1)S(1)}, u32[]{:S(2)}, u32[]{:S(2)}) collective-permute-start(bf16[2,128,256]{2,1,0:T(8,128)(2,1)S(1)} %get-tuple-element.40.refs_6_), channel_id=1, source_target_pairs={{0,2},{1,3},{2,0},{3,1},{4,6},{5,7},{6,4},{7,5},{8,10},{9,11},{10,... | collective-permute-start | bytes 393224 | tf_op jit(solution)/shard_map/ppermute | solution.py:35
  23.3 8.2 %collective-permute-start.7 = (bf16[2,128,256]{2,1,0:T(8,128)(2,1)S(1)}, bf16[2,128,256]{2,1,0:T(8,128)(2,1)S(1)}, u32[]{:S(2)}, u32[]{:S(2)}) collective-permute-start(bf16[2,128,256]{2,1,0:T(8,128)(2,1)S(1)} %get-tuple-element.40.refs_6_), channel_id=1, source_target_pairs={{0,4},{1,5},{2,6},{3,7},{4,0},{5,1},{6,2},{7,3},{8,12},{9,13},{10,... | collective-permute-start | bytes 393224 | tf_op jit(solution)/shard_map/ppermute | solution.py:35
  32.1 23.7 %collective-permute-start.18 = (bf16[512,896]{1,0:T(8,128)(2,1)}, bf16[512,896]{1,0:T(8,128)(2,1)}, u32[]{:S(2)}, u32[]{:S(2)}) collective-permute-start(bf16[512,896]{1,0:T(8,128)(2,1)} %refs_10_), channel_id=1, source_target_pairs={{0,16},{8,24},{16,0},{24,8},{1,17},{9,25},{17,1},{25,9},{2,18},{10... | collective-permute-start | bytes 2752520 | tf_op jit(solution)/shard_map/ppermute | solution.py:35
  33.6 22.4 %collective-permute-start.19 = (bf16[512,896]{1,0:T(8,128)(2,1)}, bf16[512,896]{1,0:T(8,128)(2,1)}, u32[]{:S(2)}, u32[]{:S(2)}) collective-permute-start(bf16[512,896]{1,0:T(8,128)(2,1)} %refs_13_), channel_id=1, source_target_pairs={{0,8},{8,0},{16,24},{24,16},{1,9},{9,1},{17,25},{25,17},{2,10},{10... | collective-permute-start | bytes 2752520 | tf_op jit(solution)/shard_map/ppermute | solution.py:35
  42.7 13.2 %collective-permute-start.17 = (bf16[2,128,256]{2,1,0:T(8,128)(2,1)S(1)}, bf16[2,128,256]{2,1,0:T(8,128)(2,1)S(1)}, u32[]{:S(2)}, u32[]{:S(2)}) collective-permute-start(bf16[2,128,256]{2,1,0:T(8,128)(2,1)S(1)} %get-tuple-element.49), channel_id=1, source_target_pairs={{0,4},{1,5},{2,6},{3,7},{4,0},{5,1},{6,2},{7,3},{8,12},{9,13},{10,... | collective-permute-start | bytes 393224 | tf_op jit(solution)/shard_map/ppermute | solution.py:35
  44.8 13.8 %collective-permute-start.16 = (bf16[2,128,256]{2,1,0:T(8,128)(2,1)S(1)}, bf16[2,128,256]{2,1,0:T(8,128)(2,1)S(1)}, u32[]{:S(2)}, u32[]{:S(2)}) collective-permute-start(bf16[2,128,256]{2,1,0:T(8,128)(2,1)S(1)} %get-tuple-element.48), channel_id=1, source_target_pairs={{0,2},{1,3},{2,0},{3,1},{4,6},{5,7},{6,4},{7,5},{8,10},{9,11},{10,... | collective-permute-start | bytes 393224 | tf_op jit(solution)/shard_map/ppermute | solution.py:35
  45.9 12.8 %collective-permute-start.20 = (bf16[2,128,256]{2,1,0:T(8,128)(2,1)S(1)}, bf16[2,128,256]{2,1,0:T(8,128)(2,1)S(1)}, u32[]{:S(2)}, u32[]{:S(2)}) collective-permute-start(bf16[2,128,256]{2,1,0:T(8,128)(2,1)S(1)} %get-tuple-element.55), channel_id=1, source_target_pairs={{0,6},{1,7},{2,4},{3,5},{4,2},{5,3},{6,0},{7,1},{8,14},{9,15},{10,... | collective-permute-start | bytes 393224 | tf_op jit(solution)/shard_map/ppermute | solution.py:35
  56.0 22.6 %collective-permute-start.28 = (bf16[512,896]{1,0:T(8,128)(2,1)S(1)}, bf16[512,896]{1,0:T(8,128)(2,1)S(1)}, u32[]{:S(2)}, u32[]{:S(2)}) collective-permute-start(bf16[512,896]{1,0:T(8,128)(2,1)S(1)} %collective-permute-done.13.refs_11_), channel_id=1, source_target_pairs={{0,16},{8,24},{16,0},{24,8},{1,17},{9,25},{17,1},{25,9},{2,18},{10... | collective-permute-start | bytes 2752520 | tf_op jit(solution)/shard_map/ppermute | solution.py:35
  57.7 20.9 %collective-permute-start.29 = (bf16[512,896]{1,0:T(8,128)(2,1)}, bf16[512,896]{1,0:T(8,128)(2,1)S(1)}, u32[]{:S(2)}, u32[]{:S(2)}) collective-permute-start(bf16[512,896]{1,0:T(8,128)(2,1)} %collective-permute-done.14.refs_15_), channel_id=1, source_target_pairs={{0,8},{8,0},{16,24},{24,16},{1,9},{9,1},{17,25},{25,17},{2,10},{10... | collective-permute-start | bytes 2752520 | tf_op jit(solution)/shard_map/ppermute | solution.py:35
  58.7 6.3 %collective-permute-start.21 = (bf16[2,128,256]{2,1,0:T(8,128)(2,1)S(1)}, bf16[2,128,256]{2,1,0:T(8,128)(2,1)S(1)}, u32[]{:S(2)}, u32[]{:S(2)}) collective-permute-start(bf16[2,128,256]{2,1,0:T(8,128)(2,1)S(1)} %add_convert_fusion.refs_2_), channel_id=1, source_target_pairs={{0,2},{1,3},{2,0},{3,1},{4,6},{5,7},{6,4},{7,5},{8,10},{9,11},{10,... | collective-permute-start | bytes 393224 | tf_op jit(solution)/shard_map/ppermute | solution.py:35
  60.2 11.7 %collective-permute-start.22 = (bf16[2,128,256]{2,1,0:T(8,128)(2,1)S(1)}, bf16[2,128,256]{2,1,0:T(8,128)(2,1)S(1)}, u32[]{:S(2)}, u32[]{:S(2)}) collective-permute-start(bf16[2,128,256]{2,1,0:T(8,128)(2,1)S(1)} %add_convert_fusion.refs_2_), channel_id=1, source_target_pairs={{0,4},{1,5},{2,6},{3,7},{4,0},{5,1},{6,2},{7,3},{8,12},{9,13},{10,... | collective-permute-start | bytes 393224 | tf_op jit(solution)/shard_map/ppermute | solution.py:35
  62.9 9.1 %collective-permute-start.23 = (bf16[2,128,256]{2,1,0:T(8,128)(2,1)S(1)}, bf16[2,128,256]{2,1,0:T(8,128)(2,1)S(1)}, u32[]{:S(2)}, u32[]{:S(2)}) collective-permute-start(bf16[2,128,256]{2,1,0:T(8,128)(2,1)S(1)} %add_convert_fusion.refs_2_), channel_id=1, source_target_pairs={{0,6},{1,7},{2,4},{3,5},{4,2},{5,3},{6,0},{7,1},{8,14},{9,15},{10,... | collective-permute-start | bytes 393224 | tf_op jit(solution)/shard_map/ppermute | solution.py:35
  65.0 7.5 %collective-permute-start.24 = (bf16[2,128,256]{2,1,0:T(8,128)(2,1)S(1)}, bf16[2,128,256]{2,1,0:T(8,128)(2,1)S(1)}, u32[]{:S(2)}, u32[]{:S(2)}) collective-permute-start(bf16[2,128,256]{2,1,0:T(8,128)(2,1)S(1)} %add_convert_fusion.refs_2_), channel_id=1, source_target_pairs={{0,1},{1,0},{2,3},{3,2},{4,5},{5,4},{6,7},{7,6},{8,9},{9,8},{10,11... | collective-permute-start | bytes 393224 | tf_op jit(solution)/shard_map/ppermute | solution.py:35
  80.5 10.4 %all-to-all-start = ((f32[8,8,128]{2,1,0:T(8,128)}), f32[8,8,128]{2,1,0:T(8,128)S(1)}, u32[]{:S(2)}, u32[]{:S(2)}) async-start(f32[8,8,128]{2,1,0:T(8,128)} %shard_map.163), calls=%async_computation | async-start | bytes 65536 | tf_op jit(solution)/shard_map/all_to_all | solution.py:425
  92.1 7.8 %all-to-all-start.1 = ((f32[4,1,128]{2,1,0:T(1,128)}), f32[4,1,128]{2,1,0:T(1,128)S(1)}, u32[]{:S(2)}, u32[]{:S(2)}) async-start(f32[4,1,128]{2,1,0:T(1,128)} %shard_map.164), calls=%async_computation.1 | async-start | bytes 4096 | tf_op jit(solution)/shard_map/all_to_all | solution.py:427
  (8 other events, 19.8 us)

commit v10 on v8

--- a/solution.py
+++ b/solution.py
@@ -302,7 +302,7 @@
             blocks[place], values = lax.optimization_barrier((blocks[place], values))
             blocks.update(zip(passed, values))
         spread_step(hiddens, step, lambda m, k: 0 < k and not k & bit_orders[m][step])
-    early = [(m, b) for m in range(2) for b in bits]
+    early = [(0, b) for b in bits] + [(1, bit_orders[1][0])]
     values = wait_for([hiddens[m][b] for m, b in early], lambda m, k: True)
     for (m, b), value in zip(early, values):
         hiddens[m][b] = value
@@ -435,10 +435,11 @@
     diff = call(
         last_kernel,
         jax.ShapeDtypeStruct((1, rows), jnp.float32),
-        (ids, stats, *[exchange(stats, "mp", 2 * k) for k in far]),
-    )
-    diff = jnp.concatenate([diff] + [exchange(diff, "dp", k) for k in range(1, dp)])
-    ranks = ((order ^ dp_index)[:, None] * rows + jnp.arange(rows, dtype=jnp.int32)).reshape(-1)
+        (ids, stats, *[exchange(stats, "mp", 2 * k) for k in range(half - 1, 0, -1)]),
+    )
+    came = [exchange(diff, "dp", k) for k in range(dp - 1, 0, -1)]
+    diff = jnp.concatenate(came + [diff])
+    ranks = ((order[::-1] ^ dp_index)[:, None] * rows + jnp.arange(rows, dtype=jnp.int32)).reshape(-1)
     my_code = codes(dp_index * reqs + jnp.arange(reqs, dtype=jnp.int32))
     hit = my_code[:, :, None] == ranks[None, None]
     token_diff = jnp.sum(jnp.where(hit, diff.reshape(1, 1, -1), 0.0), axis=2)

time: 97.5 us -> 100 us (1.026)
  local copies, waits for them, and re-layouts: 0.58 us -> 6.15 us
  waiting for transfers between devices: 37.8 us -> 35.4 us
    unnamed x0 -> x16, local copies, waits for them, and re-layouts: none -> 5.48 us
    ppermute x37, waiting for transfers between devices: 37.8 us -> 35.4 us  [exchange(): return lax.ppermute(values, axis, [(i, i ^ flip) for i in range(count)])]
where the time goes in v10:
time: 100 us; the launch traced here: 99.7 us
  starting transfers between devices  40 us (40%)
  waiting for transfers between devices  35.4 us (35%)
  Pallas kernels  15.2 us (15%)
  local copies, waits for them, and re-layouts  6.15 us (6%)
  other arithmetic  2.05 us (2%)
    ppermute x37, starting transfers between devices, exchange(): return lax.ppermute(values, axis, [(i, i ^ flip) for i in range(count)])  40 us
    ppermute x37, waiting for transfers between devices, exchange(): return lax.ppermute(values, axis, [(i, i ^ flip) for i in range(count)])  35.4 us
    pallas_call x8, Pallas kernels, call(): pl.pallas_call(kernel, out_shape=out_shape, in_specs=specs, out_specs=jax...  15.2 us
    unnamed x16, local copies, waits for them, and re-layouts  5.48 us
  transfers between devices with their start and end apart: 37, of which 20 were waited for; matrix products, arithmetic and copies ran while one was open for 2% of the time, Pallas kernels for 12%

profile of v10, /device:TPU:0, one launch (start us, length us, event | category | flops | bytes accessed | tf_op | source)
XLA Modules:
  0.0 99.7 jit_solution(1711885689570358000)
XLA Ops:
  1.6 3.0 %collective-permute-start.2 = (bf16[17,16,256]{2,1,0:T(8,128)(2,1)S(1)}, bf16[17,16,256]{2,1,0:T(8,128)(2,1)S(1)}, u32[]{:S(2)}, u32[]{:S(2)}) collective-permute-start(bf16[17,16,256]{2,1,0:T(8,128)(2,1)S(1)} %shard_map.158.refs_4_), channel_id=1, source_target_pairs={{0,16},{8,24},{16,0},{24,8},{1,17},{9,25},{17,1},{25,9},{2,18},{10... | collective-permute-start | bytes 417800 | tf_op jit(solution)/shard_map/ppermute | solution.py:35
  4.7 1.9 %collective-permute-start.1 = (bf16[16,16,256]{2,1,0:T(8,128)(2,1)}, bf16[16,16,256]{2,1,0:T(8,128)(2,1)S(1)}, u32[]{:S(2)}, u32[]{:S(2)}) collective-permute-start(bf16[16,16,256]{2,1,0:T(8,128)(2,1)} %refs_0_.1), channel_id=1, source_target_pairs={{0,8},{8,0},{16,24},{24,16},{1,9},{9,1},{17,25},{25,17},{2,10},{10... | collective-permute-start | bytes 393224 | tf_op jit(solution)/shard_map/ppermute | solution.py:35
  6.7 2.4 %collective-permute-done.2.refs_6_ = bf16[17,16,256]{2,1,0:T(8,128)(2,1)S(1)} collective-permute-done((bf16[17,16,256]{2,1,0:T(8,128)(2,1)S(1)}, bf16[17,16,256]{2,1,0:T(8,128)(2,1)S(1)}, u32[]{:S(2)}, u32[]{:S(2)}) %collective-permute-start.2) | collective-permute-done | bytes 139296 | tf_op jit(solution)/shard_map/ppermute | solution.py:35
  9.1 2.0 %collective-permute-start.5 = (bf16[17,16,256]{2,1,0:T(8,128)(2,1)S(1)}, bf16[17,16,256]{2,1,0:T(8,128)(2,1)S(1)}, u32[]{:S(2)}, u32[]{:S(2)}) collective-permute-start(bf16[17,16,256]{2,1,0:T(8,128)(2,1)S(1)} %collective-permute-done.2.refs_6_), channel_id=1, source_target_pairs={{0,8},{8,0},{16,24},{24,16},{1,9},{9,1},{17,25},{25,17},{2,10},{10... | collective-permute-start | bytes 417800 | tf_op jit(solution)/shard_map/ppermute | solution.py:35
  11.3 2.0 %collective-permute-start.3 = (bf16[16,16,256]{2,1,0:T(8,128)(2,1)S(1)}, bf16[16,16,256]{2,1,0:T(8,128)(2,1)S(1)}, u32[]{:S(2)}, u32[]{:S(2)}) collective-permute-start(bf16[16,16,256]{2,1,0:T(8,128)(2,1)S(1)} %collective-permute-done.1.refs_1_), channel_id=1, source_target_pairs={{0,16},{8,24},{16,0},{24,8},{1,17},{9,25},{17,1},{25,9},{2,18},{10... | collective-permute-start | bytes 393224 | tf_op jit(solution)/shard_map/ppermute | solution.py:35
  13.4 1.5 %collective-permute-start.13 = (bf16[512,896]{1,0:T(8,128)(2,1)}, bf16[512,896]{1,0:T(8,128)(2,1)S(1)}, u32[]{:S(2)}, u32[]{:S(2)}) collective-permute-start(bf16[512,896]{1,0:T(8,128)(2,1)} %refs_10_), channel_id=1, source_target_pairs={{0,8},{8,0},{16,24},{24,16},{1,9},{9,1},{17,25},{25,17},{2,10},{10... | collective-permute-start | bytes 2752520 | tf_op jit(solution)/shard_map/ppermute | solution.py:35
  15.4 1.8 %collective-permute-done.3.refs_3_ = bf16[16,16,256]{2,1,0:T(8,128)(2,1)S(1)} collective-permute-done((bf16[16,16,256]{2,1,0:T(8,128)(2,1)S(1)}, bf16[16,16,256]{2,1,0:T(8,128)(2,1)S(1)}, u32[]{:S(2)}, u32[]{:S(2)}) %collective-permute-start.3) | collective-permute-done | bytes 131104 | tf_op jit(solution)/shard_map/ppermute | solution.py:35
  17.2 1.8 %shard_map.159 = (bf16[2,128,256]{2,1,0:T(8,128)(2,1)S(1)}, f32[4,16,256]{2,1,0:T(8,128)S(1)}) custom-call(s32[4]{0:T(128)S(1)} %pad_add_fusion.ids, s32[64]{0:T(128)} %plan_far.1, bf16[16,16,256]{2,1,0:T(8,128)(2,1)} %refs_0_.1, bf16[16,16,256]{2,1,0:T(8,128)(2,1)S(1)} %collective-permute-done.1.refs_1_, ...), custom_call_target="tpu_custom_call" | custom-call | flops 10000000000 | tf_op jit(solution)/shard_map/pallas_call | solution.py:22
  19.6 4.3 %collective-permute-start.8 = (bf16[2,128,256]{2,1,0:T(8,128)(2,1)S(1)}, bf16[2,128,256]{2,1,0:T(8,128)(2,1)S(1)}, u32[]{:S(2)}, u32[]{:S(2)}) collective-permute-start(bf16[2,128,256]{2,1,0:T(8,128)(2,1)S(1)} %get-tuple-element.38.refs_6_), channel_id=1, source_target_pairs={{0,6},{1,7},{2,4},{3,5},{4,2},{5,3},{6,0},{7,1},{8,14},{9,15},{10,... | collective-permute-start | bytes 393224 | tf_op jit(solution)/shard_map/ppermute | solution.py:35
  24.4 3.3 %collective-permute-done.8.refs_9_ = bf16[2,128,256]{2,1,0:T(8,128)(2,1)S(1)} collective-permute-done((bf16[2,128,256]{2,1,0:T(8,128)(2,1)S(1)}, bf16[2,128,256]{2,1,0:T(8,128)(2,1)S(1)}, u32[]{:S(2)}, u32[]{:S(2)}) %collective-permute-start.8) | collective-permute-done | bytes 131104 | tf_op jit(solution)/shard_map/ppermute | solution.py:35
  27.8 1.6 %collective-permute-done.6.refs_7_ = bf16[2,128,256]{2,1,0:T(8,128)(2,1)S(1)} collective-permute-done((bf16[2,128,256]{2,1,0:T(8,128)(2,1)S(1)}, bf16[2,128,256]{2,1,0:T(8,128)(2,1)S(1)}, u32[]{:S(2)}, u32[]{:S(2)}) %collective-permute-start.6) | collective-permute-done | bytes 131104 | tf_op jit(solution)/shard_map/ppermute | solution.py:35
  29.3 2.8 %collective-permute-done.7.refs_8_ = bf16[2,128,256]{2,1,0:T(8,128)(2,1)S(1)} collective-permute-done((bf16[2,128,256]{2,1,0:T(8,128)(2,1)S(1)}, bf16[2,128,256]{2,1,0:T(8,128)(2,1)S(1)}, u32[]{:S(2)}, u32[]{:S(2)}) %collective-permute-start.7) | collective-permute-done | bytes 131104 | tf_op jit(solution)/shard_map/ppermute | solution.py:35
  32.6 1.5 %collective-permute-start.18 = (bf16[512,896]{1,0:T(8,128)(2,1)}, bf16[512,896]{1,0:T(8,128)(2,1)S(1)}, u32[]{:S(2)}, u32[]{:S(2)}) collective-permute-start(bf16[512,896]{1,0:T(8,128)(2,1)} %refs_10_), channel_id=1, source_target_pairs={{0,16},{8,24},{16,0},{24,8},{1,17},{9,25},{17,1},{25,9},{2,18},{10... | collective-permute-start | bytes 2752520 | tf_op jit(solution)/shard_map/ppermute | solution.py:35
  34.8 1.5 %collective-permute-start.19 = (bf16[512,896]{1,0:T(8,128)(2,1)}, bf16[512,896]{1,0:T(8,128)(2,1)}, u32[]{:S(2)}, u32[]{:S(2)}) collective-permute-start(bf16[512,896]{1,0:T(8,128)(2,1)} %refs_13_), channel_id=1, source_target_pairs={{0,8},{8,0},{16,24},{24,16},{1,9},{9,1},{17,25},{25,17},{2,10},{10... | collective-permute-start | bytes 2752520 | tf_op jit(solution)/shard_map/ppermute | solution.py:35
  37.5 5.4 %shard_map.160 = (f32[4,2,128,256]{3,2,1,0:T(8,128)S(1)}, bf16[4,2,128,256]{3,2,1,0:T(8,128)(2,1)S(1)}) custom-call(s32[4]{0:T(128)S(1)} %pad_add_fusion.ids, f32[8,1,256]{2,1,0:T(1,128)} %bitcast.13, f32[8,1,256]{2,1,0:T(1,128)} %bitcast.14, bf16[2048,512]{1,0:T(8,128)(2,1)} %refs_2_.1, bf16[2048,512]{1,0:T(8,128)(2,1)} %refs_3_.1, ...), custom_call_target="tpu_custom_call" | custom-call | tf_op jit(solution)/shard_map/pallas_call | solution.py:22
  43.1 1.8 %collective-permute-done.15.came = bf16[4,2,128,256]{3,2,1,0:T(8,128)(2,1)S(1)} collective-permute-done((bf16[4,2,128,256]{3,2,1,0:T(8,128)(2,1)S(1)}, bf16[4,2,128,256]{3,2,1,0:T(8,128)(2,1)S(1)}, u32[]{:S(2)}, u32[]{:S(2)}) %collective-permute-start.15) | collective-permute-done | bytes 524320 | tf_op jit(solution)/shard_map/ppermute | solution.py:35
  46.6 2.2 %collective-permute-start.16 = (bf16[2,128,256]{2,1,0:T(8,128)(2,1)S(1)}, bf16[2,128,256]{2,1,0:T(8,128)(2,1)S(1)}, u32[]{:S(2)}, u32[]{:S(2)}) collective-permute-start(bf16[2,128,256]{2,1,0:T(8,128)(2,1)S(1)} %get-tuple-element.46), channel_id=1, source_target_pairs={{0,2},{1,3},{2,0},{3,1},{4,6},{5,7},{6,4},{7,5},{8,10},{9,11},{10,... | collective-permute-start | bytes 393224 | tf_op jit(solution)/shard_map/ppermute | solution.py:35
  50.0 5.6 %collective-permute-done.18.refs_12_ = bf16[512,896]{1,0:T(8,128)(2,1)S(1)} collective-permute-done((bf16[512,896]{1,0:T(8,128)(2,1)}, bf16[512,896]{1,0:T(8,128)(2,1)S(1)}, u32[]{:S(2)}, u32[]{:S(2)}) %collective-permute-start.18) | collective-permute-done | bytes 917536 | tf_op jit(solution)/shard_map/ppermute | solution.py:35
  61.2 2.3 %collective-permute-start.22 = (bf16[2,128,256]{2,1,0:T(8,128)(2,1)S(1)}, bf16[2,128,256]{2,1,0:T(8,128)(2,1)S(1)}, u32[]{:S(2)}, u32[]{:S(2)}) collective-permute-start(bf16[2,128,256]{2,1,0:T(8,128)(2,1)S(1)} %add_convert_fusion.refs_2_), channel_id=1, source_target_pairs={{0,4},{1,5},{2,6},{3,7},{4,0},{5,1},{6,2},{7,3},{8,12},{9,13},{10,... | collective-permute-start | bytes 393224 | tf_op jit(solution)/shard_map/ppermute | solution.py:35
  64.5 1.6 %collective-permute-done.21.refs_3_ = bf16[2,128,256]{2,1,0:T(8,128)(2,1)S(1)} collective-permute-done((bf16[2,128,256]{2,1,0:T(8,128)(2,1)S(1)}, bf16[2,128,256]{2,1,0:T(8,128)(2,1)S(1)}, u32[]{:S(2)}, u32[]{:S(2)}) %collective-permute-start.21) | collective-permute-done | bytes 131104 | tf_op jit(solution)/shard_map/ppermute | solution.py:35
  66.5 7.4 %collective-permute-done.22.refs_4_ = bf16[2,128,256]{2,1,0:T(8,128)(2,1)S(1)} collective-permute-done((bf16[2,128,256]{2,1,0:T(8,128)(2,1)S(1)}, bf16[2,128,256]{2,1,0:T(8,128)(2,1)S(1)}, u32[]{:S(2)}, u32[]{:S(2)}) %collective-permute-start.22) | collective-permute-done | bytes 131104 | tf_op jit(solution)/shard_map/ppermute | solution.py:35
  78.3 4.1 %shard_map.162 = (f32[2,128,896]{2,1,0:T(8,128)S(1)}, bf16[2,128,512]{2,1,0:T(8,128)(2,1)S(1)}) custom-call(s32[4]{0:T(128)S(1)} %pad_add_fusion.ids, f32[8,1,256]{2,1,0:T(1,128)} %bitcast.15, f32[8,1,256]{2,1,0:T(1,128)} %bitcast.16, bf16[2,128,256]{2,1,0:T(8,128)(2,1)S(1)} %add_convert_fusion.refs_2_, ...), custom_call_target="tpu_custom_call" | custom-call | tf_op jit(solution)/shard_map/pallas_call | solution.py:22
  85.4 2.3 %collective-permute-start.31 = (f32[8,128]{1,0:T(8,128)S(1)}, f32[8,128]{1,0:T(8,128)S(1)}, u32[]{:S(2)}, u32[]{:S(2)}) collective-permute-start(f32[8,128]{1,0:T(8,128)S(1)} %shard_map.164.refs_0_), channel_id=1, source_target_pairs={{0,6},{1,7},{2,4},{3,5},{4,2},{5,3},{6,0},{7,1},{8,14},{9,15},{10,... | collective-permute-start | bytes 12296 | tf_op jit(solution)/shard_map/ppermute | solution.py:35
  95.2 1.5 %collective-permute-start.36 = (f32[1,128]{1,0:T(1,128)S(1)}, f32[1,128]{1,0:T(1,128)S(1)}, u32[]{:S(2)}, u32[]{:S(2)}) collective-permute-start(f32[1,128]{1,0:T(1,128)S(1)} %shard_map.165), channel_id=1, source_target_pairs={{0,8},{8,0},{16,24},{24,16},{1,9},{9,1},{17,25},{25,17},{2,10},{10... | collective-permute-start | bytes 1544 | tf_op jit(solution)/shard_map/ppermute | solution.py:35
  (99 shorter events, 33.4 us)
Async XLA Ops:
  1.6 7.5 %collective-permute-start.2 = (bf16[17,16,256]{2,1,0:T(8,128)(2,1)S(1)}, bf16[17,16,256]{2,1,0:T(8,128)(2,1)S(1)}, u32[]{:S(2)}, u32[]{:S(2)}) collective-permute-start(bf16[17,16,256]{2,1,0:T(8,128)(2,1)S(1)} %shard_map.158.refs_4_), channel_id=1, source_target_pairs={{0,16},{8,24},{16,0},{24,8},{1,17},{9,25},{17,1},{25,9},{2,18},{10... | collective-permute-start | bytes 417800 | tf_op jit(solution)/shard_map/ppermute | solution.py:35
  4.6 6.5 %collective-permute-start = (bf16[16,16,256]{2,1,0:T(8,128)(2,1)}, bf16[16,16,256]{2,1,0:T(8,128)(2,1)S(1)}, u32[]{:S(2)}, u32[]{:S(2)}) collective-permute-start(bf16[16,16,256]{2,1,0:T(8,128)(2,1)} %refs_0_.1), channel_id=1, source_target_pairs={{0,16},{8,24},{16,0},{24,8},{1,17},{9,25},{17,1},{25,9},{2,18},{10... | collective-permute-start | bytes 393224 | tf_op jit(solution)/shard_map/ppermute | solution.py:35
  4.7 6.6 %collective-permute-start.1 = (bf16[16,16,256]{2,1,0:T(8,128)(2,1)}, bf16[16,16,256]{2,1,0:T(8,128)(2,1)S(1)}, u32[]{:S(2)}, u32[]{:S(2)}) collective-permute-start(bf16[16,16,256]{2,1,0:T(8,128)(2,1)} %refs_0_.1), channel_id=1, source_target_pairs={{0,8},{8,0},{16,24},{24,16},{1,9},{9,1},{17,25},{25,17},{2,10},{10... | collective-permute-start | bytes 393224 | tf_op jit(solution)/shard_map/ppermute | solution.py:35
  6.6 8.8 %collective-permute-start.4 = (bf16[17,16,256]{2,1,0:T(8,128)(2,1)S(1)}, bf16[17,16,256]{2,1,0:T(8,128)(2,1)S(1)}, u32[]{:S(2)}, u32[]{:S(2)}) collective-permute-start(bf16[17,16,256]{2,1,0:T(8,128)(2,1)S(1)} %shard_map.158.refs_4_), channel_id=1, source_target_pairs={{0,8},{8,0},{16,24},{24,16},{1,9},{9,1},{17,25},{25,17},{2,10},{10... | collective-permute-start | bytes 417800 | tf_op jit(solution)/shard_map/ppermute | solution.py:35
  9.1 8.1 %collective-permute-start.5 = (bf16[17,16,256]{2,1,0:T(8,128)(2,1)S(1)}, bf16[17,16,256]{2,1,0:T(8,128)(2,1)S(1)}, u32[]{:S(2)}, u32[]{:S(2)}) collective-permute-start(bf16[17,16,256]{2,1,0:T(8,128)(2,1)S(1)} %collective-permute-done.2.refs_6_), channel_id=1, source_target_pairs={{0,8},{8,0},{16,24},{24,16},{1,9},{9,1},{17,25},{25,17},{2,10},{10... | collective-permute-start | bytes 417800 | tf_op jit(solution)/shard_map/ppermute | solution.py:35
  11.3 5.8 %collective-permute-start.3 = (bf16[16,16,256]{2,1,0:T(8,128)(2,1)S(1)}, bf16[16,16,256]{2,1,0:T(8,128)(2,1)S(1)}, u32[]{:S(2)}, u32[]{:S(2)}) collective-permute-start(bf16[16,16,256]{2,1,0:T(8,128)(2,1)S(1)} %collective-permute-done.1.refs_1_), channel_id=1, source_target_pairs={{0,16},{8,24},{16,0},{24,8},{1,17},{9,25},{17,1},{25,9},{2,18},{10... | collective-permute-start | bytes 393224 | tf_op jit(solution)/shard_map/ppermute | solution.py:35
  13.4 29.5 %collective-permute-start.13 = (bf16[512,896]{1,0:T(8,128)(2,1)}, bf16[512,896]{1,0:T(8,128)(2,1)S(1)}, u32[]{:S(2)}, u32[]{:S(2)}) collective-permute-start(bf16[512,896]{1,0:T(8,128)(2,1)} %refs_10_), channel_id=1, source_target_pairs={{0,8},{8,0},{16,24},{24,16},{1,9},{9,1},{17,25},{25,17},{2,10},{10... | collective-permute-start | bytes 2752520 | tf_op jit(solution)/shard_map/ppermute | solution.py:35
  14.9 28.0 %collective-permute-start.14 = (bf16[512,896]{1,0:T(8,128)(2,1)}, bf16[512,896]{1,0:T(8,128)(2,1)S(1)}, u32[]{:S(2)}, u32[]{:S(2)}) collective-permute-start(bf16[512,896]{1,0:T(8,128)(2,1)} %refs_13_), channel_id=1, source_target_pairs={{0,16},{8,24},{16,0},{24,8},{1,17},{9,25},{17,1},{25,9},{2,18},{10... | collective-permute-start | bytes 2752520 | tf_op jit(solution)/shard_map/ppermute | solution.py:35
  19.6 8.1 %collective-permute-start.8 = (bf16[2,128,256]{2,1,0:T(8,128)(2,1)S(1)}, bf16[2,128,256]{2,1,0:T(8,128)(2,1)S(1)}, u32[]{:S(2)}, u32[]{:S(2)}) collective-permute-start(bf16[2,128,256]{2,1,0:T(8,128)(2,1)S(1)} %get-tuple-element.38.refs_6_), channel_id=1, source_target_pairs={{0,6},{1,7},{2,4},{3,5},{4,2},{5,3},{6,0},{7,1},{8,14},{9,15},{10,... | collective-permute-start | bytes 393224 | tf_op jit(solution)/shard_map/ppermute | solution.py:35
  23.9 5.5 %collective-permute-start.6 = (bf16[2,128,256]{2,1,0:T(8,128)(2,1)S(1)}, bf16[2,128,256]{2,1,0:T(8,128)(2,1)S(1)}, u32[]{:S(2)}, u32[]{:S(2)}) collective-permute-start(bf16[2,128,256]{2,1,0:T(8,128)(2,1)S(1)} %get-tuple-element.38.refs_6_), channel_id=1, source_target_pairs={{0,2},{1,3},{2,0},{3,1},{4,6},{5,7},{6,4},{7,5},{8,10},{9,11},{10,... | collective-permute-start | bytes 393224 | tf_op jit(solution)/shard_map/ppermute | solution.py:35
  23.9 8.2 %collective-permute-start.7 = (bf16[2,128,256]{2,1,0:T(8,128)(2,1)S(1)}, bf16[2,128,256]{2,1,0:T(8,128)(2,1)S(1)}, u32[]{:S(2)}, u32[]{:S(2)}) collective-permute-start(bf16[2,128,256]{2,1,0:T(8,128)(2,1)S(1)} %get-tuple-element.38.refs_6_), channel_id=1, source_target_pairs={{0,4},{1,5},{2,6},{3,7},{4,0},{5,1},{6,2},{7,3},{8,12},{9,13},{10,... | collective-permute-start | bytes 393224 | tf_op jit(solution)/shard_map/ppermute | solution.py:35
  32.6 23.0 %collective-permute-start.18 = (bf16[512,896]{1,0:T(8,128)(2,1)}, bf16[512,896]{1,0:T(8,128)(2,1)S(1)}, u32[]{:S(2)}, u32[]{:S(2)}) collective-permute-start(bf16[512,896]{1,0:T(8,128)(2,1)} %refs_10_), channel_id=1, source_target_pairs={{0,16},{8,24},{16,0},{24,8},{1,17},{9,25},{17,1},{25,9},{2,18},{10... | collective-permute-start | bytes 2752520 | tf_op jit(solution)/shard_map/ppermute | solution.py:35
  34.8 22.4 %collective-permute-start.19 = (bf16[512,896]{1,0:T(8,128)(2,1)}, bf16[512,896]{1,0:T(8,128)(2,1)}, u32[]{:S(2)}, u32[]{:S(2)}) collective-permute-start(bf16[512,896]{1,0:T(8,128)(2,1)} %refs_13_), channel_id=1, source_target_pairs={{0,8},{8,0},{16,24},{24,16},{1,9},{9,1},{17,25},{25,17},{2,10},{10... | collective-permute-start | bytes 2752520 | tf_op jit(solution)/shard_map/ppermute | solution.py:35
  45.6 11.6 %collective-permute-start.17 = (bf16[2,128,256]{2,1,0:T(8,128)(2,1)S(1)}, bf16[2,128,256]{2,1,0:T(8,128)(2,1)S(1)}, u32[]{:S(2)}, u32[]{:S(2)}) collective-permute-start(bf16[2,128,256]{2,1,0:T(8,128)(2,1)S(1)} %get-tuple-element.47), channel_id=1, source_target_pairs={{0,4},{1,5},{2,6},{3,7},{4,0},{5,1},{6,2},{7,3},{8,12},{9,13},{10,... | collective-permute-start | bytes 393224 | tf_op jit(solution)/shard_map/ppermute | solution.py:35
  46.6 13.3 %collective-permute-start.16 = (bf16[2,128,256]{2,1,0:T(8,128)(2,1)S(1)}, bf16[2,128,256]{2,1,0:T(8,128)(2,1)S(1)}, u32[]{:S(2)}, u32[]{:S(2)}) collective-permute-start(bf16[2,128,256]{2,1,0:T(8,128)(2,1)S(1)} %get-tuple-element.46), channel_id=1, source_target_pairs={{0,2},{1,3},{2,0},{3,1},{4,6},{5,7},{6,4},{7,5},{8,10},{9,11},{10,... | collective-permute-start | bytes 393224 | tf_op jit(solution)/shard_map/ppermute | solution.py:35
  48.7 11.1 %collective-permute-start.20 = (bf16[2,128,256]{2,1,0:T(8,128)(2,1)S(1)}, bf16[2,128,256]{2,1,0:T(8,128)(2,1)S(1)}, u32[]{:S(2)}, u32[]{:S(2)}) collective-permute-start(bf16[2,128,256]{2,1,0:T(8,128)(2,1)S(1)} %get-tuple-element.53), channel_id=1, source_target_pairs={{0,6},{1,7},{2,4},{3,5},{4,2},{5,3},{6,0},{7,1},{8,14},{9,15},{10,... | collective-permute-start | bytes 393224 | tf_op jit(solution)/shard_map/ppermute | solution.py:35
  57.2 25.2 %collective-permute-start.28 = (bf16[512,896]{1,0:T(8,128)(2,1)S(1)}, bf16[512,896]{1,0:T(8,128)(2,1)S(1)}, u32[]{:S(2)}, u32[]{:S(2)}) collective-permute-start(bf16[512,896]{1,0:T(8,128)(2,1)S(1)} %collective-permute-done.13.refs_11_), channel_id=1, source_target_pairs={{0,16},{8,24},{16,0},{24,8},{1,17},{9,25},{17,1},{25,9},{2,18},{10... | collective-permute-start | bytes 2752520 | tf_op jit(solution)/shard_map/ppermute | solution.py:35
  58.4 24.0 %collective-permute-start.29 = (bf16[512,896]{1,0:T(8,128)(2,1)}, bf16[512,896]{1,0:T(8,128)(2,1)S(1)}, u32[]{:S(2)}, u32[]{:S(2)}) collective-permute-start(bf16[512,896]{1,0:T(8,128)(2,1)} %copy-done), channel_id=1, source_target_pairs={{0,8},{8,0},{16,24},{24,16},{1,9},{9,1},{17,25},{25,17},{2,10},{10... | collective-permute-start | bytes 2752520 | tf_op jit(solution)/shard_map/ppermute | solution.py:35
  59.9 6.2 %collective-permute-start.21 = (bf16[2,128,256]{2,1,0:T(8,128)(2,1)S(1)}, bf16[2,128,256]{2,1,0:T(8,128)(2,1)S(1)}, u32[]{:S(2)}, u32[]{:S(2)}) collective-permute-start(bf16[2,128,256]{2,1,0:T(8,128)(2,1)S(1)} %add_convert_fusion.refs_2_), channel_id=1, source_target_pairs={{0,2},{1,3},{2,0},{3,1},{4,6},{5,7},{6,4},{7,5},{8,10},{9,11},{10,... | collective-permute-start | bytes 393224 | tf_op jit(solution)/shard_map/ppermute | solution.py:35
  61.2 12.7 %collective-permute-start.22 = (bf16[2,128,256]{2,1,0:T(8,128)(2,1)S(1)}, bf16[2,128,256]{2,1,0:T(8,128)(2,1)S(1)}, u32[]{:S(2)}, u32[]{:S(2)}) collective-permute-start(bf16[2,128,256]{2,1,0:T(8,128)(2,1)S(1)} %add_convert_fusion.refs_2_), channel_id=1, source_target_pairs={{0,4},{1,5},{2,6},{3,7},{4,0},{5,1},{6,2},{7,3},{8,12},{9,13},{10,... | collective-permute-start | bytes 393224 | tf_op jit(solution)/shard_map/ppermute | solution.py:35
  63.5 10.4 %collective-permute-start.23 = (bf16[2,128,256]{2,1,0:T(8,128)(2,1)S(1)}, bf16[2,128,256]{2,1,0:T(8,128)(2,1)S(1)}, u32[]{:S(2)}, u32[]{:S(2)}) collective-permute-start(bf16[2,128,256]{2,1,0:T(8,128)(2,1)S(1)} %add_convert_fusion.refs_2_), channel_id=1, source_target_pairs={{0,6},{1,7},{2,4},{3,5},{4,2},{5,3},{6,0},{7,1},{8,14},{9,15},{10,... | collective-permute-start | bytes 393224 | tf_op jit(solution)/shard_map/ppermute | solution.py:35
  66.1 8.3 %collective-permute-start.24 = (bf16[2,128,256]{2,1,0:T(8,128)(2,1)S(1)}, bf16[2,128,256]{2,1,0:T(8,128)(2,1)S(1)}, u32[]{:S(2)}, u32[]{:S(2)}) collective-permute-start(bf16[2,128,256]{2,1,0:T(8,128)(2,1)S(1)} %add_convert_fusion.refs_2_), channel_id=1, source_target_pairs={{0,1},{1,0},{2,3},{3,2},{4,5},{5,4},{6,7},{7,6},{8,9},{9,8},{10,11... | collective-permute-start | bytes 393224 | tf_op jit(solution)/shard_map/ppermute | solution.py:35
  85.4 5.5 %collective-permute-start.31 = (f32[8,128]{1,0:T(8,128)S(1)}, f32[8,128]{1,0:T(8,128)S(1)}, u32[]{:S(2)}, u32[]{:S(2)}) collective-permute-start(f32[8,128]{1,0:T(8,128)S(1)} %shard_map.164.refs_0_), channel_id=1, source_target_pairs={{0,6},{1,7},{2,4},{3,5},{4,2},{5,3},{6,0},{7,1},{8,14},{9,15},{10,... | collective-permute-start | bytes 12296 | tf_op jit(solution)/shard_map/ppermute | solution.py:35
  87.7 4.5 %collective-permute-start.32 = (f32[8,128]{1,0:T(8,128)S(1)}, f32[8,128]{1,0:T(8,128)S(1)}, u32[]{:S(2)}, u32[]{:S(2)}) collective-permute-start(f32[8,128]{1,0:T(8,128)S(1)} %shard_map.164.refs_0_), channel_id=1, source_target_pairs={{0,4},{1,5},{2,6},{3,7},{4,0},{5,1},{6,2},{7,3},{8,12},{9,13},{10,... | collective-permute-start | bytes 12296 | tf_op jit(solution)/shard_map/ppermute | solution.py:35
  (21 other events, 69.6 us)

commit v11 on v10

--- a/solution.py
+++ b/solution.py
@@ -302,7 +302,7 @@
             blocks[place], values = lax.optimization_barrier((blocks[place], values))
             blocks.update(zip(passed, values))
         spread_step(hiddens, step, lambda m, k: 0 < k and not k & bit_orders[m][step])
-    early = [(0, b) for b in bits] + [(1, bit_orders[1][0])]
+    early = [(m, b) for m in range(2) for b in bits]
     values = wait_for([hiddens[m][b] for m, b in early], lambda m, k: True)
     for (m, b), value in zip(early, values):
         hiddens[m][b] = value
@@ -371,7 +371,7 @@
             pltpu.SemaphoreType.DMA((6,)),
         ],
         far=range(1, 7),
-        mib=22,
+        mib=15,
     )
     send = wait_for(send, lambda m, k: k > 0)
     came = exchange(send, "mp", 1)
@@ -419,7 +419,7 @@
             pltpu.SemaphoreType.DMA((4,)),
         ],
         far=(1, 2, 3 + mp, 2 + mp + dp),
-        mib=14,
+        mib=8,
     )
     stats = call(
         finish_kernel,

time: 100 us -> 100 us (level)
  starting transfers between devices: 40 us -> 41 us
  waiting for transfers between devices: 35.4 us -> 34.4 us
    ppermute x37, waiting for transfers between devices: 35.4 us -> 34.4 us  [exchange(): return lax.ppermute(values, axis, [(i, i ^ flip) for i in range(count)])]
    ppermute x37, starting transfers between devices: 40 us -> 41 us  [exchange(): return lax.ppermute(values, axis, [(i, i ^ flip) for i in range(count)])]
where the time goes in v11:
time: 100 us; the launch traced here: 99.7 us
  starting transfers between devices  41 us (41%)
  waiting for transfers between devices  34.4 us (34%)
  Pallas kernels  15.2 us (15%)
  local copies, waits for them, and re-layouts  6.15 us (6%)
  other arithmetic  2.05 us (2%)
    ppermute x37, starting transfers between devices, exchange(): return lax.ppermute(values, axis, [(i, i ^ flip) for i in range(count)])  41 us
    ppermute x37, waiting for transfers between devices, exchange(): return lax.ppermute(values, axis, [(i, i ^ flip) for i in range(count)])  34.4 us
    pallas_call x8, Pallas kernels, call(): pl.pallas_call(kernel, out_shape=out_shape, in_specs=specs, out_specs=jax...  15.2 us
    unnamed x16, local copies, waits for them, and re-layouts  5.48 us
  transfers between devices with their start and end apart: 37, of which 20 were waited for; matrix products, arithmetic and copies ran while one was open for 2% of the time, Pallas kernels for 12%

profile of v11, /device:TPU:0, one launch (start us, length us, event | category | flops | bytes accessed | tf_op | source)
XLA Modules:
  0.0 99.7 jit_solution(13852962720522195279)
XLA Ops:
  1.6 3.0 %collective-permute-start.3 = (bf16[17,16,256]{2,1,0:T(8,128)(2,1)S(1)}, bf16[17,16,256]{2,1,0:T(8,128)(2,1)S(1)}, u32[]{:S(2)}, u32[]{:S(2)}) collective-permute-start(bf16[17,16,256]{2,1,0:T(8,128)(2,1)S(1)} %shard_map.158.refs_4_), channel_id=1, source_target_pairs={{0,16},{8,24},{16,0},{24,8},{1,17},{9,25},{17,1},{25,9},{2,18},{10... | collective-permute-start | bytes 417800 | tf_op jit(solution)/shard_map/ppermute | solution.py:35
  4.7 1.9 %collective-permute-start.1 = (bf16[16,16,256]{2,1,0:T(8,128)(2,1)}, bf16[16,16,256]{2,1,0:T(8,128)(2,1)S(1)}, u32[]{:S(2)}, u32[]{:S(2)}) collective-permute-start(bf16[16,16,256]{2,1,0:T(8,128)(2,1)} %refs_0_.1), channel_id=1, source_target_pairs={{0,8},{8,0},{16,24},{24,16},{1,9},{9,1},{17,25},{25,17},{2,10},{10... | collective-permute-start | bytes 393224 | tf_op jit(solution)/shard_map/ppermute | solution.py:35
  6.7 2.4 %collective-permute-done.3.refs_6_ = bf16[17,16,256]{2,1,0:T(8,128)(2,1)S(1)} collective-permute-done((bf16[17,16,256]{2,1,0:T(8,128)(2,1)S(1)}, bf16[17,16,256]{2,1,0:T(8,128)(2,1)S(1)}, u32[]{:S(2)}, u32[]{:S(2)}) %collective-permute-start.3) | collective-permute-done | bytes 139296 | tf_op jit(solution)/shard_map/ppermute | solution.py:35
  9.1 2.0 %collective-permute-start.5 = (bf16[17,16,256]{2,1,0:T(8,128)(2,1)S(1)}, bf16[17,16,256]{2,1,0:T(8,128)(2,1)S(1)}, u32[]{:S(2)}, u32[]{:S(2)}) collective-permute-start(bf16[17,16,256]{2,1,0:T(8,128)(2,1)S(1)} %collective-permute-done.3.refs_6_), channel_id=1, source_target_pairs={{0,8},{8,0},{16,24},{24,16},{1,9},{9,1},{17,25},{25,17},{2,10},{10... | collective-permute-start | bytes 417800 | tf_op jit(solution)/shard_map/ppermute | solution.py:35
  11.3 2.0 %collective-permute-start.4 = (bf16[16,16,256]{2,1,0:T(8,128)(2,1)S(1)}, bf16[16,16,256]{2,1,0:T(8,128)(2,1)S(1)}, u32[]{:S(2)}, u32[]{:S(2)}) collective-permute-start(bf16[16,16,256]{2,1,0:T(8,128)(2,1)S(1)} %collective-permute-done.1.refs_1_), channel_id=1, source_target_pairs={{0,16},{8,24},{16,0},{24,8},{1,17},{9,25},{17,1},{25,9},{2,18},{10... | collective-permute-start | bytes 393224 | tf_op jit(solution)/shard_map/ppermute | solution.py:35
  14.3 1.7 %collective-permute-start.13 = (bf16[512,896]{1,0:T(8,128)(2,1)}, bf16[512,896]{1,0:T(8,128)(2,1)S(1)}, u32[]{:S(2)}, u32[]{:S(2)}) collective-permute-start(bf16[512,896]{1,0:T(8,128)(2,1)} %refs_10_), channel_id=1, source_target_pairs={{0,8},{8,0},{16,24},{24,16},{1,9},{9,1},{17,25},{25,17},{2,10},{10... | collective-permute-start | bytes 2752520 | tf_op jit(solution)/shard_map/ppermute | solution.py:35
  16.0 1.8 %collective-permute-start.14 = (bf16[512,896]{1,0:T(8,128)(2,1)}, bf16[512,896]{1,0:T(8,128)(2,1)S(1)}, u32[]{:S(2)}, u32[]{:S(2)}) collective-permute-start(bf16[512,896]{1,0:T(8,128)(2,1)} %refs_13_), channel_id=1, source_target_pairs={{0,16},{8,24},{16,0},{24,8},{1,17},{9,25},{17,1},{25,9},{2,18},{10... | collective-permute-start | bytes 2752520 | tf_op jit(solution)/shard_map/ppermute | solution.py:35
  17.8 1.8 %shard_map.159 = (bf16[2,128,256]{2,1,0:T(8,128)(2,1)S(1)}, f32[4,16,256]{2,1,0:T(8,128)S(1)}) custom-call(s32[4]{0:T(128)S(1)} %pad_add_fusion.ids, s32[64]{0:T(128)} %plan_far.1, bf16[16,16,256]{2,1,0:T(8,128)(2,1)} %refs_0_.1, bf16[16,16,256]{2,1,0:T(8,128)(2,1)S(1)} %collective-permute-done.1.refs_1_, ...), custom_call_target="tpu_custom_call" | custom-call | flops 10000000000 | tf_op jit(solution)/shard_map/pallas_call | solution.py:22
  20.2 3.7 %collective-permute-start.8 = (bf16[2,128,256]{2,1,0:T(8,128)(2,1)S(1)}, bf16[2,128,256]{2,1,0:T(8,128)(2,1)S(1)}, u32[]{:S(2)}, u32[]{:S(2)}) collective-permute-start(bf16[2,128,256]{2,1,0:T(8,128)(2,1)S(1)} %get-tuple-element.40.refs_6_), channel_id=1, source_target_pairs={{0,6},{1,7},{2,4},{3,5},{4,2},{5,3},{6,0},{7,1},{8,14},{9,15},{10,... | collective-permute-start | bytes 393224 | tf_op jit(solution)/shard_map/ppermute | solution.py:35
  24.6 3.2 %collective-permute-done.8.refs_9_ = bf16[2,128,256]{2,1,0:T(8,128)(2,1)S(1)} collective-permute-done((bf16[2,128,256]{2,1,0:T(8,128)(2,1)S(1)}, bf16[2,128,256]{2,1,0:T(8,128)(2,1)S(1)}, u32[]{:S(2)}, u32[]{:S(2)}) %collective-permute-start.8) | collective-permute-done | bytes 131104 | tf_op jit(solution)/shard_map/ppermute | solution.py:35
  27.8 1.6 %collective-permute-done.6.refs_7_ = bf16[2,128,256]{2,1,0:T(8,128)(2,1)S(1)} collective-permute-done((bf16[2,128,256]{2,1,0:T(8,128)(2,1)S(1)}, bf16[2,128,256]{2,1,0:T(8,128)(2,1)S(1)}, u32[]{:S(2)}, u32[]{:S(2)}) %collective-permute-start.6) | collective-permute-done | bytes 131104 | tf_op jit(solution)/shard_map/ppermute | solution.py:35
  29.3 2.8 %collective-permute-done.7.refs_8_ = bf16[2,128,256]{2,1,0:T(8,128)(2,1)S(1)} collective-permute-done((bf16[2,128,256]{2,1,0:T(8,128)(2,1)S(1)}, bf16[2,128,256]{2,1,0:T(8,128)(2,1)S(1)}, u32[]{:S(2)}, u32[]{:S(2)}) %collective-permute-start.7) | collective-permute-done | bytes 131104 | tf_op jit(solution)/shard_map/ppermute | solution.py:35
  32.6 1.5 %collective-permute-start.18 = (bf16[512,896]{1,0:T(8,128)(2,1)}, bf16[512,896]{1,0:T(8,128)(2,1)S(1)}, u32[]{:S(2)}, u32[]{:S(2)}) collective-permute-start(bf16[512,896]{1,0:T(8,128)(2,1)} %refs_10_), channel_id=1, source_target_pairs={{0,16},{8,24},{16,0},{24,8},{1,17},{9,25},{17,1},{25,9},{2,18},{10... | collective-permute-start | bytes 2752520 | tf_op jit(solution)/shard_map/ppermute | solution.py:35
  34.8 1.5 %collective-permute-start.19 = (bf16[512,896]{1,0:T(8,128)(2,1)}, bf16[512,896]{1,0:T(8,128)(2,1)}, u32[]{:S(2)}, u32[]{:S(2)}) collective-permute-start(bf16[512,896]{1,0:T(8,128)(2,1)} %refs_13_), channel_id=1, source_target_pairs={{0,8},{8,0},{16,24},{24,16},{1,9},{9,1},{17,25},{25,17},{2,10},{10... | collective-permute-start | bytes 2752520 | tf_op jit(solution)/shard_map/ppermute | solution.py:35
  37.5 5.4 %shard_map.160 = (f32[4,2,128,256]{3,2,1,0:T(8,128)S(1)}, bf16[4,2,128,256]{3,2,1,0:T(8,128)(2,1)S(1)}) custom-call(s32[4]{0:T(128)S(1)} %pad_add_fusion.ids, f32[8,1,256]{2,1,0:T(1,128)} %bitcast.13, f32[8,1,256]{2,1,0:T(1,128)} %bitcast.14, bf16[2048,512]{1,0:T(8,128)(2,1)} %refs_2_.1, bf16[2048,512]{1,0:T(8,128)(2,1)} %refs_3_.1, ...), custom_call_target="tpu_custom_call" | custom-call | tf_op jit(solution)/shard_map/pallas_call | solution.py:22
  43.1 1.8 %collective-permute-done.15.came = bf16[4,2,128,256]{3,2,1,0:T(8,128)(2,1)S(1)} collective-permute-done((bf16[4,2,128,256]{3,2,1,0:T(8,128)(2,1)S(1)}, bf16[4,2,128,256]{3,2,1,0:T(8,128)(2,1)S(1)}, u32[]{:S(2)}, u32[]{:S(2)}) %collective-permute-start.15) | collective-permute-done | bytes 524320 | tf_op jit(solution)/shard_map/ppermute | solution.py:35
  46.4 2.3 %collective-permute-start.16 = (bf16[2,128,256]{2,1,0:T(8,128)(2,1)S(1)}, bf16[2,128,256]{2,1,0:T(8,128)(2,1)S(1)}, u32[]{:S(2)}, u32[]{:S(2)}) collective-permute-start(bf16[2,128,256]{2,1,0:T(8,128)(2,1)S(1)} %get-tuple-element.48), channel_id=1, source_target_pairs={{0,2},{1,3},{2,0},{3,1},{4,6},{5,7},{6,4},{7,5},{8,10},{9,11},{10,... | collective-permute-start | bytes 393224 | tf_op jit(solution)/shard_map/ppermute | solution.py:35
  50.0 5.6 %collective-permute-done.18.refs_12_ = bf16[512,896]{1,0:T(8,128)(2,1)S(1)} collective-permute-done((bf16[512,896]{1,0:T(8,128)(2,1)}, bf16[512,896]{1,0:T(8,128)(2,1)S(1)}, u32[]{:S(2)}, u32[]{:S(2)}) %collective-permute-start.18) | collective-permute-done | bytes 917536 | tf_op jit(solution)/shard_map/ppermute | solution.py:35
  61.2 2.4 %collective-permute-start.22 = (bf16[2,128,256]{2,1,0:T(8,128)(2,1)S(1)}, bf16[2,128,256]{2,1,0:T(8,128)(2,1)S(1)}, u32[]{:S(2)}, u32[]{:S(2)}) collective-permute-start(bf16[2,128,256]{2,1,0:T(8,128)(2,1)S(1)} %add_convert_fusion.refs_2_), channel_id=1, source_target_pairs={{0,4},{1,5},{2,6},{3,7},{4,0},{5,1},{6,2},{7,3},{8,12},{9,13},{10,... | collective-permute-start | bytes 393224 | tf_op jit(solution)/shard_map/ppermute | solution.py:35
  66.1 7.6 %collective-permute-done.22.refs_4_ = bf16[2,128,256]{2,1,0:T(8,128)(2,1)S(1)} collective-permute-done((bf16[2,128,256]{2,1,0:T(8,128)(2,1)S(1)}, bf16[2,128,256]{2,1,0:T(8,128)(2,1)S(1)}, u32[]{:S(2)}, u32[]{:S(2)}) %collective-permute-start.22) | collective-permute-done | bytes 131104 | tf_op jit(solution)/shard_map/ppermute | solution.py:35
  78.1 4.1 %shard_map.162 = (f32[2,128,896]{2,1,0:T(8,128)S(1)}, bf16[2,128,512]{2,1,0:T(8,128)(2,1)S(1)}) custom-call(s32[4]{0:T(128)S(1)} %pad_add_fusion.ids, f32[8,1,256]{2,1,0:T(1,128)} %bitcast.15, f32[8,1,256]{2,1,0:T(1,128)} %bitcast.16, bf16[2,128,256]{2,1,0:T(8,128)(2,1)S(1)} %add_convert_fusion.refs_2_, ...), custom_call_target="tpu_custom_call" | custom-call | tf_op jit(solution)/shard_map/pallas_call | solution.py:22
  85.2 2.4 %collective-permute-start.31 = (f32[8,128]{1,0:T(8,128)S(1)}, f32[8,128]{1,0:T(8,128)S(1)}, u32[]{:S(2)}, u32[]{:S(2)}) collective-permute-start(f32[8,128]{1,0:T(8,128)S(1)} %shard_map.164.refs_0_), channel_id=1, source_target_pairs={{0,6},{1,7},{2,4},{3,5},{4,2},{5,3},{6,0},{7,1},{8,14},{9,15},{10,... | collective-permute-start | bytes 12296 | tf_op jit(solution)/shard_map/ppermute | solution.py:35
  90.7 1.5 %collective-permute-done.32.refs_2_ = f32[8,128]{1,0:T(8,128)S(1)} collective-permute-done((f32[8,128]{1,0:T(8,128)S(1)}, f32[8,128]{1,0:T(8,128)S(1)}, u32[]{:S(2)}, u32[]{:S(2)}) %collective-permute-start.32) | collective-permute-done | bytes 4128 | tf_op jit(solution)/shard_map/ppermute | solution.py:35
  95.2 1.5 %collective-permute-start.36 = (f32[1,128]{1,0:T(1,128)S(1)}, f32[1,128]{1,0:T(1,128)S(1)}, u32[]{:S(2)}, u32[]{:S(2)}) collective-permute-start(f32[1,128]{1,0:T(1,128)S(1)} %shard_map.165), channel_id=1, source_target_pairs={{0,8},{8,0},{16,24},{24,16},{1,9},{9,1},{17,25},{25,17},{2,10},{10... | collective-permute-start | bytes 1544 | tf_op jit(solution)/shard_map/ppermute | solution.py:35
  (99 shorter events, 33.5 us)
Async XLA Ops:
  1.6 7.5 %collective-permute-start.3 = (bf16[17,16,256]{2,1,0:T(8,128)(2,1)S(1)}, bf16[17,16,256]{2,1,0:T(8,128)(2,1)S(1)}, u32[]{:S(2)}, u32[]{:S(2)}) collective-permute-start(bf16[17,16,256]{2,1,0:T(8,128)(2,1)S(1)} %shard_map.158.refs_4_), channel_id=1, source_target_pairs={{0,16},{8,24},{16,0},{24,8},{1,17},{9,25},{17,1},{25,9},{2,18},{10... | collective-permute-start | bytes 417800 | tf_op jit(solution)/shard_map/ppermute | solution.py:35
  4.6 6.5 %collective-permute-start = (bf16[16,16,256]{2,1,0:T(8,128)(2,1)}, bf16[16,16,256]{2,1,0:T(8,128)(2,1)S(1)}, u32[]{:S(2)}, u32[]{:S(2)}) collective-permute-start(bf16[16,16,256]{2,1,0:T(8,128)(2,1)} %refs_0_.1), channel_id=1, source_target_pairs={{0,16},{8,24},{16,0},{24,8},{1,17},{9,25},{17,1},{25,9},{2,18},{10... | collective-permute-start | bytes 393224 | tf_op jit(solution)/shard_map/ppermute | solution.py:35
  4.7 6.6 %collective-permute-start.1 = (bf16[16,16,256]{2,1,0:T(8,128)(2,1)}, bf16[16,16,256]{2,1,0:T(8,128)(2,1)S(1)}, u32[]{:S(2)}, u32[]{:S(2)}) collective-permute-start(bf16[16,16,256]{2,1,0:T(8,128)(2,1)} %refs_0_.1), channel_id=1, source_target_pairs={{0,8},{8,0},{16,24},{24,16},{1,9},{9,1},{17,25},{25,17},{2,10},{10... | collective-permute-start | bytes 393224 | tf_op jit(solution)/shard_map/ppermute | solution.py:35
  6.6 7.7 %collective-permute-start.2 = (bf16[17,16,256]{2,1,0:T(8,128)(2,1)S(1)}, bf16[17,16,256]{2,1,0:T(8,128)(2,1)S(1)}, u32[]{:S(2)}, u32[]{:S(2)}) collective-permute-start(bf16[17,16,256]{2,1,0:T(8,128)(2,1)S(1)} %shard_map.158.refs_4_), channel_id=1, source_target_pairs={{0,8},{8,0},{16,24},{24,16},{1,9},{9,1},{17,25},{25,17},{2,10},{10... | collective-permute-start | bytes 417800 | tf_op jit(solution)/shard_map/ppermute | solution.py:35
  9.1 8.7 %collective-permute-start.5 = (bf16[17,16,256]{2,1,0:T(8,128)(2,1)S(1)}, bf16[17,16,256]{2,1,0:T(8,128)(2,1)S(1)}, u32[]{:S(2)}, u32[]{:S(2)}) collective-permute-start(bf16[17,16,256]{2,1,0:T(8,128)(2,1)S(1)} %collective-permute-done.3.refs_6_), channel_id=1, source_target_pairs={{0,8},{8,0},{16,24},{24,16},{1,9},{9,1},{17,25},{25,17},{2,10},{10... | collective-permute-start | bytes 417800 | tf_op jit(solution)/shard_map/ppermute | solution.py:35
  11.3 6.4 %collective-permute-start.4 = (bf16[16,16,256]{2,1,0:T(8,128)(2,1)S(1)}, bf16[16,16,256]{2,1,0:T(8,128)(2,1)S(1)}, u32[]{:S(2)}, u32[]{:S(2)}) collective-permute-start(bf16[16,16,256]{2,1,0:T(8,128)(2,1)S(1)} %collective-permute-done.1.refs_1_), channel_id=1, source_target_pairs={{0,16},{8,24},{16,0},{24,8},{1,17},{9,25},{17,1},{25,9},{2,18},{10... | collective-permute-start | bytes 393224 | tf_op jit(solution)/shard_map/ppermute | solution.py:35
  14.3 28.6 %collective-permute-start.13 = (bf16[512,896]{1,0:T(8,128)(2,1)}, bf16[512,896]{1,0:T(8,128)(2,1)S(1)}, u32[]{:S(2)}, u32[]{:S(2)}) collective-permute-start(bf16[512,896]{1,0:T(8,128)(2,1)} %refs_10_), channel_id=1, source_target_pairs={{0,8},{8,0},{16,24},{24,16},{1,9},{9,1},{17,25},{25,17},{2,10},{10... | collective-permute-start | bytes 2752520 | tf_op jit(solution)/shard_map/ppermute | solution.py:35
  16.0 26.9 %collective-permute-start.14 = (bf16[512,896]{1,0:T(8,128)(2,1)}, bf16[512,896]{1,0:T(8,128)(2,1)S(1)}, u32[]{:S(2)}, u32[]{:S(2)}) collective-permute-start(bf16[512,896]{1,0:T(8,128)(2,1)} %refs_13_), channel_id=1, source_target_pairs={{0,16},{8,24},{16,0},{24,8},{1,17},{9,25},{17,1},{25,9},{2,18},{10... | collective-permute-start | bytes 2752520 | tf_op jit(solution)/shard_map/ppermute | solution.py:35
  20.2 7.6 %collective-permute-start.8 = (bf16[2,128,256]{2,1,0:T(8,128)(2,1)S(1)}, bf16[2,128,256]{2,1,0:T(8,128)(2,1)S(1)}, u32[]{:S(2)}, u32[]{:S(2)}) collective-permute-start(bf16[2,128,256]{2,1,0:T(8,128)(2,1)S(1)} %get-tuple-element.40.refs_6_), channel_id=1, source_target_pairs={{0,6},{1,7},{2,4},{3,5},{4,2},{5,3},{6,0},{7,1},{8,14},{9,15},{10,... | collective-permute-start | bytes 393224 | tf_op jit(solution)/shard_map/ppermute | solution.py:35
  23.9 5.5 %collective-permute-start.6 = (bf16[2,128,256]{2,1,0:T(8,128)(2,1)S(1)}, bf16[2,128,256]{2,1,0:T(8,128)(2,1)S(1)}, u32[]{:S(2)}, u32[]{:S(2)}) collective-permute-start(bf16[2,128,256]{2,1,0:T(8,128)(2,1)S(1)} %get-tuple-element.40.refs_6_), channel_id=1, source_target_pairs={{0,2},{1,3},{2,0},{3,1},{4,6},{5,7},{6,4},{7,5},{8,10},{9,11},{10,... | collective-permute-start | bytes 393224 | tf_op jit(solution)/shard_map/ppermute | solution.py:35
  23.9 8.2 %collective-permute-start.7 = (bf16[2,128,256]{2,1,0:T(8,128)(2,1)S(1)}, bf16[2,128,256]{2,1,0:T(8,128)(2,1)S(1)}, u32[]{:S(2)}, u32[]{:S(2)}) collective-permute-start(bf16[2,128,256]{2,1,0:T(8,128)(2,1)S(1)} %get-tuple-element.40.refs_6_), channel_id=1, source_target_pairs={{0,4},{1,5},{2,6},{3,7},{4,0},{5,1},{6,2},{7,3},{8,12},{9,13},{10,... | collective-permute-start | bytes 393224 | tf_op jit(solution)/shard_map/ppermute | solution.py:35
  32.6 23.0 %collective-permute-start.18 = (bf16[512,896]{1,0:T(8,128)(2,1)}, bf16[512,896]{1,0:T(8,128)(2,1)S(1)}, u32[]{:S(2)}, u32[]{:S(2)}) collective-permute-start(bf16[512,896]{1,0:T(8,128)(2,1)} %refs_10_), channel_id=1, source_target_pairs={{0,16},{8,24},{16,0},{24,8},{1,17},{9,25},{17,1},{25,9},{2,18},{10... | collective-permute-start | bytes 2752520 | tf_op jit(solution)/shard_map/ppermute | solution.py:35
  34.8 22.4 %collective-permute-start.19 = (bf16[512,896]{1,0:T(8,128)(2,1)}, bf16[512,896]{1,0:T(8,128)(2,1)}, u32[]{:S(2)}, u32[]{:S(2)}) collective-permute-start(bf16[512,896]{1,0:T(8,128)(2,1)} %refs_13_), channel_id=1, source_target_pairs={{0,8},{8,0},{16,24},{24,16},{1,9},{9,1},{17,25},{25,17},{2,10},{10... | collective-permute-start | bytes 2752520 | tf_op jit(solution)/shard_map/ppermute | solution.py:35
  45.6 11.6 %collective-permute-start.17 = (bf16[2,128,256]{2,1,0:T(8,128)(2,1)S(1)}, bf16[2,128,256]{2,1,0:T(8,128)(2,1)S(1)}, u32[]{:S(2)}, u32[]{:S(2)}) collective-permute-start(bf16[2,128,256]{2,1,0:T(8,128)(2,1)S(1)} %get-tuple-element.49), channel_id=1, source_target_pairs={{0,4},{1,5},{2,6},{3,7},{4,0},{5,1},{6,2},{7,3},{8,12},{9,13},{10,... | collective-permute-start | bytes 393224 | tf_op jit(solution)/shard_map/ppermute | solution.py:35
  46.4 13.4 %collective-permute-start.16 = (bf16[2,128,256]{2,1,0:T(8,128)(2,1)S(1)}, bf16[2,128,256]{2,1,0:T(8,128)(2,1)S(1)}, u32[]{:S(2)}, u32[]{:S(2)}) collective-permute-start(bf16[2,128,256]{2,1,0:T(8,128)(2,1)S(1)} %get-tuple-element.48), channel_id=1, source_target_pairs={{0,2},{1,3},{2,0},{3,1},{4,6},{5,7},{6,4},{7,5},{8,10},{9,11},{10,... | collective-permute-start | bytes 393224 | tf_op jit(solution)/shard_map/ppermute | solution.py:35
  48.7 11.1 %collective-permute-start.20 = (bf16[2,128,256]{2,1,0:T(8,128)(2,1)S(1)}, bf16[2,128,256]{2,1,0:T(8,128)(2,1)S(1)}, u32[]{:S(2)}, u32[]{:S(2)}) collective-permute-start(bf16[2,128,256]{2,1,0:T(8,128)(2,1)S(1)} %get-tuple-element.55), channel_id=1, source_target_pairs={{0,6},{1,7},{2,4},{3,5},{4,2},{5,3},{6,0},{7,1},{8,14},{9,15},{10,... | collective-permute-start | bytes 393224 | tf_op jit(solution)/shard_map/ppermute | solution.py:35
  57.2 25.0 %collective-permute-start.28 = (bf16[512,896]{1,0:T(8,128)(2,1)S(1)}, bf16[512,896]{1,0:T(8,128)(2,1)S(1)}, u32[]{:S(2)}, u32[]{:S(2)}) collective-permute-start(bf16[512,896]{1,0:T(8,128)(2,1)S(1)} %collective-permute-done.13.refs_11_), channel_id=1, source_target_pairs={{0,16},{8,24},{16,0},{24,8},{1,17},{9,25},{17,1},{25,9},{2,18},{10... | collective-permute-start | bytes 2752520 | tf_op jit(solution)/shard_map/ppermute | solution.py:35
  58.6 23.6 %collective-permute-start.29 = (bf16[512,896]{1,0:T(8,128)(2,1)}, bf16[512,896]{1,0:T(8,128)(2,1)S(1)}, u32[]{:S(2)}, u32[]{:S(2)}) collective-permute-start(bf16[512,896]{1,0:T(8,128)(2,1)} %copy-done), channel_id=1, source_target_pairs={{0,8},{8,0},{16,24},{24,16},{1,9},{9,1},{17,25},{25,17},{2,10},{10... | collective-permute-start | bytes 2752520 | tf_op jit(solution)/shard_map/ppermute | solution.py:35
  59.9 5.8 %collective-permute-start.21 = (bf16[2,128,256]{2,1,0:T(8,128)(2,1)S(1)}, bf16[2,128,256]{2,1,0:T(8,128)(2,1)S(1)}, u32[]{:S(2)}, u32[]{:S(2)}) collective-permute-start(bf16[2,128,256]{2,1,0:T(8,128)(2,1)S(1)} %add_convert_fusion.refs_2_), channel_id=1, source_target_pairs={{0,2},{1,3},{2,0},{3,1},{4,6},{5,7},{6,4},{7,5},{8,10},{9,11},{10,... | collective-permute-start | bytes 393224 | tf_op jit(solution)/shard_map/ppermute | solution.py:35
  61.2 12.5 %collective-permute-start.22 = (bf16[2,128,256]{2,1,0:T(8,128)(2,1)S(1)}, bf16[2,128,256]{2,1,0:T(8,128)(2,1)S(1)}, u32[]{:S(2)}, u32[]{:S(2)}) collective-permute-start(bf16[2,128,256]{2,1,0:T(8,128)(2,1)S(1)} %add_convert_fusion.refs_2_), channel_id=1, source_target_pairs={{0,4},{1,5},{2,6},{3,7},{4,0},{5,1},{6,2},{7,3},{8,12},{9,13},{10,... | collective-permute-start | bytes 393224 | tf_op jit(solution)/shard_map/ppermute | solution.py:35
  63.6 10.1 %collective-permute-start.23 = (bf16[2,128,256]{2,1,0:T(8,128)(2,1)S(1)}, bf16[2,128,256]{2,1,0:T(8,128)(2,1)S(1)}, u32[]{:S(2)}, u32[]{:S(2)}) collective-permute-start(bf16[2,128,256]{2,1,0:T(8,128)(2,1)S(1)} %add_convert_fusion.refs_2_), channel_id=1, source_target_pairs={{0,6},{1,7},{2,4},{3,5},{4,2},{5,3},{6,0},{7,1},{8,14},{9,15},{10,... | collective-permute-start | bytes 393224 | tf_op jit(solution)/shard_map/ppermute | solution.py:35
  65.7 8.5 %collective-permute-start.24 = (bf16[2,128,256]{2,1,0:T(8,128)(2,1)S(1)}, bf16[2,128,256]{2,1,0:T(8,128)(2,1)S(1)}, u32[]{:S(2)}, u32[]{:S(2)}) collective-permute-start(bf16[2,128,256]{2,1,0:T(8,128)(2,1)S(1)} %add_convert_fusion.refs_2_), channel_id=1, source_target_pairs={{0,1},{1,0},{2,3},{3,2},{4,5},{5,4},{6,7},{7,6},{8,9},{9,8},{10,11... | collective-permute-start | bytes 393224 | tf_op jit(solution)/shard_map/ppermute | solution.py:35
  85.2 5.5 %collective-permute-start.31 = (f32[8,128]{1,0:T(8,128)S(1)}, f32[8,128]{1,0:T(8,128)S(1)}, u32[]{:S(2)}, u32[]{:S(2)}) collective-permute-start(f32[8,128]{1,0:T(8,128)S(1)} %shard_map.164.refs_0_), channel_id=1, source_target_pairs={{0,6},{1,7},{2,4},{3,5},{4,2},{5,3},{6,0},{7,1},{8,14},{9,15},{10,... | collective-permute-start | bytes 12296 | tf_op jit(solution)/shard_map/ppermute | solution.py:35
  87.6 4.5 %collective-permute-start.32 = (f32[8,128]{1,0:T(8,128)S(1)}, f32[8,128]{1,0:T(8,128)S(1)}, u32[]{:S(2)}, u32[]{:S(2)}) collective-permute-start(f32[8,128]{1,0:T(8,128)S(1)} %shard_map.164.refs_0_), channel_id=1, source_target_pairs={{0,4},{1,5},{2,6},{3,7},{4,0},{5,1},{6,2},{7,3},{8,12},{9,13},{10,... | collective-permute-start | bytes 12296 | tf_op jit(solution)/shard_map/ppermute | solution.py:35
  (21 other events, 69.5 us)

commit v12 on v10

--- a/solution.py
+++ b/solution.py
@@ -302,7 +302,7 @@
             blocks[place], values = lax.optimization_barrier((blocks[place], values))
             blocks.update(zip(passed, values))
         spread_step(hiddens, step, lambda m, k: 0 < k and not k & bit_orders[m][step])
-    early = [(0, b) for b in bits] + [(1, bit_orders[1][0])]
+    early = [(m, b) for m in range(2) for b in bits]
     values = wait_for([hiddens[m][b] for m, b in early], lambda m, k: True)
     for (m, b), value in zip(early, values):
         hiddens[m][b] = value

time: 100 us -> 100 us (level)
  starting transfers between devices: 40 us -> 41 us
  waiting for transfers between devices: 35.4 us -> 34.4 us
    ppermute x37, waiting for transfers between devices: 35.4 us -> 34.4 us  [exchange(): return lax.ppermute(values, axis, [(i, i ^ flip) for i in range(count)])]
    ppermute x37, starting transfers between devices: 40 us -> 41 us  [exchange(): return lax.ppermute(values, axis, [(i, i ^ flip) for i in range(count)])]
where the time goes in v12:
time: 100 us; the launch traced here: 99.7 us
  starting transfers between devices  41 us (41%)
  waiting for transfers between devices  34.4 us (34%)
  Pallas kernels  15.2 us (15%)
  local copies, waits for them, and re-layouts  6.15 us (6%)
  other arithmetic  2.05 us (2%)
    ppermute x37, starting transfers between devices, exchange(): return lax.ppermute(values, axis, [(i, i ^ flip) for i in range(count)])  41 us
    ppermute x37, waiting for transfers between devices, exchange(): return lax.ppermute(values, axis, [(i, i ^ flip) for i in range(count)])  34.4 us
    pallas_call x8, Pallas kernels, call(): pl.pallas_call(kernel, out_shape=out_shape, in_specs=specs, out_specs=jax...  15.2 us
    unnamed x16, local copies, waits for them, and re-layouts  5.48 us
  transfers between devices with their start and end apart: 37, of which 20 were waited for; matrix products, arithmetic and copies ran while one was open for 2% of the time, Pallas kernels for 12%

profile of v12, /device:TPU:0, one launch (start us, length us, event | category | flops | bytes accessed | tf_op | source)
XLA Modules:
  0.0 99.7 jit_solution(10965990695440023302)
XLA Ops:
  1.6 3.0 %collective-permute-start.3 = (bf16[17,16,256]{2,1,0:T(8,128)(2,1)S(1)}, bf16[17,16,256]{2,1,0:T(8,128)(2,1)S(1)}, u32[]{:S(2)}, u32[]{:S(2)}) collective-permute-start(bf16[17,16,256]{2,1,0:T(8,128)(2,1)S(1)} %shard_map.158.refs_4_), channel_id=1, source_target_pairs={{0,16},{8,24},{16,0},{24,8},{1,17},{9,25},{17,1},{25,9},{2,18},{10... | collective-permute-start | bytes 417800 | tf_op jit(solution)/shard_map/ppermute | solution.py:35
  4.7 1.9 %collective-permute-start.1 = (bf16[16,16,256]{2,1,0:T(8,128)(2,1)}, bf16[16,16,256]{2,1,0:T(8,128)(2,1)S(1)}, u32[]{:S(2)}, u32[]{:S(2)}) collective-permute-start(bf16[16,16,256]{2,1,0:T(8,128)(2,1)} %refs_0_.1), channel_id=1, source_target_pairs={{0,8},{8,0},{16,24},{24,16},{1,9},{9,1},{17,25},{25,17},{2,10},{10... | collective-permute-start | bytes 393224 | tf_op jit(solution)/shard_map/ppermute | solution.py:35
  6.7 2.4 %collective-permute-done.3.refs_6_ = bf16[17,16,256]{2,1,0:T(8,128)(2,1)S(1)} collective-permute-done((bf16[17,16,256]{2,1,0:T(8,128)(2,1)S(1)}, bf16[17,16,256]{2,1,0:T(8,128)(2,1)S(1)}, u32[]{:S(2)}, u32[]{:S(2)}) %collective-permute-start.3) | collective-permute-done | bytes 139296 | tf_op jit(solution)/shard_map/ppermute | solution.py:35
  9.1 2.0 %collective-permute-start.5 = (bf16[17,16,256]{2,1,0:T(8,128)(2,1)S(1)}, bf16[17,16,256]{2,1,0:T(8,128)(2,1)S(1)}, u32[]{:S(2)}, u32[]{:S(2)}) collective-permute-start(bf16[17,16,256]{2,1,0:T(8,128)(2,1)S(1)} %collective-permute-done.3.refs_6_), channel_id=1, source_target_pairs={{0,8},{8,0},{16,24},{24,16},{1,9},{9,1},{17,25},{25,17},{2,10},{10... | collective-permute-start | bytes 417800 | tf_op jit(solution)/shard_map/ppermute | solution.py:35
  11.3 2.0 %collective-permute-start.4 = (bf16[16,16,256]{2,1,0:T(8,128)(2,1)S(1)}, bf16[16,16,256]{2,1,0:T(8,128)(2,1)S(1)}, u32[]{:S(2)}, u32[]{:S(2)}) collective-permute-start(bf16[16,16,256]{2,1,0:T(8,128)(2,1)S(1)} %collective-permute-done.1.refs_1_), channel_id=1, source_target_pairs={{0,16},{8,24},{16,0},{24,8},{1,17},{9,25},{17,1},{25,9},{2,18},{10... | collective-permute-start | bytes 393224 | tf_op jit(solution)/shard_map/ppermute | solution.py:35
  14.3 1.7 %collective-permute-start.13 = (bf16[512,896]{1,0:T(8,128)(2,1)}, bf16[512,896]{1,0:T(8,128)(2,1)S(1)}, u32[]{:S(2)}, u32[]{:S(2)}) collective-permute-start(bf16[512,896]{1,0:T(8,128)(2,1)} %refs_10_), channel_id=1, source_target_pairs={{0,8},{8,0},{16,24},{24,16},{1,9},{9,1},{17,25},{25,17},{2,10},{10... | collective-permute-start | bytes 2752520 | tf_op jit(solution)/shard_map/ppermute | solution.py:35
  16.0 1.8 %collective-permute-start.14 = (bf16[512,896]{1,0:T(8,128)(2,1)}, bf16[512,896]{1,0:T(8,128)(2,1)S(1)}, u32[]{:S(2)}, u32[]{:S(2)}) collective-permute-start(bf16[512,896]{1,0:T(8,128)(2,1)} %refs_13_), channel_id=1, source_target_pairs={{0,16},{8,24},{16,0},{24,8},{1,17},{9,25},{17,1},{25,9},{2,18},{10... | collective-permute-start | bytes 2752520 | tf_op jit(solution)/shard_map/ppermute | solution.py:35
  17.8 1.8 %shard_map.159 = (bf16[2,128,256]{2,1,0:T(8,128)(2,1)S(1)}, f32[4,16,256]{2,1,0:T(8,128)S(1)}) custom-call(s32[4]{0:T(128)S(1)} %pad_add_fusion.ids, s32[64]{0:T(128)} %plan_far.1, bf16[16,16,256]{2,1,0:T(8,128)(2,1)} %refs_0_.1, bf16[16,16,256]{2,1,0:T(8,128)(2,1)S(1)} %collective-permute-done.1.refs_1_, ...), custom_call_target="tpu_custom_call" | custom-call | flops 10000000000 | tf_op jit(solution)/shard_map/pallas_call | solution.py:22
  20.2 3.7 %collective-permute-start.8 = (bf16[2,128,256]{2,1,0:T(8,128)(2,1)S(1)}, bf16[2,128,256]{2,1,0:T(8,128)(2,1)S(1)}, u32[]{:S(2)}, u32[]{:S(2)}) collective-permute-start(bf16[2,128,256]{2,1,0:T(8,128)(2,1)S(1)} %get-tuple-element.40.refs_6_), channel_id=1, source_target_pairs={{0,6},{1,7},{2,4},{3,5},{4,2},{5,3},{6,0},{7,1},{8,14},{9,15},{10,... | collective-permute-start | bytes 393224 | tf_op jit(solution)/shard_map/ppermute | solution.py:35
  24.6 3.2 %collective-permute-done.8.refs_9_ = bf16[2,128,256]{2,1,0:T(8,128)(2,1)S(1)} collective-permute-done((bf16[2,128,256]{2,1,0:T(8,128)(2,1)S(1)}, bf16[2,128,256]{2,1,0:T(8,128)(2,1)S(1)}, u32[]{:S(2)}, u32[]{:S(2)}) %collective-permute-start.8) | collective-permute-done | bytes 131104 | tf_op jit(solution)/shard_map/ppermute | solution.py:35
  27.8 1.6 %collective-permute-done.6.refs_7_ = bf16[2,128,256]{2,1,0:T(8,128)(2,1)S(1)} collective-permute-done((bf16[2,128,256]{2,1,0:T(8,128)(2,1)S(1)}, bf16[2,128,256]{2,1,0:T(8,128)(2,1)S(1)}, u32[]{:S(2)}, u32[]{:S(2)}) %collective-permute-start.6) | collective-permute-done | bytes 131104 | tf_op jit(solution)/shard_map/ppermute | solution.py:35
  29.3 2.8 %collective-permute-done.7.refs_8_ = bf16[2,128,256]{2,1,0:T(8,128)(2,1)S(1)} collective-permute-done((bf16[2,128,256]{2,1,0:T(8,128)(2,1)S(1)}, bf16[2,128,256]{2,1,0:T(8,128)(2,1)S(1)}, u32[]{:S(2)}, u32[]{:S(2)}) %collective-permute-start.7) | collective-permute-done | bytes 131104 | tf_op jit(solution)/shard_map/ppermute | solution.py:35
  32.6 1.5 %collective-permute-start.18 = (bf16[512,896]{1,0:T(8,128)(2,1)}, bf16[512,896]{1,0:T(8,128)(2,1)S(1)}, u32[]{:S(2)}, u32[]{:S(2)}) collective-permute-start(bf16[512,896]{1,0:T(8,128)(2,1)} %refs_10_), channel_id=1, source_target_pairs={{0,16},{8,24},{16,0},{24,8},{1,17},{9,25},{17,1},{25,9},{2,18},{10... | collective-permute-start | bytes 2752520 | tf_op jit(solution)/shard_map/ppermute | solution.py:35
  34.8 1.5 %collective-permute-start.19 = (bf16[512,896]{1,0:T(8,128)(2,1)}, bf16[512,896]{1,0:T(8,128)(2,1)}, u32[]{:S(2)}, u32[]{:S(2)}) collective-permute-start(bf16[512,896]{1,0:T(8,128)(2,1)} %refs_13_), channel_id=1, source_target_pairs={{0,8},{8,0},{16,24},{24,16},{1,9},{9,1},{17,25},{25,17},{2,10},{10... | collective-permute-start | bytes 2752520 | tf_op jit(solution)/shard_map/ppermute | solution.py:35
  37.5 5.4 %shard_map.160 = (f32[4,2,128,256]{3,2,1,0:T(8,128)S(1)}, bf16[4,2,128,256]{3,2,1,0:T(8,128)(2,1)S(1)}) custom-call(s32[4]{0:T(128)S(1)} %pad_add_fusion.ids, f32[8,1,256]{2,1,0:T(1,128)} %bitcast.13, f32[8,1,256]{2,1,0:T(1,128)} %bitcast.14, bf16[2048,512]{1,0:T(8,128)(2,1)} %refs_2_.1, bf16[2048,512]{1,0:T(8,128)(2,1)} %refs_3_.1, ...), custom_call_target="tpu_custom_call" | custom-call | tf_op jit(solution)/shard_map/pallas_call | solution.py:22
  43.1 1.8 %collective-permute-done.15.came = bf16[4,2,128,256]{3,2,1,0:T(8,128)(2,1)S(1)} collective-permute-done((bf16[4,2,128,256]{3,2,1,0:T(8,128)(2,1)S(1)}, bf16[4,2,128,256]{3,2,1,0:T(8,128)(2,1)S(1)}, u32[]{:S(2)}, u32[]{:S(2)}) %collective-permute-start.15) | collective-permute-done | bytes 524320 | tf_op jit(solution)/shard_map/ppermute | solution.py:35
  46.4 2.3 %collective-permute-start.16 = (bf16[2,128,256]{2,1,0:T(8,128)(2,1)S(1)}, bf16[2,128,256]{2,1,0:T(8,128)(2,1)S(1)}, u32[]{:S(2)}, u32[]{:S(2)}) collective-permute-start(bf16[2,128,256]{2,1,0:T(8,128)(2,1)S(1)} %get-tuple-element.48), channel_id=1, source_target_pairs={{0,2},{1,3},{2,0},{3,1},{4,6},{5,7},{6,4},{7,5},{8,10},{9,11},{10,... | collective-permute-start | bytes 393224 | tf_op jit(solution)/shard_map/ppermute | solution.py:35
  50.0 5.6 %collective-permute-done.18.refs_12_ = bf16[512,896]{1,0:T(8,128)(2,1)S(1)} collective-permute-done((bf16[512,896]{1,0:T(8,128)(2,1)}, bf16[512,896]{1,0:T(8,128)(2,1)S(1)}, u32[]{:S(2)}, u32[]{:S(2)}) %collective-permute-start.18) | collective-permute-done | bytes 917536 | tf_op jit(solution)/shard_map/ppermute | solution.py:35
  61.2 2.4 %collective-permute-start.22 = (bf16[2,128,256]{2,1,0:T(8,128)(2,1)S(1)}, bf16[2,128,256]{2,1,0:T(8,128)(2,1)S(1)}, u32[]{:S(2)}, u32[]{:S(2)}) collective-permute-start(bf16[2,128,256]{2,1,0:T(8,128)(2,1)S(1)} %add_convert_fusion.refs_2_), channel_id=1, source_target_pairs={{0,4},{1,5},{2,6},{3,7},{4,0},{5,1},{6,2},{7,3},{8,12},{9,13},{10,... | collective-permute-start | bytes 393224 | tf_op jit(solution)/shard_map/ppermute | solution.py:35
  66.1 7.6 %collective-permute-done.22.refs_4_ = bf16[2,128,256]{2,1,0:T(8,128)(2,1)S(1)} collective-permute-done((bf16[2,128,256]{2,1,0:T(8,128)(2,1)S(1)}, bf16[2,128,256]{2,1,0:T(8,128)(2,1)S(1)}, u32[]{:S(2)}, u32[]{:S(2)}) %collective-permute-start.22) | collective-permute-done | bytes 131104 | tf_op jit(solution)/shard_map/ppermute | solution.py:35
  78.1 4.1 %shard_map.162 = (f32[2,128,896]{2,1,0:T(8,128)S(1)}, bf16[2,128,512]{2,1,0:T(8,128)(2,1)S(1)}) custom-call(s32[4]{0:T(128)S(1)} %pad_add_fusion.ids, f32[8,1,256]{2,1,0:T(1,128)} %bitcast.15, f32[8,1,256]{2,1,0:T(1,128)} %bitcast.16, bf16[2,128,256]{2,1,0:T(8,128)(2,1)S(1)} %add_convert_fusion.refs_2_, ...), custom_call_target="tpu_custom_call" | custom-call | tf_op jit(solution)/shard_map/pallas_call | solution.py:22
  85.2 2.4 %collective-permute-start.31 = (f32[8,128]{1,0:T(8,128)S(1)}, f32[8,128]{1,0:T(8,128)S(1)}, u32[]{:S(2)}, u32[]{:S(2)}) collective-permute-start(f32[8,128]{1,0:T(8,128)S(1)} %shard_map.164.refs_0_), channel_id=1, source_target_pairs={{0,6},{1,7},{2,4},{3,5},{4,2},{5,3},{6,0},{7,1},{8,14},{9,15},{10,... | collective-permute-start | bytes 12296 | tf_op jit(solution)/shard_map/ppermute | solution.py:35
  90.7 1.5 %collective-permute-done.32.refs_2_ = f32[8,128]{1,0:T(8,128)S(1)} collective-permute-done((f32[8,128]{1,0:T(8,128)S(1)}, f32[8,128]{1,0:T(8,128)S(1)}, u32[]{:S(2)}, u32[]{:S(2)}) %collective-permute-start.32) | collective-permute-done | bytes 4128 | tf_op jit(solution)/shard_map/ppermute | solution.py:35
  95.2 1.5 %collective-permute-start.36 = (f32[1,128]{1,0:T(1,128)S(1)}, f32[1,128]{1,0:T(1,128)S(1)}, u32[]{:S(2)}, u32[]{:S(2)}) collective-permute-start(f32[1,128]{1,0:T(1,128)S(1)} %shard_map.165), channel_id=1, source_target_pairs={{0,8},{8,0},{16,24},{24,16},{1,9},{9,1},{17,25},{25,17},{2,10},{10... | collective-permute-start | bytes 1544 | tf_op jit(solution)/shard_map/ppermute | solution.py:35
  (99 shorter events, 33.5 us)
Async XLA Ops:
  1.6 7.5 %collective-permute-start.3 = (bf16[17,16,256]{2,1,0:T(8,128)(2,1)S(1)}, bf16[17,16,256]{2,1,0:T(8,128)(2,1)S(1)}, u32[]{:S(2)}, u32[]{:S(2)}) collective-permute-start(bf16[17,16,256]{2,1,0:T(8,128)(2,1)S(1)} %shard_map.158.refs_4_), channel_id=1, source_target_pairs={{0,16},{8,24},{16,0},{24,8},{1,17},{9,25},{17,1},{25,9},{2,18},{10... | collective-permute-start | bytes 417800 | tf_op jit(solution)/shard_map/ppermute | solution.py:35
  4.6 6.5 %collective-permute-start = (bf16[16,16,256]{2,1,0:T(8,128)(2,1)}, bf16[16,16,256]{2,1,0:T(8,128)(2,1)S(1)}, u32[]{:S(2)}, u32[]{:S(2)}) collective-permute-start(bf16[16,16,256]{2,1,0:T(8,128)(2,1)} %refs_0_.1), channel_id=1, source_target_pairs={{0,16},{8,24},{16,0},{24,8},{1,17},{9,25},{17,1},{25,9},{2,18},{10... | collective-permute-start | bytes 393224 | tf_op jit(solution)/shard_map/ppermute | solution.py:35
  4.7 6.6 %collective-permute-start.1 = (bf16[16,16,256]{2,1,0:T(8,128)(2,1)}, bf16[16,16,256]{2,1,0:T(8,128)(2,1)S(1)}, u32[]{:S(2)}, u32[]{:S(2)}) collective-permute-start(bf16[16,16,256]{2,1,0:T(8,128)(2,1)} %refs_0_.1), channel_id=1, source_target_pairs={{0,8},{8,0},{16,24},{24,16},{1,9},{9,1},{17,25},{25,17},{2,10},{10... | collective-permute-start | bytes 393224 | tf_op jit(solution)/shard_map/ppermute | solution.py:35
  6.6 7.7 %collective-permute-start.2 = (bf16[17,16,256]{2,1,0:T(8,128)(2,1)S(1)}, bf16[17,16,256]{2,1,0:T(8,128)(2,1)S(1)}, u32[]{:S(2)}, u32[]{:S(2)}) collective-permute-start(bf16[17,16,256]{2,1,0:T(8,128)(2,1)S(1)} %shard_map.158.refs_4_), channel_id=1, source_target_pairs={{0,8},{8,0},{16,24},{24,16},{1,9},{9,1},{17,25},{25,17},{2,10},{10... | collective-permute-start | bytes 417800 | tf_op jit(solution)/shard_map/ppermute | solution.py:35
  9.1 8.7 %collective-permute-start.5 = (bf16[17,16,256]{2,1,0:T(8,128)(2,1)S(1)}, bf16[17,16,256]{2,1,0:T(8,128)(2,1)S(1)}, u32[]{:S(2)}, u32[]{:S(2)}) collective-permute-start(bf16[17,16,256]{2,1,0:T(8,128)(2,1)S(1)} %collective-permute-done.3.refs_6_), channel_id=1, source_target_pairs={{0,8},{8,0},{16,24},{24,16},{1,9},{9,1},{17,25},{25,17},{2,10},{10... | collective-permute-start | bytes 417800 | tf_op jit(solution)/shard_map/ppermute | solution.py:35
  11.3 6.4 %collective-permute-start.4 = (bf16[16,16,256]{2,1,0:T(8,128)(2,1)S(1)}, bf16[16,16,256]{2,1,0:T(8,128)(2,1)S(1)}, u32[]{:S(2)}, u32[]{:S(2)}) collective-permute-start(bf16[16,16,256]{2,1,0:T(8,128)(2,1)S(1)} %collective-permute-done.1.refs_1_), channel_id=1, source_target_pairs={{0,16},{8,24},{16,0},{24,8},{1,17},{9,25},{17,1},{25,9},{2,18},{10... | collective-permute-start | bytes 393224 | tf_op jit(solution)/shard_map/ppermute | solution.py:35
  14.3 28.6 %collective-permute-start.13 = (bf16[512,896]{1,0:T(8,128)(2,1)}, bf16[512,896]{1,0:T(8,128)(2,1)S(1)}, u32[]{:S(2)}, u32[]{:S(2)}) collective-permute-start(bf16[512,896]{1,0:T(8,128)(2,1)} %refs_10_), channel_id=1, source_target_pairs={{0,8},{8,0},{16,24},{24,16},{1,9},{9,1},{17,25},{25,17},{2,10},{10... | collective-permute-start | bytes 2752520 | tf_op jit(solution)/shard_map/ppermute | solution.py:35
  16.0 26.9 %collective-permute-start.14 = (bf16[512,896]{1,0:T(8,128)(2,1)}, bf16[512,896]{1,0:T(8,128)(2,1)S(1)}, u32[]{:S(2)}, u32[]{:S(2)}) collective-permute-start(bf16[512,896]{1,0:T(8,128)(2,1)} %refs_13_), channel_id=1, source_target_pairs={{0,16},{8,24},{16,0},{24,8},{1,17},{9,25},{17,1},{25,9},{2,18},{10... | collective-permute-start | bytes 2752520 | tf_op jit(solution)/shard_map/ppermute | solution.py:35
  20.2 7.6 %collective-permute-start.8 = (bf16[2,128,256]{2,1,0:T(8,128)(2,1)S(1)}, bf16[2,128,256]{2,1,0:T(8,128)(2,1)S(1)}, u32[]{:S(2)}, u32[]{:S(2)}) collective-permute-start(bf16[2,128,256]{2,1,0:T(8,128)(2,1)S(1)} %get-tuple-element.40.refs_6_), channel_id=1, source_target_pairs={{0,6},{1,7},{2,4},{3,5},{4,2},{5,3},{6,0},{7,1},{8,14},{9,15},{10,... | collective-permute-start | bytes 393224 | tf_op jit(solution)/shard_map/ppermute | solution.py:35
  23.9 5.5 %collective-permute-start.6 = (bf16[2,128,256]{2,1,0:T(8,128)(2,1)S(1)}, bf16[2,128,256]{2,1,0:T(8,128)(2,1)S(1)}, u32[]{:S(2)}, u32[]{:S(2)}) collective-permute-start(bf16[2,128,256]{2,1,0:T(8,128)(2,1)S(1)} %get-tuple-element.40.refs_6_), channel_id=1, source_target_pairs={{0,2},{1,3},{2,0},{3,1},{4,6},{5,7},{6,4},{7,5},{8,10},{9,11},{10,... | collective-permute-start | bytes 393224 | tf_op jit(solution)/shard_map/ppermute | solution.py:35
  23.9 8.2 %collective-permute-start.7 = (bf16[2,128,256]{2,1,0:T(8,128)(2,1)S(1)}, bf16[2,128,256]{2,1,0:T(8,128)(2,1)S(1)}, u32[]{:S(2)}, u32[]{:S(2)}) collective-permute-start(bf16[2,128,256]{2,1,0:T(8,128)(2,1)S(1)} %get-tuple-element.40.refs_6_), channel_id=1, source_target_pairs={{0,4},{1,5},{2,6},{3,7},{4,0},{5,1},{6,2},{7,3},{8,12},{9,13},{10,... | collective-permute-start | bytes 393224 | tf_op jit(solution)/shard_map/ppermute | solution.py:35
  32.6 23.0 %collective-permute-start.18 = (bf16[512,896]{1,0:T(8,128)(2,1)}, bf16[512,896]{1,0:T(8,128)(2,1)S(1)}, u32[]{:S(2)}, u32[]{:S(2)}) collective-permute-start(bf16[512,896]{1,0:T(8,128)(2,1)} %refs_10_), channel_id=1, source_target_pairs={{0,16},{8,24},{16,0},{24,8},{1,17},{9,25},{17,1},{25,9},{2,18},{10... | collective-permute-start | bytes 2752520 | tf_op jit(solution)/shard_map/ppermute | solution.py:35
  34.8 22.4 %collective-permute-start.19 = (bf16[512,896]{1,0:T(8,128)(2,1)}, bf16[512,896]{1,0:T(8,128)(2,1)}, u32[]{:S(2)}, u32[]{:S(2)}) collective-permute-start(bf16[512,896]{1,0:T(8,128)(2,1)} %refs_13_), channel_id=1, source_target_pairs={{0,8},{8,0},{16,24},{24,16},{1,9},{9,1},{17,25},{25,17},{2,10},{10... | collective-permute-start | bytes 2752520 | tf_op jit(solution)/shard_map/ppermute | solution.py:35
  45.6 11.6 %collective-permute-start.17 = (bf16[2,128,256]{2,1,0:T(8,128)(2,1)S(1)}, bf16[2,128,256]{2,1,0:T(8,128)(2,1)S(1)}, u32[]{:S(2)}, u32[]{:S(2)}) collective-permute-start(bf16[2,128,256]{2,1,0:T(8,128)(2,1)S(1)} %get-tuple-element.49), channel_id=1, source_target_pairs={{0,4},{1,5},{2,6},{3,7},{4,0},{5,1},{6,2},{7,3},{8,12},{9,13},{10,... | collective-permute-start | bytes 393224 | tf_op jit(solution)/shard_map/ppermute | solution.py:35
  46.4 13.4 %collective-permute-start.16 = (bf16[2,128,256]{2,1,0:T(8,128)(2,1)S(1)}, bf16[2,128,256]{2,1,0:T(8,128)(2,1)S(1)}, u32[]{:S(2)}, u32[]{:S(2)}) collective-permute-start(bf16[2,128,256]{2,1,0:T(8,128)(2,1)S(1)} %get-tuple-element.48), channel_id=1, source_target_pairs={{0,2},{1,3},{2,0},{3,1},{4,6},{5,7},{6,4},{7,5},{8,10},{9,11},{10,... | collective-permute-start | bytes 393224 | tf_op jit(solution)/shard_map/ppermute | solution.py:35
  48.7 11.1 %collective-permute-start.20 = (bf16[2,128,256]{2,1,0:T(8,128)(2,1)S(1)}, bf16[2,128,256]{2,1,0:T(8,128)(2,1)S(1)}, u32[]{:S(2)}, u32[]{:S(2)}) collective-permute-start(bf16[2,128,256]{2,1,0:T(8,128)(2,1)S(1)} %get-tuple-element.55), channel_id=1, source_target_pairs={{0,6},{1,7},{2,4},{3,5},{4,2},{5,3},{6,0},{7,1},{8,14},{9,15},{10,... | collective-permute-start | bytes 393224 | tf_op jit(solution)/shard_map/ppermute | solution.py:35
  57.2 25.0 %collective-permute-start.28 = (bf16[512,896]{1,0:T(8,128)(2,1)S(1)}, bf16[512,896]{1,0:T(8,128)(2,1)S(1)}, u32[]{:S(2)}, u32[]{:S(2)}) collective-permute-start(bf16[512,896]{1,0:T(8,128)(2,1)S(1)} %collective-permute-done.13.refs_11_), channel_id=1, source_target_pairs={{0,16},{8,24},{16,0},{24,8},{1,17},{9,25},{17,1},{25,9},{2,18},{10... | collective-permute-start | bytes 2752520 | tf_op jit(solution)/shard_map/ppermute | solution.py:35
  58.6 23.6 %collective-permute-start.29 = (bf16[512,896]{1,0:T(8,128)(2,1)}, bf16[512,896]{1,0:T(8,128)(2,1)S(1)}, u32[]{:S(2)}, u32[]{:S(2)}) collective-permute-start(bf16[512,896]{1,0:T(8,128)(2,1)} %copy-done), channel_id=1, source_target_pairs={{0,8},{8,0},{16,24},{24,16},{1,9},{9,1},{17,25},{25,17},{2,10},{10... | collective-permute-start | bytes 2752520 | tf_op jit(solution)/shard_map/ppermute | solution.py:35
  59.9 5.8 %collective-permute-start.21 = (bf16[2,128,256]{2,1,0:T(8,128)(2,1)S(1)}, bf16[2,128,256]{2,1,0:T(8,128)(2,1)S(1)}, u32[]{:S(2)}, u32[]{:S(2)}) collective-permute-start(bf16[2,128,256]{2,1,0:T(8,128)(2,1)S(1)} %add_convert_fusion.refs_2_), channel_id=1, source_target_pairs={{0,2},{1,3},{2,0},{3,1},{4,6},{5,7},{6,4},{7,5},{8,10},{9,11},{10,... | collective-permute-start | bytes 393224 | tf_op jit(solution)/shard_map/ppermute | solution.py:35
  61.2 12.5 %collective-permute-start.22 = (bf16[2,128,256]{2,1,0:T(8,128)(2,1)S(1)}, bf16[2,128,256]{2,1,0:T(8,128)(2,1)S(1)}, u32[]{:S(2)}, u32[]{:S(2)}) collective-permute-start(bf16[2,128,256]{2,1,0:T(8,128)(2,1)S(1)} %add_convert_fusion.refs_2_), channel_id=1, source_target_pairs={{0,4},{1,5},{2,6},{3,7},{4,0},{5,1},{6,2},{7,3},{8,12},{9,13},{10,... | collective-permute-start | bytes 393224 | tf_op jit(solution)/shard_map/ppermute | solution.py:35
  63.6 10.1 %collective-permute-start.23 = (bf16[2,128,256]{2,1,0:T(8,128)(2,1)S(1)}, bf16[2,128,256]{2,1,0:T(8,128)(2,1)S(1)}, u32[]{:S(2)}, u32[]{:S(2)}) collective-permute-start(bf16[2,128,256]{2,1,0:T(8,128)(2,1)S(1)} %add_convert_fusion.refs_2_), channel_id=1, source_target_pairs={{0,6},{1,7},{2,4},{3,5},{4,2},{5,3},{6,0},{7,1},{8,14},{9,15},{10,... | collective-permute-start | bytes 393224 | tf_op jit(solution)/shard_map/ppermute | solution.py:35
  65.7 8.5 %collective-permute-start.24 = (bf16[2,128,256]{2,1,0:T(8,128)(2,1)S(1)}, bf16[2,128,256]{2,1,0:T(8,128)(2,1)S(1)}, u32[]{:S(2)}, u32[]{:S(2)}) collective-permute-start(bf16[2,128,256]{2,1,0:T(8,128)(2,1)S(1)} %add_convert_fusion.refs_2_), channel_id=1, source_target_pairs={{0,1},{1,0},{2,3},{3,2},{4,5},{5,4},{6,7},{7,6},{8,9},{9,8},{10,11... | collective-permute-start | bytes 393224 | tf_op jit(solution)/shard_map/ppermute | solution.py:35
  85.2 5.5 %collective-permute-start.31 = (f32[8,128]{1,0:T(8,128)S(1)}, f32[8,128]{1,0:T(8,128)S(1)}, u32[]{:S(2)}, u32[]{:S(2)}) collective-permute-start(f32[8,128]{1,0:T(8,128)S(1)} %shard_map.164.refs_0_), channel_id=1, source_target_pairs={{0,6},{1,7},{2,4},{3,5},{4,2},{5,3},{6,0},{7,1},{8,14},{9,15},{10,... | collective-permute-start | bytes 12296 | tf_op jit(solution)/shard_map/ppermute | solution.py:35
  87.6 4.5 %collective-permute-start.32 = (f32[8,128]{1,0:T(8,128)S(1)}, f32[8,128]{1,0:T(8,128)S(1)}, u32[]{:S(2)}, u32[]{:S(2)}) collective-permute-start(f32[8,128]{1,0:T(8,128)S(1)} %shard_map.164.refs_0_), channel_id=1, source_target_pairs={{0,4},{1,5},{2,6},{3,7},{4,0},{5,1},{6,2},{7,3},{8,12},{9,13},{10,... | collective-permute-start | bytes 12296 | tf_op jit(solution)/shard_map/ppermute | solution.py:35
  (21 other events, 69.5 us)

commit v13 on v8

--- a/solution.py
+++ b/solution.py
@@ -72,17 +72,15 @@
 
 
 def select_kernel(dp, ids, plan_far, *refs):
-    parts, (out, facts, own, plan, sems) = list(refs[: 2 * dp]), refs[2 * dp :]
+    parts, (out, picks, marks, own, plan, sems) = list(refs[: 2 * dp]), refs[2 * dp :]
     plan_copy, copy = fetch([plan_far, parts[0]], [plan, own], sems)
     parts[0] = own
     rows = out.shape[1]
     reqs, slots, _ = own.shape
     here = reqs * slots
     me = ids[0]
-    for k in range(dp):
-        facts[k] = parts[dp + k][reqs].astype(jnp.float32)
-    lengths = [facts[k][:, 0:1].astype(jnp.int32) for k in range(dp)]
-    lengths = jnp.concatenate(lengths, axis=0)
+    facts = jnp.concatenate([parts[dp + k][reqs].astype(jnp.float32) for k in range(dp)], axis=0)
+    lengths = facts[:, 0:1].astype(jnp.int32)
     row = lax.broadcasted_iota(jnp.int32, (reqs, here), 0)
     slot = jnp.concatenate([row + (me ^ k) * reqs for k in range(dp)], axis=0)
     position = lax.rem(lax.broadcasted_iota(jnp.int32, (1, here), 1), slots)
@@ -108,6 +106,33 @@
             total = found if total is None else total + found
         out[m] = total.astype(out.dtype)
 
+    count = dp * reqs
+    down = lax.broadcasted_iota(jnp.int32, (reqs, count), 0)
+    along = lax.broadcasted_iota(jnp.int32, (1, count), 1)
+    here_slot = lax.rem(along, reqs)
+    for k in range(dp):
+        here_slot = jnp.where(lax.div(along, reqs) == k, here_slot + (me ^ k) * reqs, here_slot)
+    slot = jnp.concatenate([down + (me ^ k) * reqs for k in range(dp)], axis=0)
+    start = jnp.sum(jnp.where(slot < here_slot, lengths, 0), axis=0, keepdims=True)
+    live = jnp.sum(jnp.where(slot == here_slot, lengths, 0), axis=0, keepdims=True)
+
+    rank = me * rows + lax.broadcasted_iota(jnp.int32, (rows, count), 0)
+    held = jnp.logical_and(rank >= start, rank < start + live)
+    first = jnp.sum(jnp.where(held, start, 0), axis=1, keepdims=True)
+    spot = rank[:, 0:1] - first
+    held = held.astype(jnp.float32).astype(jnp.bfloat16)
+    rows_of = jnp.dot(held, facts.astype(jnp.bfloat16), preferred_element_type=jnp.float32)
+    lane = lax.broadcasted_iota(jnp.int32, rows_of.shape, 1)
+    high = jnp.sum(jnp.where(lane == spot + 1, rows_of, 0.0), axis=1, keepdims=True)
+    low = jnp.sum(jnp.where(lane == spot + 1 + slots, rows_of, 0.0), axis=1, keepdims=True)
+    picks[...] = (high * 128.0 + low).astype(jnp.int32)
+
+    mine = me * reqs + down
+    begin = jnp.sum(jnp.where(here_slot < mine, live, 0), axis=1, keepdims=True)
+    length = jnp.sum(jnp.where(here_slot == mine, live, 0), axis=1, keepdims=True)
+    position = lax.broadcasted_iota(jnp.int32, (reqs, slots), 1)
+    marks[...] = jnp.where(position < length, begin + position, -1)
+
 
 def normalise(values, gain, chip, core, store, copy):
     half = len(values) // 2
@@ -229,6 +254,29 @@
     top, total, picked = merge(refs[:-1])
     logprob = picked - (top + jnp.log(total))
     out[...] = logprob[0:1] - logprob[1:2]
+
+
+def place_kernel(dp, ids, marks, *refs):
+    *diffs, tokens, sums = refs
+    reqs, slots = marks.shape
+    rows = diffs[0].shape[1]
+    along = lax.broadcasted_iota(jnp.int32, (1, rows), 1)
+    lane = lax.broadcasted_iota(jnp.int32, (reqs, slots), 1)
+    codes = marks[...]
+    result = jnp.zeros((reqs, slots), jnp.float32)
+    for p in range(slots):
+        code = codes[:, p : p + 1]
+        found = jnp.zeros((reqs, rows), jnp.float32)
+        for k in range(dp):
+            ranks = (ids[0] ^ ((k + 1) % dp)) * rows + along
+            found = jnp.where(code == ranks, diffs[k][...], found)
+        value = jnp.sum(found, axis=1, keepdims=True)
+        result = jnp.where(lane == p, value, result)
+    tokens[...] = result
+    total = jnp.sum(result, axis=1, keepdims=True)
+    down = lax.broadcasted_iota(jnp.int32, (reqs, reqs), 0)
+    across = lax.broadcasted_iota(jnp.int32, (reqs, reqs), 1)
+    sums[...] = jnp.sum(jnp.where(down == across, total, 0.0), axis=0, keepdims=True)
 
 
 def local(
@@ -309,12 +357,12 @@
     spread_step(outs, 0, lambda m, k: True)
     hidden_parts = [hiddens[m][k] for m in range(2) for k in range(dp)]
 
-    order = jnp.arange(dp, dtype=jnp.int32)
-    moved, facts = call(
+    moved, wanted, marks = call(
         functools.partial(select_kernel, dp),
         (
             jax.ShapeDtypeStruct((2, rows, part), jnp.bfloat16),
-            jax.ShapeDtypeStruct((dp, reqs, part), jnp.float32),
+            jax.ShapeDtypeStruct((rows, 1), jnp.int32),
+            jax.ShapeDtypeStruct((reqs, slots), jnp.int32),
         ),
         (ids, move_plan, *hidden_parts),
         [
@@ -325,19 +373,6 @@
         far=(1, 2),
         cost=10000000000,
     )
-
-    facts = facts[:, :, : 2 * slots + 1].astype(jnp.int32)
-    all_lengths = facts[:, :, 0].reshape(-1)
-    all_targets = (facts[:, :, 1 : slots + 1] * 128 + facts[:, :, slots + 1 :]).reshape(-1)
-    slot_ids = ((order ^ dp_index)[:, None] * reqs + jnp.arange(reqs, dtype=jnp.int32)).reshape(-1)
-    positions = jnp.arange(slots, dtype=jnp.int32)
-
-    def codes(slot):
-        start = jnp.sum(jnp.where(slot_ids[None] < slot[:, None], all_lengths[None], 0), axis=1)
-        live = jnp.sum(jnp.where(slot_ids[None] == slot[:, None], all_lengths[None], 0), axis=1)
-        return jnp.where(
-            positions[None] < live[:, None], start[:, None] + positions[None], jnp.int32(-1)
-        )
 
     far = sorted(range(1, half), key=lambda k: (k.bit_length() <= 1, k))
 
@@ -393,13 +428,6 @@
         stream = wait_for(stream, lambda m, k: True)
         spread_step(outs, step, lambda m, k: True)
 
-    owner_code = codes(slot_ids).reshape(-1)
-    my_ranks = dp_index * rows + jnp.arange(rows, dtype=jnp.int32)
-    wanted = jnp.sum(
-        jnp.where(owner_code[None] == my_ranks[:, None], all_targets[None], 0),
-        axis=1,
-        keepdims=True,
-    )
     partial, tail = call(
         functools.partial(score_kernel, half, dp),
         (
@@ -435,14 +463,18 @@
     diff = call(
         last_kernel,
         jax.ShapeDtypeStruct((1, rows), jnp.float32),
-        (ids, stats, *[exchange(stats, "mp", 2 * k) for k in far]),
-    )
-    diff = jnp.concatenate([diff] + [exchange(diff, "dp", k) for k in range(1, dp)])
-    ranks = ((order ^ dp_index)[:, None] * rows + jnp.arange(rows, dtype=jnp.int32)).reshape(-1)
-    my_code = codes(dp_index * reqs + jnp.arange(reqs, dtype=jnp.int32))
-    hit = my_code[:, :, None] == ranks[None, None]
-    token_diff = jnp.sum(jnp.where(hit, diff.reshape(1, 1, -1), 0.0), axis=2)
-    return (token_diff, jnp.sum(token_diff, axis=1))
+        (ids, stats, *[exchange(stats, "mp", 2 * k) for k in range(1, half)]),
+    )
+    came = [exchange(diff, "dp", k) for k in range(1, dp)]
+    token_diff, seq_diff = call(
+        functools.partial(place_kernel, dp),
+        (
+            jax.ShapeDtypeStruct((reqs, slots), jnp.float32),
+            jax.ShapeDtypeStruct((1, reqs), jnp.float32),
+        ),
+        (ids, marks, *came, diff),
+    )
+    return (token_diff, seq_diff.reshape(reqs))
 
 
 def solution(mesh):

time: 97.5 us -> 106 us (1.087)
  waiting for transfers between devices: 37.8 us -> 46.8 us
  other arithmetic: 2.05 us -> 0.14 us
  starting transfers between devices: 40.6 us -> 41.7 us
    ppermute x37, waiting for transfers between devices: 37.8 us -> 46.8 us  [exchange(): return lax.ppermute(values, axis, [(i, i ^ flip) for i in range(count)])]
    reduce_sum x4 -> x0, other arithmetic: 1.5 us -> none  [the longest x1 0.94 us: local(): return (token_diff, jnp.sum(token_diff, axis=1))]
    ppermute x37, starting transfers between devices: 40.6 us -> 41.7 us  [exchange(): return lax.ppermute(values, axis, [(i, i ^ flip) for i in range(count)])]
    pallas_call x8 -> x9, Pallas kernels: 15.3 us -> 16 us  [call(): pl.pallas_call(kernel, out_shape=out_shape, in_specs=specs, out_specs=jax...]
  transfers between devices with their start and end apart: 37 -> 37, of which waited for: 20 -> 22; matrix products, arithmetic and copies ran while one was open for 2% -> 0% of each run, Pallas kernels for 12% -> 10%
where the time goes in v13:
time: 106 us
  waiting for transfers between devices  46.8 us (44%)
  starting transfers between devices  41.7 us (39%)
  Pallas kernels  16 us (15%)
    ppermute x37, waiting for transfers between devices, exchange(): return lax.ppermute(values, axis, [(i, i ^ flip) for i in range(count)])  46.8 us
    ppermute x37, starting transfers between devices, exchange(): return lax.ppermute(values, axis, [(i, i ^ flip) for i in range(count)])  41.7 us
    pallas_call x9, Pallas kernels, call(): pl.pallas_call(kernel, out_shape=out_shape, in_specs=specs, out_specs=jax...  16 us
  transfers between devices with their start and end apart: 37, of which 22 were waited for; matrix products, arithmetic and copies ran while one was open for 0% of the time, Pallas kernels for 10%

profile of v13, /device:TPU:0, one launch (start us, length us, event | category | flops | bytes accessed | tf_op | source)
XLA Modules:
  0.0 105.5 jit_solution(2405815243061711885)
XLA Ops:
  1.6 3.0 %collective-permute-start.3 = (bf16[17,16,256]{2,1,0:T(8,128)(2,1)S(1)}, bf16[17,16,256]{2,1,0:T(8,128)(2,1)S(1)}, u32[]{:S(2)}, u32[]{:S(2)}) collective-permute-start(bf16[17,16,256]{2,1,0:T(8,128)(2,1)S(1)} %shard_map.158.refs_4_), channel_id=1, source_target_pairs={{0,16},{8,24},{16,0},{24,8},{1,17},{9,25},{17,1},{25,9},{2,18},{10... | collective-permute-start | bytes 417800 | tf_op jit(solution)/shard_map/ppermute | solution.py:35
  4.7 1.9 %collective-permute-start.1 = (bf16[16,16,256]{2,1,0:T(8,128)(2,1)}, bf16[16,16,256]{2,1,0:T(8,128)(2,1)S(1)}, u32[]{:S(2)}, u32[]{:S(2)}) collective-permute-start(bf16[16,16,256]{2,1,0:T(8,128)(2,1)} %refs_0_.1), channel_id=1, source_target_pairs={{0,8},{8,0},{16,24},{24,16},{1,9},{9,1},{17,25},{25,17},{2,10},{10... | collective-permute-start | bytes 393224 | tf_op jit(solution)/shard_map/ppermute | solution.py:35
  6.7 2.4 %collective-permute-done.3.refs_6_ = bf16[17,16,256]{2,1,0:T(8,128)(2,1)S(1)} collective-permute-done((bf16[17,16,256]{2,1,0:T(8,128)(2,1)S(1)}, bf16[17,16,256]{2,1,0:T(8,128)(2,1)S(1)}, u32[]{:S(2)}, u32[]{:S(2)}) %collective-permute-start.3) | collective-permute-done | bytes 139296 | tf_op jit(solution)/shard_map/ppermute | solution.py:35
  9.1 2.0 %collective-permute-start.5 = (bf16[17,16,256]{2,1,0:T(8,128)(2,1)S(1)}, bf16[17,16,256]{2,1,0:T(8,128)(2,1)S(1)}, u32[]{:S(2)}, u32[]{:S(2)}) collective-permute-start(bf16[17,16,256]{2,1,0:T(8,128)(2,1)S(1)} %collective-permute-done.3.refs_6_), channel_id=1, source_target_pairs={{0,8},{8,0},{16,24},{24,16},{1,9},{9,1},{17,25},{25,17},{2,10},{10... | collective-permute-start | bytes 417800 | tf_op jit(solution)/shard_map/ppermute | solution.py:35
  11.3 2.0 %collective-permute-start.4 = (bf16[16,16,256]{2,1,0:T(8,128)(2,1)S(1)}, bf16[16,16,256]{2,1,0:T(8,128)(2,1)S(1)}, u32[]{:S(2)}, u32[]{:S(2)}) collective-permute-start(bf16[16,16,256]{2,1,0:T(8,128)(2,1)S(1)} %collective-permute-done.1.refs_1_), channel_id=1, source_target_pairs={{0,16},{8,24},{16,0},{24,8},{1,17},{9,25},{17,1},{25,9},{2,18},{10... | collective-permute-start | bytes 393224 | tf_op jit(solution)/shard_map/ppermute | solution.py:35
  16.0 1.8 %collective-permute-start.14 = (bf16[512,896]{1,0:T(8,128)(2,1)}, bf16[512,896]{1,0:T(8,128)(2,1)S(1)}, u32[]{:S(2)}, u32[]{:S(2)}) collective-permute-start(bf16[512,896]{1,0:T(8,128)(2,1)} %refs_13_), channel_id=1, source_target_pairs={{0,16},{8,24},{16,0},{24,8},{1,17},{9,25},{17,1},{25,9},{2,18},{10... | collective-permute-start | bytes 2752520 | tf_op jit(solution)/shard_map/ppermute | solution.py:35
  17.8 1.9 %shard_map.159 = (bf16[2,128,256]{2,1,0:T(8,128)(2,1)S(1)}, s32[128,1]{1,0:T(8,128)S(1)}, s32[16,16]{1,0:T(8,128)S(1)}) custom-call(s32[4]{0:T(128)S(1)} %pad_add_fusion.ids, s32[64]{0:T(128)} %plan_far.1, bf16[16,16,256]{2,1,0:T(8,128)(2,1)} %refs_0_.1, bf16[16,16,256]{2,1,0:T(8,128)(2,1)S(1)} %collective-permute-done.1.refs_1_, ...), custom_call_target="tpu_custom_call" | custom-call | flops 10000000000 | tf_op jit(solution)/shard_map/pallas_call | solution.py:22
  19.7 3.8 %collective-permute-start.8 = (bf16[2,128,256]{2,1,0:T(8,128)(2,1)S(1)}, bf16[2,128,256]{2,1,0:T(8,128)(2,1)S(1)}, u32[]{:S(2)}, u32[]{:S(2)}) collective-permute-start(bf16[2,128,256]{2,1,0:T(8,128)(2,1)S(1)} %get-tuple-element.44.refs_6_), channel_id=1, source_target_pairs={{0,6},{1,7},{2,4},{3,5},{4,2},{5,3},{6,0},{7,1},{8,14},{9,15},{10,... | collective-permute-start | bytes 393224 | tf_op jit(solution)/shard_map/ppermute | solution.py:35
  23.5 3.2 %collective-permute-done.8.refs_9_ = bf16[2,128,256]{2,1,0:T(8,128)(2,1)S(1)} collective-permute-done((bf16[2,128,256]{2,1,0:T(8,128)(2,1)S(1)}, bf16[2,128,256]{2,1,0:T(8,128)(2,1)S(1)}, u32[]{:S(2)}, u32[]{:S(2)}) %collective-permute-start.8) | collective-permute-done | bytes 131104 | tf_op jit(solution)/shard_map/ppermute | solution.py:35
  27.1 4.1 %collective-permute-done.7.refs_8_ = bf16[2,128,256]{2,1,0:T(8,128)(2,1)S(1)} collective-permute-done((bf16[2,128,256]{2,1,0:T(8,128)(2,1)S(1)}, bf16[2,128,256]{2,1,0:T(8,128)(2,1)S(1)}, u32[]{:S(2)}, u32[]{:S(2)}) %collective-permute-start.7) | collective-permute-done | bytes 131104 | tf_op jit(solution)/shard_map/ppermute | solution.py:35
  32.8 3.3 %collective-permute-done.6.refs_7_ = bf16[2,128,256]{2,1,0:T(8,128)(2,1)S(1)} collective-permute-done((bf16[2,128,256]{2,1,0:T(8,128)(2,1)S(1)}, bf16[2,128,256]{2,1,0:T(8,128)(2,1)S(1)}, u32[]{:S(2)}, u32[]{:S(2)}) %collective-permute-start.6) | collective-permute-done | bytes 131104 | tf_op jit(solution)/shard_map/ppermute | solution.py:35
  39.0 5.0 %shard_map.160 = (f32[4,2,128,256]{3,2,1,0:T(8,128)S(1)}, bf16[4,2,128,256]{3,2,1,0:T(8,128)(2,1)S(1)}) custom-call(s32[4]{0:T(128)S(1)} %pad_add_fusion.ids, f32[8,1,256]{2,1,0:T(1,128)} %bitcast.9, f32[8,1,256]{2,1,0:T(1,128)} %bitcast.10, bf16[2048,512]{1,0:T(8,128)(2,1)} %refs_2_.1, bf16[2048,512]{1,0:T(8,128)(2,1)} %refs_3_.1, ...), custom_call_target="tpu_custom_call" | custom-call | tf_op jit(solution)/shard_map/pallas_call | solution.py:22
  47.9 7.8 %collective-permute-done.18.refs_12_ = bf16[512,896]{1,0:T(8,128)(2,1)S(1)} collective-permute-done((bf16[512,896]{1,0:T(8,128)(2,1)S(1)}, bf16[512,896]{1,0:T(8,128)(2,1)S(1)}, u32[]{:S(2)}, u32[]{:S(2)}) %collective-permute-start.18) | collective-permute-done | bytes 917536 | tf_op jit(solution)/shard_map/ppermute | solution.py:35
  58.5 1.8 %collective-permute-start.16 = (bf16[2,128,256]{2,1,0:T(8,128)(2,1)S(1)}, bf16[2,128,256]{2,1,0:T(8,128)(2,1)S(1)}, u32[]{:S(2)}, u32[]{:S(2)}) collective-permute-start(bf16[2,128,256]{2,1,0:T(8,128)(2,1)S(1)} %get-tuple-element.52), channel_id=1, source_target_pairs={{0,2},{1,3},{2,0},{3,1},{4,6},{5,7},{6,4},{7,5},{8,10},{9,11},{10,... | collective-permute-start | bytes 393224 | tf_op jit(solution)/shard_map/ppermute | solution.py:35
  60.4 2.5 %collective-permute-start.20 = (bf16[2,128,256]{2,1,0:T(8,128)(2,1)S(1)}, bf16[2,128,256]{2,1,0:T(8,128)(2,1)S(1)}, u32[]{:S(2)}, u32[]{:S(2)}) collective-permute-start(bf16[2,128,256]{2,1,0:T(8,128)(2,1)S(1)} %get-tuple-element.59), channel_id=1, source_target_pairs={{0,6},{1,7},{2,4},{3,5},{4,2},{5,3},{6,0},{7,1},{8,14},{9,15},{10,... | collective-permute-start | bytes 393224 | tf_op jit(solution)/shard_map/ppermute | solution.py:35
  62.8 2.1 %collective-permute-done.16 = bf16[2,128,256]{2,1,0:T(8,128)(2,1)S(1)} collective-permute-done((bf16[2,128,256]{2,1,0:T(8,128)(2,1)S(1)}, bf16[2,128,256]{2,1,0:T(8,128)(2,1)S(1)}, u32[]{:S(2)}, u32[]{:S(2)}) %collective-permute-start.16) | collective-permute-done | bytes 131104 | tf_op jit(solution)/shard_map/ppermute | solution.py:35
  64.9 2.4 %collective-permute-done.20 = bf16[2,128,256]{2,1,0:T(8,128)(2,1)S(1)} collective-permute-done((bf16[2,128,256]{2,1,0:T(8,128)(2,1)S(1)}, bf16[2,128,256]{2,1,0:T(8,128)(2,1)S(1)}, u32[]{:S(2)}, u32[]{:S(2)}) %collective-permute-start.20) | collective-permute-done | bytes 131104 | tf_op jit(solution)/shard_map/ppermute | solution.py:35
  67.5 2.4 %collective-permute-start.23 = (bf16[2,128,256]{2,1,0:T(8,128)(2,1)S(1)}, bf16[2,128,256]{2,1,0:T(8,128)(2,1)S(1)}, u32[]{:S(2)}, u32[]{:S(2)}) collective-permute-start(bf16[2,128,256]{2,1,0:T(8,128)(2,1)S(1)} %add_convert_fusion.refs_2_), channel_id=1, source_target_pairs={{0,6},{1,7},{2,4},{3,5},{4,2},{5,3},{6,0},{7,1},{8,14},{9,15},{10,... | collective-permute-start | bytes 393224 | tf_op jit(solution)/shard_map/ppermute | solution.py:35
  69.9 2.0 %collective-permute-start.21 = (bf16[2,128,256]{2,1,0:T(8,128)(2,1)S(1)}, bf16[2,128,256]{2,1,0:T(8,128)(2,1)S(1)}, u32[]{:S(2)}, u32[]{:S(2)}) collective-permute-start(bf16[2,128,256]{2,1,0:T(8,128)(2,1)S(1)} %add_convert_fusion.refs_2_), channel_id=1, source_target_pairs={{0,2},{1,3},{2,0},{3,1},{4,6},{5,7},{6,4},{7,5},{8,10},{9,11},{10,... | collective-permute-start | bytes 393224 | tf_op jit(solution)/shard_map/ppermute | solution.py:35
  71.9 3.8 %collective-permute-done.23.refs_5_ = bf16[2,128,256]{2,1,0:T(8,128)(2,1)S(1)} collective-permute-done((bf16[2,128,256]{2,1,0:T(8,128)(2,1)S(1)}, bf16[2,128,256]{2,1,0:T(8,128)(2,1)S(1)}, u32[]{:S(2)}, u32[]{:S(2)}) %collective-permute-start.23) | collective-permute-done | bytes 131104 | tf_op jit(solution)/shard_map/ppermute | solution.py:35
  75.8 6.2 %collective-permute-done.22.refs_4_ = bf16[2,128,256]{2,1,0:T(8,128)(2,1)S(1)} collective-permute-done((bf16[2,128,256]{2,1,0:T(8,128)(2,1)S(1)}, bf16[2,128,256]{2,1,0:T(8,128)(2,1)S(1)}, u32[]{:S(2)}, u32[]{:S(2)}) %collective-permute-start.22) | collective-permute-done | bytes 131104 | tf_op jit(solution)/shard_map/ppermute | solution.py:35
  83.5 3.2 %shard_map.162 = (f32[2,128,896]{2,1,0:T(8,128)S(1)}, bf16[2,128,512]{2,1,0:T(8,128)(2,1)S(1)}) custom-call(s32[4]{0:T(128)S(1)} %pad_add_fusion.ids, f32[8,1,256]{2,1,0:T(1,128)} %bitcast.11, f32[8,1,256]{2,1,0:T(1,128)} %bitcast.12, bf16[2,128,256]{2,1,0:T(8,128)(2,1)S(1)} %add_convert_fusion.refs_2_, ...), custom_call_target="tpu_custom_call" | custom-call | tf_op jit(solution)/shard_map/pallas_call | solution.py:22
  89.8 2.7 %collective-permute-start.33 = (f32[8,128]{1,0:T(8,128)S(1)}, f32[8,128]{1,0:T(8,128)S(1)}, u32[]{:S(2)}, u32[]{:S(2)}) collective-permute-start(f32[8,128]{1,0:T(8,128)S(1)} %shard_map.164.refs_0_), channel_id=1, source_target_pairs={{0,6},{1,7},{2,4},{3,5},{4,2},{5,3},{6,0},{7,1},{8,14},{9,15},{10,... | collective-permute-start | bytes 12296 | tf_op jit(solution)/shard_map/ppermute | solution.py:35
  103.6 2.0 %shard_map.166 = (f32[16,16]{1,0:T(8,128)}, f32[1,16]{1,0:T(1,128)}) custom-call(s32[4]{0:T(128)S(1)} %pad_add_fusion.ids, s32[16,16]{1,0:T(8,128)S(1)} %get-tuple-element.42.marks, f32[1,128]{1,0:T(1,128)S(1)} %collective-permute-done.34.refs_0_, f32[1,128]{1,0:T(1,128)S(1)} %collective-permute-done.35.refs_1_, ...), custom_call_target="tpu_custom_call" | custom-call | tf_op jit(solution)/shard_map/pallas_call | solution.py:22
  (65 shorter events, 31.4 us)
Async XLA Ops:
  1.6 7.5 %collective-permute-start.3 = (bf16[17,16,256]{2,1,0:T(8,128)(2,1)S(1)}, bf16[17,16,256]{2,1,0:T(8,128)(2,1)S(1)}, u32[]{:S(2)}, u32[]{:S(2)}) collective-permute-start(bf16[17,16,256]{2,1,0:T(8,128)(2,1)S(1)} %shard_map.158.refs_4_), channel_id=1, source_target_pairs={{0,16},{8,24},{16,0},{24,8},{1,17},{9,25},{17,1},{25,9},{2,18},{10... | collective-permute-start | bytes 417800 | tf_op jit(solution)/shard_map/ppermute | solution.py:35
  4.6 6.5 %collective-permute-start = (bf16[16,16,256]{2,1,0:T(8,128)(2,1)}, bf16[16,16,256]{2,1,0:T(8,128)(2,1)S(1)}, u32[]{:S(2)}, u32[]{:S(2)}) collective-permute-start(bf16[16,16,256]{2,1,0:T(8,128)(2,1)} %refs_0_.1), channel_id=1, source_target_pairs={{0,16},{8,24},{16,0},{24,8},{1,17},{9,25},{17,1},{25,9},{2,18},{10... | collective-permute-start | bytes 393224 | tf_op jit(solution)/shard_map/ppermute | solution.py:35
  4.7 6.6 %collective-permute-start.1 = (bf16[16,16,256]{2,1,0:T(8,128)(2,1)}, bf16[16,16,256]{2,1,0:T(8,128)(2,1)S(1)}, u32[]{:S(2)}, u32[]{:S(2)}) collective-permute-start(bf16[16,16,256]{2,1,0:T(8,128)(2,1)} %refs_0_.1), channel_id=1, source_target_pairs={{0,8},{8,0},{16,24},{24,16},{1,9},{9,1},{17,25},{25,17},{2,10},{10... | collective-permute-start | bytes 393224 | tf_op jit(solution)/shard_map/ppermute | solution.py:35
  6.6 7.7 %collective-permute-start.2 = (bf16[17,16,256]{2,1,0:T(8,128)(2,1)S(1)}, bf16[17,16,256]{2,1,0:T(8,128)(2,1)S(1)}, u32[]{:S(2)}, u32[]{:S(2)}) collective-permute-start(bf16[17,16,256]{2,1,0:T(8,128)(2,1)S(1)} %shard_map.158.refs_4_), channel_id=1, source_target_pairs={{0,8},{8,0},{16,24},{24,16},{1,9},{9,1},{17,25},{25,17},{2,10},{10... | collective-permute-start | bytes 417800 | tf_op jit(solution)/shard_map/ppermute | solution.py:35
  9.1 8.7 %collective-permute-start.5 = (bf16[17,16,256]{2,1,0:T(8,128)(2,1)S(1)}, bf16[17,16,256]{2,1,0:T(8,128)(2,1)S(1)}, u32[]{:S(2)}, u32[]{:S(2)}) collective-permute-start(bf16[17,16,256]{2,1,0:T(8,128)(2,1)S(1)} %collective-permute-done.3.refs_6_), channel_id=1, source_target_pairs={{0,8},{8,0},{16,24},{24,16},{1,9},{9,1},{17,25},{25,17},{2,10},{10... | collective-permute-start | bytes 417800 | tf_op jit(solution)/shard_map/ppermute | solution.py:35
  11.3 6.4 %collective-permute-start.4 = (bf16[16,16,256]{2,1,0:T(8,128)(2,1)S(1)}, bf16[16,16,256]{2,1,0:T(8,128)(2,1)S(1)}, u32[]{:S(2)}, u32[]{:S(2)}) collective-permute-start(bf16[16,16,256]{2,1,0:T(8,128)(2,1)S(1)} %collective-permute-done.1.refs_1_), channel_id=1, source_target_pairs={{0,16},{8,24},{16,0},{24,8},{1,17},{9,25},{17,1},{25,9},{2,18},{10... | collective-permute-start | bytes 393224 | tf_op jit(solution)/shard_map/ppermute | solution.py:35
  14.3 29.7 %collective-permute-start.13 = (bf16[512,896]{1,0:T(8,128)(2,1)}, bf16[512,896]{1,0:T(8,128)(2,1)S(1)}, u32[]{:S(2)}, u32[]{:S(2)}) collective-permute-start(bf16[512,896]{1,0:T(8,128)(2,1)} %refs_10_), channel_id=1, source_target_pairs={{0,8},{8,0},{16,24},{24,16},{1,9},{9,1},{17,25},{25,17},{2,10},{10... | collective-permute-start | bytes 2752520 | tf_op jit(solution)/shard_map/ppermute | solution.py:35
  16.0 28.1 %collective-permute-start.14 = (bf16[512,896]{1,0:T(8,128)(2,1)}, bf16[512,896]{1,0:T(8,128)(2,1)S(1)}, u32[]{:S(2)}, u32[]{:S(2)}) collective-permute-start(bf16[512,896]{1,0:T(8,128)(2,1)} %refs_13_), channel_id=1, source_target_pairs={{0,16},{8,24},{16,0},{24,8},{1,17},{9,25},{17,1},{25,9},{2,18},{10... | collective-permute-start | bytes 2752520 | tf_op jit(solution)/shard_map/ppermute | solution.py:35
  19.7 6.9 %collective-permute-start.8 = (bf16[2,128,256]{2,1,0:T(8,128)(2,1)S(1)}, bf16[2,128,256]{2,1,0:T(8,128)(2,1)S(1)}, u32[]{:S(2)}, u32[]{:S(2)}) collective-permute-start(bf16[2,128,256]{2,1,0:T(8,128)(2,1)S(1)} %get-tuple-element.44.refs_6_), channel_id=1, source_target_pairs={{0,6},{1,7},{2,4},{3,5},{4,2},{5,3},{6,0},{7,1},{8,14},{9,15},{10,... | collective-permute-start | bytes 393224 | tf_op jit(solution)/shard_map/ppermute | solution.py:35
  23.5 7.8 %collective-permute-start.7 = (bf16[2,128,256]{2,1,0:T(8,128)(2,1)S(1)}, bf16[2,128,256]{2,1,0:T(8,128)(2,1)S(1)}, u32[]{:S(2)}, u32[]{:S(2)}) collective-permute-start(bf16[2,128,256]{2,1,0:T(8,128)(2,1)S(1)} %get-tuple-element.44.refs_6_), channel_id=1, source_target_pairs={{0,4},{1,5},{2,6},{3,7},{4,0},{5,1},{6,2},{7,3},{8,12},{9,13},{10,... | collective-permute-start | bytes 393224 | tf_op jit(solution)/shard_map/ppermute | solution.py:35
  31.2 5.0 %collective-permute-start.6 = (bf16[2,128,256]{2,1,0:T(8,128)(2,1)S(1)}, bf16[2,128,256]{2,1,0:T(8,128)(2,1)S(1)}, u32[]{:S(2)}, u32[]{:S(2)}) collective-permute-start(bf16[2,128,256]{2,1,0:T(8,128)(2,1)S(1)} %get-tuple-element.44.refs_6_), channel_id=1, source_target_pairs={{0,2},{1,3},{2,0},{3,1},{4,6},{5,7},{6,4},{7,5},{8,10},{9,11},{10,... | collective-permute-start | bytes 393224 | tf_op jit(solution)/shard_map/ppermute | solution.py:35
  31.2 6.5 %collective-permute-start.11 = (bf16[2,128,256]{2,1,0:T(8,128)(2,1)S(1)}, bf16[2,128,256]{2,1,0:T(8,128)(2,1)S(1)}, u32[]{:S(2)}, u32[]{:S(2)}) collective-permute-start(bf16[2,128,256]{2,1,0:T(8,128)(2,1)S(1)} %collective-permute-done.7.refs_8_), channel_id=1, source_target_pairs={{0,1},{1,0},{2,3},{3,2},{4,5},{5,4},{6,7},{7,6},{8,9},{9,8},{10,11... | collective-permute-start | bytes 393224 | tf_op jit(solution)/shard_map/ppermute | solution.py:35
  31.3 24.4 %collective-permute-start.18 = (bf16[512,896]{1,0:T(8,128)(2,1)S(1)}, bf16[512,896]{1,0:T(8,128)(2,1)S(1)}, u32[]{:S(2)}, u32[]{:S(2)}) collective-permute-start(bf16[512,896]{1,0:T(8,128)(2,1)S(1)} %copy-done), channel_id=1, source_target_pairs={{0,16},{8,24},{16,0},{24,8},{1,17},{9,25},{17,1},{25,9},{2,18},{10... | collective-permute-start | bytes 2752520 | tf_op jit(solution)/shard_map/ppermute | solution.py:35
  36.2 19.5 %collective-permute-start.19 = (bf16[512,896]{1,0:T(8,128)(2,1)S(1)}, bf16[512,896]{1,0:T(8,128)(2,1)S(1)}, u32[]{:S(2)}, u32[]{:S(2)}) collective-permute-start(bf16[512,896]{1,0:T(8,128)(2,1)S(1)} %copy-done.1), channel_id=1, source_target_pairs={{0,8},{8,0},{16,24},{24,16},{1,9},{9,1},{17,25},{25,17},{2,10},{10... | collective-permute-start | bytes 2752520 | tf_op jit(solution)/shard_map/ppermute | solution.py:35
  46.7 9.2 %collective-permute-start.17 = (bf16[2,128,256]{2,1,0:T(8,128)(2,1)S(1)}, bf16[2,128,256]{2,1,0:T(8,128)(2,1)S(1)}, u32[]{:S(2)}, u32[]{:S(2)}) collective-permute-start(bf16[2,128,256]{2,1,0:T(8,128)(2,1)S(1)} %get-tuple-element.53), channel_id=1, source_target_pairs={{0,4},{1,5},{2,6},{3,7},{4,0},{5,1},{6,2},{7,3},{8,12},{9,13},{10,... | collective-permute-start | bytes 393224 | tf_op jit(solution)/shard_map/ppermute | solution.py:35
  55.8 30.9 %collective-permute-start.28 = (bf16[512,896]{1,0:T(8,128)(2,1)S(1)}, bf16[512,896]{1,0:T(8,128)(2,1)S(1)}, u32[]{:S(2)}, u32[]{:S(2)}) collective-permute-start(bf16[512,896]{1,0:T(8,128)(2,1)S(1)} %collective-permute-done.13.refs_11_), channel_id=1, source_target_pairs={{0,16},{8,24},{16,0},{24,8},{1,17},{9,25},{17,1},{25,9},{2,18},{10... | collective-permute-start | bytes 2752520 | tf_op jit(solution)/shard_map/ppermute | solution.py:35
  57.6 29.2 %collective-permute-start.29 = (bf16[512,896]{1,0:T(8,128)(2,1)S(1)}, bf16[512,896]{1,0:T(8,128)(2,1)S(1)}, u32[]{:S(2)}, u32[]{:S(2)}) collective-permute-start(bf16[512,896]{1,0:T(8,128)(2,1)S(1)} %collective-permute-done.14.refs_15_), channel_id=1, source_target_pairs={{0,8},{8,0},{16,24},{24,16},{1,9},{9,1},{17,25},{25,17},{2,10},{10... | collective-permute-start | bytes 2752520 | tf_op jit(solution)/shard_map/ppermute | solution.py:35
  58.5 6.4 %collective-permute-start.16 = (bf16[2,128,256]{2,1,0:T(8,128)(2,1)S(1)}, bf16[2,128,256]{2,1,0:T(8,128)(2,1)S(1)}, u32[]{:S(2)}, u32[]{:S(2)}) collective-permute-start(bf16[2,128,256]{2,1,0:T(8,128)(2,1)S(1)} %get-tuple-element.52), channel_id=1, source_target_pairs={{0,2},{1,3},{2,0},{3,1},{4,6},{5,7},{6,4},{7,5},{8,10},{9,11},{10,... | collective-permute-start | bytes 393224 | tf_op jit(solution)/shard_map/ppermute | solution.py:35
  60.4 7.0 %collective-permute-start.20 = (bf16[2,128,256]{2,1,0:T(8,128)(2,1)S(1)}, bf16[2,128,256]{2,1,0:T(8,128)(2,1)S(1)}, u32[]{:S(2)}, u32[]{:S(2)}) collective-permute-start(bf16[2,128,256]{2,1,0:T(8,128)(2,1)S(1)} %get-tuple-element.59), channel_id=1, source_target_pairs={{0,6},{1,7},{2,4},{3,5},{4,2},{5,3},{6,0},{7,1},{8,14},{9,15},{10,... | collective-permute-start | bytes 393224 | tf_op jit(solution)/shard_map/ppermute | solution.py:35
  67.5 8.3 %collective-permute-start.23 = (bf16[2,128,256]{2,1,0:T(8,128)(2,1)S(1)}, bf16[2,128,256]{2,1,0:T(8,128)(2,1)S(1)}, u32[]{:S(2)}, u32[]{:S(2)}) collective-permute-start(bf16[2,128,256]{2,1,0:T(8,128)(2,1)S(1)} %add_convert_fusion.refs_2_), channel_id=1, source_target_pairs={{0,6},{1,7},{2,4},{3,5},{4,2},{5,3},{6,0},{7,1},{8,14},{9,15},{10,... | collective-permute-start | bytes 393224 | tf_op jit(solution)/shard_map/ppermute | solution.py:35
  69.9 12.1 %collective-permute-start.22 = (bf16[2,128,256]{2,1,0:T(8,128)(2,1)S(1)}, bf16[2,128,256]{2,1,0:T(8,128)(2,1)S(1)}, u32[]{:S(2)}, u32[]{:S(2)}) collective-permute-start(bf16[2,128,256]{2,1,0:T(8,128)(2,1)S(1)} %add_convert_fusion.refs_2_), channel_id=1, source_target_pairs={{0,4},{1,5},{2,6},{3,7},{4,0},{5,1},{6,2},{7,3},{8,12},{9,13},{10,... | collective-permute-start | bytes 393224 | tf_op jit(solution)/shard_map/ppermute | solution.py:35
  69.9 12.1 %collective-permute-start.21 = (bf16[2,128,256]{2,1,0:T(8,128)(2,1)S(1)}, bf16[2,128,256]{2,1,0:T(8,128)(2,1)S(1)}, u32[]{:S(2)}, u32[]{:S(2)}) collective-permute-start(bf16[2,128,256]{2,1,0:T(8,128)(2,1)S(1)} %add_convert_fusion.refs_2_), channel_id=1, source_target_pairs={{0,2},{1,3},{2,0},{3,1},{4,6},{5,7},{6,4},{7,5},{8,10},{9,11},{10,... | collective-permute-start | bytes 393224 | tf_op jit(solution)/shard_map/ppermute | solution.py:35
  75.8 6.7 %collective-permute-start.27 = (bf16[2,128,256]{2,1,0:T(8,128)(2,1)S(1)}, bf16[2,128,256]{2,1,0:T(8,128)(2,1)S(1)}, u32[]{:S(2)}, u32[]{:S(2)}) collective-permute-start(bf16[2,128,256]{2,1,0:T(8,128)(2,1)S(1)} %collective-permute-done.23.refs_5_), channel_id=1, source_target_pairs={{0,1},{1,0},{2,3},{3,2},{4,5},{5,4},{6,7},{7,6},{8,9},{9,8},{10,11... | collective-permute-start | bytes 393224 | tf_op jit(solution)/shard_map/ppermute | solution.py:35
  89.8 5.5 %collective-permute-start.33 = (f32[8,128]{1,0:T(8,128)S(1)}, f32[8,128]{1,0:T(8,128)S(1)}, u32[]{:S(2)}, u32[]{:S(2)}) collective-permute-start(f32[8,128]{1,0:T(8,128)S(1)} %shard_map.164.refs_0_), channel_id=1, source_target_pairs={{0,6},{1,7},{2,4},{3,5},{4,2},{5,3},{6,0},{7,1},{8,14},{9,15},{10,... | collective-permute-start | bytes 12296 | tf_op jit(solution)/shard_map/ppermute | solution.py:35
  (15 other events, 80.5 us)

commit v14 on v13

--- a/solution.py
+++ b/solution.py
@@ -256,29 +256,6 @@
     out[...] = logprob[0:1] - logprob[1:2]
 
 
-def place_kernel(dp, ids, marks, *refs):
-    *diffs, tokens, sums = refs
-    reqs, slots = marks.shape
-    rows = diffs[0].shape[1]
-    along = lax.broadcasted_iota(jnp.int32, (1, rows), 1)
-    lane = lax.broadcasted_iota(jnp.int32, (reqs, slots), 1)
-    codes = marks[...]
-    result = jnp.zeros((reqs, slots), jnp.float32)
-    for p in range(slots):
-        code = codes[:, p : p + 1]
-        found = jnp.zeros((reqs, rows), jnp.float32)
-        for k in range(dp):
-            ranks = (ids[0] ^ ((k + 1) % dp)) * rows + along
-            found = jnp.where(code == ranks, diffs[k][...], found)
-        value = jnp.sum(found, axis=1, keepdims=True)
-        result = jnp.where(lane == p, value, result)
-    tokens[...] = result
-    total = jnp.sum(result, axis=1, keepdims=True)
-    down = lax.broadcasted_iota(jnp.int32, (reqs, reqs), 0)
-    across = lax.broadcasted_iota(jnp.int32, (reqs, reqs), 1)
-    sums[...] = jnp.sum(jnp.where(down == across, total, 0.0), axis=0, keepdims=True)
-
-
 def local(
     hidden_policy,
     hidden_reference,
@@ -380,6 +357,8 @@
         same = {0: own}
         for k in far:
             same[k] = exchange(own, "mp", 2 * k)
+        passed = lax.optimization_barrier([same[k] for k in far])
+        same.update(zip(far, passed))
         same = [same[k] for k in range(half)]
         return same + [exchange(v, "mp", 1) for v in same]
 
@@ -419,7 +398,7 @@
     if len(bits) > 1:
         for m in range(2):
             outs[m].update(later[m])
-        arrived[far[0]] = wait_for(arrived[far[0]], lambda m, k: True)
+        arrived = wait_for(arrived, lambda m, k: True)
         spread_step(outs, 1, lambda m, k: k == bit_orders[m][0])
     for k in range(1, half):
         own = own + arrived[k].astype(jnp.float32)
@@ -463,18 +442,15 @@
     diff = call(
         last_kernel,
         jax.ShapeDtypeStruct((1, rows), jnp.float32),
-        (ids, stats, *[exchange(stats, "mp", 2 * k) for k in range(1, half)]),
-    )
-    came = [exchange(diff, "dp", k) for k in range(1, dp)]
-    token_diff, seq_diff = call(
-        functools.partial(place_kernel, dp),
-        (
-            jax.ShapeDtypeStruct((reqs, slots), jnp.float32),
-            jax.ShapeDtypeStruct((1, reqs), jnp.float32),
-        ),
-        (ids, marks, *came, diff),
-    )
-    return (token_diff, seq_diff.reshape(reqs))
+        (ids, stats, *[exchange(stats, "mp", 2 * k) for k in range(half - 1, 0, -1)]),
+    )
+    came = [exchange(diff, "dp", k) for k in range(dp - 1, 0, -1)]
+    places = jnp.arange(dp, dtype=jnp.int32)[::-1] ^ dp_index
+    ranks = places[:, None] * rows + jnp.arange(rows, dtype=jnp.int32)
+    values = jnp.concatenate(came + [diff])
+    hit = marks[:, :, None, None] == ranks
+    token_diff = jnp.sum(jnp.where(hit, values, 0.0), axis=(2, 3))
+    return (token_diff, jnp.sum(token_diff, axis=1))
 
 
 def solution(mesh):

time: 106 us -> 98.4 us (0.928)
  waiting for transfers between devices: 46.8 us -> 41.2 us
  Pallas kernels: 16 us -> 14.1 us
    ppermute x37, waiting for transfers between devices: 46.8 us -> 41.2 us  [exchange(): return lax.ppermute(values, axis, [(i, i ^ flip) for i in range(count)])]
    pallas_call x9 -> x8, Pallas kernels: 16 us -> 14.1 us  [call(): pl.pallas_call(kernel, out_shape=out_shape, in_specs=specs, out_specs=jax...]
  transfers between devices with their start and end apart: 37 -> 37, of which waited for: 22 -> 25; matrix products, arithmetic and copies ran while one was open for 0% -> 0% of each run, Pallas kernels for 10% -> 11%
where the time goes in v14:
time: 98.4 us; the launch traced here: 98.1 us
  waiting for transfers between devices  41.2 us (42%)
  starting transfers between devices  40.8 us (41%)
  Pallas kernels  14.1 us (14%)
  other arithmetic  1.16 us (1%)
    ppermute x37, waiting for transfers between devices, exchange(): return lax.ppermute(values, axis, [(i, i ^ flip) for i in range(count)])  41.2 us
    ppermute x37, starting transfers between devices, exchange(): return lax.ppermute(values, axis, [(i, i ^ flip) for i in range(count)])  40.8 us
    pallas_call x8, Pallas kernels, call(): pl.pallas_call(kernel, out_shape=out_shape, in_specs=specs, out_specs=jax...  14.1 us
  transfers between devices with their start and end apart: 37, of which 25 were waited for; matrix products, arithmetic and copies ran while one was open for 0% of the time, Pallas kernels for 11%

profile of v14, /device:TPU:0, one launch (start us, length us, event | category | flops | bytes accessed | tf_op | source)
XLA Modules:
  0.0 98.1 jit_solution(18070950334073756858)
XLA Ops:
  1.6 3.0 %collective-permute-start.3 = (bf16[17,16,256]{2,1,0:T(8,128)(2,1)S(1)}, bf16[17,16,256]{2,1,0:T(8,128)(2,1)S(1)}, u32[]{:S(2)}, u32[]{:S(2)}) collective-permute-start(bf16[17,16,256]{2,1,0:T(8,128)(2,1)S(1)} %shard_map.158.refs_4_), channel_id=1, source_target_pairs={{0,16},{8,24},{16,0},{24,8},{1,17},{9,25},{17,1},{25,9},{2,18},{10... | collective-permute-start | bytes 417800 | tf_op jit(solution)/shard_map/ppermute | solution.py:35
  4.7 1.9 %collective-permute-start.1 = (bf16[16,16,256]{2,1,0:T(8,128)(2,1)}, bf16[16,16,256]{2,1,0:T(8,128)(2,1)S(1)}, u32[]{:S(2)}, u32[]{:S(2)}) collective-permute-start(bf16[16,16,256]{2,1,0:T(8,128)(2,1)} %refs_0_.1), channel_id=1, source_target_pairs={{0,8},{8,0},{16,24},{24,16},{1,9},{9,1},{17,25},{25,17},{2,10},{10... | collective-permute-start | bytes 393224 | tf_op jit(solution)/shard_map/ppermute | solution.py:35
  6.7 2.4 %collective-permute-done.3.refs_6_ = bf16[17,16,256]{2,1,0:T(8,128)(2,1)S(1)} collective-permute-done((bf16[17,16,256]{2,1,0:T(8,128)(2,1)S(1)}, bf16[17,16,256]{2,1,0:T(8,128)(2,1)S(1)}, u32[]{:S(2)}, u32[]{:S(2)}) %collective-permute-start.3) | collective-permute-done | bytes 139296 | tf_op jit(solution)/shard_map/ppermute | solution.py:35
  9.1 2.0 %collective-permute-start.5 = (bf16[17,16,256]{2,1,0:T(8,128)(2,1)S(1)}, bf16[17,16,256]{2,1,0:T(8,128)(2,1)S(1)}, u32[]{:S(2)}, u32[]{:S(2)}) collective-permute-start(bf16[17,16,256]{2,1,0:T(8,128)(2,1)S(1)} %collective-permute-done.3.refs_6_), channel_id=1, source_target_pairs={{0,8},{8,0},{16,24},{24,16},{1,9},{9,1},{17,25},{25,17},{2,10},{10... | collective-permute-start | bytes 417800 | tf_op jit(solution)/shard_map/ppermute | solution.py:35
  11.3 2.0 %collective-permute-start.4 = (bf16[16,16,256]{2,1,0:T(8,128)(2,1)S(1)}, bf16[16,16,256]{2,1,0:T(8,128)(2,1)S(1)}, u32[]{:S(2)}, u32[]{:S(2)}) collective-permute-start(bf16[16,16,256]{2,1,0:T(8,128)(2,1)S(1)} %collective-permute-done.1.refs_1_), channel_id=1, source_target_pairs={{0,16},{8,24},{16,0},{24,8},{1,17},{9,25},{17,1},{25,9},{2,18},{10... | collective-permute-start | bytes 393224 | tf_op jit(solution)/shard_map/ppermute | solution.py:35
  14.3 1.7 %collective-permute-start.13 = (bf16[512,896]{1,0:T(8,128)(2,1)}, bf16[512,896]{1,0:T(8,128)(2,1)S(1)}, u32[]{:S(2)}, u32[]{:S(2)}) collective-permute-start(bf16[512,896]{1,0:T(8,128)(2,1)} %refs_10_), channel_id=1, source_target_pairs={{0,8},{8,0},{16,24},{24,16},{1,9},{9,1},{17,25},{25,17},{2,10},{10... | collective-permute-start | bytes 2752520 | tf_op jit(solution)/shard_map/ppermute | solution.py:35
  16.0 1.8 %collective-permute-start.14 = (bf16[512,896]{1,0:T(8,128)(2,1)}, bf16[512,896]{1,0:T(8,128)(2,1)S(1)}, u32[]{:S(2)}, u32[]{:S(2)}) collective-permute-start(bf16[512,896]{1,0:T(8,128)(2,1)} %refs_13_), channel_id=1, source_target_pairs={{0,16},{8,24},{16,0},{24,8},{1,17},{9,25},{17,1},{25,9},{2,18},{10... | collective-permute-start | bytes 2752520 | tf_op jit(solution)/shard_map/ppermute | solution.py:35
  17.8 1.9 %shard_map.159 = (bf16[2,128,256]{2,1,0:T(8,128)(2,1)S(1)}, s32[128,1]{1,0:T(8,128)S(1)}, s32[16,16]{1,0:T(8,128)S(1)}) custom-call(s32[4]{0:T(128)S(1)} %pad_add_fusion.ids, s32[64]{0:T(128)} %plan_far.1, bf16[16,16,256]{2,1,0:T(8,128)(2,1)} %refs_0_.1, bf16[16,16,256]{2,1,0:T(8,128)(2,1)S(1)} %collective-permute-done.1.refs_1_, ...), custom_call_target="tpu_custom_call" | custom-call | flops 10000000000 | tf_op jit(solution)/shard_map/pallas_call | solution.py:22
  19.7 2.8 %collective-permute-start.6 = (bf16[2,128,256]{2,1,0:T(8,128)(2,1)S(1)}, bf16[2,128,256]{2,1,0:T(8,128)(2,1)S(1)}, u32[]{:S(2)}, u32[]{:S(2)}) collective-permute-start(bf16[2,128,256]{2,1,0:T(8,128)(2,1)S(1)} %get-tuple-element.50.refs_6_), channel_id=1, source_target_pairs={{0,4},{1,5},{2,6},{3,7},{4,0},{5,1},{6,2},{7,3},{8,12},{9,13},{10,... | collective-permute-start | bytes 393224 | tf_op jit(solution)/shard_map/ppermute | solution.py:35
  24.0 5.9 %collective-permute-done.6.refs_8_ = bf16[2,128,256]{2,1,0:T(8,128)(2,1)S(1)} collective-permute-done((bf16[2,128,256]{2,1,0:T(8,128)(2,1)S(1)}, bf16[2,128,256]{2,1,0:T(8,128)(2,1)S(1)}, u32[]{:S(2)}, u32[]{:S(2)}) %collective-permute-start.6) | collective-permute-done | bytes 131104 | tf_op jit(solution)/shard_map/ppermute | solution.py:35
  32.2 1.7 %collective-permute-start.19 = (bf16[512,896]{1,0:T(8,128)(2,1)S(1)}, bf16[512,896]{1,0:T(8,128)(2,1)S(1)}, u32[]{:S(2)}, u32[]{:S(2)}) collective-permute-start(bf16[512,896]{1,0:T(8,128)(2,1)S(1)} %copy-done), channel_id=1, source_target_pairs={{0,16},{8,24},{16,0},{24,8},{1,17},{9,25},{17,1},{25,9},{2,18},{10... | collective-permute-start | bytes 2752520 | tf_op jit(solution)/shard_map/ppermute | solution.py:35
  36.8 5.0 %shard_map.160 = (f32[4,2,128,256]{3,2,1,0:T(8,128)S(1)}, bf16[4,2,128,256]{3,2,1,0:T(8,128)(2,1)S(1)}) custom-call(s32[4]{0:T(128)S(1)} %pad_add_fusion.ids, f32[8,1,256]{2,1,0:T(1,128)} %bitcast.8, f32[8,1,256]{2,1,0:T(1,128)} %bitcast.9, bf16[2048,512]{1,0:T(8,128)(2,1)} %refs_2_.1, bf16[2048,512]{1,0:T(8,128)(2,1)} %refs_3_.1, ...), custom_call_target="tpu_custom_call" | custom-call | tf_op jit(solution)/shard_map/pallas_call | solution.py:22
  42.0 1.8 %collective-permute-done.15.came = bf16[4,2,128,256]{3,2,1,0:T(8,128)(2,1)S(1)} collective-permute-done((bf16[4,2,128,256]{3,2,1,0:T(8,128)(2,1)S(1)}, bf16[4,2,128,256]{3,2,1,0:T(8,128)(2,1)S(1)}, u32[]{:S(2)}, u32[]{:S(2)}) %collective-permute-start.15) | collective-permute-done | bytes 524320 | tf_op jit(solution)/shard_map/ppermute | solution.py:35
  45.3 2.5 %collective-permute-start.17 = (bf16[2,128,256]{2,1,0:T(8,128)(2,1)S(1)}, bf16[2,128,256]{2,1,0:T(8,128)(2,1)S(1)}, u32[]{:S(2)}, u32[]{:S(2)}) collective-permute-start(bf16[2,128,256]{2,1,0:T(8,128)(2,1)S(1)} %get-tuple-element.62), channel_id=1, source_target_pairs={{0,4},{1,5},{2,6},{3,7},{4,0},{5,1},{6,2},{7,3},{8,12},{9,13},{10,... | collective-permute-start | bytes 393224 | tf_op jit(solution)/shard_map/ppermute | solution.py:35
  48.9 6.8 %collective-permute-done.19.refs_12_ = bf16[512,896]{1,0:T(8,128)(2,1)S(1)} collective-permute-done((bf16[512,896]{1,0:T(8,128)(2,1)S(1)}, bf16[512,896]{1,0:T(8,128)(2,1)S(1)}, u32[]{:S(2)}, u32[]{:S(2)}) %collective-permute-start.19) | collective-permute-done | bytes 917536 | tf_op jit(solution)/shard_map/ppermute | solution.py:35
  56.0 1.8 %collective-permute-done.18 = bf16[2,128,256]{2,1,0:T(8,128)(2,1)S(1)} collective-permute-done((bf16[2,128,256]{2,1,0:T(8,128)(2,1)S(1)}, bf16[2,128,256]{2,1,0:T(8,128)(2,1)S(1)}, u32[]{:S(2)}, u32[]{:S(2)}) %collective-permute-start.18) | collective-permute-done | bytes 131104 | tf_op jit(solution)/shard_map/ppermute | solution.py:35
  59.0 4.4 %collective-permute-start.21 = (bf16[2,128,256]{2,1,0:T(8,128)(2,1)S(1)}, bf16[2,128,256]{2,1,0:T(8,128)(2,1)S(1)}, u32[]{:S(2)}, u32[]{:S(2)}) collective-permute-start(bf16[2,128,256]{2,1,0:T(8,128)(2,1)S(1)} %add_convert_fusion.refs_2_), channel_id=1, source_target_pairs={{0,4},{1,5},{2,6},{3,7},{4,0},{5,1},{6,2},{7,3},{8,12},{9,13},{10,... | collective-permute-start | bytes 393224 | tf_op jit(solution)/shard_map/ppermute | solution.py:35
  64.0 7.9 %collective-permute-done.21.refs_4_ = bf16[2,128,256]{2,1,0:T(8,128)(2,1)S(1)} collective-permute-done((bf16[2,128,256]{2,1,0:T(8,128)(2,1)S(1)}, bf16[2,128,256]{2,1,0:T(8,128)(2,1)S(1)}, u32[]{:S(2)}, u32[]{:S(2)}) %collective-permute-start.21) | collective-permute-done | bytes 131104 | tf_op jit(solution)/shard_map/ppermute | solution.py:35
  74.9 3.2 %shard_map.162 = (f32[2,128,896]{2,1,0:T(8,128)S(1)}, bf16[2,128,512]{2,1,0:T(8,128)(2,1)S(1)}) custom-call(s32[4]{0:T(128)S(1)} %pad_add_fusion.ids, f32[8,1,256]{2,1,0:T(1,128)} %bitcast.10, f32[8,1,256]{2,1,0:T(1,128)} %bitcast.11, bf16[2,128,256]{2,1,0:T(8,128)(2,1)S(1)} %add_convert_fusion.refs_2_, ...), custom_call_target="tpu_custom_call" | custom-call | tf_op jit(solution)/shard_map/pallas_call | solution.py:22
  82.6 2.9 %collective-permute-start.31 = (f32[8,128]{1,0:T(8,128)S(1)}, f32[8,128]{1,0:T(8,128)S(1)}, u32[]{:S(2)}, u32[]{:S(2)}) collective-permute-start(f32[8,128]{1,0:T(8,128)S(1)} %shard_map.164.refs_0_), channel_id=1, source_target_pairs={{0,6},{1,7},{2,4},{3,5},{4,2},{5,3},{6,0},{7,1},{8,14},{9,15},{10,... | collective-permute-start | bytes 12296 | tf_op jit(solution)/shard_map/ppermute | solution.py:35
  85.5 2.0 %collective-permute-start.32 = (f32[8,128]{1,0:T(8,128)S(1)}, f32[8,128]{1,0:T(8,128)S(1)}, u32[]{:S(2)}, u32[]{:S(2)}) collective-permute-start(f32[8,128]{1,0:T(8,128)S(1)} %shard_map.164.refs_0_), channel_id=1, source_target_pairs={{0,4},{1,5},{2,6},{3,7},{4,0},{5,1},{6,2},{7,3},{8,12},{9,13},{10,... | collective-permute-start | bytes 12296 | tf_op jit(solution)/shard_map/ppermute | solution.py:35
  88.1 1.9 %collective-permute-done.32.refs_2_ = f32[8,128]{1,0:T(8,128)S(1)} collective-permute-done((f32[8,128]{1,0:T(8,128)S(1)}, f32[8,128]{1,0:T(8,128)S(1)}, u32[]{:S(2)}, u32[]{:S(2)}) %collective-permute-start.32) | collective-permute-done | bytes 4128 | tf_op jit(solution)/shard_map/ppermute | solution.py:35
  91.7 1.5 %collective-permute-start.34 = (f32[1,128]{1,0:T(1,128)S(1)}, f32[1,128]{1,0:T(1,128)S(1)}, u32[]{:S(2)}, u32[]{:S(2)}) collective-permute-start(f32[1,128]{1,0:T(1,128)S(1)} %shard_map.165), channel_id=1, source_target_pairs={{0,24},{8,16},{16,8},{24,0},{1,25},{9,17},{17,9},{25,1},{2,26},{10... | collective-permute-start | bytes 1544 | tf_op jit(solution)/shard_map/ppermute | solution.py:35
  93.7 1.6 %collective-permute-start.36 = (f32[1,128]{1,0:T(1,128)S(1)}, f32[1,128]{1,0:T(1,128)S(1)}, u32[]{:S(2)}, u32[]{:S(2)}) collective-permute-start(f32[1,128]{1,0:T(1,128)S(1)} %shard_map.165), channel_id=1, source_target_pairs={{0,8},{8,0},{16,24},{24,16},{1,9},{9,1},{17,25},{25,17},{2,10},{10... | collective-permute-start | bytes 1544 | tf_op jit(solution)/shard_map/ppermute | solution.py:35
  (70 shorter events, 27.0 us)
Async XLA Ops:
  1.6 7.5 %collective-permute-start.3 = (bf16[17,16,256]{2,1,0:T(8,128)(2,1)S(1)}, bf16[17,16,256]{2,1,0:T(8,128)(2,1)S(1)}, u32[]{:S(2)}, u32[]{:S(2)}) collective-permute-start(bf16[17,16,256]{2,1,0:T(8,128)(2,1)S(1)} %shard_map.158.refs_4_), channel_id=1, source_target_pairs={{0,16},{8,24},{16,0},{24,8},{1,17},{9,25},{17,1},{25,9},{2,18},{10... | collective-permute-start | bytes 417800 | tf_op jit(solution)/shard_map/ppermute | solution.py:35
  4.6 6.5 %collective-permute-start = (bf16[16,16,256]{2,1,0:T(8,128)(2,1)}, bf16[16,16,256]{2,1,0:T(8,128)(2,1)S(1)}, u32[]{:S(2)}, u32[]{:S(2)}) collective-permute-start(bf16[16,16,256]{2,1,0:T(8,128)(2,1)} %refs_0_.1), channel_id=1, source_target_pairs={{0,16},{8,24},{16,0},{24,8},{1,17},{9,25},{17,1},{25,9},{2,18},{10... | collective-permute-start | bytes 393224 | tf_op jit(solution)/shard_map/ppermute | solution.py:35
  4.7 6.6 %collective-permute-start.1 = (bf16[16,16,256]{2,1,0:T(8,128)(2,1)}, bf16[16,16,256]{2,1,0:T(8,128)(2,1)S(1)}, u32[]{:S(2)}, u32[]{:S(2)}) collective-permute-start(bf16[16,16,256]{2,1,0:T(8,128)(2,1)} %refs_0_.1), channel_id=1, source_target_pairs={{0,8},{8,0},{16,24},{24,16},{1,9},{9,1},{17,25},{25,17},{2,10},{10... | collective-permute-start | bytes 393224 | tf_op jit(solution)/shard_map/ppermute | solution.py:35
  6.6 7.7 %collective-permute-start.2 = (bf16[17,16,256]{2,1,0:T(8,128)(2,1)S(1)}, bf16[17,16,256]{2,1,0:T(8,128)(2,1)S(1)}, u32[]{:S(2)}, u32[]{:S(2)}) collective-permute-start(bf16[17,16,256]{2,1,0:T(8,128)(2,1)S(1)} %shard_map.158.refs_4_), channel_id=1, source_target_pairs={{0,8},{8,0},{16,24},{24,16},{1,9},{9,1},{17,25},{25,17},{2,10},{10... | collective-permute-start | bytes 417800 | tf_op jit(solution)/shard_map/ppermute | solution.py:35
  9.1 8.7 %collective-permute-start.5 = (bf16[17,16,256]{2,1,0:T(8,128)(2,1)S(1)}, bf16[17,16,256]{2,1,0:T(8,128)(2,1)S(1)}, u32[]{:S(2)}, u32[]{:S(2)}) collective-permute-start(bf16[17,16,256]{2,1,0:T(8,128)(2,1)S(1)} %collective-permute-done.3.refs_6_), channel_id=1, source_target_pairs={{0,8},{8,0},{16,24},{24,16},{1,9},{9,1},{17,25},{25,17},{2,10},{10... | collective-permute-start | bytes 417800 | tf_op jit(solution)/shard_map/ppermute | solution.py:35
  11.3 6.4 %collective-permute-start.4 = (bf16[16,16,256]{2,1,0:T(8,128)(2,1)S(1)}, bf16[16,16,256]{2,1,0:T(8,128)(2,1)S(1)}, u32[]{:S(2)}, u32[]{:S(2)}) collective-permute-start(bf16[16,16,256]{2,1,0:T(8,128)(2,1)S(1)} %collective-permute-done.1.refs_1_), channel_id=1, source_target_pairs={{0,16},{8,24},{16,0},{24,8},{1,17},{9,25},{17,1},{25,9},{2,18},{10... | collective-permute-start | bytes 393224 | tf_op jit(solution)/shard_map/ppermute | solution.py:35
  14.3 27.5 %collective-permute-start.13 = (bf16[512,896]{1,0:T(8,128)(2,1)}, bf16[512,896]{1,0:T(8,128)(2,1)S(1)}, u32[]{:S(2)}, u32[]{:S(2)}) collective-permute-start(bf16[512,896]{1,0:T(8,128)(2,1)} %refs_10_), channel_id=1, source_target_pairs={{0,8},{8,0},{16,24},{24,16},{1,9},{9,1},{17,25},{25,17},{2,10},{10... | collective-permute-start | bytes 2752520 | tf_op jit(solution)/shard_map/ppermute | solution.py:35
  16.0 25.8 %collective-permute-start.14 = (bf16[512,896]{1,0:T(8,128)(2,1)}, bf16[512,896]{1,0:T(8,128)(2,1)S(1)}, u32[]{:S(2)}, u32[]{:S(2)}) collective-permute-start(bf16[512,896]{1,0:T(8,128)(2,1)} %refs_13_), channel_id=1, source_target_pairs={{0,16},{8,24},{16,0},{24,8},{1,17},{9,25},{17,1},{25,9},{2,18},{10... | collective-permute-start | bytes 2752520 | tf_op jit(solution)/shard_map/ppermute | solution.py:35
  19.7 10.2 %collective-permute-start.6 = (bf16[2,128,256]{2,1,0:T(8,128)(2,1)S(1)}, bf16[2,128,256]{2,1,0:T(8,128)(2,1)S(1)}, u32[]{:S(2)}, u32[]{:S(2)}) collective-permute-start(bf16[2,128,256]{2,1,0:T(8,128)(2,1)S(1)} %get-tuple-element.50.refs_6_), channel_id=1, source_target_pairs={{0,4},{1,5},{2,6},{3,7},{4,0},{5,1},{6,2},{7,3},{8,12},{9,13},{10,... | collective-permute-start | bytes 393224 | tf_op jit(solution)/shard_map/ppermute | solution.py:35
  22.4 7.5 %collective-permute-start.7 = (bf16[2,128,256]{2,1,0:T(8,128)(2,1)S(1)}, bf16[2,128,256]{2,1,0:T(8,128)(2,1)S(1)}, u32[]{:S(2)}, u32[]{:S(2)}) collective-permute-start(bf16[2,128,256]{2,1,0:T(8,128)(2,1)S(1)} %get-tuple-element.50.refs_6_), channel_id=1, source_target_pairs={{0,6},{1,7},{2,4},{3,5},{4,2},{5,3},{6,0},{7,1},{8,14},{9,15},{10,... | collective-permute-start | bytes 393224 | tf_op jit(solution)/shard_map/ppermute | solution.py:35
  23.8 7.1 %collective-permute-start.8 = (bf16[2,128,256]{2,1,0:T(8,128)(2,1)S(1)}, bf16[2,128,256]{2,1,0:T(8,128)(2,1)S(1)}, u32[]{:S(2)}, u32[]{:S(2)}) collective-permute-start(bf16[2,128,256]{2,1,0:T(8,128)(2,1)S(1)} %get-tuple-element.50.refs_6_), channel_id=1, source_target_pairs={{0,2},{1,3},{2,0},{3,1},{4,6},{5,7},{6,4},{7,5},{8,10},{9,11},{10,... | collective-permute-start | bytes 393224 | tf_op jit(solution)/shard_map/ppermute | solution.py:35
  32.2 23.4 %collective-permute-start.19 = (bf16[512,896]{1,0:T(8,128)(2,1)S(1)}, bf16[512,896]{1,0:T(8,128)(2,1)S(1)}, u32[]{:S(2)}, u32[]{:S(2)}) collective-permute-start(bf16[512,896]{1,0:T(8,128)(2,1)S(1)} %copy-done), channel_id=1, source_target_pairs={{0,16},{8,24},{16,0},{24,8},{1,17},{9,25},{17,1},{25,9},{2,18},{10... | collective-permute-start | bytes 2752520 | tf_op jit(solution)/shard_map/ppermute | solution.py:35
  33.9 22.1 %collective-permute-start.20 = (bf16[512,896]{1,0:T(8,128)(2,1)S(1)}, bf16[512,896]{1,0:T(8,128)(2,1)S(1)}, u32[]{:S(2)}, u32[]{:S(2)}) collective-permute-start(bf16[512,896]{1,0:T(8,128)(2,1)S(1)} %copy-done.1), channel_id=1, source_target_pairs={{0,8},{8,0},{16,24},{24,16},{1,9},{9,1},{17,25},{25,17},{2,10},{10... | collective-permute-start | bytes 2752520 | tf_op jit(solution)/shard_map/ppermute | solution.py:35
  44.4 11.6 %collective-permute-start.16 = (bf16[2,128,256]{2,1,0:T(8,128)(2,1)S(1)}, bf16[2,128,256]{2,1,0:T(8,128)(2,1)S(1)}, u32[]{:S(2)}, u32[]{:S(2)}) collective-permute-start(bf16[2,128,256]{2,1,0:T(8,128)(2,1)S(1)} %get-tuple-element.61), channel_id=1, source_target_pairs={{0,2},{1,3},{2,0},{3,1},{4,6},{5,7},{6,4},{7,5},{8,10},{9,11},{10,... | collective-permute-start | bytes 393224 | tf_op jit(solution)/shard_map/ppermute | solution.py:35
  45.3 10.8 %collective-permute-start.17 = (bf16[2,128,256]{2,1,0:T(8,128)(2,1)S(1)}, bf16[2,128,256]{2,1,0:T(8,128)(2,1)S(1)}, u32[]{:S(2)}, u32[]{:S(2)}) collective-permute-start(bf16[2,128,256]{2,1,0:T(8,128)(2,1)S(1)} %get-tuple-element.62), channel_id=1, source_target_pairs={{0,4},{1,5},{2,6},{3,7},{4,0},{5,1},{6,2},{7,3},{8,12},{9,13},{10,... | collective-permute-start | bytes 393224 | tf_op jit(solution)/shard_map/ppermute | solution.py:35
  47.8 10.1 %collective-permute-start.18 = (bf16[2,128,256]{2,1,0:T(8,128)(2,1)S(1)}, bf16[2,128,256]{2,1,0:T(8,128)(2,1)S(1)}, u32[]{:S(2)}, u32[]{:S(2)}) collective-permute-start(bf16[2,128,256]{2,1,0:T(8,128)(2,1)S(1)} %get-tuple-element.63), channel_id=1, source_target_pairs={{0,6},{1,7},{2,4},{3,5},{4,2},{5,3},{6,0},{7,1},{8,14},{9,15},{10,... | collective-permute-start | bytes 393224 | tf_op jit(solution)/shard_map/ppermute | solution.py:35
  57.9 21.5 %collective-permute-start.28 = (bf16[512,896]{1,0:T(8,128)(2,1)S(1)}, bf16[512,896]{1,0:T(8,128)(2,1)S(1)}, u32[]{:S(2)}, u32[]{:S(2)}) collective-permute-start(bf16[512,896]{1,0:T(8,128)(2,1)S(1)} %collective-permute-done.13.refs_11_), channel_id=1, source_target_pairs={{0,16},{8,24},{16,0},{24,8},{1,17},{9,25},{17,1},{25,9},{2,18},{10... | collective-permute-start | bytes 2752520 | tf_op jit(solution)/shard_map/ppermute | solution.py:35
  58.4 21.2 %collective-permute-start.29 = (bf16[512,896]{1,0:T(8,128)(2,1)S(1)}, bf16[512,896]{1,0:T(8,128)(2,1)S(1)}, u32[]{:S(2)}, u32[]{:S(2)}) collective-permute-start(bf16[512,896]{1,0:T(8,128)(2,1)S(1)} %collective-permute-done.14.refs_15_), channel_id=1, source_target_pairs={{0,8},{8,0},{16,24},{24,16},{1,9},{9,1},{17,25},{25,17},{2,10},{10... | collective-permute-start | bytes 2752520 | tf_op jit(solution)/shard_map/ppermute | solution.py:35
  59.0 13.0 %collective-permute-start.21 = (bf16[2,128,256]{2,1,0:T(8,128)(2,1)S(1)}, bf16[2,128,256]{2,1,0:T(8,128)(2,1)S(1)}, u32[]{:S(2)}, u32[]{:S(2)}) collective-permute-start(bf16[2,128,256]{2,1,0:T(8,128)(2,1)S(1)} %add_convert_fusion.refs_2_), channel_id=1, source_target_pairs={{0,4},{1,5},{2,6},{3,7},{4,0},{5,1},{6,2},{7,3},{8,12},{9,13},{10,... | collective-permute-start | bytes 393224 | tf_op jit(solution)/shard_map/ppermute | solution.py:35
  63.4 8.6 %collective-permute-start.22 = (bf16[2,128,256]{2,1,0:T(8,128)(2,1)S(1)}, bf16[2,128,256]{2,1,0:T(8,128)(2,1)S(1)}, u32[]{:S(2)}, u32[]{:S(2)}) collective-permute-start(bf16[2,128,256]{2,1,0:T(8,128)(2,1)S(1)} %add_convert_fusion.refs_2_), channel_id=1, source_target_pairs={{0,6},{1,7},{2,4},{3,5},{4,2},{5,3},{6,0},{7,1},{8,14},{9,15},{10,... | collective-permute-start | bytes 393224 | tf_op jit(solution)/shard_map/ppermute | solution.py:35
  64.0 9.1 %collective-permute-start.23 = (bf16[2,128,256]{2,1,0:T(8,128)(2,1)S(1)}, bf16[2,128,256]{2,1,0:T(8,128)(2,1)S(1)}, u32[]{:S(2)}, u32[]{:S(2)}) collective-permute-start(bf16[2,128,256]{2,1,0:T(8,128)(2,1)S(1)} %add_convert_fusion.refs_2_), channel_id=1, source_target_pairs={{0,2},{1,3},{2,0},{3,1},{4,6},{5,7},{6,4},{7,5},{8,10},{9,11},{10,... | collective-permute-start | bytes 393224 | tf_op jit(solution)/shard_map/ppermute | solution.py:35
  82.6 5.5 %collective-permute-start.31 = (f32[8,128]{1,0:T(8,128)S(1)}, f32[8,128]{1,0:T(8,128)S(1)}, u32[]{:S(2)}, u32[]{:S(2)}) collective-permute-start(f32[8,128]{1,0:T(8,128)S(1)} %shard_map.164.refs_0_), channel_id=1, source_target_pairs={{0,6},{1,7},{2,4},{3,5},{4,2},{5,3},{6,0},{7,1},{8,14},{9,15},{10,... | collective-permute-start | bytes 12296 | tf_op jit(solution)/shard_map/ppermute | solution.py:35
  85.5 4.5 %collective-permute-start.32 = (f32[8,128]{1,0:T(8,128)S(1)}, f32[8,128]{1,0:T(8,128)S(1)}, u32[]{:S(2)}, u32[]{:S(2)}) collective-permute-start(f32[8,128]{1,0:T(8,128)S(1)} %shard_map.164.refs_0_), channel_id=1, source_target_pairs={{0,4},{1,5},{2,6},{3,7},{4,0},{5,1},{6,2},{7,3},{8,12},{9,13},{10,... | collective-permute-start | bytes 12296 | tf_op jit(solution)/shard_map/ppermute | solution.py:35
  91.7 4.5 %collective-permute-start.34 = (f32[1,128]{1,0:T(1,128)S(1)}, f32[1,128]{1,0:T(1,128)S(1)}, u32[]{:S(2)}, u32[]{:S(2)}) collective-permute-start(f32[1,128]{1,0:T(1,128)S(1)} %shard_map.165), channel_id=1, source_target_pairs={{0,24},{8,16},{16,8},{24,0},{1,25},{9,17},{17,9},{25,1},{2,26},{10... | collective-permute-start | bytes 1544 | tf_op jit(solution)/shard_map/ppermute | solution.py:35
  (15 other events, 68.9 us)

commit v15 on v8

--- a/solution.py
+++ b/solution.py
@@ -345,6 +345,8 @@
         same = {0: own}
         for k in far:
             same[k] = exchange(own, "mp", 2 * k)
+        passed = lax.optimization_barrier([same[k] for k in far])
+        same.update(zip(far, passed))
         same = [same[k] for k in range(half)]
         return same + [exchange(v, "mp", 1) for v in same]
 
@@ -435,7 +437,7 @@
     diff = call(
         last_kernel,
         jax.ShapeDtypeStruct((1, rows), jnp.float32),
-        (ids, stats, *[exchange(stats, "mp", 2 * k) for k in far]),
+        (ids, stats, *[exchange(stats, "mp", 2 * k) for k in range(half - 1, 0, -1)]),
     )
     diff = jnp.concatenate([diff] + [exchange(diff, "dp", k) for k in range(1, dp)])
     ranks = ((order ^ dp_index)[:, None] * rows + jnp.arange(rows, dtype=jnp.int32)).reshape(-1)

time: 97.5 us -> 98.1 us (level)
  waiting for transfers between devices: 37.8 us -> 38.8 us
  transfers between devices with their start and end apart: 37 -> 37, of which waited for: 20 -> 19; matrix products, arithmetic and copies ran while one was open for 2% -> 2% of each run, Pallas kernels for 12% -> 12%
where the time goes in v15:
time: 98.1 us; the launch traced here: 97.9 us
  starting transfers between devices  40.4 us (41%)
  waiting for transfers between devices  38.8 us (40%)
  Pallas kernels  15.3 us (16%)
  other arithmetic  2.05 us (2%)
    ppermute x37, starting transfers between devices, exchange(): return lax.ppermute(values, axis, [(i, i ^ flip) for i in range(count)])  40.4 us
    ppermute x37, waiting for transfers between devices, exchange(): return lax.ppermute(values, axis, [(i, i ^ flip) for i in range(count)])  38.8 us
    pallas_call x8, Pallas kernels, call(): pl.pallas_call(kernel, out_shape=out_shape, in_specs=specs, out_specs=jax...  15.3 us
  transfers between devices with their start and end apart: 37, of which 19 were waited for; matrix products, arithmetic and copies ran while one was open for 2% of the time, Pallas kernels for 12%

profile of v15, /device:TPU:0, one launch (start us, length us, event | category | flops | bytes accessed | tf_op | source)
XLA Modules:
  0.0 97.9 jit_solution(13653479547500634764)
XLA Ops:
  1.6 3.0 %collective-permute-start.3 = (bf16[17,16,256]{2,1,0:T(8,128)(2,1)S(1)}, bf16[17,16,256]{2,1,0:T(8,128)(2,1)S(1)}, u32[]{:S(2)}, u32[]{:S(2)}) collective-permute-start(bf16[17,16,256]{2,1,0:T(8,128)(2,1)S(1)} %shard_map.158.refs_4_), channel_id=1, source_target_pairs={{0,16},{8,24},{16,0},{24,8},{1,17},{9,25},{17,1},{25,9},{2,18},{10... | collective-permute-start | bytes 417800 | tf_op jit(solution)/shard_map/ppermute | solution.py:35
  4.7 1.9 %collective-permute-start.1 = (bf16[16,16,256]{2,1,0:T(8,128)(2,1)}, bf16[16,16,256]{2,1,0:T(8,128)(2,1)S(1)}, u32[]{:S(2)}, u32[]{:S(2)}) collective-permute-start(bf16[16,16,256]{2,1,0:T(8,128)(2,1)} %refs_0_.1), channel_id=1, source_target_pairs={{0,8},{8,0},{16,24},{24,16},{1,9},{9,1},{17,25},{25,17},{2,10},{10... | collective-permute-start | bytes 393224 | tf_op jit(solution)/shard_map/ppermute | solution.py:35
  6.7 2.4 %collective-permute-done.3.refs_6_ = bf16[17,16,256]{2,1,0:T(8,128)(2,1)S(1)} collective-permute-done((bf16[17,16,256]{2,1,0:T(8,128)(2,1)S(1)}, bf16[17,16,256]{2,1,0:T(8,128)(2,1)S(1)}, u32[]{:S(2)}, u32[]{:S(2)}) %collective-permute-start.3) | collective-permute-done | bytes 139296 | tf_op jit(solution)/shard_map/ppermute | solution.py:35
  9.1 2.0 %collective-permute-start.5 = (bf16[17,16,256]{2,1,0:T(8,128)(2,1)S(1)}, bf16[17,16,256]{2,1,0:T(8,128)(2,1)S(1)}, u32[]{:S(2)}, u32[]{:S(2)}) collective-permute-start(bf16[17,16,256]{2,1,0:T(8,128)(2,1)S(1)} %collective-permute-done.3.refs_6_), channel_id=1, source_target_pairs={{0,8},{8,0},{16,24},{24,16},{1,9},{9,1},{17,25},{25,17},{2,10},{10... | collective-permute-start | bytes 417800 | tf_op jit(solution)/shard_map/ppermute | solution.py:35
  11.3 2.0 %collective-permute-start.4 = (bf16[16,16,256]{2,1,0:T(8,128)(2,1)S(1)}, bf16[16,16,256]{2,1,0:T(8,128)(2,1)S(1)}, u32[]{:S(2)}, u32[]{:S(2)}) collective-permute-start(bf16[16,16,256]{2,1,0:T(8,128)(2,1)S(1)} %collective-permute-done.1.refs_1_), channel_id=1, source_target_pairs={{0,16},{8,24},{16,0},{24,8},{1,17},{9,25},{17,1},{25,9},{2,18},{10... | collective-permute-start | bytes 393224 | tf_op jit(solution)/shard_map/ppermute | solution.py:35
  14.3 1.7 %collective-permute-start.13 = (bf16[512,896]{1,0:T(8,128)(2,1)}, bf16[512,896]{1,0:T(8,128)(2,1)S(1)}, u32[]{:S(2)}, u32[]{:S(2)}) collective-permute-start(bf16[512,896]{1,0:T(8,128)(2,1)} %refs_10_), channel_id=1, source_target_pairs={{0,8},{8,0},{16,24},{24,16},{1,9},{9,1},{17,25},{25,17},{2,10},{10... | collective-permute-start | bytes 2752520 | tf_op jit(solution)/shard_map/ppermute | solution.py:35
  16.0 1.8 %collective-permute-start.14 = (bf16[512,896]{1,0:T(8,128)(2,1)}, bf16[512,896]{1,0:T(8,128)(2,1)}, u32[]{:S(2)}, u32[]{:S(2)}) collective-permute-start(bf16[512,896]{1,0:T(8,128)(2,1)} %refs_13_), channel_id=1, source_target_pairs={{0,16},{8,24},{16,0},{24,8},{1,17},{9,25},{17,1},{25,9},{2,18},{10... | collective-permute-start | bytes 2752520 | tf_op jit(solution)/shard_map/ppermute | solution.py:35
  17.8 1.8 %shard_map.159 = (bf16[2,128,256]{2,1,0:T(8,128)(2,1)S(1)}, f32[4,16,256]{2,1,0:T(8,128)S(1)}) custom-call(s32[4]{0:T(128)S(1)} %pad_add_fusion.ids, s32[64]{0:T(128)} %plan_far.1, bf16[16,16,256]{2,1,0:T(8,128)(2,1)} %refs_0_.1, bf16[16,16,256]{2,1,0:T(8,128)(2,1)S(1)} %collective-permute-done.1.refs_1_, ...), custom_call_target="tpu_custom_call" | custom-call | flops 10000000000 | tf_op jit(solution)/shard_map/pallas_call | solution.py:22
  19.6 2.7 %collective-permute-start.6 = (bf16[2,128,256]{2,1,0:T(8,128)(2,1)S(1)}, bf16[2,128,256]{2,1,0:T(8,128)(2,1)S(1)}, u32[]{:S(2)}, u32[]{:S(2)}) collective-permute-start(bf16[2,128,256]{2,1,0:T(8,128)(2,1)S(1)} %get-tuple-element.46.refs_6_), channel_id=1, source_target_pairs={{0,4},{1,5},{2,6},{3,7},{4,0},{5,1},{6,2},{7,3},{8,12},{9,13},{10,... | collective-permute-start | bytes 393224 | tf_op jit(solution)/shard_map/ppermute | solution.py:35
  23.9 5.9 %collective-permute-done.6.refs_8_ = bf16[2,128,256]{2,1,0:T(8,128)(2,1)S(1)} collective-permute-done((bf16[2,128,256]{2,1,0:T(8,128)(2,1)S(1)}, bf16[2,128,256]{2,1,0:T(8,128)(2,1)S(1)}, u32[]{:S(2)}, u32[]{:S(2)}) %collective-permute-start.6) | collective-permute-done | bytes 131104 | tf_op jit(solution)/shard_map/ppermute | solution.py:35
  32.3 1.7 %collective-permute-start.18 = (bf16[512,896]{1,0:T(8,128)(2,1)}, bf16[512,896]{1,0:T(8,128)(2,1)}, u32[]{:S(2)}, u32[]{:S(2)}) collective-permute-start(bf16[512,896]{1,0:T(8,128)(2,1)} %refs_10_), channel_id=1, source_target_pairs={{0,16},{8,24},{16,0},{24,8},{1,17},{9,25},{17,1},{25,9},{2,18},{10... | collective-permute-start | bytes 2752520 | tf_op jit(solution)/shard_map/ppermute | solution.py:35
  34.0 1.5 %collective-permute-start.19 = (bf16[512,896]{1,0:T(8,128)(2,1)}, bf16[512,896]{1,0:T(8,128)(2,1)}, u32[]{:S(2)}, u32[]{:S(2)}) collective-permute-start(bf16[512,896]{1,0:T(8,128)(2,1)} %refs_13_), channel_id=1, source_target_pairs={{0,8},{8,0},{16,24},{24,16},{1,9},{9,1},{17,25},{25,17},{2,10},{10... | collective-permute-start | bytes 2752520 | tf_op jit(solution)/shard_map/ppermute | solution.py:35
  35.5 5.0 %shard_map.160 = (f32[4,2,128,256]{3,2,1,0:T(8,128)S(1)}, bf16[4,2,128,256]{3,2,1,0:T(8,128)(2,1)S(1)}) custom-call(s32[4]{0:T(128)S(1)} %pad_add_fusion.ids, f32[8,1,256]{2,1,0:T(1,128)} %bitcast.13, f32[8,1,256]{2,1,0:T(1,128)} %bitcast.14, bf16[2048,512]{1,0:T(8,128)(2,1)} %refs_2_.1, bf16[2048,512]{1,0:T(8,128)(2,1)} %refs_3_.1, ...), custom_call_target="tpu_custom_call" | custom-call | tf_op jit(solution)/shard_map/pallas_call | solution.py:22
  40.8 1.7 %collective-permute-done.15.came = bf16[4,2,128,256]{3,2,1,0:T(8,128)(2,1)S(1)} collective-permute-done((bf16[4,2,128,256]{3,2,1,0:T(8,128)(2,1)S(1)}, bf16[4,2,128,256]{3,2,1,0:T(8,128)(2,1)S(1)}, u32[]{:S(2)}, u32[]{:S(2)}) %collective-permute-start.15) | collective-permute-done | bytes 524320 | tf_op jit(solution)/shard_map/ppermute | solution.py:35
  43.1 2.8 %collective-permute-start.17 = (bf16[2,128,256]{2,1,0:T(8,128)(2,1)S(1)}, bf16[2,128,256]{2,1,0:T(8,128)(2,1)S(1)}, u32[]{:S(2)}, u32[]{:S(2)}) collective-permute-start(bf16[2,128,256]{2,1,0:T(8,128)(2,1)S(1)} %get-tuple-element.58), channel_id=1, source_target_pairs={{0,4},{1,5},{2,6},{3,7},{4,0},{5,1},{6,2},{7,3},{8,12},{9,13},{10,... | collective-permute-start | bytes 393224 | tf_op jit(solution)/shard_map/ppermute | solution.py:35
  47.6 8.1 %collective-permute-done.18.refs_12_ = bf16[512,896]{1,0:T(8,128)(2,1)} collective-permute-done((bf16[512,896]{1,0:T(8,128)(2,1)}, bf16[512,896]{1,0:T(8,128)(2,1)}, u32[]{:S(2)}, u32[]{:S(2)}) %collective-permute-start.18) | collective-permute-done | bytes 917536 | tf_op jit(solution)/shard_map/ppermute | solution.py:35
  58.7 2.8 %collective-permute-start.21 = (bf16[2,128,256]{2,1,0:T(8,128)(2,1)S(1)}, bf16[2,128,256]{2,1,0:T(8,128)(2,1)S(1)}, u32[]{:S(2)}, u32[]{:S(2)}) collective-permute-start(bf16[2,128,256]{2,1,0:T(8,128)(2,1)S(1)} %add_convert_fusion.refs_2_), channel_id=1, source_target_pairs={{0,4},{1,5},{2,6},{3,7},{4,0},{5,1},{6,2},{7,3},{8,12},{9,13},{10,... | collective-permute-start | bytes 393224 | tf_op jit(solution)/shard_map/ppermute | solution.py:35
  63.0 7.7 %collective-permute-done.21.refs_4_ = bf16[2,128,256]{2,1,0:T(8,128)(2,1)S(1)} collective-permute-done((bf16[2,128,256]{2,1,0:T(8,128)(2,1)S(1)}, bf16[2,128,256]{2,1,0:T(8,128)(2,1)S(1)}, u32[]{:S(2)}, u32[]{:S(2)}) %collective-permute-start.21) | collective-permute-done | bytes 131104 | tf_op jit(solution)/shard_map/ppermute | solution.py:35
  73.5 4.6 %shard_map.162 = (f32[2,128,896]{2,1,0:T(8,128)S(1)}, bf16[2,128,512]{2,1,0:T(8,128)(2,1)S(1)}) custom-call(s32[4]{0:T(128)S(1)} %pad_add_fusion.ids, f32[8,1,256]{2,1,0:T(1,128)} %bitcast.15, f32[8,1,256]{2,1,0:T(1,128)} %bitcast.16, bf16[2,128,256]{2,1,0:T(8,128)(2,1)S(1)} %add_convert_fusion.refs_2_, ...), custom_call_target="tpu_custom_call" | custom-call | tf_op jit(solution)/shard_map/pallas_call | solution.py:22
  82.3 3.0 %collective-permute-start.31 = (f32[8,128]{1,0:T(8,128)S(1)}, f32[8,128]{1,0:T(8,128)S(1)}, u32[]{:S(2)}, u32[]{:S(2)}) collective-permute-start(f32[8,128]{1,0:T(8,128)S(1)} %shard_map.164.refs_0_), channel_id=1, source_target_pairs={{0,6},{1,7},{2,4},{3,5},{4,2},{5,3},{6,0},{7,1},{8,14},{9,15},{10,... | collective-permute-start | bytes 12296 | tf_op jit(solution)/shard_map/ppermute | solution.py:35
  87.7 2.0 %collective-permute-done.32.refs_2_ = f32[8,128]{1,0:T(8,128)S(1)} collective-permute-done((f32[8,128]{1,0:T(8,128)S(1)}, f32[8,128]{1,0:T(8,128)S(1)}, u32[]{:S(2)}, u32[]{:S(2)}) %collective-permute-start.32) | collective-permute-done | bytes 4128 | tf_op jit(solution)/shard_map/ppermute | solution.py:35
  90.3 1.6 %collective-permute-start.34 = (f32[1,128]{1,0:T(1,128)S(1)}, f32[1,128]{1,0:T(1,128)S(1)}, u32[]{:S(2)}, u32[]{:S(2)}) collective-permute-start(f32[1,128]{1,0:T(1,128)S(1)} %shard_map.165), channel_id=1, source_target_pairs={{0,8},{8,0},{16,24},{24,16},{1,9},{9,1},{17,25},{25,17},{2,10},{10... | collective-permute-start | bytes 1544 | tf_op jit(solution)/shard_map/ppermute | solution.py:35
  93.9 1.5 %collective-permute-done.35 = f32[1,128]{1,0:T(1,128)S(1)} collective-permute-done((f32[1,128]{1,0:T(1,128)S(1)}, f32[1,128]{1,0:T(1,128)S(1)}, u32[]{:S(2)}, u32[]{:S(2)}) %collective-permute-start.35) | collective-permute-done | bytes 544 | tf_op jit(solution)/shard_map/ppermute | solution.py:35
  95.4 1.5 %collective-permute-done.36 = f32[1,128]{1,0:T(1,128)S(1)} collective-permute-done((f32[1,128]{1,0:T(1,128)S(1)}, f32[1,128]{1,0:T(1,128)S(1)}, u32[]{:S(2)}, u32[]{:S(2)}) %collective-permute-start.36) | collective-permute-done | bytes 544 | tf_op jit(solution)/shard_map/ppermute | solution.py:35
  (81 shorter events, 26.5 us)
Async XLA Ops:
  1.6 7.5 %collective-permute-start.3 = (bf16[17,16,256]{2,1,0:T(8,128)(2,1)S(1)}, bf16[17,16,256]{2,1,0:T(8,128)(2,1)S(1)}, u32[]{:S(2)}, u32[]{:S(2)}) collective-permute-start(bf16[17,16,256]{2,1,0:T(8,128)(2,1)S(1)} %shard_map.158.refs_4_), channel_id=1, source_target_pairs={{0,16},{8,24},{16,0},{24,8},{1,17},{9,25},{17,1},{25,9},{2,18},{10... | collective-permute-start | bytes 417800 | tf_op jit(solution)/shard_map/ppermute | solution.py:35
  4.6 6.5 %collective-permute-start = (bf16[16,16,256]{2,1,0:T(8,128)(2,1)}, bf16[16,16,256]{2,1,0:T(8,128)(2,1)S(1)}, u32[]{:S(2)}, u32[]{:S(2)}) collective-permute-start(bf16[16,16,256]{2,1,0:T(8,128)(2,1)} %refs_0_.1), channel_id=1, source_target_pairs={{0,16},{8,24},{16,0},{24,8},{1,17},{9,25},{17,1},{25,9},{2,18},{10... | collective-permute-start | bytes 393224 | tf_op jit(solution)/shard_map/ppermute | solution.py:35
  4.7 6.6 %collective-permute-start.1 = (bf16[16,16,256]{2,1,0:T(8,128)(2,1)}, bf16[16,16,256]{2,1,0:T(8,128)(2,1)S(1)}, u32[]{:S(2)}, u32[]{:S(2)}) collective-permute-start(bf16[16,16,256]{2,1,0:T(8,128)(2,1)} %refs_0_.1), channel_id=1, source_target_pairs={{0,8},{8,0},{16,24},{24,16},{1,9},{9,1},{17,25},{25,17},{2,10},{10... | collective-permute-start | bytes 393224 | tf_op jit(solution)/shard_map/ppermute | solution.py:35
  6.6 7.7 %collective-permute-start.2 = (bf16[17,16,256]{2,1,0:T(8,128)(2,1)S(1)}, bf16[17,16,256]{2,1,0:T(8,128)(2,1)S(1)}, u32[]{:S(2)}, u32[]{:S(2)}) collective-permute-start(bf16[17,16,256]{2,1,0:T(8,128)(2,1)S(1)} %shard_map.158.refs_4_), channel_id=1, source_target_pairs={{0,8},{8,0},{16,24},{24,16},{1,9},{9,1},{17,25},{25,17},{2,10},{10... | collective-permute-start | bytes 417800 | tf_op jit(solution)/shard_map/ppermute | solution.py:35
  9.1 8.7 %collective-permute-start.5 = (bf16[17,16,256]{2,1,0:T(8,128)(2,1)S(1)}, bf16[17,16,256]{2,1,0:T(8,128)(2,1)S(1)}, u32[]{:S(2)}, u32[]{:S(2)}) collective-permute-start(bf16[17,16,256]{2,1,0:T(8,128)(2,1)S(1)} %collective-permute-done.3.refs_6_), channel_id=1, source_target_pairs={{0,8},{8,0},{16,24},{24,16},{1,9},{9,1},{17,25},{25,17},{2,10},{10... | collective-permute-start | bytes 417800 | tf_op jit(solution)/shard_map/ppermute | solution.py:35
  11.3 6.4 %collective-permute-start.4 = (bf16[16,16,256]{2,1,0:T(8,128)(2,1)S(1)}, bf16[16,16,256]{2,1,0:T(8,128)(2,1)S(1)}, u32[]{:S(2)}, u32[]{:S(2)}) collective-permute-start(bf16[16,16,256]{2,1,0:T(8,128)(2,1)S(1)} %collective-permute-done.1.refs_1_), channel_id=1, source_target_pairs={{0,16},{8,24},{16,0},{24,8},{1,17},{9,25},{17,1},{25,9},{2,18},{10... | collective-permute-start | bytes 393224 | tf_op jit(solution)/shard_map/ppermute | solution.py:35
  14.3 26.2 %collective-permute-start.13 = (bf16[512,896]{1,0:T(8,128)(2,1)}, bf16[512,896]{1,0:T(8,128)(2,1)S(1)}, u32[]{:S(2)}, u32[]{:S(2)}) collective-permute-start(bf16[512,896]{1,0:T(8,128)(2,1)} %refs_10_), channel_id=1, source_target_pairs={{0,8},{8,0},{16,24},{24,16},{1,9},{9,1},{17,25},{25,17},{2,10},{10... | collective-permute-start | bytes 2752520 | tf_op jit(solution)/shard_map/ppermute | solution.py:35
  16.0 24.5 %collective-permute-start.14 = (bf16[512,896]{1,0:T(8,128)(2,1)}, bf16[512,896]{1,0:T(8,128)(2,1)}, u32[]{:S(2)}, u32[]{:S(2)}) collective-permute-start(bf16[512,896]{1,0:T(8,128)(2,1)} %refs_13_), channel_id=1, source_target_pairs={{0,16},{8,24},{16,0},{24,8},{1,17},{9,25},{17,1},{25,9},{2,18},{10... | collective-permute-start | bytes 2752520 | tf_op jit(solution)/shard_map/ppermute | solution.py:35
  19.6 10.2 %collective-permute-start.6 = (bf16[2,128,256]{2,1,0:T(8,128)(2,1)S(1)}, bf16[2,128,256]{2,1,0:T(8,128)(2,1)S(1)}, u32[]{:S(2)}, u32[]{:S(2)}) collective-permute-start(bf16[2,128,256]{2,1,0:T(8,128)(2,1)S(1)} %get-tuple-element.46.refs_6_), channel_id=1, source_target_pairs={{0,4},{1,5},{2,6},{3,7},{4,0},{5,1},{6,2},{7,3},{8,12},{9,13},{10,... | collective-permute-start | bytes 393224 | tf_op jit(solution)/shard_map/ppermute | solution.py:35
  22.3 7.5 %collective-permute-start.7 = (bf16[2,128,256]{2,1,0:T(8,128)(2,1)S(1)}, bf16[2,128,256]{2,1,0:T(8,128)(2,1)S(1)}, u32[]{:S(2)}, u32[]{:S(2)}) collective-permute-start(bf16[2,128,256]{2,1,0:T(8,128)(2,1)S(1)} %get-tuple-element.46.refs_6_), channel_id=1, source_target_pairs={{0,6},{1,7},{2,4},{3,5},{4,2},{5,3},{6,0},{7,1},{8,14},{9,15},{10,... | collective-permute-start | bytes 393224 | tf_op jit(solution)/shard_map/ppermute | solution.py:35
  23.6 7.1 %collective-permute-start.8 = (bf16[2,128,256]{2,1,0:T(8,128)(2,1)S(1)}, bf16[2,128,256]{2,1,0:T(8,128)(2,1)S(1)}, u32[]{:S(2)}, u32[]{:S(2)}) collective-permute-start(bf16[2,128,256]{2,1,0:T(8,128)(2,1)S(1)} %get-tuple-element.46.refs_6_), channel_id=1, source_target_pairs={{0,2},{1,3},{2,0},{3,1},{4,6},{5,7},{6,4},{7,5},{8,10},{9,11},{10,... | collective-permute-start | bytes 393224 | tf_op jit(solution)/shard_map/ppermute | solution.py:35
  32.3 23.5 %collective-permute-start.18 = (bf16[512,896]{1,0:T(8,128)(2,1)}, bf16[512,896]{1,0:T(8,128)(2,1)}, u32[]{:S(2)}, u32[]{:S(2)}) collective-permute-start(bf16[512,896]{1,0:T(8,128)(2,1)} %refs_10_), channel_id=1, source_target_pairs={{0,16},{8,24},{16,0},{24,8},{1,17},{9,25},{17,1},{25,9},{2,18},{10... | collective-permute-start | bytes 2752520 | tf_op jit(solution)/shard_map/ppermute | solution.py:35
  34.0 22.6 %collective-permute-start.19 = (bf16[512,896]{1,0:T(8,128)(2,1)}, bf16[512,896]{1,0:T(8,128)(2,1)}, u32[]{:S(2)}, u32[]{:S(2)}) collective-permute-start(bf16[512,896]{1,0:T(8,128)(2,1)} %refs_13_), channel_id=1, source_target_pairs={{0,8},{8,0},{16,24},{24,16},{1,9},{9,1},{17,25},{25,17},{2,10},{10... | collective-permute-start | bytes 2752520 | tf_op jit(solution)/shard_map/ppermute | solution.py:35
  43.1 13.5 %collective-permute-start.17 = (bf16[2,128,256]{2,1,0:T(8,128)(2,1)S(1)}, bf16[2,128,256]{2,1,0:T(8,128)(2,1)S(1)}, u32[]{:S(2)}, u32[]{:S(2)}) collective-permute-start(bf16[2,128,256]{2,1,0:T(8,128)(2,1)S(1)} %get-tuple-element.58), channel_id=1, source_target_pairs={{0,4},{1,5},{2,6},{3,7},{4,0},{5,1},{6,2},{7,3},{8,12},{9,13},{10,... | collective-permute-start | bytes 393224 | tf_op jit(solution)/shard_map/ppermute | solution.py:35
  45.9 12.7 %collective-permute-start.16 = (bf16[2,128,256]{2,1,0:T(8,128)(2,1)S(1)}, bf16[2,128,256]{2,1,0:T(8,128)(2,1)S(1)}, u32[]{:S(2)}, u32[]{:S(2)}) collective-permute-start(bf16[2,128,256]{2,1,0:T(8,128)(2,1)S(1)} %get-tuple-element.57), channel_id=1, source_target_pairs={{0,2},{1,3},{2,0},{3,1},{4,6},{5,7},{6,4},{7,5},{8,10},{9,11},{10,... | collective-permute-start | bytes 393224 | tf_op jit(solution)/shard_map/ppermute | solution.py:35
  46.5 12.1 %collective-permute-start.20 = (bf16[2,128,256]{2,1,0:T(8,128)(2,1)S(1)}, bf16[2,128,256]{2,1,0:T(8,128)(2,1)S(1)}, u32[]{:S(2)}, u32[]{:S(2)}) collective-permute-start(bf16[2,128,256]{2,1,0:T(8,128)(2,1)S(1)} %get-tuple-element.64), channel_id=1, source_target_pairs={{0,6},{1,7},{2,4},{3,5},{4,2},{5,3},{6,0},{7,1},{8,14},{9,15},{10,... | collective-permute-start | bytes 393224 | tf_op jit(solution)/shard_map/ppermute | solution.py:35
  56.6 21.5 %collective-permute-start.28 = (bf16[512,896]{1,0:T(8,128)(2,1)S(1)}, bf16[512,896]{1,0:T(8,128)(2,1)S(1)}, u32[]{:S(2)}, u32[]{:S(2)}) collective-permute-start(bf16[512,896]{1,0:T(8,128)(2,1)S(1)} %collective-permute-done.13.refs_11_), channel_id=1, source_target_pairs={{0,16},{8,24},{16,0},{24,8},{1,17},{9,25},{17,1},{25,9},{2,18},{10... | collective-permute-start | bytes 2752520 | tf_op jit(solution)/shard_map/ppermute | solution.py:35
  57.7 21.5 %collective-permute-start.29 = (bf16[512,896]{1,0:T(8,128)(2,1)}, bf16[512,896]{1,0:T(8,128)(2,1)S(1)}, u32[]{:S(2)}, u32[]{:S(2)}) collective-permute-start(bf16[512,896]{1,0:T(8,128)(2,1)} %collective-permute-done.14.refs_15_), channel_id=1, source_target_pairs={{0,8},{8,0},{16,24},{24,16},{1,9},{9,1},{17,25},{25,17},{2,10},{10... | collective-permute-start | bytes 2752520 | tf_op jit(solution)/shard_map/ppermute | solution.py:35
  58.7 12.0 %collective-permute-start.21 = (bf16[2,128,256]{2,1,0:T(8,128)(2,1)S(1)}, bf16[2,128,256]{2,1,0:T(8,128)(2,1)S(1)}, u32[]{:S(2)}, u32[]{:S(2)}) collective-permute-start(bf16[2,128,256]{2,1,0:T(8,128)(2,1)S(1)} %add_convert_fusion.refs_2_), channel_id=1, source_target_pairs={{0,4},{1,5},{2,6},{3,7},{4,0},{5,1},{6,2},{7,3},{8,12},{9,13},{10,... | collective-permute-start | bytes 393224 | tf_op jit(solution)/shard_map/ppermute | solution.py:35
  61.5 9.6 %collective-permute-start.22 = (bf16[2,128,256]{2,1,0:T(8,128)(2,1)S(1)}, bf16[2,128,256]{2,1,0:T(8,128)(2,1)S(1)}, u32[]{:S(2)}, u32[]{:S(2)}) collective-permute-start(bf16[2,128,256]{2,1,0:T(8,128)(2,1)S(1)} %add_convert_fusion.refs_2_), channel_id=1, source_target_pairs={{0,6},{1,7},{2,4},{3,5},{4,2},{5,3},{6,0},{7,1},{8,14},{9,15},{10,... | collective-permute-start | bytes 393224 | tf_op jit(solution)/shard_map/ppermute | solution.py:35
  62.7 8.4 %collective-permute-start.23 = (bf16[2,128,256]{2,1,0:T(8,128)(2,1)S(1)}, bf16[2,128,256]{2,1,0:T(8,128)(2,1)S(1)}, u32[]{:S(2)}, u32[]{:S(2)}) collective-permute-start(bf16[2,128,256]{2,1,0:T(8,128)(2,1)S(1)} %add_convert_fusion.refs_2_), channel_id=1, source_target_pairs={{0,2},{1,3},{2,0},{3,1},{4,6},{5,7},{6,4},{7,5},{8,10},{9,11},{10,... | collective-permute-start | bytes 393224 | tf_op jit(solution)/shard_map/ppermute | solution.py:35
  82.3 5.5 %collective-permute-start.31 = (f32[8,128]{1,0:T(8,128)S(1)}, f32[8,128]{1,0:T(8,128)S(1)}, u32[]{:S(2)}, u32[]{:S(2)}) collective-permute-start(f32[8,128]{1,0:T(8,128)S(1)} %shard_map.164.refs_0_), channel_id=1, source_target_pairs={{0,6},{1,7},{2,4},{3,5},{4,2},{5,3},{6,0},{7,1},{8,14},{9,15},{10,... | collective-permute-start | bytes 12296 | tf_op jit(solution)/shard_map/ppermute | solution.py:35
  85.2 4.5 %collective-permute-start.32 = (f32[8,128]{1,0:T(8,128)S(1)}, f32[8,128]{1,0:T(8,128)S(1)}, u32[]{:S(2)}, u32[]{:S(2)}) collective-permute-start(f32[8,128]{1,0:T(8,128)S(1)} %shard_map.164.refs_0_), channel_id=1, source_target_pairs={{0,4},{1,5},{2,6},{3,7},{4,0},{5,1},{6,2},{7,3},{8,12},{9,13},{10,... | collective-permute-start | bytes 12296 | tf_op jit(solution)/shard_map/ppermute | solution.py:35
  85.2 4.5 %collective-permute-start.33 = (f32[8,128]{1,0:T(8,128)S(1)}, f32[8,128]{1,0:T(8,128)S(1)}, u32[]{:S(2)}, u32[]{:S(2)}) collective-permute-start(f32[8,128]{1,0:T(8,128)S(1)} %shard_map.164.refs_0_), channel_id=1, source_target_pairs={{0,2},{1,3},{2,0},{3,1},{4,6},{5,7},{6,4},{7,5},{8,10},{9,11},{10,... | collective-permute-start | bytes 12296 | tf_op jit(solution)/shard_map/ppermute | solution.py:35
  (13 other events, 29.8 us)

commit v16 on v14

--- a/solution.py
+++ b/solution.py
@@ -357,10 +357,12 @@
         same = {0: own}
         for k in far:
             same[k] = exchange(own, "mp", 2 * k)
-        passed = lax.optimization_barrier([same[k] for k in far])
+        *passed, beside = lax.optimization_barrier(
+            [same[k] for k in far] + [exchange(own, "mp", 1)]
+        )
         same.update(zip(far, passed))
         same = [same[k] for k in range(half)]
-        return same + [exchange(v, "mp", 1) for v in same]
+        return same + [beside] + [exchange(v, "mp", 1) for v in same[1:]]
 
     parts = gather_pair(moved)
     if len(bits) > 1:

time: 98.4 us -> 98.5 us (level)
  transfers between devices with their start and end apart: 37 -> 37, of which waited for: 25 -> 27; matrix products, arithmetic and copies ran while one was open for 0% -> 0% of each run, Pallas kernels for 11% -> 11%
where the time goes in v16:
time: 98.5 us; the launch traced here: 98.2 us
  waiting for transfers between devices  41.9 us (43%)
  starting transfers between devices  40.2 us (41%)
  Pallas kernels  14.1 us (14%)
  other arithmetic  1.16 us (1%)
    ppermute x37, waiting for transfers between devices, exchange(): return lax.ppermute(values, axis, [(i, i ^ flip) for i in range(count)])  41.9 us
    ppermute x37, starting transfers between devices, exchange(): return lax.ppermute(values, axis, [(i, i ^ flip) for i in range(count)])  40.2 us
    pallas_call x8, Pallas kernels, call(): pl.pallas_call(kernel, out_shape=out_shape, in_specs=specs, out_specs=jax...  14.1 us
  transfers between devices with their start and end apart: 37, of which 27 were waited for; matrix products, arithmetic and copies ran while one was open for 0% of the time, Pallas kernels for 11%

profile of v16, /device:TPU:0, one launch (start us, length us, event | category | flops | bytes accessed | tf_op | source)
XLA Modules:
  0.0 98.2 jit_solution(803470219730159627)
XLA Ops:
  1.6 3.0 %collective-permute-start.3 = (bf16[17,16,256]{2,1,0:T(8,128)(2,1)S(1)}, bf16[17,16,256]{2,1,0:T(8,128)(2,1)S(1)}, u32[]{:S(2)}, u32[]{:S(2)}) collective-permute-start(bf16[17,16,256]{2,1,0:T(8,128)(2,1)S(1)} %shard_map.158.refs_4_), channel_id=1, source_target_pairs={{0,16},{8,24},{16,0},{24,8},{1,17},{9,25},{17,1},{25,9},{2,18},{10... | collective-permute-start | bytes 417800 | tf_op jit(solution)/shard_map/ppermute | solution.py:35
  4.7 1.9 %collective-permute-start.1 = (bf16[16,16,256]{2,1,0:T(8,128)(2,1)}, bf16[16,16,256]{2,1,0:T(8,128)(2,1)S(1)}, u32[]{:S(2)}, u32[]{:S(2)}) collective-permute-start(bf16[16,16,256]{2,1,0:T(8,128)(2,1)} %refs_0_.1), channel_id=1, source_target_pairs={{0,8},{8,0},{16,24},{24,16},{1,9},{9,1},{17,25},{25,17},{2,10},{10... | collective-permute-start | bytes 393224 | tf_op jit(solution)/shard_map/ppermute | solution.py:35
  6.7 2.4 %collective-permute-done.3.refs_6_ = bf16[17,16,256]{2,1,0:T(8,128)(2,1)S(1)} collective-permute-done((bf16[17,16,256]{2,1,0:T(8,128)(2,1)S(1)}, bf16[17,16,256]{2,1,0:T(8,128)(2,1)S(1)}, u32[]{:S(2)}, u32[]{:S(2)}) %collective-permute-start.3) | collective-permute-done | bytes 139296 | tf_op jit(solution)/shard_map/ppermute | solution.py:35
  9.1 2.0 %collective-permute-start.5 = (bf16[17,16,256]{2,1,0:T(8,128)(2,1)S(1)}, bf16[17,16,256]{2,1,0:T(8,128)(2,1)S(1)}, u32[]{:S(2)}, u32[]{:S(2)}) collective-permute-start(bf16[17,16,256]{2,1,0:T(8,128)(2,1)S(1)} %collective-permute-done.3.refs_6_), channel_id=1, source_target_pairs={{0,8},{8,0},{16,24},{24,16},{1,9},{9,1},{17,25},{25,17},{2,10},{10... | collective-permute-start | bytes 417800 | tf_op jit(solution)/shard_map/ppermute | solution.py:35
  11.3 2.0 %collective-permute-start.4 = (bf16[16,16,256]{2,1,0:T(8,128)(2,1)S(1)}, bf16[16,16,256]{2,1,0:T(8,128)(2,1)S(1)}, u32[]{:S(2)}, u32[]{:S(2)}) collective-permute-start(bf16[16,16,256]{2,1,0:T(8,128)(2,1)S(1)} %collective-permute-done.1.refs_1_), channel_id=1, source_target_pairs={{0,16},{8,24},{16,0},{24,8},{1,17},{9,25},{17,1},{25,9},{2,18},{10... | collective-permute-start | bytes 393224 | tf_op jit(solution)/shard_map/ppermute | solution.py:35
  14.3 1.7 %collective-permute-start.13 = (bf16[512,896]{1,0:T(8,128)(2,1)}, bf16[512,896]{1,0:T(8,128)(2,1)S(1)}, u32[]{:S(2)}, u32[]{:S(2)}) collective-permute-start(bf16[512,896]{1,0:T(8,128)(2,1)} %refs_10_), channel_id=1, source_target_pairs={{0,8},{8,0},{16,24},{24,16},{1,9},{9,1},{17,25},{25,17},{2,10},{10... | collective-permute-start | bytes 2752520 | tf_op jit(solution)/shard_map/ppermute | solution.py:35
  16.0 1.8 %collective-permute-start.14 = (bf16[512,896]{1,0:T(8,128)(2,1)}, bf16[512,896]{1,0:T(8,128)(2,1)S(1)}, u32[]{:S(2)}, u32[]{:S(2)}) collective-permute-start(bf16[512,896]{1,0:T(8,128)(2,1)} %refs_13_), channel_id=1, source_target_pairs={{0,16},{8,24},{16,0},{24,8},{1,17},{9,25},{17,1},{25,9},{2,18},{10... | collective-permute-start | bytes 2752520 | tf_op jit(solution)/shard_map/ppermute | solution.py:35
  17.8 1.9 %shard_map.159 = (bf16[2,128,256]{2,1,0:T(8,128)(2,1)S(1)}, s32[128,1]{1,0:T(8,128)S(1)}, s32[16,16]{1,0:T(8,128)S(1)}) custom-call(s32[4]{0:T(128)S(1)} %pad_add_fusion.ids, s32[64]{0:T(128)} %plan_far.1, bf16[16,16,256]{2,1,0:T(8,128)(2,1)} %refs_0_.1, bf16[16,16,256]{2,1,0:T(8,128)(2,1)S(1)} %collective-permute-done.1.refs_1_, ...), custom_call_target="tpu_custom_call" | custom-call | flops 10000000000 | tf_op jit(solution)/shard_map/pallas_call | solution.py:22
  19.7 2.8 %collective-permute-start.6 = (bf16[2,128,256]{2,1,0:T(8,128)(2,1)S(1)}, bf16[2,128,256]{2,1,0:T(8,128)(2,1)S(1)}, u32[]{:S(2)}, u32[]{:S(2)}) collective-permute-start(bf16[2,128,256]{2,1,0:T(8,128)(2,1)S(1)} %get-tuple-element.52.refs_6_), channel_id=1, source_target_pairs={{0,4},{1,5},{2,6},{3,7},{4,0},{5,1},{6,2},{7,3},{8,12},{9,13},{10,... | collective-permute-start | bytes 393224 | tf_op jit(solution)/shard_map/ppermute | solution.py:35
  24.0 5.9 %collective-permute-done.6.refs_8_ = bf16[2,128,256]{2,1,0:T(8,128)(2,1)S(1)} collective-permute-done((bf16[2,128,256]{2,1,0:T(8,128)(2,1)S(1)}, bf16[2,128,256]{2,1,0:T(8,128)(2,1)S(1)}, u32[]{:S(2)}, u32[]{:S(2)}) %collective-permute-start.6) | collective-permute-done | bytes 131104 | tf_op jit(solution)/shard_map/ppermute | solution.py:35
  34.0 1.5 %collective-permute-start.20 = (bf16[512,896]{1,0:T(8,128)(2,1)S(1)}, bf16[512,896]{1,0:T(8,128)(2,1)S(1)}, u32[]{:S(2)}, u32[]{:S(2)}) collective-permute-start(bf16[512,896]{1,0:T(8,128)(2,1)S(1)} %copy-done.1), channel_id=1, source_target_pairs={{0,8},{8,0},{16,24},{24,16},{1,9},{9,1},{17,25},{25,17},{2,10},{10... | collective-permute-start | bytes 2752520 | tf_op jit(solution)/shard_map/ppermute | solution.py:35
  36.9 5.0 %shard_map.160 = (f32[4,2,128,256]{3,2,1,0:T(8,128)S(1)}, bf16[4,2,128,256]{3,2,1,0:T(8,128)(2,1)S(1)}) custom-call(s32[4]{0:T(128)S(1)} %pad_add_fusion.ids, f32[8,1,256]{2,1,0:T(1,128)} %bitcast.8, f32[8,1,256]{2,1,0:T(1,128)} %bitcast.9, bf16[2048,512]{1,0:T(8,128)(2,1)} %refs_2_.1, bf16[2048,512]{1,0:T(8,128)(2,1)} %refs_3_.1, ...), custom_call_target="tpu_custom_call" | custom-call | tf_op jit(solution)/shard_map/pallas_call | solution.py:22
  42.1 1.8 %collective-permute-done.15.came = bf16[4,2,128,256]{3,2,1,0:T(8,128)(2,1)S(1)} collective-permute-done((bf16[4,2,128,256]{3,2,1,0:T(8,128)(2,1)S(1)}, bf16[4,2,128,256]{3,2,1,0:T(8,128)(2,1)S(1)}, u32[]{:S(2)}, u32[]{:S(2)}) %collective-permute-start.15) | collective-permute-done | bytes 524320 | tf_op jit(solution)/shard_map/ppermute | solution.py:35
  45.3 3.4 %collective-permute-start.17 = (bf16[2,128,256]{2,1,0:T(8,128)(2,1)S(1)}, bf16[2,128,256]{2,1,0:T(8,128)(2,1)S(1)}, u32[]{:S(2)}, u32[]{:S(2)}) collective-permute-start(bf16[2,128,256]{2,1,0:T(8,128)(2,1)S(1)} %get-tuple-element.65), channel_id=1, source_target_pairs={{0,4},{1,5},{2,6},{3,7},{4,0},{5,1},{6,2},{7,3},{8,12},{9,13},{10,... | collective-permute-start | bytes 393224 | tf_op jit(solution)/shard_map/ppermute | solution.py:35
  49.0 6.7 %collective-permute-done.19.refs_12_ = bf16[512,896]{1,0:T(8,128)(2,1)S(1)} collective-permute-done((bf16[512,896]{1,0:T(8,128)(2,1)S(1)}, bf16[512,896]{1,0:T(8,128)(2,1)S(1)}, u32[]{:S(2)}, u32[]{:S(2)}) %collective-permute-start.19) | collective-permute-done | bytes 917536 | tf_op jit(solution)/shard_map/ppermute | solution.py:35
  56.2 2.4 %collective-permute-done.17 = bf16[2,128,256]{2,1,0:T(8,128)(2,1)S(1)} collective-permute-done((bf16[2,128,256]{2,1,0:T(8,128)(2,1)S(1)}, bf16[2,128,256]{2,1,0:T(8,128)(2,1)S(1)}, u32[]{:S(2)}, u32[]{:S(2)}) %collective-permute-start.17) | collective-permute-done | bytes 131104 | tf_op jit(solution)/shard_map/ppermute | solution.py:35
  59.7 3.8 %collective-permute-start.21 = (bf16[2,128,256]{2,1,0:T(8,128)(2,1)S(1)}, bf16[2,128,256]{2,1,0:T(8,128)(2,1)S(1)}, u32[]{:S(2)}, u32[]{:S(2)}) collective-permute-start(bf16[2,128,256]{2,1,0:T(8,128)(2,1)S(1)} %add_convert_fusion.refs_2_), channel_id=1, source_target_pairs={{0,4},{1,5},{2,6},{3,7},{4,0},{5,1},{6,2},{7,3},{8,12},{9,13},{10,... | collective-permute-start | bytes 393224 | tf_op jit(solution)/shard_map/ppermute | solution.py:35
  64.7 7.9 %collective-permute-done.21.refs_4_ = bf16[2,128,256]{2,1,0:T(8,128)(2,1)S(1)} collective-permute-done((bf16[2,128,256]{2,1,0:T(8,128)(2,1)S(1)}, bf16[2,128,256]{2,1,0:T(8,128)(2,1)S(1)}, u32[]{:S(2)}, u32[]{:S(2)}) %collective-permute-start.21) | collective-permute-done | bytes 131104 | tf_op jit(solution)/shard_map/ppermute | solution.py:35
  75.8 3.2 %shard_map.162 = (f32[2,128,896]{2,1,0:T(8,128)S(1)}, bf16[2,128,512]{2,1,0:T(8,128)(2,1)S(1)}) custom-call(s32[4]{0:T(128)S(1)} %pad_add_fusion.ids, f32[8,1,256]{2,1,0:T(1,128)} %bitcast.10, f32[8,1,256]{2,1,0:T(1,128)} %bitcast.11, bf16[2,128,256]{2,1,0:T(8,128)(2,1)S(1)} %add_convert_fusion.refs_2_, ...), custom_call_target="tpu_custom_call" | custom-call | tf_op jit(solution)/shard_map/pallas_call | solution.py:22
  82.6 2.6 %collective-permute-start.31 = (f32[8,128]{1,0:T(8,128)S(1)}, f32[8,128]{1,0:T(8,128)S(1)}, u32[]{:S(2)}, u32[]{:S(2)}) collective-permute-start(f32[8,128]{1,0:T(8,128)S(1)} %shard_map.164.refs_0_), channel_id=1, source_target_pairs={{0,6},{1,7},{2,4},{3,5},{4,2},{5,3},{6,0},{7,1},{8,14},{9,15},{10,... | collective-permute-start | bytes 12296 | tf_op jit(solution)/shard_map/ppermute | solution.py:35
  85.2 2.3 %collective-permute-start.32 = (f32[8,128]{1,0:T(8,128)S(1)}, f32[8,128]{1,0:T(8,128)S(1)}, u32[]{:S(2)}, u32[]{:S(2)}) collective-permute-start(f32[8,128]{1,0:T(8,128)S(1)} %shard_map.164.refs_0_), channel_id=1, source_target_pairs={{0,4},{1,5},{2,6},{3,7},{4,0},{5,1},{6,2},{7,3},{8,12},{9,13},{10,... | collective-permute-start | bytes 12296 | tf_op jit(solution)/shard_map/ppermute | solution.py:35
  88.1 1.6 %collective-permute-done.32.refs_2_ = f32[8,128]{1,0:T(8,128)S(1)} collective-permute-done((f32[8,128]{1,0:T(8,128)S(1)}, f32[8,128]{1,0:T(8,128)S(1)}, u32[]{:S(2)}, u32[]{:S(2)}) %collective-permute-start.32) | collective-permute-done | bytes 4128 | tf_op jit(solution)/shard_map/ppermute | solution.py:35
  91.7 1.6 %collective-permute-start.34 = (f32[1,128]{1,0:T(1,128)S(1)}, f32[1,128]{1,0:T(1,128)S(1)}, u32[]{:S(2)}, u32[]{:S(2)}) collective-permute-start(f32[1,128]{1,0:T(1,128)S(1)} %shard_map.165), channel_id=1, source_target_pairs={{0,24},{8,16},{16,8},{24,0},{1,25},{9,17},{17,9},{25,1},{2,26},{10... | collective-permute-start | bytes 1544 | tf_op jit(solution)/shard_map/ppermute | solution.py:35
  93.7 1.5 %collective-permute-start.36 = (f32[1,128]{1,0:T(1,128)S(1)}, f32[1,128]{1,0:T(1,128)S(1)}, u32[]{:S(2)}, u32[]{:S(2)}) collective-permute-start(f32[1,128]{1,0:T(1,128)S(1)} %shard_map.165), channel_id=1, source_target_pairs={{0,8},{8,0},{16,24},{24,16},{1,9},{9,1},{17,25},{25,17},{2,10},{10... | collective-permute-start | bytes 1544 | tf_op jit(solution)/shard_map/ppermute | solution.py:35
  (70 shorter events, 26.9 us)
Async XLA Ops:
  1.6 7.5 %collective-permute-start.3 = (bf16[17,16,256]{2,1,0:T(8,128)(2,1)S(1)}, bf16[17,16,256]{2,1,0:T(8,128)(2,1)S(1)}, u32[]{:S(2)}, u32[]{:S(2)}) collective-permute-start(bf16[17,16,256]{2,1,0:T(8,128)(2,1)S(1)} %shard_map.158.refs_4_), channel_id=1, source_target_pairs={{0,16},{8,24},{16,0},{24,8},{1,17},{9,25},{17,1},{25,9},{2,18},{10... | collective-permute-start | bytes 417800 | tf_op jit(solution)/shard_map/ppermute | solution.py:35
  4.6 6.5 %collective-permute-start = (bf16[16,16,256]{2,1,0:T(8,128)(2,1)}, bf16[16,16,256]{2,1,0:T(8,128)(2,1)S(1)}, u32[]{:S(2)}, u32[]{:S(2)}) collective-permute-start(bf16[16,16,256]{2,1,0:T(8,128)(2,1)} %refs_0_.1), channel_id=1, source_target_pairs={{0,16},{8,24},{16,0},{24,8},{1,17},{9,25},{17,1},{25,9},{2,18},{10... | collective-permute-start | bytes 393224 | tf_op jit(solution)/shard_map/ppermute | solution.py:35
  4.7 6.6 %collective-permute-start.1 = (bf16[16,16,256]{2,1,0:T(8,128)(2,1)}, bf16[16,16,256]{2,1,0:T(8,128)(2,1)S(1)}, u32[]{:S(2)}, u32[]{:S(2)}) collective-permute-start(bf16[16,16,256]{2,1,0:T(8,128)(2,1)} %refs_0_.1), channel_id=1, source_target_pairs={{0,8},{8,0},{16,24},{24,16},{1,9},{9,1},{17,25},{25,17},{2,10},{10... | collective-permute-start | bytes 393224 | tf_op jit(solution)/shard_map/ppermute | solution.py:35
  6.6 7.7 %collective-permute-start.2 = (bf16[17,16,256]{2,1,0:T(8,128)(2,1)S(1)}, bf16[17,16,256]{2,1,0:T(8,128)(2,1)S(1)}, u32[]{:S(2)}, u32[]{:S(2)}) collective-permute-start(bf16[17,16,256]{2,1,0:T(8,128)(2,1)S(1)} %shard_map.158.refs_4_), channel_id=1, source_target_pairs={{0,8},{8,0},{16,24},{24,16},{1,9},{9,1},{17,25},{25,17},{2,10},{10... | collective-permute-start | bytes 417800 | tf_op jit(solution)/shard_map/ppermute | solution.py:35
  9.1 8.7 %collective-permute-start.5 = (bf16[17,16,256]{2,1,0:T(8,128)(2,1)S(1)}, bf16[17,16,256]{2,1,0:T(8,128)(2,1)S(1)}, u32[]{:S(2)}, u32[]{:S(2)}) collective-permute-start(bf16[17,16,256]{2,1,0:T(8,128)(2,1)S(1)} %collective-permute-done.3.refs_6_), channel_id=1, source_target_pairs={{0,8},{8,0},{16,24},{24,16},{1,9},{9,1},{17,25},{25,17},{2,10},{10... | collective-permute-start | bytes 417800 | tf_op jit(solution)/shard_map/ppermute | solution.py:35
  11.3 6.4 %collective-permute-start.4 = (bf16[16,16,256]{2,1,0:T(8,128)(2,1)S(1)}, bf16[16,16,256]{2,1,0:T(8,128)(2,1)S(1)}, u32[]{:S(2)}, u32[]{:S(2)}) collective-permute-start(bf16[16,16,256]{2,1,0:T(8,128)(2,1)S(1)} %collective-permute-done.1.refs_1_), channel_id=1, source_target_pairs={{0,16},{8,24},{16,0},{24,8},{1,17},{9,25},{17,1},{25,9},{2,18},{10... | collective-permute-start | bytes 393224 | tf_op jit(solution)/shard_map/ppermute | solution.py:35
  14.3 27.6 %collective-permute-start.13 = (bf16[512,896]{1,0:T(8,128)(2,1)}, bf16[512,896]{1,0:T(8,128)(2,1)S(1)}, u32[]{:S(2)}, u32[]{:S(2)}) collective-permute-start(bf16[512,896]{1,0:T(8,128)(2,1)} %refs_10_), channel_id=1, source_target_pairs={{0,8},{8,0},{16,24},{24,16},{1,9},{9,1},{17,25},{25,17},{2,10},{10... | collective-permute-start | bytes 2752520 | tf_op jit(solution)/shard_map/ppermute | solution.py:35
  16.0 25.9 %collective-permute-start.14 = (bf16[512,896]{1,0:T(8,128)(2,1)}, bf16[512,896]{1,0:T(8,128)(2,1)S(1)}, u32[]{:S(2)}, u32[]{:S(2)}) collective-permute-start(bf16[512,896]{1,0:T(8,128)(2,1)} %refs_13_), channel_id=1, source_target_pairs={{0,16},{8,24},{16,0},{24,8},{1,17},{9,25},{17,1},{25,9},{2,18},{10... | collective-permute-start | bytes 2752520 | tf_op jit(solution)/shard_map/ppermute | solution.py:35
  19.7 10.2 %collective-permute-start.6 = (bf16[2,128,256]{2,1,0:T(8,128)(2,1)S(1)}, bf16[2,128,256]{2,1,0:T(8,128)(2,1)S(1)}, u32[]{:S(2)}, u32[]{:S(2)}) collective-permute-start(bf16[2,128,256]{2,1,0:T(8,128)(2,1)S(1)} %get-tuple-element.52.refs_6_), channel_id=1, source_target_pairs={{0,4},{1,5},{2,6},{3,7},{4,0},{5,1},{6,2},{7,3},{8,12},{9,13},{10,... | collective-permute-start | bytes 393224 | tf_op jit(solution)/shard_map/ppermute | solution.py:35
  22.4 7.5 %collective-permute-start.7 = (bf16[2,128,256]{2,1,0:T(8,128)(2,1)S(1)}, bf16[2,128,256]{2,1,0:T(8,128)(2,1)S(1)}, u32[]{:S(2)}, u32[]{:S(2)}) collective-permute-start(bf16[2,128,256]{2,1,0:T(8,128)(2,1)S(1)} %get-tuple-element.52.refs_6_), channel_id=1, source_target_pairs={{0,6},{1,7},{2,4},{3,5},{4,2},{5,3},{6,0},{7,1},{8,14},{9,15},{10,... | collective-permute-start | bytes 393224 | tf_op jit(solution)/shard_map/ppermute | solution.py:35
  23.8 7.1 %collective-permute-start.8 = (bf16[2,128,256]{2,1,0:T(8,128)(2,1)S(1)}, bf16[2,128,256]{2,1,0:T(8,128)(2,1)S(1)}, u32[]{:S(2)}, u32[]{:S(2)}) collective-permute-start(bf16[2,128,256]{2,1,0:T(8,128)(2,1)S(1)} %get-tuple-element.52.refs_6_), channel_id=1, source_target_pairs={{0,2},{1,3},{2,0},{3,1},{4,6},{5,7},{6,4},{7,5},{8,10},{9,11},{10,... | collective-permute-start | bytes 393224 | tf_op jit(solution)/shard_map/ppermute | solution.py:35
  32.6 23.0 %collective-permute-start.19 = (bf16[512,896]{1,0:T(8,128)(2,1)S(1)}, bf16[512,896]{1,0:T(8,128)(2,1)S(1)}, u32[]{:S(2)}, u32[]{:S(2)}) collective-permute-start(bf16[512,896]{1,0:T(8,128)(2,1)S(1)} %copy-done), channel_id=1, source_target_pairs={{0,16},{8,24},{16,0},{24,8},{1,17},{9,25},{17,1},{25,9},{2,18},{10... | collective-permute-start | bytes 2752520 | tf_op jit(solution)/shard_map/ppermute | solution.py:35
  34.0 22.1 %collective-permute-start.20 = (bf16[512,896]{1,0:T(8,128)(2,1)S(1)}, bf16[512,896]{1,0:T(8,128)(2,1)S(1)}, u32[]{:S(2)}, u32[]{:S(2)}) collective-permute-start(bf16[512,896]{1,0:T(8,128)(2,1)S(1)} %copy-done.1), channel_id=1, source_target_pairs={{0,8},{8,0},{16,24},{24,16},{1,9},{9,1},{17,25},{25,17},{2,10},{10... | collective-permute-start | bytes 2752520 | tf_op jit(solution)/shard_map/ppermute | solution.py:35
  44.5 11.6 %collective-permute-start.16 = (bf16[2,128,256]{2,1,0:T(8,128)(2,1)S(1)}, bf16[2,128,256]{2,1,0:T(8,128)(2,1)S(1)}, u32[]{:S(2)}, u32[]{:S(2)}) collective-permute-start(bf16[2,128,256]{2,1,0:T(8,128)(2,1)S(1)} %get-tuple-element.64), channel_id=1, source_target_pairs={{0,2},{1,3},{2,0},{3,1},{4,6},{5,7},{6,4},{7,5},{8,10},{9,11},{10,... | collective-permute-start | bytes 393224 | tf_op jit(solution)/shard_map/ppermute | solution.py:35
  45.3 13.4 %collective-permute-start.17 = (bf16[2,128,256]{2,1,0:T(8,128)(2,1)S(1)}, bf16[2,128,256]{2,1,0:T(8,128)(2,1)S(1)}, u32[]{:S(2)}, u32[]{:S(2)}) collective-permute-start(bf16[2,128,256]{2,1,0:T(8,128)(2,1)S(1)} %get-tuple-element.65), channel_id=1, source_target_pairs={{0,4},{1,5},{2,6},{3,7},{4,0},{5,1},{6,2},{7,3},{8,12},{9,13},{10,... | collective-permute-start | bytes 393224 | tf_op jit(solution)/shard_map/ppermute | solution.py:35
  48.6 10.0 %collective-permute-start.18 = (bf16[2,128,256]{2,1,0:T(8,128)(2,1)S(1)}, bf16[2,128,256]{2,1,0:T(8,128)(2,1)S(1)}, u32[]{:S(2)}, u32[]{:S(2)}) collective-permute-start(bf16[2,128,256]{2,1,0:T(8,128)(2,1)S(1)} %get-tuple-element.66), channel_id=1, source_target_pairs={{0,6},{1,7},{2,4},{3,5},{4,2},{5,3},{6,0},{7,1},{8,14},{9,15},{10,... | collective-permute-start | bytes 393224 | tf_op jit(solution)/shard_map/ppermute | solution.py:35
  58.6 20.8 %collective-permute-start.28 = (bf16[512,896]{1,0:T(8,128)(2,1)S(1)}, bf16[512,896]{1,0:T(8,128)(2,1)S(1)}, u32[]{:S(2)}, u32[]{:S(2)}) collective-permute-start(bf16[512,896]{1,0:T(8,128)(2,1)S(1)} %collective-permute-done.13.refs_11_), channel_id=1, source_target_pairs={{0,16},{8,24},{16,0},{24,8},{1,17},{9,25},{17,1},{25,9},{2,18},{10... | collective-permute-start | bytes 2752520 | tf_op jit(solution)/shard_map/ppermute | solution.py:35
  59.1 20.5 %collective-permute-start.29 = (bf16[512,896]{1,0:T(8,128)(2,1)S(1)}, bf16[512,896]{1,0:T(8,128)(2,1)S(1)}, u32[]{:S(2)}, u32[]{:S(2)}) collective-permute-start(bf16[512,896]{1,0:T(8,128)(2,1)S(1)} %collective-permute-done.14.refs_15_), channel_id=1, source_target_pairs={{0,8},{8,0},{16,24},{24,16},{1,9},{9,1},{17,25},{25,17},{2,10},{10... | collective-permute-start | bytes 2752520 | tf_op jit(solution)/shard_map/ppermute | solution.py:35
  59.7 12.9 %collective-permute-start.21 = (bf16[2,128,256]{2,1,0:T(8,128)(2,1)S(1)}, bf16[2,128,256]{2,1,0:T(8,128)(2,1)S(1)}, u32[]{:S(2)}, u32[]{:S(2)}) collective-permute-start(bf16[2,128,256]{2,1,0:T(8,128)(2,1)S(1)} %add_convert_fusion.refs_2_), channel_id=1, source_target_pairs={{0,4},{1,5},{2,6},{3,7},{4,0},{5,1},{6,2},{7,3},{8,12},{9,13},{10,... | collective-permute-start | bytes 393224 | tf_op jit(solution)/shard_map/ppermute | solution.py:35
  63.5 9.1 %collective-permute-start.22 = (bf16[2,128,256]{2,1,0:T(8,128)(2,1)S(1)}, bf16[2,128,256]{2,1,0:T(8,128)(2,1)S(1)}, u32[]{:S(2)}, u32[]{:S(2)}) collective-permute-start(bf16[2,128,256]{2,1,0:T(8,128)(2,1)S(1)} %add_convert_fusion.refs_2_), channel_id=1, source_target_pairs={{0,6},{1,7},{2,4},{3,5},{4,2},{5,3},{6,0},{7,1},{8,14},{9,15},{10,... | collective-permute-start | bytes 393224 | tf_op jit(solution)/shard_map/ppermute | solution.py:35
  64.7 8.0 %collective-permute-start.23 = (bf16[2,128,256]{2,1,0:T(8,128)(2,1)S(1)}, bf16[2,128,256]{2,1,0:T(8,128)(2,1)S(1)}, u32[]{:S(2)}, u32[]{:S(2)}) collective-permute-start(bf16[2,128,256]{2,1,0:T(8,128)(2,1)S(1)} %add_convert_fusion.refs_2_), channel_id=1, source_target_pairs={{0,2},{1,3},{2,0},{3,1},{4,6},{5,7},{6,4},{7,5},{8,10},{9,11},{10,... | collective-permute-start | bytes 393224 | tf_op jit(solution)/shard_map/ppermute | solution.py:35
  82.6 5.5 %collective-permute-start.31 = (f32[8,128]{1,0:T(8,128)S(1)}, f32[8,128]{1,0:T(8,128)S(1)}, u32[]{:S(2)}, u32[]{:S(2)}) collective-permute-start(f32[8,128]{1,0:T(8,128)S(1)} %shard_map.164.refs_0_), channel_id=1, source_target_pairs={{0,6},{1,7},{2,4},{3,5},{4,2},{5,3},{6,0},{7,1},{8,14},{9,15},{10,... | collective-permute-start | bytes 12296 | tf_op jit(solution)/shard_map/ppermute | solution.py:35
  85.2 4.5 %collective-permute-start.32 = (f32[8,128]{1,0:T(8,128)S(1)}, f32[8,128]{1,0:T(8,128)S(1)}, u32[]{:S(2)}, u32[]{:S(2)}) collective-permute-start(f32[8,128]{1,0:T(8,128)S(1)} %shard_map.164.refs_0_), channel_id=1, source_target_pairs={{0,4},{1,5},{2,6},{3,7},{4,0},{5,1},{6,2},{7,3},{8,12},{9,13},{10,... | collective-permute-start | bytes 12296 | tf_op jit(solution)/shard_map/ppermute | solution.py:35
  91.7 4.5 %collective-permute-start.34 = (f32[1,128]{1,0:T(1,128)S(1)}, f32[1,128]{1,0:T(1,128)S(1)}, u32[]{:S(2)}, u32[]{:S(2)}) collective-permute-start(f32[1,128]{1,0:T(1,128)S(1)} %shard_map.165), channel_id=1, source_target_pairs={{0,24},{8,16},{16,8},{24,0},{1,25},{9,17},{17,9},{25,1},{2,26},{10... | collective-permute-start | bytes 1544 | tf_op jit(solution)/shard_map/ppermute | solution.py:35
  (15 other events, 67.4 us)

commit v17 on v16

--- a/solution.py
+++ b/solution.py
@@ -400,7 +400,8 @@
     if len(bits) > 1:
         for m in range(2):
             outs[m].update(later[m])
-        arrived = wait_for(arrived, lambda m, k: True)
+        passed = wait_for([arrived[k] for k in far], lambda m, k: True)
+        arrived = dict(zip(far, passed))
         spread_step(outs, 1, lambda m, k: k == bit_orders[m][0])
     for k in range(1, half):
         own = own + arrived[k].astype(jnp.float32)

time: 98.5 us -> 98.7 us (level)
  no operation moved by 1% of the time
where the time goes in v17:
time: 98.7 us; the launch traced here: 98.4 us
  waiting for transfers between devices  41.6 us (42%)
  starting transfers between devices  40.7 us (41%)
  Pallas kernels  14.1 us (14%)
  other arithmetic  1.16 us (1%)
    ppermute x37, waiting for transfers between devices, exchange(): return lax.ppermute(values, axis, [(i, i ^ flip) for i in range(count)])  41.6 us
    ppermute x37, starting transfers between devices, exchange(): return lax.ppermute(values, axis, [(i, i ^ flip) for i in range(count)])  40.7 us
    pallas_call x8, Pallas kernels, call(): pl.pallas_call(kernel, out_shape=out_shape, in_specs=specs, out_specs=jax...  14.1 us
  transfers between devices with their start and end apart: 37, of which 27 were waited for; matrix products, arithmetic and copies ran while one was open for 0% of the time, Pallas kernels for 11%

profile of v17, /device:TPU:0, one launch (start us, length us, event | category | flops | bytes accessed | tf_op | source)
XLA Modules:
  0.0 98.4 jit_solution(14352514152192284523)
XLA Ops:
  1.6 3.0 %collective-permute-start.3 = (bf16[17,16,256]{2,1,0:T(8,128)(2,1)S(1)}, bf16[17,16,256]{2,1,0:T(8,128)(2,1)S(1)}, u32[]{:S(2)}, u32[]{:S(2)}) collective-permute-start(bf16[17,16,256]{2,1,0:T(8,128)(2,1)S(1)} %shard_map.158.refs_4_), channel_id=1, source_target_pairs={{0,16},{8,24},{16,0},{24,8},{1,17},{9,25},{17,1},{25,9},{2,18},{10... | collective-permute-start | bytes 417800 | tf_op jit(solution)/shard_map/ppermute | solution.py:35
  4.7 1.9 %collective-permute-start.1 = (bf16[16,16,256]{2,1,0:T(8,128)(2,1)}, bf16[16,16,256]{2,1,0:T(8,128)(2,1)S(1)}, u32[]{:S(2)}, u32[]{:S(2)}) collective-permute-start(bf16[16,16,256]{2,1,0:T(8,128)(2,1)} %refs_0_.1), channel_id=1, source_target_pairs={{0,8},{8,0},{16,24},{24,16},{1,9},{9,1},{17,25},{25,17},{2,10},{10... | collective-permute-start | bytes 393224 | tf_op jit(solution)/shard_map/ppermute | solution.py:35
  6.7 2.4 %collective-permute-done.3.refs_6_ = bf16[17,16,256]{2,1,0:T(8,128)(2,1)S(1)} collective-permute-done((bf16[17,16,256]{2,1,0:T(8,128)(2,1)S(1)}, bf16[17,16,256]{2,1,0:T(8,128)(2,1)S(1)}, u32[]{:S(2)}, u32[]{:S(2)}) %collective-permute-start.3) | collective-permute-done | bytes 139296 | tf_op jit(solution)/shard_map/ppermute | solution.py:35
  9.1 2.0 %collective-permute-start.5 = (bf16[17,16,256]{2,1,0:T(8,128)(2,1)S(1)}, bf16[17,16,256]{2,1,0:T(8,128)(2,1)S(1)}, u32[]{:S(2)}, u32[]{:S(2)}) collective-permute-start(bf16[17,16,256]{2,1,0:T(8,128)(2,1)S(1)} %collective-permute-done.3.refs_6_), channel_id=1, source_target_pairs={{0,8},{8,0},{16,24},{24,16},{1,9},{9,1},{17,25},{25,17},{2,10},{10... | collective-permute-start | bytes 417800 | tf_op jit(solution)/shard_map/ppermute | solution.py:35
  11.3 2.0 %collective-permute-start.4 = (bf16[16,16,256]{2,1,0:T(8,128)(2,1)S(1)}, bf16[16,16,256]{2,1,0:T(8,128)(2,1)S(1)}, u32[]{:S(2)}, u32[]{:S(2)}) collective-permute-start(bf16[16,16,256]{2,1,0:T(8,128)(2,1)S(1)} %collective-permute-done.1.refs_1_), channel_id=1, source_target_pairs={{0,16},{8,24},{16,0},{24,8},{1,17},{9,25},{17,1},{25,9},{2,18},{10... | collective-permute-start | bytes 393224 | tf_op jit(solution)/shard_map/ppermute | solution.py:35
  14.3 1.7 %collective-permute-start.13 = (bf16[512,896]{1,0:T(8,128)(2,1)}, bf16[512,896]{1,0:T(8,128)(2,1)S(1)}, u32[]{:S(2)}, u32[]{:S(2)}) collective-permute-start(bf16[512,896]{1,0:T(8,128)(2,1)} %refs_10_), channel_id=1, source_target_pairs={{0,8},{8,0},{16,24},{24,16},{1,9},{9,1},{17,25},{25,17},{2,10},{10... | collective-permute-start | bytes 2752520 | tf_op jit(solution)/shard_map/ppermute | solution.py:35
  16.0 1.8 %collective-permute-start.14 = (bf16[512,896]{1,0:T(8,128)(2,1)}, bf16[512,896]{1,0:T(8,128)(2,1)S(1)}, u32[]{:S(2)}, u32[]{:S(2)}) collective-permute-start(bf16[512,896]{1,0:T(8,128)(2,1)} %refs_13_), channel_id=1, source_target_pairs={{0,16},{8,24},{16,0},{24,8},{1,17},{9,25},{17,1},{25,9},{2,18},{10... | collective-permute-start | bytes 2752520 | tf_op jit(solution)/shard_map/ppermute | solution.py:35
  17.8 1.9 %shard_map.159 = (bf16[2,128,256]{2,1,0:T(8,128)(2,1)S(1)}, s32[128,1]{1,0:T(8,128)S(1)}, s32[16,16]{1,0:T(8,128)S(1)}) custom-call(s32[4]{0:T(128)S(1)} %pad_add_fusion.ids, s32[64]{0:T(128)} %plan_far.1, bf16[16,16,256]{2,1,0:T(8,128)(2,1)} %refs_0_.1, bf16[16,16,256]{2,1,0:T(8,128)(2,1)S(1)} %collective-permute-done.1.refs_1_, ...), custom_call_target="tpu_custom_call" | custom-call | flops 10000000000 | tf_op jit(solution)/shard_map/pallas_call | solution.py:22
  19.7 2.8 %collective-permute-start.6 = (bf16[2,128,256]{2,1,0:T(8,128)(2,1)S(1)}, bf16[2,128,256]{2,1,0:T(8,128)(2,1)S(1)}, u32[]{:S(2)}, u32[]{:S(2)}) collective-permute-start(bf16[2,128,256]{2,1,0:T(8,128)(2,1)S(1)} %get-tuple-element.52.refs_6_), channel_id=1, source_target_pairs={{0,4},{1,5},{2,6},{3,7},{4,0},{5,1},{6,2},{7,3},{8,12},{9,13},{10,... | collective-permute-start | bytes 393224 | tf_op jit(solution)/shard_map/ppermute | solution.py:35
  24.0 5.9 %collective-permute-done.6.refs_8_ = bf16[2,128,256]{2,1,0:T(8,128)(2,1)S(1)} collective-permute-done((bf16[2,128,256]{2,1,0:T(8,128)(2,1)S(1)}, bf16[2,128,256]{2,1,0:T(8,128)(2,1)S(1)}, u32[]{:S(2)}, u32[]{:S(2)}) %collective-permute-start.6) | collective-permute-done | bytes 131104 | tf_op jit(solution)/shard_map/ppermute | solution.py:35
  32.6 1.4 %collective-permute-start.19 = (bf16[512,896]{1,0:T(8,128)(2,1)S(1)}, bf16[512,896]{1,0:T(8,128)(2,1)S(1)}, u32[]{:S(2)}, u32[]{:S(2)}) collective-permute-start(bf16[512,896]{1,0:T(8,128)(2,1)S(1)} %copy-done), channel_id=1, source_target_pairs={{0,16},{8,24},{16,0},{24,8},{1,17},{9,25},{17,1},{25,9},{2,18},{10... | collective-permute-start | bytes 2752520 | tf_op jit(solution)/shard_map/ppermute | solution.py:35
  34.0 1.5 %collective-permute-start.20 = (bf16[512,896]{1,0:T(8,128)(2,1)S(1)}, bf16[512,896]{1,0:T(8,128)(2,1)S(1)}, u32[]{:S(2)}, u32[]{:S(2)}) collective-permute-start(bf16[512,896]{1,0:T(8,128)(2,1)S(1)} %copy-done.1), channel_id=1, source_target_pairs={{0,8},{8,0},{16,24},{24,16},{1,9},{9,1},{17,25},{25,17},{2,10},{10... | collective-permute-start | bytes 2752520 | tf_op jit(solution)/shard_map/ppermute | solution.py:35
  36.9 5.0 %shard_map.160 = (f32[4,2,128,256]{3,2,1,0:T(8,128)S(1)}, bf16[4,2,128,256]{3,2,1,0:T(8,128)(2,1)S(1)}) custom-call(s32[4]{0:T(128)S(1)} %pad_add_fusion.ids, f32[8,1,256]{2,1,0:T(1,128)} %bitcast.8, f32[8,1,256]{2,1,0:T(1,128)} %bitcast.9, bf16[2048,512]{1,0:T(8,128)(2,1)} %refs_2_.1, bf16[2048,512]{1,0:T(8,128)(2,1)} %refs_3_.1, ...), custom_call_target="tpu_custom_call" | custom-call | tf_op jit(solution)/shard_map/pallas_call | solution.py:22
  42.1 1.8 %collective-permute-done.15.came = bf16[4,2,128,256]{3,2,1,0:T(8,128)(2,1)S(1)} collective-permute-done((bf16[4,2,128,256]{3,2,1,0:T(8,128)(2,1)S(1)}, bf16[4,2,128,256]{3,2,1,0:T(8,128)(2,1)S(1)}, u32[]{:S(2)}, u32[]{:S(2)}) %collective-permute-start.15) | collective-permute-done | bytes 524320 | tf_op jit(solution)/shard_map/ppermute | solution.py:35
  44.5 2.7 %collective-permute-start.16 = (bf16[2,128,256]{2,1,0:T(8,128)(2,1)S(1)}, bf16[2,128,256]{2,1,0:T(8,128)(2,1)S(1)}, u32[]{:S(2)}, u32[]{:S(2)}) collective-permute-start(bf16[2,128,256]{2,1,0:T(8,128)(2,1)S(1)} %get-tuple-element.64), channel_id=1, source_target_pairs={{0,4},{1,5},{2,6},{3,7},{4,0},{5,1},{6,2},{7,3},{8,12},{9,13},{10,... | collective-permute-start | bytes 393224 | tf_op jit(solution)/shard_map/ppermute | solution.py:35
  48.6 7.0 %collective-permute-done.19.refs_12_ = bf16[512,896]{1,0:T(8,128)(2,1)S(1)} collective-permute-done((bf16[512,896]{1,0:T(8,128)(2,1)S(1)}, bf16[512,896]{1,0:T(8,128)(2,1)S(1)}, u32[]{:S(2)}, u32[]{:S(2)}) %collective-permute-start.19) | collective-permute-done | bytes 917536 | tf_op jit(solution)/shard_map/ppermute | solution.py:35
  59.3 4.0 %collective-permute-start.21 = (bf16[2,128,256]{2,1,0:T(8,128)(2,1)S(1)}, bf16[2,128,256]{2,1,0:T(8,128)(2,1)S(1)}, u32[]{:S(2)}, u32[]{:S(2)}) collective-permute-start(bf16[2,128,256]{2,1,0:T(8,128)(2,1)S(1)} %add_convert_fusion.refs_2_), channel_id=1, source_target_pairs={{0,4},{1,5},{2,6},{3,7},{4,0},{5,1},{6,2},{7,3},{8,12},{9,13},{10,... | collective-permute-start | bytes 393224 | tf_op jit(solution)/shard_map/ppermute | solution.py:35
  63.9 8.4 %collective-permute-done.21.refs_4_ = bf16[2,128,256]{2,1,0:T(8,128)(2,1)S(1)} collective-permute-done((bf16[2,128,256]{2,1,0:T(8,128)(2,1)S(1)}, bf16[2,128,256]{2,1,0:T(8,128)(2,1)S(1)}, u32[]{:S(2)}, u32[]{:S(2)}) %collective-permute-start.21) | collective-permute-done | bytes 131104 | tf_op jit(solution)/shard_map/ppermute | solution.py:35
  75.5 3.2 %shard_map.162 = (f32[2,128,896]{2,1,0:T(8,128)S(1)}, bf16[2,128,512]{2,1,0:T(8,128)(2,1)S(1)}) custom-call(s32[4]{0:T(128)S(1)} %pad_add_fusion.ids, f32[8,1,256]{2,1,0:T(1,128)} %bitcast.10, f32[8,1,256]{2,1,0:T(1,128)} %bitcast.11, bf16[2,128,256]{2,1,0:T(8,128)(2,1)S(1)} %add_convert_fusion.refs_2_, ...), custom_call_target="tpu_custom_call" | custom-call | tf_op jit(solution)/shard_map/pallas_call | solution.py:22
  82.3 3.9 %collective-permute-start.31 = (f32[8,128]{1,0:T(8,128)S(1)}, f32[8,128]{1,0:T(8,128)S(1)}, u32[]{:S(2)}, u32[]{:S(2)}) collective-permute-start(f32[8,128]{1,0:T(8,128)S(1)} %shard_map.164.refs_0_), channel_id=1, source_target_pairs={{0,6},{1,7},{2,4},{3,5},{4,2},{5,3},{6,0},{7,1},{8,14},{9,15},{10,... | collective-permute-start | bytes 12296 | tf_op jit(solution)/shard_map/ppermute | solution.py:35
  86.1 1.7 %collective-permute-start.32 = (f32[8,128]{1,0:T(8,128)S(1)}, f32[8,128]{1,0:T(8,128)S(1)}, u32[]{:S(2)}, u32[]{:S(2)}) collective-permute-start(f32[8,128]{1,0:T(8,128)S(1)} %shard_map.164.refs_0_), channel_id=1, source_target_pairs={{0,4},{1,5},{2,6},{3,7},{4,0},{5,1},{6,2},{7,3},{8,12},{9,13},{10,... | collective-permute-start | bytes 12296 | tf_op jit(solution)/shard_map/ppermute | solution.py:35
  88.3 2.4 %collective-permute-done.32.refs_2_ = f32[8,128]{1,0:T(8,128)S(1)} collective-permute-done((f32[8,128]{1,0:T(8,128)S(1)}, f32[8,128]{1,0:T(8,128)S(1)}, u32[]{:S(2)}, u32[]{:S(2)}) %collective-permute-start.32) | collective-permute-done | bytes 4128 | tf_op jit(solution)/shard_map/ppermute | solution.py:35
  91.9 1.5 %collective-permute-start.34 = (f32[1,128]{1,0:T(1,128)S(1)}, f32[1,128]{1,0:T(1,128)S(1)}, u32[]{:S(2)}, u32[]{:S(2)}) collective-permute-start(f32[1,128]{1,0:T(1,128)S(1)} %shard_map.165), channel_id=1, source_target_pairs={{0,24},{8,16},{16,8},{24,0},{1,25},{9,17},{17,9},{25,1},{2,26},{10... | collective-permute-start | bytes 1544 | tf_op jit(solution)/shard_map/ppermute | solution.py:35
  93.9 1.6 %collective-permute-start.36 = (f32[1,128]{1,0:T(1,128)S(1)}, f32[1,128]{1,0:T(1,128)S(1)}, u32[]{:S(2)}, u32[]{:S(2)}) collective-permute-start(f32[1,128]{1,0:T(1,128)S(1)} %shard_map.165), channel_id=1, source_target_pairs={{0,8},{8,0},{16,24},{24,16},{1,9},{9,1},{17,25},{25,17},{2,10},{10... | collective-permute-start | bytes 1544 | tf_op jit(solution)/shard_map/ppermute | solution.py:35
  (70 shorter events, 26.5 us)
Async XLA Ops:
  1.6 7.5 %collective-permute-start.3 = (bf16[17,16,256]{2,1,0:T(8,128)(2,1)S(1)}, bf16[17,16,256]{2,1,0:T(8,128)(2,1)S(1)}, u32[]{:S(2)}, u32[]{:S(2)}) collective-permute-start(bf16[17,16,256]{2,1,0:T(8,128)(2,1)S(1)} %shard_map.158.refs_4_), channel_id=1, source_target_pairs={{0,16},{8,24},{16,0},{24,8},{1,17},{9,25},{17,1},{25,9},{2,18},{10... | collective-permute-start | bytes 417800 | tf_op jit(solution)/shard_map/ppermute | solution.py:35
  4.6 6.5 %collective-permute-start = (bf16[16,16,256]{2,1,0:T(8,128)(2,1)}, bf16[16,16,256]{2,1,0:T(8,128)(2,1)S(1)}, u32[]{:S(2)}, u32[]{:S(2)}) collective-permute-start(bf16[16,16,256]{2,1,0:T(8,128)(2,1)} %refs_0_.1), channel_id=1, source_target_pairs={{0,16},{8,24},{16,0},{24,8},{1,17},{9,25},{17,1},{25,9},{2,18},{10... | collective-permute-start | bytes 393224 | tf_op jit(solution)/shard_map/ppermute | solution.py:35
  4.7 6.6 %collective-permute-start.1 = (bf16[16,16,256]{2,1,0:T(8,128)(2,1)}, bf16[16,16,256]{2,1,0:T(8,128)(2,1)S(1)}, u32[]{:S(2)}, u32[]{:S(2)}) collective-permute-start(bf16[16,16,256]{2,1,0:T(8,128)(2,1)} %refs_0_.1), channel_id=1, source_target_pairs={{0,8},{8,0},{16,24},{24,16},{1,9},{9,1},{17,25},{25,17},{2,10},{10... | collective-permute-start | bytes 393224 | tf_op jit(solution)/shard_map/ppermute | solution.py:35
  6.6 7.7 %collective-permute-start.2 = (bf16[17,16,256]{2,1,0:T(8,128)(2,1)S(1)}, bf16[17,16,256]{2,1,0:T(8,128)(2,1)S(1)}, u32[]{:S(2)}, u32[]{:S(2)}) collective-permute-start(bf16[17,16,256]{2,1,0:T(8,128)(2,1)S(1)} %shard_map.158.refs_4_), channel_id=1, source_target_pairs={{0,8},{8,0},{16,24},{24,16},{1,9},{9,1},{17,25},{25,17},{2,10},{10... | collective-permute-start | bytes 417800 | tf_op jit(solution)/shard_map/ppermute | solution.py:35
  9.1 8.7 %collective-permute-start.5 = (bf16[17,16,256]{2,1,0:T(8,128)(2,1)S(1)}, bf16[17,16,256]{2,1,0:T(8,128)(2,1)S(1)}, u32[]{:S(2)}, u32[]{:S(2)}) collective-permute-start(bf16[17,16,256]{2,1,0:T(8,128)(2,1)S(1)} %collective-permute-done.3.refs_6_), channel_id=1, source_target_pairs={{0,8},{8,0},{16,24},{24,16},{1,9},{9,1},{17,25},{25,17},{2,10},{10... | collective-permute-start | bytes 417800 | tf_op jit(solution)/shard_map/ppermute | solution.py:35
  11.3 6.4 %collective-permute-start.4 = (bf16[16,16,256]{2,1,0:T(8,128)(2,1)S(1)}, bf16[16,16,256]{2,1,0:T(8,128)(2,1)S(1)}, u32[]{:S(2)}, u32[]{:S(2)}) collective-permute-start(bf16[16,16,256]{2,1,0:T(8,128)(2,1)S(1)} %collective-permute-done.1.refs_1_), channel_id=1, source_target_pairs={{0,16},{8,24},{16,0},{24,8},{1,17},{9,25},{17,1},{25,9},{2,18},{10... | collective-permute-start | bytes 393224 | tf_op jit(solution)/shard_map/ppermute | solution.py:35
  14.3 27.6 %collective-permute-start.13 = (bf16[512,896]{1,0:T(8,128)(2,1)}, bf16[512,896]{1,0:T(8,128)(2,1)S(1)}, u32[]{:S(2)}, u32[]{:S(2)}) collective-permute-start(bf16[512,896]{1,0:T(8,128)(2,1)} %refs_10_), channel_id=1, source_target_pairs={{0,8},{8,0},{16,24},{24,16},{1,9},{9,1},{17,25},{25,17},{2,10},{10... | collective-permute-start | bytes 2752520 | tf_op jit(solution)/shard_map/ppermute | solution.py:35
  16.0 25.9 %collective-permute-start.14 = (bf16[512,896]{1,0:T(8,128)(2,1)}, bf16[512,896]{1,0:T(8,128)(2,1)S(1)}, u32[]{:S(2)}, u32[]{:S(2)}) collective-permute-start(bf16[512,896]{1,0:T(8,128)(2,1)} %refs_13_), channel_id=1, source_target_pairs={{0,16},{8,24},{16,0},{24,8},{1,17},{9,25},{17,1},{25,9},{2,18},{10... | collective-permute-start | bytes 2752520 | tf_op jit(solution)/shard_map/ppermute | solution.py:35
  19.7 10.2 %collective-permute-start.6 = (bf16[2,128,256]{2,1,0:T(8,128)(2,1)S(1)}, bf16[2,128,256]{2,1,0:T(8,128)(2,1)S(1)}, u32[]{:S(2)}, u32[]{:S(2)}) collective-permute-start(bf16[2,128,256]{2,1,0:T(8,128)(2,1)S(1)} %get-tuple-element.52.refs_6_), channel_id=1, source_target_pairs={{0,4},{1,5},{2,6},{3,7},{4,0},{5,1},{6,2},{7,3},{8,12},{9,13},{10,... | collective-permute-start | bytes 393224 | tf_op jit(solution)/shard_map/ppermute | solution.py:35
  22.4 7.5 %collective-permute-start.7 = (bf16[2,128,256]{2,1,0:T(8,128)(2,1)S(1)}, bf16[2,128,256]{2,1,0:T(8,128)(2,1)S(1)}, u32[]{:S(2)}, u32[]{:S(2)}) collective-permute-start(bf16[2,128,256]{2,1,0:T(8,128)(2,1)S(1)} %get-tuple-element.52.refs_6_), channel_id=1, source_target_pairs={{0,6},{1,7},{2,4},{3,5},{4,2},{5,3},{6,0},{7,1},{8,14},{9,15},{10,... | collective-permute-start | bytes 393224 | tf_op jit(solution)/shard_map/ppermute | solution.py:35
  23.8 7.1 %collective-permute-start.8 = (bf16[2,128,256]{2,1,0:T(8,128)(2,1)S(1)}, bf16[2,128,256]{2,1,0:T(8,128)(2,1)S(1)}, u32[]{:S(2)}, u32[]{:S(2)}) collective-permute-start(bf16[2,128,256]{2,1,0:T(8,128)(2,1)S(1)} %get-tuple-element.52.refs_6_), channel_id=1, source_target_pairs={{0,2},{1,3},{2,0},{3,1},{4,6},{5,7},{6,4},{7,5},{8,10},{9,11},{10,... | collective-permute-start | bytes 393224 | tf_op jit(solution)/shard_map/ppermute | solution.py:35
  32.6 23.0 %collective-permute-start.19 = (bf16[512,896]{1,0:T(8,128)(2,1)S(1)}, bf16[512,896]{1,0:T(8,128)(2,1)S(1)}, u32[]{:S(2)}, u32[]{:S(2)}) collective-permute-start(bf16[512,896]{1,0:T(8,128)(2,1)S(1)} %copy-done), channel_id=1, source_target_pairs={{0,16},{8,24},{16,0},{24,8},{1,17},{9,25},{17,1},{25,9},{2,18},{10... | collective-permute-start | bytes 2752520 | tf_op jit(solution)/shard_map/ppermute | solution.py:35
  34.0 22.1 %collective-permute-start.20 = (bf16[512,896]{1,0:T(8,128)(2,1)S(1)}, bf16[512,896]{1,0:T(8,128)(2,1)S(1)}, u32[]{:S(2)}, u32[]{:S(2)}) collective-permute-start(bf16[512,896]{1,0:T(8,128)(2,1)S(1)} %copy-done.1), channel_id=1, source_target_pairs={{0,8},{8,0},{16,24},{24,16},{1,9},{9,1},{17,25},{25,17},{2,10},{10... | collective-permute-start | bytes 2752520 | tf_op jit(solution)/shard_map/ppermute | solution.py:35
  44.5 13.0 %collective-permute-start.16 = (bf16[2,128,256]{2,1,0:T(8,128)(2,1)S(1)}, bf16[2,128,256]{2,1,0:T(8,128)(2,1)S(1)}, u32[]{:S(2)}, u32[]{:S(2)}) collective-permute-start(bf16[2,128,256]{2,1,0:T(8,128)(2,1)S(1)} %get-tuple-element.64), channel_id=1, source_target_pairs={{0,4},{1,5},{2,6},{3,7},{4,0},{5,1},{6,2},{7,3},{8,12},{9,13},{10,... | collective-permute-start | bytes 393224 | tf_op jit(solution)/shard_map/ppermute | solution.py:35
  47.2 10.3 %collective-permute-start.17 = (bf16[2,128,256]{2,1,0:T(8,128)(2,1)S(1)}, bf16[2,128,256]{2,1,0:T(8,128)(2,1)S(1)}, u32[]{:S(2)}, u32[]{:S(2)}) collective-permute-start(bf16[2,128,256]{2,1,0:T(8,128)(2,1)S(1)} %get-tuple-element.65), channel_id=1, source_target_pairs={{0,6},{1,7},{2,4},{3,5},{4,2},{5,3},{6,0},{7,1},{8,14},{9,15},{10,... | collective-permute-start | bytes 393224 | tf_op jit(solution)/shard_map/ppermute | solution.py:35
  48.1 9.9 %collective-permute-start.18 = (bf16[2,128,256]{2,1,0:T(8,128)(2,1)S(1)}, bf16[2,128,256]{2,1,0:T(8,128)(2,1)S(1)}, u32[]{:S(2)}, u32[]{:S(2)}) collective-permute-start(bf16[2,128,256]{2,1,0:T(8,128)(2,1)S(1)} %get-tuple-element.66), channel_id=1, source_target_pairs={{0,2},{1,3},{2,0},{3,1},{4,6},{5,7},{6,4},{7,5},{8,10},{9,11},{10,... | collective-permute-start | bytes 393224 | tf_op jit(solution)/shard_map/ppermute | solution.py:35
  58.1 20.9 %collective-permute-start.28 = (bf16[512,896]{1,0:T(8,128)(2,1)S(1)}, bf16[512,896]{1,0:T(8,128)(2,1)S(1)}, u32[]{:S(2)}, u32[]{:S(2)}) collective-permute-start(bf16[512,896]{1,0:T(8,128)(2,1)S(1)} %collective-permute-done.13.refs_11_), channel_id=1, source_target_pairs={{0,16},{8,24},{16,0},{24,8},{1,17},{9,25},{17,1},{25,9},{2,18},{10... | collective-permute-start | bytes 2752520 | tf_op jit(solution)/shard_map/ppermute | solution.py:35
  58.6 20.7 %collective-permute-start.29 = (bf16[512,896]{1,0:T(8,128)(2,1)S(1)}, bf16[512,896]{1,0:T(8,128)(2,1)S(1)}, u32[]{:S(2)}, u32[]{:S(2)}) collective-permute-start(bf16[512,896]{1,0:T(8,128)(2,1)S(1)} %collective-permute-done.14.refs_15_), channel_id=1, source_target_pairs={{0,8},{8,0},{16,24},{24,16},{1,9},{9,1},{17,25},{25,17},{2,10},{10... | collective-permute-start | bytes 2752520 | tf_op jit(solution)/shard_map/ppermute | solution.py:35
  59.3 13.0 %collective-permute-start.21 = (bf16[2,128,256]{2,1,0:T(8,128)(2,1)S(1)}, bf16[2,128,256]{2,1,0:T(8,128)(2,1)S(1)}, u32[]{:S(2)}, u32[]{:S(2)}) collective-permute-start(bf16[2,128,256]{2,1,0:T(8,128)(2,1)S(1)} %add_convert_fusion.refs_2_), channel_id=1, source_target_pairs={{0,4},{1,5},{2,6},{3,7},{4,0},{5,1},{6,2},{7,3},{8,12},{9,13},{10,... | collective-permute-start | bytes 393224 | tf_op jit(solution)/shard_map/ppermute | solution.py:35
  63.2 9.0 %collective-permute-start.22 = (bf16[2,128,256]{2,1,0:T(8,128)(2,1)S(1)}, bf16[2,128,256]{2,1,0:T(8,128)(2,1)S(1)}, u32[]{:S(2)}, u32[]{:S(2)}) collective-permute-start(bf16[2,128,256]{2,1,0:T(8,128)(2,1)S(1)} %add_convert_fusion.refs_2_), channel_id=1, source_target_pairs={{0,6},{1,7},{2,4},{3,5},{4,2},{5,3},{6,0},{7,1},{8,14},{9,15},{10,... | collective-permute-start | bytes 393224 | tf_op jit(solution)/shard_map/ppermute | solution.py:35
  63.7 9.7 %collective-permute-start.23 = (bf16[2,128,256]{2,1,0:T(8,128)(2,1)S(1)}, bf16[2,128,256]{2,1,0:T(8,128)(2,1)S(1)}, u32[]{:S(2)}, u32[]{:S(2)}) collective-permute-start(bf16[2,128,256]{2,1,0:T(8,128)(2,1)S(1)} %add_convert_fusion.refs_2_), channel_id=1, source_target_pairs={{0,2},{1,3},{2,0},{3,1},{4,6},{5,7},{6,4},{7,5},{8,10},{9,11},{10,... | collective-permute-start | bytes 393224 | tf_op jit(solution)/shard_map/ppermute | solution.py:35
  82.3 6.0 %collective-permute-start.31 = (f32[8,128]{1,0:T(8,128)S(1)}, f32[8,128]{1,0:T(8,128)S(1)}, u32[]{:S(2)}, u32[]{:S(2)}) collective-permute-start(f32[8,128]{1,0:T(8,128)S(1)} %shard_map.164.refs_0_), channel_id=1, source_target_pairs={{0,6},{1,7},{2,4},{3,5},{4,2},{5,3},{6,0},{7,1},{8,14},{9,15},{10,... | collective-permute-start | bytes 12296 | tf_op jit(solution)/shard_map/ppermute | solution.py:35
  86.1 4.5 %collective-permute-start.32 = (f32[8,128]{1,0:T(8,128)S(1)}, f32[8,128]{1,0:T(8,128)S(1)}, u32[]{:S(2)}, u32[]{:S(2)}) collective-permute-start(f32[8,128]{1,0:T(8,128)S(1)} %shard_map.164.refs_0_), channel_id=1, source_target_pairs={{0,4},{1,5},{2,6},{3,7},{4,0},{5,1},{6,2},{7,3},{8,12},{9,13},{10,... | collective-permute-start | bytes 12296 | tf_op jit(solution)/shard_map/ppermute | solution.py:35
  91.9 4.5 %collective-permute-start.34 = (f32[1,128]{1,0:T(1,128)S(1)}, f32[1,128]{1,0:T(1,128)S(1)}, u32[]{:S(2)}, u32[]{:S(2)}) collective-permute-start(f32[1,128]{1,0:T(1,128)S(1)} %shard_map.165), channel_id=1, source_target_pairs={{0,24},{8,16},{16,8},{24,0},{1,25},{9,17},{17,9},{25,1},{2,26},{10... | collective-permute-start | bytes 1544 | tf_op jit(solution)/shard_map/ppermute | solution.py:35
  (15 other events, 67.4 us)

commit v18 on v16

--- a/solution.py
+++ b/solution.py
@@ -327,7 +327,7 @@
             blocks[place], values = lax.optimization_barrier((blocks[place], values))
             blocks.update(zip(passed, values))
         spread_step(hiddens, step, lambda m, k: 0 < k and not k & bit_orders[m][step])
-    early = [(m, b) for m in range(2) for b in bits]
+    early = [(0, b) for b in bits] + [(1, bit_orders[1][0])]
     values = wait_for([hiddens[m][b] for m, b in early], lambda m, k: True)
     for (m, b), value in zip(early, values):
         hiddens[m][b] = value

time: 98.5 us -> 98.5 us (level)
  no operation moved by 1% of the time
where the time goes in v18:
time: 98.5 us; the launch traced here: 98.2 us
  waiting for transfers between devices  42.8 us (43%)
  starting transfers between devices  39.4 us (40%)
  Pallas kernels  14.1 us (14%)
  other arithmetic  1.16 us (1%)
    ppermute x37, waiting for transfers between devices, exchange(): return lax.ppermute(values, axis, [(i, i ^ flip) for i in range(count)])  42.8 us
    ppermute x37, starting transfers between devices, exchange(): return lax.ppermute(values, axis, [(i, i ^ flip) for i in range(count)])  39.4 us
    pallas_call x8, Pallas kernels, call(): pl.pallas_call(kernel, out_shape=out_shape, in_specs=specs, out_specs=jax...  14.1 us
  transfers between devices with their start and end apart: 37, of which 27 were waited for; matrix products, arithmetic and copies ran while one was open for 0% of the time, Pallas kernels for 11%

profile of v18, /device:TPU:0, one launch (start us, length us, event | category | flops | bytes accessed | tf_op | source)
XLA Modules:
  0.0 98.2 jit_solution(8276788488585750499)
XLA Ops:
  1.6 3.0 %collective-permute-start.2 = (bf16[17,16,256]{2,1,0:T(8,128)(2,1)S(1)}, bf16[17,16,256]{2,1,0:T(8,128)(2,1)S(1)}, u32[]{:S(2)}, u32[]{:S(2)}) collective-permute-start(bf16[17,16,256]{2,1,0:T(8,128)(2,1)S(1)} %shard_map.158.refs_4_), channel_id=1, source_target_pairs={{0,16},{8,24},{16,0},{24,8},{1,17},{9,25},{17,1},{25,9},{2,18},{10... | collective-permute-start | bytes 417800 | tf_op jit(solution)/shard_map/ppermute | solution.py:35
  4.7 1.9 %collective-permute-start.1 = (bf16[16,16,256]{2,1,0:T(8,128)(2,1)}, bf16[16,16,256]{2,1,0:T(8,128)(2,1)S(1)}, u32[]{:S(2)}, u32[]{:S(2)}) collective-permute-start(bf16[16,16,256]{2,1,0:T(8,128)(2,1)} %refs_0_.1), channel_id=1, source_target_pairs={{0,8},{8,0},{16,24},{24,16},{1,9},{9,1},{17,25},{25,17},{2,10},{10... | collective-permute-start | bytes 393224 | tf_op jit(solution)/shard_map/ppermute | solution.py:35
  6.7 2.4 %collective-permute-done.2.refs_6_ = bf16[17,16,256]{2,1,0:T(8,128)(2,1)S(1)} collective-permute-done((bf16[17,16,256]{2,1,0:T(8,128)(2,1)S(1)}, bf16[17,16,256]{2,1,0:T(8,128)(2,1)S(1)}, u32[]{:S(2)}, u32[]{:S(2)}) %collective-permute-start.2) | collective-permute-done | bytes 139296 | tf_op jit(solution)/shard_map/ppermute | solution.py:35
  9.1 2.0 %collective-permute-start.5 = (bf16[17,16,256]{2,1,0:T(8,128)(2,1)S(1)}, bf16[17,16,256]{2,1,0:T(8,128)(2,1)S(1)}, u32[]{:S(2)}, u32[]{:S(2)}) collective-permute-start(bf16[17,16,256]{2,1,0:T(8,128)(2,1)S(1)} %collective-permute-done.2.refs_6_), channel_id=1, source_target_pairs={{0,8},{8,0},{16,24},{24,16},{1,9},{9,1},{17,25},{25,17},{2,10},{10... | collective-permute-start | bytes 417800 | tf_op jit(solution)/shard_map/ppermute | solution.py:35
  11.3 2.0 %collective-permute-start.3 = (bf16[16,16,256]{2,1,0:T(8,128)(2,1)S(1)}, bf16[16,16,256]{2,1,0:T(8,128)(2,1)S(1)}, u32[]{:S(2)}, u32[]{:S(2)}) collective-permute-start(bf16[16,16,256]{2,1,0:T(8,128)(2,1)S(1)} %collective-permute-done.1.refs_1_), channel_id=1, source_target_pairs={{0,16},{8,24},{16,0},{24,8},{1,17},{9,25},{17,1},{25,9},{2,18},{10... | collective-permute-start | bytes 393224 | tf_op jit(solution)/shard_map/ppermute | solution.py:35
  13.4 1.5 %collective-permute-start.13 = (bf16[512,896]{1,0:T(8,128)(2,1)}, bf16[512,896]{1,0:T(8,128)(2,1)S(1)}, u32[]{:S(2)}, u32[]{:S(2)}) collective-permute-start(bf16[512,896]{1,0:T(8,128)(2,1)} %refs_10_), channel_id=1, source_target_pairs={{0,8},{8,0},{16,24},{24,16},{1,9},{9,1},{17,25},{25,17},{2,10},{10... | collective-permute-start | bytes 2752520 | tf_op jit(solution)/shard_map/ppermute | solution.py:35
  15.4 1.7 %collective-permute-done.3.refs_3_ = bf16[16,16,256]{2,1,0:T(8,128)(2,1)S(1)} collective-permute-done((bf16[16,16,256]{2,1,0:T(8,128)(2,1)S(1)}, bf16[16,16,256]{2,1,0:T(8,128)(2,1)S(1)}, u32[]{:S(2)}, u32[]{:S(2)}) %collective-permute-start.3) | collective-permute-done | bytes 131104 | tf_op jit(solution)/shard_map/ppermute | solution.py:35
  17.2 1.9 %shard_map.159 = (bf16[2,128,256]{2,1,0:T(8,128)(2,1)S(1)}, s32[128,1]{1,0:T(8,128)S(1)}, s32[16,16]{1,0:T(8,128)S(1)}) custom-call(s32[4]{0:T(128)S(1)} %pad_add_fusion.ids, s32[64]{0:T(128)} %plan_far.1, bf16[16,16,256]{2,1,0:T(8,128)(2,1)} %refs_0_.1, bf16[16,16,256]{2,1,0:T(8,128)(2,1)S(1)} %collective-permute-done.1.refs_1_, ...), custom_call_target="tpu_custom_call" | custom-call | flops 10000000000 | tf_op jit(solution)/shard_map/pallas_call | solution.py:22
  19.1 3.3 %collective-permute-start.6 = (bf16[2,128,256]{2,1,0:T(8,128)(2,1)S(1)}, bf16[2,128,256]{2,1,0:T(8,128)(2,1)S(1)}, u32[]{:S(2)}, u32[]{:S(2)}) collective-permute-start(bf16[2,128,256]{2,1,0:T(8,128)(2,1)S(1)} %get-tuple-element.50.refs_6_), channel_id=1, source_target_pairs={{0,4},{1,5},{2,6},{3,7},{4,0},{5,1},{6,2},{7,3},{8,12},{9,13},{10,... | collective-permute-start | bytes 393224 | tf_op jit(solution)/shard_map/ppermute | solution.py:35
  24.0 5.9 %collective-permute-done.6.refs_8_ = bf16[2,128,256]{2,1,0:T(8,128)(2,1)S(1)} collective-permute-done((bf16[2,128,256]{2,1,0:T(8,128)(2,1)S(1)}, bf16[2,128,256]{2,1,0:T(8,128)(2,1)S(1)}, u32[]{:S(2)}, u32[]{:S(2)}) %collective-permute-start.6) | collective-permute-done | bytes 131104 | tf_op jit(solution)/shard_map/ppermute | solution.py:35
  34.0 1.5 %collective-permute-start.20 = (bf16[512,896]{1,0:T(8,128)(2,1)S(1)}, bf16[512,896]{1,0:T(8,128)(2,1)S(1)}, u32[]{:S(2)}, u32[]{:S(2)}) collective-permute-start(bf16[512,896]{1,0:T(8,128)(2,1)S(1)} %copy-done.1), channel_id=1, source_target_pairs={{0,8},{8,0},{16,24},{24,16},{1,9},{9,1},{17,25},{25,17},{2,10},{10... | collective-permute-start | bytes 2752520 | tf_op jit(solution)/shard_map/ppermute | solution.py:35
  36.9 5.0 %shard_map.160 = (f32[4,2,128,256]{3,2,1,0:T(8,128)S(1)}, bf16[4,2,128,256]{3,2,1,0:T(8,128)(2,1)S(1)}) custom-call(s32[4]{0:T(128)S(1)} %pad_add_fusion.ids, f32[8,1,256]{2,1,0:T(1,128)} %bitcast.8, f32[8,1,256]{2,1,0:T(1,128)} %bitcast.9, bf16[2048,512]{1,0:T(8,128)(2,1)} %refs_2_.1, bf16[2048,512]{1,0:T(8,128)(2,1)} %refs_3_.1, ...), custom_call_target="tpu_custom_call" | custom-call | tf_op jit(solution)/shard_map/pallas_call | solution.py:22
  42.1 1.8 %collective-permute-done.15.came = bf16[4,2,128,256]{3,2,1,0:T(8,128)(2,1)S(1)} collective-permute-done((bf16[4,2,128,256]{3,2,1,0:T(8,128)(2,1)S(1)}, bf16[4,2,128,256]{3,2,1,0:T(8,128)(2,1)S(1)}, u32[]{:S(2)}, u32[]{:S(2)}) %collective-permute-start.15) | collective-permute-done | bytes 524320 | tf_op jit(solution)/shard_map/ppermute | solution.py:35
  45.3 3.4 %collective-permute-start.17 = (bf16[2,128,256]{2,1,0:T(8,128)(2,1)S(1)}, bf16[2,128,256]{2,1,0:T(8,128)(2,1)S(1)}, u32[]{:S(2)}, u32[]{:S(2)}) collective-permute-start(bf16[2,128,256]{2,1,0:T(8,128)(2,1)S(1)} %get-tuple-element.63), channel_id=1, source_target_pairs={{0,4},{1,5},{2,6},{3,7},{4,0},{5,1},{6,2},{7,3},{8,12},{9,13},{10,... | collective-permute-start | bytes 393224 | tf_op jit(solution)/shard_map/ppermute | solution.py:35
  49.0 6.7 %collective-permute-done.19.refs_12_ = bf16[512,896]{1,0:T(8,128)(2,1)S(1)} collective-permute-done((bf16[512,896]{1,0:T(8,128)(2,1)S(1)}, bf16[512,896]{1,0:T(8,128)(2,1)S(1)}, u32[]{:S(2)}, u32[]{:S(2)}) %collective-permute-start.19) | collective-permute-done | bytes 917536 | tf_op jit(solution)/shard_map/ppermute | solution.py:35
  56.2 2.4 %collective-permute-done.17 = bf16[2,128,256]{2,1,0:T(8,128)(2,1)S(1)} collective-permute-done((bf16[2,128,256]{2,1,0:T(8,128)(2,1)S(1)}, bf16[2,128,256]{2,1,0:T(8,128)(2,1)S(1)}, u32[]{:S(2)}, u32[]{:S(2)}) %collective-permute-start.17) | collective-permute-done | bytes 131104 | tf_op jit(solution)/shard_map/ppermute | solution.py:35
  59.7 3.8 %collective-permute-start.21 = (bf16[2,128,256]{2,1,0:T(8,128)(2,1)S(1)}, bf16[2,128,256]{2,1,0:T(8,128)(2,1)S(1)}, u32[]{:S(2)}, u32[]{:S(2)}) collective-permute-start(bf16[2,128,256]{2,1,0:T(8,128)(2,1)S(1)} %add_convert_fusion.refs_2_), channel_id=1, source_target_pairs={{0,4},{1,5},{2,6},{3,7},{4,0},{5,1},{6,2},{7,3},{8,12},{9,13},{10,... | collective-permute-start | bytes 393224 | tf_op jit(solution)/shard_map/ppermute | solution.py:35
  64.7 7.9 %collective-permute-done.21.refs_4_ = bf16[2,128,256]{2,1,0:T(8,128)(2,1)S(1)} collective-permute-done((bf16[2,128,256]{2,1,0:T(8,128)(2,1)S(1)}, bf16[2,128,256]{2,1,0:T(8,128)(2,1)S(1)}, u32[]{:S(2)}, u32[]{:S(2)}) %collective-permute-start.21) | collective-permute-done | bytes 131104 | tf_op jit(solution)/shard_map/ppermute | solution.py:35
  75.8 3.2 %shard_map.162 = (f32[2,128,896]{2,1,0:T(8,128)S(1)}, bf16[2,128,512]{2,1,0:T(8,128)(2,1)S(1)}) custom-call(s32[4]{0:T(128)S(1)} %pad_add_fusion.ids, f32[8,1,256]{2,1,0:T(1,128)} %bitcast.10, f32[8,1,256]{2,1,0:T(1,128)} %bitcast.11, bf16[2,128,256]{2,1,0:T(8,128)(2,1)S(1)} %add_convert_fusion.refs_2_, ...), custom_call_target="tpu_custom_call" | custom-call | tf_op jit(solution)/shard_map/pallas_call | solution.py:22
  82.6 2.6 %collective-permute-start.31 = (f32[8,128]{1,0:T(8,128)S(1)}, f32[8,128]{1,0:T(8,128)S(1)}, u32[]{:S(2)}, u32[]{:S(2)}) collective-permute-start(f32[8,128]{1,0:T(8,128)S(1)} %shard_map.164.refs_0_), channel_id=1, source_target_pairs={{0,6},{1,7},{2,4},{3,5},{4,2},{5,3},{6,0},{7,1},{8,14},{9,15},{10,... | collective-permute-start | bytes 12296 | tf_op jit(solution)/shard_map/ppermute | solution.py:35
  85.2 2.3 %collective-permute-start.32 = (f32[8,128]{1,0:T(8,128)S(1)}, f32[8,128]{1,0:T(8,128)S(1)}, u32[]{:S(2)}, u32[]{:S(2)}) collective-permute-start(f32[8,128]{1,0:T(8,128)S(1)} %shard_map.164.refs_0_), channel_id=1, source_target_pairs={{0,4},{1,5},{2,6},{3,7},{4,0},{5,1},{6,2},{7,3},{8,12},{9,13},{10,... | collective-permute-start | bytes 12296 | tf_op jit(solution)/shard_map/ppermute | solution.py:35
  88.1 1.6 %collective-permute-done.32.refs_2_ = f32[8,128]{1,0:T(8,128)S(1)} collective-permute-done((f32[8,128]{1,0:T(8,128)S(1)}, f32[8,128]{1,0:T(8,128)S(1)}, u32[]{:S(2)}, u32[]{:S(2)}) %collective-permute-start.32) | collective-permute-done | bytes 4128 | tf_op jit(solution)/shard_map/ppermute | solution.py:35
  91.7 1.6 %collective-permute-start.34 = (f32[1,128]{1,0:T(1,128)S(1)}, f32[1,128]{1,0:T(1,128)S(1)}, u32[]{:S(2)}, u32[]{:S(2)}) collective-permute-start(f32[1,128]{1,0:T(1,128)S(1)} %shard_map.165), channel_id=1, source_target_pairs={{0,24},{8,16},{16,8},{24,0},{1,25},{9,17},{17,9},{25,1},{2,26},{10... | collective-permute-start | bytes 1544 | tf_op jit(solution)/shard_map/ppermute | solution.py:35
  93.7 1.5 %collective-permute-start.36 = (f32[1,128]{1,0:T(1,128)S(1)}, f32[1,128]{1,0:T(1,128)S(1)}, u32[]{:S(2)}, u32[]{:S(2)}) collective-permute-start(f32[1,128]{1,0:T(1,128)S(1)} %shard_map.165), channel_id=1, source_target_pairs={{0,8},{8,0},{16,24},{24,16},{1,9},{9,1},{17,25},{25,17},{2,10},{10... | collective-permute-start | bytes 1544 | tf_op jit(solution)/shard_map/ppermute | solution.py:35
  (70 shorter events, 26.4 us)
Async XLA Ops:
  1.6 7.5 %collective-permute-start.2 = (bf16[17,16,256]{2,1,0:T(8,128)(2,1)S(1)}, bf16[17,16,256]{2,1,0:T(8,128)(2,1)S(1)}, u32[]{:S(2)}, u32[]{:S(2)}) collective-permute-start(bf16[17,16,256]{2,1,0:T(8,128)(2,1)S(1)} %shard_map.158.refs_4_), channel_id=1, source_target_pairs={{0,16},{8,24},{16,0},{24,8},{1,17},{9,25},{17,1},{25,9},{2,18},{10... | collective-permute-start | bytes 417800 | tf_op jit(solution)/shard_map/ppermute | solution.py:35
  4.6 6.5 %collective-permute-start = (bf16[16,16,256]{2,1,0:T(8,128)(2,1)}, bf16[16,16,256]{2,1,0:T(8,128)(2,1)S(1)}, u32[]{:S(2)}, u32[]{:S(2)}) collective-permute-start(bf16[16,16,256]{2,1,0:T(8,128)(2,1)} %refs_0_.1), channel_id=1, source_target_pairs={{0,16},{8,24},{16,0},{24,8},{1,17},{9,25},{17,1},{25,9},{2,18},{10... | collective-permute-start | bytes 393224 | tf_op jit(solution)/shard_map/ppermute | solution.py:35
  4.7 6.6 %collective-permute-start.1 = (bf16[16,16,256]{2,1,0:T(8,128)(2,1)}, bf16[16,16,256]{2,1,0:T(8,128)(2,1)S(1)}, u32[]{:S(2)}, u32[]{:S(2)}) collective-permute-start(bf16[16,16,256]{2,1,0:T(8,128)(2,1)} %refs_0_.1), channel_id=1, source_target_pairs={{0,8},{8,0},{16,24},{24,16},{1,9},{9,1},{17,25},{25,17},{2,10},{10... | collective-permute-start | bytes 393224 | tf_op jit(solution)/shard_map/ppermute | solution.py:35
  6.6 8.8 %collective-permute-start.4 = (bf16[17,16,256]{2,1,0:T(8,128)(2,1)S(1)}, bf16[17,16,256]{2,1,0:T(8,128)(2,1)S(1)}, u32[]{:S(2)}, u32[]{:S(2)}) collective-permute-start(bf16[17,16,256]{2,1,0:T(8,128)(2,1)S(1)} %shard_map.158.refs_4_), channel_id=1, source_target_pairs={{0,8},{8,0},{16,24},{24,16},{1,9},{9,1},{17,25},{25,17},{2,10},{10... | collective-permute-start | bytes 417800 | tf_op jit(solution)/shard_map/ppermute | solution.py:35
  9.1 8.0 %collective-permute-start.5 = (bf16[17,16,256]{2,1,0:T(8,128)(2,1)S(1)}, bf16[17,16,256]{2,1,0:T(8,128)(2,1)S(1)}, u32[]{:S(2)}, u32[]{:S(2)}) collective-permute-start(bf16[17,16,256]{2,1,0:T(8,128)(2,1)S(1)} %collective-permute-done.2.refs_6_), channel_id=1, source_target_pairs={{0,8},{8,0},{16,24},{24,16},{1,9},{9,1},{17,25},{25,17},{2,10},{10... | collective-permute-start | bytes 417800 | tf_op jit(solution)/shard_map/ppermute | solution.py:35
  11.3 5.8 %collective-permute-start.3 = (bf16[16,16,256]{2,1,0:T(8,128)(2,1)S(1)}, bf16[16,16,256]{2,1,0:T(8,128)(2,1)S(1)}, u32[]{:S(2)}, u32[]{:S(2)}) collective-permute-start(bf16[16,16,256]{2,1,0:T(8,128)(2,1)S(1)} %collective-permute-done.1.refs_1_), channel_id=1, source_target_pairs={{0,16},{8,24},{16,0},{24,8},{1,17},{9,25},{17,1},{25,9},{2,18},{10... | collective-permute-start | bytes 393224 | tf_op jit(solution)/shard_map/ppermute | solution.py:35
  13.4 28.5 %collective-permute-start.13 = (bf16[512,896]{1,0:T(8,128)(2,1)}, bf16[512,896]{1,0:T(8,128)(2,1)S(1)}, u32[]{:S(2)}, u32[]{:S(2)}) collective-permute-start(bf16[512,896]{1,0:T(8,128)(2,1)} %refs_10_), channel_id=1, source_target_pairs={{0,8},{8,0},{16,24},{24,16},{1,9},{9,1},{17,25},{25,17},{2,10},{10... | collective-permute-start | bytes 2752520 | tf_op jit(solution)/shard_map/ppermute | solution.py:35
  14.9 27.0 %collective-permute-start.14 = (bf16[512,896]{1,0:T(8,128)(2,1)}, bf16[512,896]{1,0:T(8,128)(2,1)S(1)}, u32[]{:S(2)}, u32[]{:S(2)}) collective-permute-start(bf16[512,896]{1,0:T(8,128)(2,1)} %refs_13_), channel_id=1, source_target_pairs={{0,16},{8,24},{16,0},{24,8},{1,17},{9,25},{17,1},{25,9},{2,18},{10... | collective-permute-start | bytes 2752520 | tf_op jit(solution)/shard_map/ppermute | solution.py:35
  19.1 10.8 %collective-permute-start.6 = (bf16[2,128,256]{2,1,0:T(8,128)(2,1)S(1)}, bf16[2,128,256]{2,1,0:T(8,128)(2,1)S(1)}, u32[]{:S(2)}, u32[]{:S(2)}) collective-permute-start(bf16[2,128,256]{2,1,0:T(8,128)(2,1)S(1)} %get-tuple-element.50.refs_6_), channel_id=1, source_target_pairs={{0,4},{1,5},{2,6},{3,7},{4,0},{5,1},{6,2},{7,3},{8,12},{9,13},{10,... | collective-permute-start | bytes 393224 | tf_op jit(solution)/shard_map/ppermute | solution.py:35
  22.4 7.5 %collective-permute-start.7 = (bf16[2,128,256]{2,1,0:T(8,128)(2,1)S(1)}, bf16[2,128,256]{2,1,0:T(8,128)(2,1)S(1)}, u32[]{:S(2)}, u32[]{:S(2)}) collective-permute-start(bf16[2,128,256]{2,1,0:T(8,128)(2,1)S(1)} %get-tuple-element.50.refs_6_), channel_id=1, source_target_pairs={{0,6},{1,7},{2,4},{3,5},{4,2},{5,3},{6,0},{7,1},{8,14},{9,15},{10,... | collective-permute-start | bytes 393224 | tf_op jit(solution)/shard_map/ppermute | solution.py:35
  23.8 7.1 %collective-permute-start.8 = (bf16[2,128,256]{2,1,0:T(8,128)(2,1)S(1)}, bf16[2,128,256]{2,1,0:T(8,128)(2,1)S(1)}, u32[]{:S(2)}, u32[]{:S(2)}) collective-permute-start(bf16[2,128,256]{2,1,0:T(8,128)(2,1)S(1)} %get-tuple-element.50.refs_6_), channel_id=1, source_target_pairs={{0,2},{1,3},{2,0},{3,1},{4,6},{5,7},{6,4},{7,5},{8,10},{9,11},{10,... | collective-permute-start | bytes 393224 | tf_op jit(solution)/shard_map/ppermute | solution.py:35
  32.6 23.0 %collective-permute-start.19 = (bf16[512,896]{1,0:T(8,128)(2,1)S(1)}, bf16[512,896]{1,0:T(8,128)(2,1)S(1)}, u32[]{:S(2)}, u32[]{:S(2)}) collective-permute-start(bf16[512,896]{1,0:T(8,128)(2,1)S(1)} %copy-done), channel_id=1, source_target_pairs={{0,16},{8,24},{16,0},{24,8},{1,17},{9,25},{17,1},{25,9},{2,18},{10... | collective-permute-start | bytes 2752520 | tf_op jit(solution)/shard_map/ppermute | solution.py:35
  34.0 22.1 %collective-permute-start.20 = (bf16[512,896]{1,0:T(8,128)(2,1)S(1)}, bf16[512,896]{1,0:T(8,128)(2,1)S(1)}, u32[]{:S(2)}, u32[]{:S(2)}) collective-permute-start(bf16[512,896]{1,0:T(8,128)(2,1)S(1)} %copy-done.1), channel_id=1, source_target_pairs={{0,8},{8,0},{16,24},{24,16},{1,9},{9,1},{17,25},{25,17},{2,10},{10... | collective-permute-start | bytes 2752520 | tf_op jit(solution)/shard_map/ppermute | solution.py:35
  44.5 11.6 %collective-permute-start.16 = (bf16[2,128,256]{2,1,0:T(8,128)(2,1)S(1)}, bf16[2,128,256]{2,1,0:T(8,128)(2,1)S(1)}, u32[]{:S(2)}, u32[]{:S(2)}) collective-permute-start(bf16[2,128,256]{2,1,0:T(8,128)(2,1)S(1)} %get-tuple-element.62), channel_id=1, source_target_pairs={{0,2},{1,3},{2,0},{3,1},{4,6},{5,7},{6,4},{7,5},{8,10},{9,11},{10,... | collective-permute-start | bytes 393224 | tf_op jit(solution)/shard_map/ppermute | solution.py:35
  45.3 13.4 %collective-permute-start.17 = (bf16[2,128,256]{2,1,0:T(8,128)(2,1)S(1)}, bf16[2,128,256]{2,1,0:T(8,128)(2,1)S(1)}, u32[]{:S(2)}, u32[]{:S(2)}) collective-permute-start(bf16[2,128,256]{2,1,0:T(8,128)(2,1)S(1)} %get-tuple-element.63), channel_id=1, source_target_pairs={{0,4},{1,5},{2,6},{3,7},{4,0},{5,1},{6,2},{7,3},{8,12},{9,13},{10,... | collective-permute-start | bytes 393224 | tf_op jit(solution)/shard_map/ppermute | solution.py:35
  48.6 10.0 %collective-permute-start.18 = (bf16[2,128,256]{2,1,0:T(8,128)(2,1)S(1)}, bf16[2,128,256]{2,1,0:T(8,128)(2,1)S(1)}, u32[]{:S(2)}, u32[]{:S(2)}) collective-permute-start(bf16[2,128,256]{2,1,0:T(8,128)(2,1)S(1)} %get-tuple-element.64), channel_id=1, source_target_pairs={{0,6},{1,7},{2,4},{3,5},{4,2},{5,3},{6,0},{7,1},{8,14},{9,15},{10,... | collective-permute-start | bytes 393224 | tf_op jit(solution)/shard_map/ppermute | solution.py:35
  58.6 20.8 %collective-permute-start.28 = (bf16[512,896]{1,0:T(8,128)(2,1)S(1)}, bf16[512,896]{1,0:T(8,128)(2,1)S(1)}, u32[]{:S(2)}, u32[]{:S(2)}) collective-permute-start(bf16[512,896]{1,0:T(8,128)(2,1)S(1)} %collective-permute-done.13.refs_11_), channel_id=1, source_target_pairs={{0,16},{8,24},{16,0},{24,8},{1,17},{9,25},{17,1},{25,9},{2,18},{10... | collective-permute-start | bytes 2752520 | tf_op jit(solution)/shard_map/ppermute | solution.py:35
  59.1 20.5 %collective-permute-start.29 = (bf16[512,896]{1,0:T(8,128)(2,1)S(1)}, bf16[512,896]{1,0:T(8,128)(2,1)S(1)}, u32[]{:S(2)}, u32[]{:S(2)}) collective-permute-start(bf16[512,896]{1,0:T(8,128)(2,1)S(1)} %collective-permute-done.14.refs_15_), channel_id=1, source_target_pairs={{0,8},{8,0},{16,24},{24,16},{1,9},{9,1},{17,25},{25,17},{2,10},{10... | collective-permute-start | bytes 2752520 | tf_op jit(solution)/shard_map/ppermute | solution.py:35
  59.7 12.9 %collective-permute-start.21 = (bf16[2,128,256]{2,1,0:T(8,128)(2,1)S(1)}, bf16[2,128,256]{2,1,0:T(8,128)(2,1)S(1)}, u32[]{:S(2)}, u32[]{:S(2)}) collective-permute-start(bf16[2,128,256]{2,1,0:T(8,128)(2,1)S(1)} %add_convert_fusion.refs_2_), channel_id=1, source_target_pairs={{0,4},{1,5},{2,6},{3,7},{4,0},{5,1},{6,2},{7,3},{8,12},{9,13},{10,... | collective-permute-start | bytes 393224 | tf_op jit(solution)/shard_map/ppermute | solution.py:35
  63.5 9.1 %collective-permute-start.22 = (bf16[2,128,256]{2,1,0:T(8,128)(2,1)S(1)}, bf16[2,128,256]{2,1,0:T(8,128)(2,1)S(1)}, u32[]{:S(2)}, u32[]{:S(2)}) collective-permute-start(bf16[2,128,256]{2,1,0:T(8,128)(2,1)S(1)} %add_convert_fusion.refs_2_), channel_id=1, source_target_pairs={{0,6},{1,7},{2,4},{3,5},{4,2},{5,3},{6,0},{7,1},{8,14},{9,15},{10,... | collective-permute-start | bytes 393224 | tf_op jit(solution)/shard_map/ppermute | solution.py:35
  64.7 8.0 %collective-permute-start.23 = (bf16[2,128,256]{2,1,0:T(8,128)(2,1)S(1)}, bf16[2,128,256]{2,1,0:T(8,128)(2,1)S(1)}, u32[]{:S(2)}, u32[]{:S(2)}) collective-permute-start(bf16[2,128,256]{2,1,0:T(8,128)(2,1)S(1)} %add_convert_fusion.refs_2_), channel_id=1, source_target_pairs={{0,2},{1,3},{2,0},{3,1},{4,6},{5,7},{6,4},{7,5},{8,10},{9,11},{10,... | collective-permute-start | bytes 393224 | tf_op jit(solution)/shard_map/ppermute | solution.py:35
  82.6 5.5 %collective-permute-start.31 = (f32[8,128]{1,0:T(8,128)S(1)}, f32[8,128]{1,0:T(8,128)S(1)}, u32[]{:S(2)}, u32[]{:S(2)}) collective-permute-start(f32[8,128]{1,0:T(8,128)S(1)} %shard_map.164.refs_0_), channel_id=1, source_target_pairs={{0,6},{1,7},{2,4},{3,5},{4,2},{5,3},{6,0},{7,1},{8,14},{9,15},{10,... | collective-permute-start | bytes 12296 | tf_op jit(solution)/shard_map/ppermute | solution.py:35
  85.2 4.5 %collective-permute-start.32 = (f32[8,128]{1,0:T(8,128)S(1)}, f32[8,128]{1,0:T(8,128)S(1)}, u32[]{:S(2)}, u32[]{:S(2)}) collective-permute-start(f32[8,128]{1,0:T(8,128)S(1)} %shard_map.164.refs_0_), channel_id=1, source_target_pairs={{0,4},{1,5},{2,6},{3,7},{4,0},{5,1},{6,2},{7,3},{8,12},{9,13},{10,... | collective-permute-start | bytes 12296 | tf_op jit(solution)/shard_map/ppermute | solution.py:35
  91.7 4.5 %collective-permute-start.34 = (f32[1,128]{1,0:T(1,128)S(1)}, f32[1,128]{1,0:T(1,128)S(1)}, u32[]{:S(2)}, u32[]{:S(2)}) collective-permute-start(f32[1,128]{1,0:T(1,128)S(1)} %shard_map.165), channel_id=1, source_target_pairs={{0,24},{8,16},{16,8},{24,0},{1,25},{9,17},{17,9},{25,1},{2,26},{10... | collective-permute-start | bytes 1544 | tf_op jit(solution)/shard_map/ppermute | solution.py:35
  (15 other events, 67.4 us)
